TPU v7x, 32 devices: a whole 2x2x4 slice. The times are simulated.
32 devices in a mesh: parts: 2 (over y), branch: 4 (over x, core), tensor: 4 (over z).
Axes of the slice: x: 2, y: 2, z: 4, core: 2. Of those that a mesh axis runs over, the one named last changes fastest.
Arguments:
- layer_input: bfloat16 [2048, 3584], P(('parts', 'branch')), parts along dimension 0
- norm_gain: float32 [3584], replicated, may hold values from -2.5 to 2.5
- w_query: bfloat16 [3584, 4096], P(None, 'tensor'), may hold values from -0.09375 to 0.09375
- w_key: bfloat16 [3584, 2048], P(None, 'tensor'), may hold values from -0.09375 to 0.09375
- w_value: bfloat16 [3584, 2048], P(None, 'tensor'), may hold values from -0.09375 to 0.09375
- head_grad: bfloat16 [2048, 4096], P(('parts', 'branch'), 'tensor'), parts along dimension 0, may hold values from -6 to 6
- parents: int32 [2048], P(('parts', 'branch')), parts along dimension 0, may hold values from -1 to 126, as said below
- row_counts: int32 [16], P('parts'), parts along dimension 0, may hold values from 0 to 128, as said below
Outputs:
- grad_input: bfloat16 [2048, 3584], P(('parts', 'branch'), 'tensor'), parts along dimension 0
- grad_query: float32 [7168, 4096], P(('parts', 'branch'), 'tensor'), parts along dimension 0
- grad_key: float32 [7168, 2048], P(('parts', 'branch'), 'tensor'), parts along dimension 0
- grad_value: float32 [7168, 2048], P(('parts', 'branch'), 'tensor'), parts along dimension 0
- grad_gain: float32 [7168], P(('parts', 'tensor')), parts along dimension 0
There are 2 independent parts, one for each index of `parts`. A program takes and returns all parts, laid end to end along the dimension named above; an argument that names none is the same for every part. Nothing has to cross between parts.
Inputs may be any that keep to these rules, and one draw needn't show every extreme that they name: `row_counts`: the 2 blocks of one branch index (blocks b * 2 to b * 2 + 1) hold their live trees first; a live tree has 32 to 128 rows, an empty block 0. `parents`: inside its block a row's parent is an earlier row of that block; the first row of every block has parent -1.
All inputs are finite; a program needn't handle non-finite values.
Results may differ from a plain program's by a relative error of at most 0.011.
Values may be sent and summed in bfloat16 or wider, within the bound.
No kernel may reach another device: no remote copies, remote signals or barrier semaphores. Data moves between devices by JAX's collectives and lax.ppermute only.
A program may use at most 128 MiB of HBM per device.

v0:
```python
import jax
import jax.numpy as jnp
from jax import lax
from jax.sharding import PartitionSpec as P

HEAD_DIM = 256


epsilon = 1e-06
softcap_limit = 50.0


def ancestor_mask(parent_rows):
    row_total = parent_rows.shape[0]
    position = jnp.arange(row_total, dtype=jnp.int32)
    reached = (parent_rows[:, None] == position[None, :]).astype(jnp.float32)
    reached = reached + (position[:, None] == position[None, :]).astype(jnp.float32)
    for squaring in range(row_total.bit_length() - 1):
        halfway = reached.astype(jnp.bfloat16)
        reached = jnp.minimum(jnp.dot(halfway, halfway, preferred_element_type=jnp.float32), 1.0)
    return reached > 0.5


def normalize(tree_input, norm_gain):
    values = tree_input.astype(jnp.float32)
    inverse = lax.rsqrt(jnp.mean(values * values, axis=-1, keepdims=True) + epsilon)
    scaled = values * inverse
    normed = (scaled * (1.0 + norm_gain)).astype(jnp.bfloat16)
    return (inverse, scaled, normed)


def attention_backward(
    normed, tree_grad, parent_rows, row_count, w_query, w_key, w_value, kv_heads, head_dim
):
    row_total = normed.shape[0]
    queries = jnp.dot(normed, w_query, preferred_element_type=jnp.float32).astype(jnp.bfloat16)
    key_rows = jnp.dot(normed, w_key, preferred_element_type=jnp.float32).astype(jnp.bfloat16)
    value_rows = jnp.dot(normed, w_value, preferred_element_type=jnp.float32).astype(jnp.bfloat16)
    group_size = queries.shape[1] // head_dim // kv_heads
    query_four = queries.reshape(row_total, kv_heads, group_size, head_dim)
    key_three = key_rows.reshape(row_total, kv_heads, head_dim)
    value_three = value_rows.reshape(row_total, kv_heads, head_dim)
    live_rows = jnp.arange(row_total, dtype=jnp.int32) < row_count
    grad_live = jnp.where(live_rows[:, None], tree_grad, jnp.zeros_like(tree_grad))
    grad_four = grad_live.reshape(row_total, kv_heads, group_size, head_dim)
    scale_factor = head_dim ** (-0.5)
    scores = (
        jnp.einsum("ikgd,jkd->kgij", query_four, key_three, preferred_element_type=jnp.float32)
        * scale_factor
    )
    bounded = jnp.tanh(scores / softcap_limit)
    allowed = ancestor_mask(parent_rows)
    weights = jnp.where(allowed[None, None], jnp.exp(softcap_limit * bounded), 0.0)
    probabilities = weights / jnp.sum(weights, axis=-1, keepdims=True)
    d_probs = jnp.einsum(
        "ikgd,jkd->kgij", grad_four, value_three, preferred_element_type=jnp.float32
    )
    d_scores = probabilities * (d_probs - jnp.sum(probabilities * d_probs, axis=-1, keepdims=True))
    d_raw = (d_scores * (1.0 - bounded * bounded) * scale_factor).astype(jnp.bfloat16)
    prob_half = probabilities.astype(jnp.bfloat16)
    d_query = (
        jnp.einsum("kgij,jkd->ikgd", d_raw, key_three, preferred_element_type=jnp.float32)
        .reshape(row_total, -1)
        .astype(jnp.bfloat16)
    )
    d_key = (
        jnp.einsum("kgij,ikgd->jkd", d_raw, query_four, preferred_element_type=jnp.float32)
        .reshape(row_total, -1)
        .astype(jnp.bfloat16)
    )
    d_value = (
        jnp.einsum("kgij,ikgd->jkd", prob_half, grad_four, preferred_element_type=jnp.float32)
        .reshape(row_total, -1)
        .astype(jnp.bfloat16)
    )
    return (d_query, d_key, d_value)


def transpose_dot(left, right):
    return lax.dot_general(
        left, right, (((0,), (0,)), ((), ())), preferred_element_type=jnp.float32
    )


def back_dot(left, right):
    return lax.dot_general(
        left, right, (((1,), (1,)), ((), ())), preferred_element_type=jnp.float32
    )


def local(layer_input, norm_gain, w_query, w_key, w_value, head_grad, parents, row_counts):
    branch_total = lax.axis_size("branch")
    branch_index = lax.axis_index("branch")
    tensor_total = lax.axis_size("tensor")
    tensor_index = lax.axis_index("tensor")
    slot_total = row_counts.shape[0] // branch_total
    block_rows = layer_input.shape[0] // slot_total
    model_width = layer_input.shape[1]
    column_width = model_width // tensor_total
    head_dim = HEAD_DIM
    kv_local = w_key.shape[1] // head_dim
    move_slots = slot_total // 2
    column_start = tensor_index * column_width
    counts_grid = row_counts.reshape(branch_total, slot_total)
    tree_loads = jnp.sum((counts_grid > 0).astype(jnp.int32), axis=1)
    own_load = lax.dynamic_index_in_dim(tree_loads, branch_index, 0, keepdims=False)
    own_counts = lax.dynamic_index_in_dim(counts_grid, branch_index, 0, keepdims=False)
    input_slots = layer_input.reshape(slot_total, block_rows, model_width)
    grad_slots = head_grad.reshape(slot_total, block_rows, head_grad.shape[1])
    parent_slots = parents.reshape(slot_total, block_rows)

    def one_tree(tree_slot, carried_state):
        acc_query, acc_key, acc_value, acc_gain, grad_buffer = carried_state
        tree_input = lax.dynamic_index_in_dim(input_slots, tree_slot, 0, keepdims=False)
        tree_grad = lax.dynamic_index_in_dim(grad_slots, tree_slot, 0, keepdims=False)
        parent_rows = lax.dynamic_index_in_dim(parent_slots, tree_slot, 0, keepdims=False)
        stored_count = lax.dynamic_index_in_dim(own_counts, tree_slot, 0, keepdims=False)
        row_count = jnp.where(tree_slot < own_load, stored_count, 0)
        inverse, scaled, normed = normalize(tree_input, norm_gain)
        d_query, d_key, d_value = attention_backward(
            normed, tree_grad, parent_rows, row_count, w_query, w_key, w_value, kv_local, head_dim
        )
        partial_rows = (
            back_dot(d_query, w_query) + back_dot(d_key, w_key) + back_dot(d_value, w_value)
        )
        d_normed = lax.psum(partial_rows, "tensor")
        adjusted = (1.0 + norm_gain) * d_normed
        centred = jnp.mean(scaled * adjusted, axis=-1, keepdims=True)
        grad_full = inverse * (adjusted - scaled * centred)
        grad_columns = lax.dynamic_slice_in_dim(grad_full, column_start, column_width, 1)
        gain_term = lax.dynamic_slice_in_dim(
            jnp.sum(d_normed * scaled, axis=0), column_start, column_width
        )
        grad_buffer = lax.dynamic_update_index_in_dim(
            grad_buffer, grad_columns.astype(jnp.bfloat16), tree_slot, 0
        )
        acc_query = acc_query + transpose_dot(normed, d_query)
        acc_key = acc_key + transpose_dot(normed, d_key)
        acc_value = acc_value + transpose_dot(normed, d_value)
        acc_gain = acc_gain + gain_term
        return (acc_query, acc_key, acc_value, acc_gain, grad_buffer)

    initial = (
        jnp.zeros((model_width, w_query.shape[1]), jnp.float32),
        jnp.zeros((model_width, w_key.shape[1]), jnp.float32),
        jnp.zeros((model_width, w_value.shape[1]), jnp.float32),
        jnp.zeros((column_width,), jnp.float32),
        jnp.zeros((slot_total + move_slots, block_rows, column_width), jnp.bfloat16),
    )
    acc_query, acc_key, acc_value, acc_gain, grad_buffer = lax.fori_loop(
        0, slot_total, one_tree, initial
    )
    owned = (jnp.arange(slot_total, dtype=jnp.int32) < own_load)[:, None, None]
    grad_owned = jnp.where(
        owned, grad_buffer[:slot_total], jnp.zeros_like(grad_buffer[:slot_total])
    )
    grad_input = grad_owned.reshape(slot_total * block_rows, column_width)
    grad_query, grad_key, grad_value = (
        lax.psum_scatter(acc_query, "branch", scatter_dimension=0, tiled=True),
        lax.psum_scatter(acc_key, "branch", scatter_dimension=0, tiled=True),
        lax.psum_scatter(acc_value, "branch", scatter_dimension=0, tiled=True),
    )
    grad_gain = lax.psum(acc_gain, "branch")
    return (grad_input, grad_query, grad_key, grad_value, grad_gain)


def solution(mesh):
    placed = (
        P(("parts", "branch"), None),
        P(),
        P(None, "tensor"),
        P(None, "tensor"),
        P(None, "tensor"),
        P(("parts", "branch"), "tensor"),
        P(("parts", "branch")),
        P("parts"),
    )
    return jax.shard_map(
        local,
        mesh=mesh,
        in_specs=placed,
        out_specs=(
            P(("parts", "branch"), "tensor"),
            P(("parts", "branch"), "tensor"),
            P(("parts", "branch"), "tensor"),
            P(("parts", "branch"), "tensor"),
            P(("parts", "tensor")),
        ),
        check_vma=False,
    )
```

profile of v0, /device:TPU:0, one launch (start us, length us, event | category | flops | bytes accessed | tf_op | source)
XLA Modules:
  0.0 497.2 jit_solution(17397288881742681486)
XLA Ops:
  8.0 0.7 reshape.227
  8.9 0.6 dynamic_slice.72
  9.5 0.9 broadcast_in_dim.111
  10.4 226.9 %while.24 = (s32[]{:T(128)}, f32[3584,1024]{1,0:T(8,128)}, f32[3584,512]{1,0:T(8,128)}, f32[3584,512]{1,0:T(8,128)}, f32[896]{0:T(1024)}, /*index=5*/bf16[3,128,...) while((s32[]{:T(128)}, f32[3584,1024]{1,0:T(8,128)}, ...), condition=%wide.region_8.9_spmd.clone, body=%wide.region_1.8_spmd.clone.sunk | while | flops 5869865984 | bytes 170434208 | solution.py:150
  10.4 1.4 fusion.159
  11.9 0.7 broadcast_add_fusion.2
  12.6 4.7 convolution_convert_fusion.10
  17.5 2.7 convolution_convert_fusion.8
  21.5 0.7 copy.61
  22.2 2.8 convolution_convert_fusion.9
  27.7 1.0 fusion.165
  28.7 0.9 convolution_bitcast_fusion.4
  29.6 1.2 fusion.166
  31.5 5.8 %fusion.168 = f32[128,3584]{1,0:T(8,128)S(1)} fusion(bf16[128,1024]{0,1:T(8,128)(2,1)S(1)} %bitcast.221, bf16[3584,1024]{1,0:T(8,128)(2,1)} %get-tuple-element.652), kind=kOutput, calls=%fused_computation.102.clone.1 | convolution fusion | flops 939524096 | bytes 9437184 | tf_op jit(solution)/shard_map/while/body/eval_jaxpr/dot_general | solution.py:86
  37.3 1.3 convolution_add_fusion.4
  38.7 0.7 copy-done.2
  39.3 2.6 convolution_add_fusion.5
  42.6 4.2 select_add_fusion.9
  46.7 4.2 select_add_fusion.10
  50.9 7.4 %select_add_fusion.8 = f32[3584,1024]{1,0:T(8,128)} fusion(f32[3584,1024]{1,0:T(8,128)} %get-tuple-element.625, bf16[128,1024]{0,1:T(8,128)(2,1)S(1)} %bitcast.222, pred[]{:T(512)S(6)} %compare.3, f32[3584]{0:T(1024)S(1)} %broadcast_add_fusion.2, f32[128]{0:T(128)S(1)} %copy-done.8, bf16[2,128,3584]{2,1,0:T(8,128)(2,1)S(1)} %copy-done, s32[]{:T(128)S(6)} %copy.71), kind=kOutput, calls=%fused_computation.1.clone.1 | convolution fusion | flops 948699136 | bytes 30556676 | tf_op jit(solution)/shard_map/while/body/eval_jaxpr/dot_general | solution.py:80
  58.3 64.2 %all-reduce.2.cloned.1.call-done = f32[128,3584]{1,0:T(8,128)} async-done(((f32[128,3584]{1,0:T(8,128)}), f32[128,3584]{1,0:T(8,128)}) %all-reduce.2.cloned.1.call-update) | async-done | bytes 1835024 | tf_op jit(solution)/shard_map/while/body/eval_jaxpr/psum | solution.py:126
  122.5 2.2 multiply_reduce_fusion.4
  124.8 0.8 fusion.169
  125.7 1.5 fusion.159
  127.2 0.7 broadcast_add_fusion.2
  127.9 4.7 convolution_convert_fusion.10
  132.8 2.7 convolution_convert_fusion.8
  136.8 0.7 copy.61
  137.5 2.8 convolution_convert_fusion.9
  143.0 1.0 fusion.165
  144.0 0.9 convolution_bitcast_fusion.4
  144.9 1.2 fusion.166
  146.8 5.8 %fusion.168 = f32[128,3584]{1,0:T(8,128)S(1)} fusion(bf16[128,1024]{0,1:T(8,128)(2,1)S(1)} %bitcast.221, bf16[3584,1024]{1,0:T(8,128)(2,1)} %get-tuple-element.652), kind=kOutput, calls=%fused_computation.102.clone.1 | convolution fusion | flops 939524096 | bytes 9437184 | tf_op jit(solution)/shard_map/while/body/eval_jaxpr/dot_general | solution.py:86
  152.6 1.3 convolution_add_fusion.4
  153.9 0.7 copy-done.2
  154.6 2.6 convolution_add_fusion.5
  157.9 7.2 %select_add_fusion.9 = f32[3584,512]{1,0:T(8,128)} fusion(f32[3584,512]{1,0:T(8,128)} %get-tuple-element.626, bf16[128,512]{0,1:T(8,128)(2,1)S(1)} %bitcast.226, pred[]{:T(512)S(6)} %compare.3, f32[3584]{0:T(1024)S(1)} %broadcast_add_fusion.2, f32[128]{0:T(128)S(1)} %copy-done.8, bf16[2,128,3584]{2,1,0:T(8,128)(2,1)S(1)} %copy-done, s32[]{:T(128)S(6)} %copy.71), kind=kOutput, calls=%fused_computation.3.clone.1 | convolution fusion | flops 475267072 | bytes 15745541 | tf_op jit(solution)/shard_map/while/body/eval_jaxpr/dot_general | solution.py:80
  165.1 7.3 %select_add_fusion.10 = f32[3584,512]{1,0:T(8,128)} fusion(f32[3584,512]{1,0:T(8,128)} %get-tuple-element.627, bf16[128,512]{0,1:T(8,128)(2,1)S(1)} %bitcast.228, pred[]{:T(512)S(6)} %compare.3, f32[3584]{0:T(1024)S(1)} %broadcast_add_fusion.2, f32[128]{0:T(128)S(1)} %copy-done.8, bf16[2,128,3584]{2,1,0:T(8,128)(2,1)S(1)} %copy-done, s32[]{:T(128)S(6)} %copy.71), kind=kOutput, calls=%fused_computation.2.clone.1 | convolution fusion | flops 475267072 | bytes 15745541 | tf_op jit(solution)/shard_map/while/body/eval_jaxpr/dot_general | solution.py:80
  172.4 12.7 %select_add_fusion.8 = f32[3584,1024]{1,0:T(8,128)} fusion(f32[3584,1024]{1,0:T(8,128)} %get-tuple-element.625, bf16[128,1024]{0,1:T(8,128)(2,1)S(1)} %bitcast.222, pred[]{:T(512)S(6)} %compare.3, f32[3584]{0:T(1024)S(1)} %broadcast_add_fusion.2, f32[128]{0:T(128)S(1)} %copy-done.8, bf16[2,128,3584]{2,1,0:T(8,128)(2,1)S(1)} %copy-done, s32[]{:T(128)S(6)} %copy.71), kind=kOutput, calls=%fused_computation.1.clone.1 | convolution fusion | flops 948699136 | bytes 30556676 | tf_op jit(solution)/shard_map/while/body/eval_jaxpr/dot_general | solution.py:80
  185.0 49.1 %all-reduce.2.cloned.1.call-done = f32[128,3584]{1,0:T(8,128)} async-done(((f32[128,3584]{1,0:T(8,128)}), f32[128,3584]{1,0:T(8,128)}) %all-reduce.2.cloned.1.call-update) | async-done | bytes 1835024 | tf_op jit(solution)/shard_map/while/body/eval_jaxpr/psum | solution.py:126
  234.2 2.2 multiply_reduce_fusion.4
  236.5 0.8 fusion.169
  239.2 6.2 %psum.21 = f32[896]{0:T(1024)} all-reduce(f32[896]{0:T(1024)S(1)} %copy-done.12), channel_id=1, replica_groups=mesh['parts'=2,'branch'=4,'tensor'=4] {'branch'}, use_global_device_ids=true, to_apply=%region_12.13 | all-reduce | flops 896 | bytes 7168 | tf_op jit(solution)/shard_map/psum | solution.py:163
  245.4 0.6 iota_compare_fusion.3
  246.1 0.9 slice_select_fusion
  247.0 58.2 %reduce-scatter.6.cloned.1.call-done = f32[896,512]{1,0:T(8,128)} async-done(((f32[3584,512]{1,0:T(8,128)}), f32[896,512]{1,0:T(8,128)}) %reduce-scatter.6.cloned.1.call-update) | async-done | bytes 1835024 | tf_op jit(solution)/shard_map/reduce_scatter | solution.py:160
  305.2 68.5 %reduce-scatter.8.cloned.1.call-done = f32[896,512]{1,0:T(8,128)} async-done(((f32[3584,512]{1,0:T(8,128)}), f32[896,512]{1,0:T(8,128)}) %reduce-scatter.8.cloned.1.call-update) | async-done | bytes 1835024 | tf_op jit(solution)/shard_map/reduce_scatter | solution.py:161
  373.7 115.9 %reduce-scatter.4.cloned.1.call-done = f32[896,1024]{1,0:T(8,128)} async-done(((f32[3584,1024]{1,0:T(8,128)}), f32[896,1024]{1,0:T(8,128)}) %reduce-scatter.4.cloned.1.call-update) | async-done | bytes 3670032 | tf_op jit(solution)/shard_map/reduce_scatter | solution.py:159
  (114 shorter events, 10.3 us)
Async XLA Ops:
  10.4 14.7 %copy-start.15 = (s32[2]{0:T(128)}, s32[2]{0:T(128)S(1)}, u32[]{:S(2)}) copy-start(s32[2]{0:T(128)S(1)} %get-tuple-element.655) | copy-start | bytes 28 | tf_op jit(solution)/shard_map/while
  10.4 112.1 %all-reduce.2.cloned.1.call-start = ((), (), s32[]{:S(2)}) async-start(), calls=%async_computation.6 | async-start | bytes 3670016 | tf_op jit(solution)/shard_map/while/body/eval_jaxpr/psum | solution.py:126
  11.9 10.3 %copy-start.7 = (f32[128]{0:T(128)}, f32[128]{0:T(128)S(1)}, u32[]{:S(2)}) copy-start(f32[128]{0:T(128)S(1)} %add_rsqrt_fusion.2) | copy-start | bytes 1540 | tf_op jit(solution)/shard_map/while
  12.6 4.8 copy-start
  17.5 2.9 copy-start.14
  20.4 7.3 %copy-start.4 = (bf16[128,2,256,1]{0,2,3,1:T(8,128)(2,1)}, bf16[128,2,256,1]{0,2,3,1:T(8,128)(2,1)S(1)}, u32[]{:S(2)}) copy-start(bf16[128,2,256,1]{0,2,3,1:T(8,128)(2,1)S(1)} %copy.59) | copy-start | bytes 393220 | tf_op jit(solution)/shard_map/while
  22.2 5.3 %copy-start.3 = (bf16[2,128,1024]{2,1,0:T(8,128)(2,1)S(1)}, bf16[2,128,1024]{2,1,0:T(8,128)(2,1)}, u32[]{:S(2)}) copy-start(bf16[2,128,1024]{2,1,0:T(8,128)(2,1)} %get-tuple-element.656) | copy-start | bytes 1572868 | tf_op jit(solution)/shard_map/while
  27.5 3.3 copy-start.9
  28.7 2.1 copy-start.5
  29.6 1.6 copy-start.13
  31.5 5.8 %copy-start.1 = (bf16[3584,512]{1,0:T(8,128)(2,1)S(1)}, bf16[3584,512]{1,0:T(8,128)(2,1)}, u32[]{:S(2)}) copy-start(bf16[3584,512]{1,0:T(8,128)(2,1)} %get-tuple-element.650) | copy-start | bytes 11010052 | tf_op jit(solution)/shard_map/while
  37.3 2.0 copy-start.2
  41.9 0.6 copy-start.8
  58.3 66.4 %copy-start.10 = (f32[896]{0:T(1024)S(1)}, f32[896]{0:T(1024)}, u32[]{:S(2)}) copy-start(f32[896]{0:T(1024)} %get-tuple-element.628) | copy-start | bytes 10756 | tf_op jit(solution)/shard_map/while
  58.3 67.3 %copy-start.16 = (s32[2]{0:T(128)S(1)}, s32[2]{0:T(128)}, u32[]{:S(2)}) copy-start(s32[2]{0:T(128)} %copy-done.15) | copy-start | bytes 28 | tf_op jit(solution)/shard_map/while
  124.8 0.9 copy-start.11
  125.7 14.7 %copy-start.15 = (s32[2]{0:T(128)}, s32[2]{0:T(128)S(1)}, u32[]{:S(2)}) copy-start(s32[2]{0:T(128)S(1)} %get-tuple-element.655) | copy-start | bytes 28 | tf_op jit(solution)/shard_map/while
  125.7 108.5 %all-reduce.2.cloned.1.call-start = ((), (), s32[]{:S(2)}) async-start(), calls=%async_computation.6 | async-start | bytes 3670016 | tf_op jit(solution)/shard_map/while/body/eval_jaxpr/psum | solution.py:126
  127.2 10.3 %copy-start.7 = (f32[128]{0:T(128)}, f32[128]{0:T(128)S(1)}, u32[]{:S(2)}) copy-start(f32[128]{0:T(128)S(1)} %add_rsqrt_fusion.2) | copy-start | bytes 1540 | tf_op jit(solution)/shard_map/while
  127.9 4.8 copy-start
  132.8 2.9 copy-start.14
  135.7 7.3 %copy-start.4 = (bf16[128,2,256,1]{0,2,3,1:T(8,128)(2,1)}, bf16[128,2,256,1]{0,2,3,1:T(8,128)(2,1)S(1)}, u32[]{:S(2)}) copy-start(bf16[128,2,256,1]{0,2,3,1:T(8,128)(2,1)S(1)} %copy.59) | copy-start | bytes 393220 | tf_op jit(solution)/shard_map/while
  137.5 5.3 %copy-start.3 = (bf16[2,128,1024]{2,1,0:T(8,128)(2,1)S(1)}, bf16[2,128,1024]{2,1,0:T(8,128)(2,1)}, u32[]{:S(2)}) copy-start(bf16[2,128,1024]{2,1,0:T(8,128)(2,1)} %get-tuple-element.656) | copy-start | bytes 1572868 | tf_op jit(solution)/shard_map/while
  142.8 3.3 copy-start.9
  144.0 2.1 copy-start.5
  144.9 1.6 copy-start.13
  146.8 5.8 %copy-start.1 = (bf16[3584,512]{1,0:T(8,128)(2,1)S(1)}, bf16[3584,512]{1,0:T(8,128)(2,1)}, u32[]{:S(2)}) copy-start(bf16[3584,512]{1,0:T(8,128)(2,1)} %get-tuple-element.650) | copy-start | bytes 11010052 | tf_op jit(solution)/shard_map/while
  152.6 2.0 copy-start.2
  157.2 0.6 copy-start.8
  185.0 51.4 %copy-start.10 = (f32[896]{0:T(1024)S(1)}, f32[896]{0:T(1024)}, u32[]{:S(2)}) copy-start(f32[896]{0:T(1024)} %get-tuple-element.628) | copy-start | bytes 10756 | tf_op jit(solution)/shard_map/while
  185.0 52.3 %copy-start.16 = (s32[2]{0:T(128)S(1)}, s32[2]{0:T(128)}, u32[]{:S(2)}) copy-start(s32[2]{0:T(128)} %copy-done.15) | copy-start | bytes 28 | tf_op jit(solution)/shard_map/while
  236.5 0.8 copy-start.11
  237.3 67.9 %reduce-scatter.6.cloned.1.call-start = ((), (), s32[]{:S(2)}) async-start(), calls=%async_computation.4 | async-start | bytes 9175040 | tf_op jit(solution)/shard_map/reduce_scatter | solution.py:160
  237.9 135.8 %reduce-scatter.8.cloned.1.call-start = ((), (), s32[]{:S(2)}) async-start(), calls=%async_computation.5 | async-start | bytes 9175040 | tf_op jit(solution)/shard_map/reduce_scatter | solution.py:161
  238.5 251.1 %reduce-scatter.4.cloned.1.call-start = ((), (), s32[]{:S(2)}) async-start(), calls=%async_computation.3 | async-start | bytes 18350080 | tf_op jit(solution)/shard_map/reduce_scatter | solution.py:159
  238.5 0.7 copy-start.12
  238.5 7.5 %copy-start.6 = (bf16[3,128,896]{2,1,0:T(8,128)(2,1)S(1)}, bf16[3,128,896]{2,1,0:T(8,128)(2,1)}, u32[]{:S(2)}) copy-start(bf16[3,128,896]{2,1,0:T(8,128)(2,1)} %get-tuple-element.387) | copy-start | bytes 2064388
Sparse Core Ops, SparseCore 0:
  42.1 80.3 all-reduce.1
  157.4 76.7 all-reduce.1
Sparse Core Ops, SparseCore 1:
  240.9 64.3 reduce-scatter.5
  308.3 65.3 reduce-scatter.7
  376.7 112.8 reduce-scatter.3
where the time goes:
time: 498 us; the launch traced here: 497 us
  waiting for transfers between devices  357 us (72%)
  matrix products  92.2 us (19%)
  between operations  15.7 us (3%)
  other arithmetic  13.3 us (3%)
  local copies, waits for them, and re-layouts  8.91 us (2%)
  blocking collectives  6.22 us (1%)
    reduce_scatter x1, waiting for transfers between devices, local(): lax.psum_scatter(acc_query, 'branch', scatter_dimension=0, tiled=True)  116 us
    psum x2, waiting for transfers between devices, one_tree(): d_normed = lax.psum(partial_rows, 'tensor')  113 us
    reduce_scatter x1, waiting for transfers between devices, local(): lax.psum_scatter(acc_value, 'branch', scatter_dimension=0, tiled=True)  68.5 us
    reduce_scatter x1, waiting for transfers between devices, local(): lax.psum_scatter(acc_key, 'branch', scatter_dimension=0, tiled=True)  58.2 us
    dot_general x6, matrix products, transpose_dot(): lax.dot_general(left, right, (((0,), (0,)), ((), ())), preferred_element_...  42.9 us
    dot_general x6, matrix products, back_dot(): lax.dot_general(left, right, (((1,), (1,)), ((), ())), preferred_element_...  19.5 us
  transfers between devices with their start and end apart: 5, of which 5 were waited for; matrix products, arithmetic and copies ran while one was open for 9% of the time, Pallas kernels for 0%

commit v1 on v0

v1 whole, which is shorter than its diff:
```python
import functools

import jax
import jax.numpy as jnp
from jax import lax
from jax.experimental import pallas as pl
from jax.experimental.pallas import tpu as pltpu
from jax.sharding import PartitionSpec as P

HEAD_DIM = 256
MIB = 1024 * 1024

epsilon = 1e-06
softcap_limit = 50.0


def nn_dot(left, right):
    return lax.dot_general(
        left, right, (((1,), (0,)), ((), ())), preferred_element_type=jnp.float32
    )


def nt_dot(left, right):
    return lax.dot_general(
        left, right, (((1,), (1,)), ((), ())), preferred_element_type=jnp.float32
    )


def tn_dot(left, right):
    return lax.dot_general(
        left, right, (((0,), (0,)), ((), ())), preferred_element_type=jnp.float32
    )


def norm_kernel(targets, input_ref, gain_ref, normed_ref, inverse_ref, *rest):
    piece_refs, turned = rest[:-1], rest[-1]
    rows, width = input_ref.shape
    values = input_ref[...].astype(jnp.float32)
    inverse = lax.rsqrt(jnp.mean(values * values, axis=-1, keepdims=True) + epsilon)
    inverse_ref[...] = inverse
    normed = (values * inverse * (1.0 + gain_ref[...])).astype(jnp.bfloat16)
    normed_ref[...] = normed
    turned[...] = normed.T
    depth = width // len(piece_refs)
    for target, piece_ref in zip(targets(), piece_refs):
        start = pl.multiple_of(target * depth, 16)
        piece_ref[...] = turned[pl.ds(start, depth), :]


def normalize(layer_input, norm_gain, targets, pieces):
    rows, width = layer_input.shape
    vmem = pl.BlockSpec(memory_space=pltpu.VMEM)
    out = pl.pallas_call(
        functools.partial(norm_kernel, targets),
        out_shape=(
            jax.ShapeDtypeStruct((rows, width), jnp.bfloat16),
            jax.ShapeDtypeStruct((rows, 1), jnp.float32),
        )
        + (jax.ShapeDtypeStruct((width // pieces, rows), jnp.bfloat16),) * pieces,
        in_specs=[vmem, vmem],
        out_specs=(vmem,) * (2 + pieces),
        scratch_shapes=[pltpu.VMEM((width, rows), jnp.bfloat16)],
        compiler_params=pltpu.CompilerParams(vmem_limit_bytes=40 * MIB),
        name="norm",
    )(layer_input, norm_gain.reshape(1, width))
    return out[0], out[1], out[2:]


def ancestor_mask(parent_column):
    rows = parent_column.shape[0]
    row = lax.broadcasted_iota(jnp.int32, (rows, rows), 0)
    column = lax.broadcasted_iota(jnp.int32, (rows, rows), 1)
    reached = jnp.where((parent_column == column) | (row == column), 1.0, 0.0)
    for squaring in range(rows.bit_length() - 1):
        halfway = reached.astype(jnp.bfloat16)
        reached = jnp.minimum(nn_dot(halfway, halfway), 1.0)
    return reached


def attention_kernel(
    slots,
    count_ref,
    normed_ref,
    query_ref,
    key_ref,
    value_ref,
    grad_ref,
    parent_ref,
    delta_ref,
    centre_ref,
    allowed_ref,
):
    head_dim = HEAD_DIM
    block = normed_ref.shape[0] // slots
    group = query_ref.shape[1] // head_dim
    step = pl.program_id(0)

    @pl.when(step == 0)
    def _():
        centre_ref[...] = jnp.zeros_like(centre_ref)
        for slot in range(slots):
            allowed_ref[slot] = ancestor_mask(parent_ref[slot * block : (slot + 1) * block, :])

    normed = normed_ref[...]
    query_sum = nn_dot(normed, query_ref[...])
    key_sum = nn_dot(normed, key_ref[...])
    value_sum = nn_dot(normed, value_ref[...])
    scale = head_dim ** (-0.5)
    for slot in range(slots):
        rows = slice(slot * block, (slot + 1) * block)
        query_parts = [
            query_sum[rows, g * head_dim : (g + 1) * head_dim] for g in range(group)
        ]
        queries = jnp.concatenate(query_parts, axis=0).astype(jnp.bfloat16)
        keys = key_sum[rows].astype(jnp.bfloat16)
        values = value_sum[rows].astype(jnp.bfloat16)
        live = lax.broadcasted_iota(jnp.int32, (block, head_dim), 0) < count_ref[slot]
        grads = jnp.concatenate(
            [
                jnp.where(
                    live,
                    grad_ref[rows, g * head_dim : (g + 1) * head_dim].astype(jnp.float32),
                    0.0,
                )
                for g in range(group)
            ],
            axis=0,
        ).astype(jnp.bfloat16)
        allowed = jnp.concatenate([allowed_ref[slot]] * group, axis=0) > 0.5
        bounded = jnp.tanh(nt_dot(queries, keys) * (scale / softcap_limit))
        weights = jnp.where(allowed, jnp.exp(softcap_limit * bounded), 0.0)
        probabilities = weights / jnp.sum(weights, axis=-1, keepdims=True)
        d_probs = nt_dot(grads, values)
        d_scores = probabilities * (
            d_probs - jnp.sum(probabilities * d_probs, axis=-1, keepdims=True)
        )
        d_raw = (d_scores * (1.0 - bounded * bounded) * scale).astype(jnp.bfloat16)
        prob_half = probabilities.astype(jnp.bfloat16)
        d_query = nn_dot(d_raw, keys).astype(jnp.bfloat16)
        d_key = tn_dot(d_raw, queries).astype(jnp.bfloat16)
        d_value = tn_dot(prob_half, grads).astype(jnp.bfloat16)
        centre = jnp.sum(
            d_key.astype(jnp.float32) * key_sum[rows]
            + d_value.astype(jnp.float32) * value_sum[rows],
            axis=-1,
            keepdims=True,
        )
        for g in range(group):
            part = d_query[g * block : (g + 1) * block]
            delta_ref[rows, g * head_dim : (g + 1) * head_dim] = part
            centre += jnp.sum(
                part.astype(jnp.float32) * query_parts[g], axis=-1, keepdims=True
            )
        delta_ref[rows, group * head_dim : (group + 1) * head_dim] = d_key
        delta_ref[rows, (group + 1) * head_dim : (group + 2) * head_dim] = d_value
        centre_ref[rows, :] += centre


def attention_backward(normed, w_query, w_key, w_value, head_grad, parents, counts):
    rows, width = normed.shape
    slots = counts.shape[0]
    kv_local = w_key.shape[1] // HEAD_DIM
    group = w_query.shape[1] // w_key.shape[1]
    delta_width = (group + 2) * HEAD_DIM
    block = rows // slots
    whole = lambda h: (0, 0)
    by_head = lambda h: (0, h)
    return pl.pallas_call(
        functools.partial(attention_kernel, slots),
        out_shape=(
            jax.ShapeDtypeStruct((rows, kv_local * delta_width), jnp.bfloat16),
            jax.ShapeDtypeStruct((rows, 1), jnp.float32),
        ),
        grid=(kv_local,),
        in_specs=[
            pl.BlockSpec(memory_space=pltpu.SMEM),
            pl.BlockSpec((rows, width), whole),
            pl.BlockSpec((width, group * HEAD_DIM), by_head),
            pl.BlockSpec((width, HEAD_DIM), by_head),
            pl.BlockSpec((width, HEAD_DIM), by_head),
            pl.BlockSpec((rows, group * HEAD_DIM), by_head),
            pl.BlockSpec((rows, 1), whole),
        ],
        out_specs=(
            pl.BlockSpec((rows, delta_width), by_head),
            pl.BlockSpec((rows, 1), whole),
        ),
        scratch_shapes=[pltpu.VMEM((slots, block, block), jnp.float32)],
        compiler_params=pltpu.CompilerParams(vmem_limit_bytes=48 * MIB),
        name="attention",
    )(counts, normed, w_query, w_key, w_value, head_grad, parents.reshape(rows, 1))


def back_kernel(order_ref, delta_ref, query_ref, key_ref, value_ref, *out_refs):
    del order_ref
    step = pl.program_id(0)
    head_dim = HEAD_DIM
    kv_local = key_ref.shape[1] // head_dim
    group = query_ref.shape[1] // key_ref.shape[1]
    span = (group + 2) * head_dim
    total = None
    for h in range(kv_local):
        base = h * span
        mid = base + group * head_dim
        term = nt_dot(
            delta_ref[:, base:mid],
            query_ref[:, h * group * head_dim : (h + 1) * group * head_dim],
        )
        term += nt_dot(
            delta_ref[:, mid : mid + head_dim], key_ref[:, h * head_dim : (h + 1) * head_dim]
        )
        term += nt_dot(
            delta_ref[:, mid + head_dim : mid + 2 * head_dim],
            value_ref[:, h * head_dim : (h + 1) * head_dim],
        )
        total = term if total is None else total + term
    total = total.astype(jnp.bfloat16)
    for place, out_ref in enumerate(out_refs):

        @pl.when(step == place)
        def _():
            out_ref[...] = total


def back_project(order, delta, w_query, w_key, w_value):
    rows = delta.shape[0]
    pieces = order.shape[0]
    depth = w_query.shape[0] // pieces
    picked = lambda i, order: (order[i], 0)
    whole = lambda i, order: (0, 0)
    return pl.pallas_call(
        back_kernel,
        out_shape=(jax.ShapeDtypeStruct((rows, depth), jnp.bfloat16),) * pieces,
        grid_spec=pltpu.PrefetchScalarGridSpec(
            num_scalar_prefetch=1,
            grid=(pieces,),
            in_specs=[
                pl.BlockSpec(delta.shape, whole),
                pl.BlockSpec((depth, w_query.shape[1]), picked),
                pl.BlockSpec((depth, w_key.shape[1]), picked),
                pl.BlockSpec((depth, w_value.shape[1]), picked),
            ],
            out_specs=(pl.BlockSpec((rows, depth), whole),) * pieces,
        ),
        compiler_params=pltpu.CompilerParams(vmem_limit_bytes=48 * MIB),
        name="back",
    )(order, delta, w_query, w_key, w_value)


def weight_kernel(group, *refs):
    sources = (len(refs) - 3) // 2
    turned_refs, delta_refs = refs[:sources], refs[sources : 2 * sources]
    query_ref, key_ref, value_ref = refs[2 * sources :]
    total = None
    for turned_ref, delta_ref in zip(turned_refs, delta_refs):
        term = nn_dot(turned_ref[...], delta_ref[...])
        total = term if total is None else total + term
    mid = group * HEAD_DIM
    query_ref[...] = total[:, :mid]
    key_ref[...] = total[:, mid : mid + HEAD_DIM]
    value_ref[...] = total[:, mid + HEAD_DIM :]


def weight_gradients(turned, deltas, group):
    depth, rows = turned[0].shape
    span = (group + 2) * HEAD_DIM
    kv_local = deltas[0].shape[1] // span
    cuts = 2
    cut = depth // cuts
    out_block = lambda h, i: (i, h)
    return pl.pallas_call(
        functools.partial(weight_kernel, group),
        out_shape=(
            jax.ShapeDtypeStruct((depth, kv_local * group * HEAD_DIM), jnp.float32),
            jax.ShapeDtypeStruct((depth, kv_local * HEAD_DIM), jnp.float32),
            jax.ShapeDtypeStruct((depth, kv_local * HEAD_DIM), jnp.float32),
        ),
        grid=(kv_local, cuts),
        in_specs=[pl.BlockSpec((cut, rows), lambda h, i: (i, 0))] * len(turned)
        + [pl.BlockSpec((rows, span), lambda h, i: (0, h))] * len(deltas),
        out_specs=(
            pl.BlockSpec((cut, group * HEAD_DIM), out_block),
            pl.BlockSpec((cut, HEAD_DIM), out_block),
            pl.BlockSpec((cut, HEAD_DIM), out_block),
        ),
        compiler_params=pltpu.CompilerParams(vmem_limit_bytes=48 * MIB),
        name="weights",
    )(*turned, *deltas)


def branch_send(array, chips, shift, swap):
    pairs = [
        (c * 2 + k, ((c + shift) % chips) * 2 + (k ^ swap)) for c in range(chips) for k in range(2)
    ]
    return lax.ppermute(array, "branch", pairs)


def local(layer_input, norm_gain, w_query, w_key, w_value, head_grad, parents, row_counts):
    branch_total = lax.axis_size("branch")
    branch_index = lax.axis_index("branch")
    tensor_total = lax.axis_size("tensor")
    tensor_index = lax.axis_index("tensor")
    slots = row_counts.shape[0] // branch_total
    rows, width = layer_input.shape
    column_width = width // tensor_total
    chips = branch_total // 2
    group = w_query.shape[1] // w_key.shape[1]
    own_counts = lax.dynamic_slice_in_dim(row_counts, branch_index * slots, slots, 0)
    offsets = [(shift, swap) for shift in range(chips) for swap in range(2)]

    def targets():
        index = lax.axis_index("branch")
        chip, core = index // 2, index % 2
        return [lax.rem(chip + s, chips) * 2 + lax.rem(core + e, 2) for s, e in offsets]

    normed, inverse, pieces = normalize(layer_input, norm_gain, targets, branch_total)
    turned = [
        piece if (s, e) == (0, 0) else branch_send(piece, chips, s, e)
        for piece, (s, e) in zip(pieces, offsets)
    ]
    delta, centre_part = attention_backward(
        normed, w_query, w_key, w_value, head_grad, parents, own_counts
    )
    direct = [delta] + [branch_send(delta, chips, s, 0) for s in range(1, chips)]
    deltas = []
    for part in direct:
        deltas += [part, branch_send(part, chips, 0, 1)]
    centre = lax.psum(centre_part, "tensor") * (1.0 / width)

    shifts = list(range(1, tensor_total)) + [0]
    order = lax.rem(tensor_index + jnp.array(shifts, jnp.int32), tensor_total)
    partials = back_project(order, delta, w_query, w_key, w_value)
    d_normed = partials[-1].astype(jnp.float32)
    for shift, partial in zip(shifts[:-1], partials[:-1]):
        pairs = [(t, (t + shift) % tensor_total) for t in range(tensor_total)]
        d_normed = d_normed + lax.ppermute(partial, "tensor", pairs).astype(jnp.float32)

    column_start = tensor_index * column_width
    input_columns = lax.dynamic_slice_in_dim(layer_input, column_start, column_width, 1)
    gain_columns = lax.dynamic_slice_in_dim(norm_gain, column_start, column_width, 0)
    scaled = input_columns.astype(jnp.float32) * inverse
    grad_input = (inverse * ((1.0 + gain_columns) * d_normed - scaled * centre)).astype(
        jnp.bfloat16
    )
    grad_gain = lax.psum(jnp.sum(d_normed * scaled, axis=0), "branch")
    grad_query, grad_key, grad_value = weight_gradients(turned, deltas, group)
    return (grad_input, grad_query, grad_key, grad_value, grad_gain)


def solution(mesh):
    placed = (
        P(("parts", "branch"), None),
        P(),
        P(None, "tensor"),
        P(None, "tensor"),
        P(None, "tensor"),
        P(("parts", "branch"), "tensor"),
        P(("parts", "branch")),
        P("parts"),
    )
    return jax.shard_map(
        local,
        mesh=mesh,
        in_specs=placed,
        out_specs=(
            P(("parts", "branch"), "tensor"),
            P(("parts", "branch"), "tensor"),
            P(("parts", "branch"), "tensor"),
            P(("parts", "branch"), "tensor"),
            P(("parts", "tensor")),
        ),
        check_vma=False,
    )
```

time: 498 us -> 142 us (0.29)
  waiting for transfers between devices: 357 us -> 52.5 us
  matrix products: 92.2 us -> 0 us
  Pallas kernels: 0 us -> 30 us
  blocking collectives: 6.22 us -> 35.8 us
  between operations: 15.7 us -> 0.73 us
  starting transfers between devices: 0.13 us -> 10.3 us
  other arithmetic: 13.3 us -> 3.82 us
    reduce_scatter x3 -> x0, waiting for transfers between devices: 243 us -> none  [the longest x1 116 us: local(): lax.psum_scatter(acc_query, 'branch', scatter_dimension=0, tiled=True)]
    psum x2 -> x0, waiting for transfers between devices: 113 us -> none  [one_tree(): d_normed = lax.psum(partial_rows, 'tensor')]
    dot_general x36 -> x0, matrix products: 92.2 us -> none  [the longest x6 42.9 us: transpose_dot(): lax.dot_general(left, right, (((0,), (0,)), ((), ())), preferred_element_...]
    ppermute x0 -> x9, waiting for transfers between devices: none -> 52.5 us  [the longest x3 29.4 us: local(): lax.ppermute(partial, 'tensor', pairs).astype(jnp.float32)]
    pallas_call x0 -> x4, Pallas kernels: none -> 30 us  [the longest x1 11.2 us: attention_backward(): pl.pallas_call(functools.partial(attention_kernel, slots), out_shape=(jax...]
    psum x1 -> x2, blocking collectives: 6.22 us -> 35.8 us  [the longest x1 29.6 us: local(): centre = lax.psum(centre_part, 'tensor') * (1.0 / width)]
    ppermute x0 -> x9, starting transfers between devices: none -> 10.3 us  [the longest x3 5.76 us: local(): lax.ppermute(partial, 'tensor', pairs).astype(jnp.float32)]
    unnamed x4 -> x18, local copies, waits for them, and re-layouts: 0.17 us -> 6.38 us
  transfers between devices with their start and end apart: 5 -> 9, of which waited for: 5 -> 3; matrix products, arithmetic and copies ran while one was open for 9% -> 3% of each run, Pallas kernels for 0% -> 7%
where the time goes in v1:
time: 142 us
  waiting for transfers between devices  52.5 us (37%)
  blocking collectives  35.8 us (25%)
  Pallas kernels  30 us (21%)
  starting transfers between devices  10.3 us (7%)
  local copies, waits for them, and re-layouts  8.65 us (6%)
  other arithmetic  3.82 us (3%)
    psum x1, blocking collectives, local(): centre = lax.psum(centre_part, 'tensor') * (1.0 / width)  29.6 us
    ppermute x3, waiting for transfers between devices, local(): lax.ppermute(partial, 'tensor', pairs).astype(jnp.float32)  29.4 us
    ppermute x6, waiting for transfers between devices, branch_send(): return lax.ppermute(array, 'branch', pairs)  23.2 us
    pallas_call x1, Pallas kernels, attention_backward(): pl.pallas_call(functools.partial(attention_kernel, slots), out_shape=(jax...  11.2 us
    pallas_call x1, Pallas kernels, back_project(): pl.pallas_call(back_kernel, out_shape=(jax.ShapeDtypeStruct((rows, depth)...  9.86 us
    pallas_call x1, Pallas kernels, weight_gradients(): pl.pallas_call(functools.partial(weight_kernel, group), out_shape=(jax.Sh...  7.82 us
    unnamed x18, local copies, waits for them, and re-layouts  6.38 us
    psum x1, blocking collectives, local(): grad_gain = lax.psum(jnp.sum(d_normed * scaled, axis=0), 'branch')  6.22 us
  transfers between devices with their start and end apart: 9, of which 3 were waited for; matrix products, arithmetic and copies ran while one was open for 3% of the time, Pallas kernels for 7%

profile of v1, /device:TPU:0, one launch (start us, length us, event | category | flops | bytes accessed | tf_op | source)
XLA Modules:
  0.0 141.8 jit_solution(4129633312711108801)
XLA Ops:
  0.6 0.7 reshape.17.gain_ref
  1.4 0.8 copy.14.parent_ref
  2.2 0.7 dynamic_slice.10.count_ref
  2.9 0.0 copy-start
  2.9 1.5 %copy-done = bf16[256,3584]{1,0:T(8,128)(2,1)S(1)} copy-done((bf16[256,3584]{1,0:T(8,128)(2,1)S(1)}, bf16[256,3584]{1,0:T(8,128)(2,1)}, u32[]{:S(2)}) %copy-start) | copy-done | bytes 1835032
  4.4 0.0 copy-start.1
  4.4 1.2 norm.1
  5.6 0.0 copy-start.2
  5.6 0.8 copy-done.2
  6.4 0.0 copy-start.5
  6.4 0.8 copy-done.5
  7.2 0.0 copy-start.6
  7.2 0.8 copy-done.6
  7.9 0.0 copy-start.7
  7.9 0.8 copy-done.7
  8.7 0.0 copy-done.1
  8.7 0.0 copy-start.8
  8.7 11.2 %attention.1 = (bf16[256,2048]{1,0:T(8,128)(2,1)S(1)}, f32[256,1]{1,0:T(8,128)S(1)}) custom-call(s32[2]{0:T(128)S(1)} %dynamic_slice.10.count_ref, bf16[256,3584]{1,0:T(8,128)(2,1)S(1)} %get-tuple-element.21.normed_ref, bf16[3584,1024]{1,0:T(8,128)(2,1)} %query_ref.3, bf16[3584,512]{1,0:T(8,128)(2,1)} %key_ref.3, bf16[3584,512]{1,0:T(8,128)(2,1)} %value_ref.3, ...), custom_call_target="tpu_custom_call" | custom-call | tf_op jit(solution)/shard_map/attention/pallas_call | solution.py:168
  19.9 3.0 %collective-permute-start.7 = (bf16[256,2048]{1,0:T(8,128)(2,1)S(1)}, bf16[256,2048]{1,0:T(8,128)(2,1)S(1)}, u32[]{:S(2)}, u32[]{:S(2)}) collective-permute-start(bf16[256,2048]{1,0:T(8,128)(2,1)S(1)} %get-tuple-element.22.delta_ref.refs_4_), channel_id=1, source_target_pairs={{0,8},{4,12},{8,0},{12,4},{1,9},{5,13},{9,1},{13,5},{2,10},{6,14},... | collective-permute-start | bytes 3145736 | tf_op jit(solution)/shard_map/ppermute | solution.py:295
  22.9 0.0 collective-permute-start.6
  22.9 23.2 %collective-permute-done.7.refs_6_ = bf16[256,2048]{1,0:T(8,128)(2,1)S(1)} collective-permute-done((bf16[256,2048]{1,0:T(8,128)(2,1)S(1)}, bf16[256,2048]{1,0:T(8,128)(2,1)S(1)}, u32[]{:S(2)}, u32[]{:S(2)}) %collective-permute-start.7) | collective-permute-done | bytes 1048608 | tf_op jit(solution)/shard_map/ppermute | solution.py:295
  46.0 0.0 collective-permute-start.8
  46.0 0.0 copy-done.8
  46.1 9.9 %back.1 = (bf16[256,896]{1,0:T(8,128)(2,1)}, bf16[256,896]{1,0:T(8,128)(2,1)}, bf16[256,896]{1,0:T(8,128)(2,1)}, bf16[256,896]{1,0:T(8,128)(2,1)S(1)}) custom-call(s32[4]{0:T(128)S(1)} %compare_select_fusion.order_ref, bf16[256,2048]{1,0:T(8,128)(2,1)S(1)} %get-tuple-element.22.delta_ref.refs_4_, bf16[3584,1024]{1,0:T(8,128)(2,1)} %query_ref.3, ...), custom_call_target="tpu_custom_call" | custom-call | tf_op jit(solution)/shard_map/back/pallas_call | solution.py:231
  55.9 0.8 copy-done.4
  56.7 1.8 %collective-permute-start = (bf16[256,896]{1,0:T(8,128)(2,1)}, bf16[256,896]{1,0:T(8,128)(2,1)}, u32[]{:S(2)}, u32[]{:S(2)}) collective-permute-start(bf16[256,896]{1,0:T(8,128)(2,1)} %get-tuple-element.24), channel_id=1, source_target_pairs={{0,1},{1,2},{2,3},{3,0},{4,5},{5,6},{6,7},{7,4},{8,9},{9,10},{10,1... | collective-permute-start | bytes 1376264 | tf_op jit(solution)/shard_map/ppermute | solution.py:336
  58.5 2.6 %collective-permute-start.1 = (bf16[256,896]{1,0:T(8,128)(2,1)}, bf16[256,896]{1,0:T(8,128)(2,1)}, u32[]{:S(2)}, u32[]{:S(2)}) collective-permute-start(bf16[256,896]{1,0:T(8,128)(2,1)} %get-tuple-element.25), channel_id=1, source_target_pairs={{0,2},{1,3},{2,0},{3,1},{4,6},{5,7},{6,4},{7,5},{8,10},{9,11},{10,... | collective-permute-start | bytes 1376264 | tf_op jit(solution)/shard_map/ppermute | solution.py:336
  61.1 1.3 collective-permute-start.2
  62.4 9.9 %collective-permute-done = bf16[256,896]{1,0:T(8,128)(2,1)} collective-permute-done((bf16[256,896]{1,0:T(8,128)(2,1)}, bf16[256,896]{1,0:T(8,128)(2,1)}, u32[]{:S(2)}, u32[]{:S(2)}) %collective-permute-start) | collective-permute-done | bytes 458784 | tf_op jit(solution)/shard_map/ppermute | solution.py:336
  72.4 0.0 collective-permute-start.3
  72.4 19.4 %collective-permute-done.1 = bf16[256,896]{1,0:T(8,128)(2,1)} collective-permute-done((bf16[256,896]{1,0:T(8,128)(2,1)}, bf16[256,896]{1,0:T(8,128)(2,1)}, u32[]{:S(2)}, u32[]{:S(2)}) %collective-permute-start.1) | collective-permute-done | bytes 458784 | tf_op jit(solution)/shard_map/ppermute | solution.py:336
  91.8 1.5 %collective-permute-start.4 = (bf16[896,256]{1,0:T(8,128)(2,1)}, bf16[896,256]{1,0:T(8,128)(2,1)}, u32[]{:S(2)}, u32[]{:S(2)}) collective-permute-start(bf16[896,256]{1,0:T(8,128)(2,1)} %copy-done.6), channel_id=1, source_target_pairs={{0,8},{4,12},{8,0},{12,4},{1,9},{5,13},{9,1},{13,5},{2,10},{6,14},... | collective-permute-start | bytes 1376264 | tf_op jit(solution)/shard_map/ppermute | solution.py:295
  93.3 0.0 collective-permute-done.2
  93.3 0.0 collective-permute-start.5
  93.3 0.8 dynamic-slice_add_fusion
  94.1 0.1 reduce
  94.2 29.6 %psum.14 = f32[256,1]{1,0:T(8,128)S(1)} all-reduce(f32[256,1]{1,0:T(8,128)S(1)} %get-tuple-element.27), channel_id=1, replica_groups=mesh['parts'=2,'branch'=4,'tensor'=4] {'tensor'}, use_global_device_ids=true, to_apply=%region_0.0 | all-reduce | flops 256 | bytes 2048 | tf_op jit(solution)/shard_map/psum | solution.py:328
  123.8 0.1 multiply_reduce_fusion.1
  123.9 2.8 %multiply_reduce_fusion = (f32[896]{0:T(1024)S(1)}, bf16[256,896]{1,0:T(8,128)(2,1)}) fusion(f32[256]{0:T(256)S(1)} %reduce, bf16[256,3584]{1,0:T(8,128)(2,1)} %input_ref.1, s32[]{:T(128)S(6)} %select_n.7, bf16[256,896]{1,0:T(8,128)(2,1)} %collective-permute-done.2, bf16[256,896]{1,0:T(8,128)(2,1)} %collective-permute-done.1, ...), kind=kLoop, calls=%fused_computation | loop fusion | flops 3669120 | bytes 2761732 | tf_op jit(solution)/shard_map/reduce_sum | solution.py:345
  126.8 6.2 %psum.15 = f32[896]{0:T(1024)} all-reduce(f32[896]{0:T(1024)S(1)} %get-tuple-element.35), channel_id=1, replica_groups=mesh['parts'=2,'branch'=4,'tensor'=4] {'branch'}, use_global_device_ids=true, to_apply=%region_2.0 | all-reduce | flops 896 | bytes 7168 | tf_op jit(solution)/shard_map/psum | solution.py:345
  133.0 0.0 collective-permute-done.3.refs_1_
  133.0 0.0 collective-permute-done.4.refs_2_
  133.0 0.0 collective-permute-done.5.refs_3_
  133.0 0.0 collective-permute-done.6.refs_5_
  133.0 0.0 collective-permute-done.8.refs_7_
  133.0 0.0 copy-start.3
  133.0 1.0 copy-done.3
  134.0 7.8 %weights.1 = (f32[896,1024]{1,0:T(8,128)}, f32[896,512]{1,0:T(8,128)}, f32[896,512]{1,0:T(8,128)}) custom-call(bf16[896,256]{1,0:T(8,128)(2,1)S(1)} %copy-done.3, bf16[896,256]{1,0:T(8,128)(2,1)} %collective-permute-done.3.refs_1_, bf16[896,256]{1,0:T(8,128)(2,1)} %collective-permute-done.4.refs_2_, bf16[896,256]{1,0:T(8,128)(2,1)} %collective-permute-done.5.refs_3_, ...), custom_call_target="tpu_custom_call" | custom-call | tf_op jit(solution)/shard_map/weights/pallas_call | solution.py:271
  (2 shorter events, 0.0 us)
Async XLA Ops:
  2.9 1.5 %copy-start = (bf16[256,3584]{1,0:T(8,128)(2,1)S(1)}, bf16[256,3584]{1,0:T(8,128)(2,1)}, u32[]{:S(2)}) copy-start(bf16[256,3584]{1,0:T(8,128)(2,1)} %input_ref.1) | copy-start | bytes 5505028
  4.4 4.3 %copy-start.1 = (bf16[256,1024]{1,0:T(8,128)(2,1)S(1)}, bf16[256,1024]{1,0:T(8,128)(2,1)}, u32[]{:S(2)}) copy-start(bf16[256,1024]{1,0:T(8,128)(2,1)} %grad_ref.1) | copy-start | bytes 1572868
  5.6 0.8 copy-start.2
  6.4 0.8 copy-start.5
  7.2 0.8 copy-start.6
  7.9 0.8 copy-start.7
  8.7 37.3 %copy-start.8 = (s32[4]{0:T(128)S(1)}, s32[4]{0:T(128)}, u32[]{:S(2)}) copy-start(s32[4]{0:T(128)} %constant.29.clone) | copy-start | bytes 52
  19.9 26.2 %collective-permute-start.7 = (bf16[256,2048]{1,0:T(8,128)(2,1)S(1)}, bf16[256,2048]{1,0:T(8,128)(2,1)S(1)}, u32[]{:S(2)}, u32[]{:S(2)}) collective-permute-start(bf16[256,2048]{1,0:T(8,128)(2,1)S(1)} %get-tuple-element.22.delta_ref.refs_4_), channel_id=1, source_target_pairs={{0,8},{4,12},{8,0},{12,4},{1,9},{5,13},{9,1},{13,5},{2,10},{6,14},... | collective-permute-start | bytes 3145736 | tf_op jit(solution)/shard_map/ppermute | solution.py:295
  22.9 110.1 %collective-permute-start.6 = (bf16[256,2048]{1,0:T(8,128)(2,1)S(1)}, bf16[256,2048]{1,0:T(8,128)(2,1)S(1)}, u32[]{:S(2)}, u32[]{:S(2)}) collective-permute-start(bf16[256,2048]{1,0:T(8,128)(2,1)S(1)} %get-tuple-element.22.delta_ref.refs_4_), channel_id=1, source_target_pairs={{0,4},{4,0},{8,12},{12,8},{1,5},{5,1},{9,13},{13,9},{2,6},{6,2},{1... | collective-permute-start | bytes 3145736 | tf_op jit(solution)/shard_map/ppermute | solution.py:295
  46.0 87.0 %collective-permute-start.8 = (bf16[256,2048]{1,0:T(8,128)(2,1)S(1)}, bf16[256,2048]{1,0:T(8,128)(2,1)}, u32[]{:S(2)}, u32[]{:S(2)}) collective-permute-start(bf16[256,2048]{1,0:T(8,128)(2,1)S(1)} %collective-permute-done.7.refs_6_), channel_id=1, source_target_pairs={{0,4},{4,0},{8,12},{12,8},{1,5},{5,1},{9,13},{13,9},{2,6},{6,2},{1... | collective-permute-start | bytes 3145736 | tf_op jit(solution)/shard_map/ppermute | solution.py:295
  55.9 0.8 copy-start.4
  56.7 15.7 %collective-permute-start = (bf16[256,896]{1,0:T(8,128)(2,1)}, bf16[256,896]{1,0:T(8,128)(2,1)}, u32[]{:S(2)}, u32[]{:S(2)}) collective-permute-start(bf16[256,896]{1,0:T(8,128)(2,1)} %get-tuple-element.24), channel_id=1, source_target_pairs={{0,1},{1,2},{2,3},{3,0},{4,5},{5,6},{6,7},{7,4},{8,9},{9,10},{10,1... | collective-permute-start | bytes 1376264 | tf_op jit(solution)/shard_map/ppermute | solution.py:336
  58.5 33.3 %collective-permute-start.1 = (bf16[256,896]{1,0:T(8,128)(2,1)}, bf16[256,896]{1,0:T(8,128)(2,1)}, u32[]{:S(2)}, u32[]{:S(2)}) collective-permute-start(bf16[256,896]{1,0:T(8,128)(2,1)} %get-tuple-element.25), channel_id=1, source_target_pairs={{0,2},{1,3},{2,0},{3,1},{4,6},{5,7},{6,4},{7,5},{8,10},{9,11},{10,... | collective-permute-start | bytes 1376264 | tf_op jit(solution)/shard_map/ppermute | solution.py:336
  61.1 32.2 %collective-permute-start.2 = (bf16[256,896]{1,0:T(8,128)(2,1)}, bf16[256,896]{1,0:T(8,128)(2,1)}, u32[]{:S(2)}, u32[]{:S(2)}) collective-permute-start(bf16[256,896]{1,0:T(8,128)(2,1)} %get-tuple-element.26), channel_id=1, source_target_pairs={{0,3},{1,0},{2,1},{3,2},{4,7},{5,4},{6,5},{7,6},{8,11},{9,8},{10,9... | collective-permute-start | bytes 1376264 | tf_op jit(solution)/shard_map/ppermute | solution.py:336
  72.4 60.6 %collective-permute-start.3 = (bf16[896,256]{1,0:T(8,128)(2,1)}, bf16[896,256]{1,0:T(8,128)(2,1)}, u32[]{:S(2)}, u32[]{:S(2)}) collective-permute-start(bf16[896,256]{1,0:T(8,128)(2,1)} %copy-done.7), channel_id=1, source_target_pairs={{0,4},{4,0},{8,12},{12,8},{1,5},{5,1},{9,13},{13,9},{2,6},{6,2},{1... | collective-permute-start | bytes 1376264 | tf_op jit(solution)/shard_map/ppermute | solution.py:295
  91.8 41.2 %collective-permute-start.4 = (bf16[896,256]{1,0:T(8,128)(2,1)}, bf16[896,256]{1,0:T(8,128)(2,1)}, u32[]{:S(2)}, u32[]{:S(2)}) collective-permute-start(bf16[896,256]{1,0:T(8,128)(2,1)} %copy-done.6), channel_id=1, source_target_pairs={{0,8},{4,12},{8,0},{12,4},{1,9},{5,13},{9,1},{13,5},{2,10},{6,14},... | collective-permute-start | bytes 1376264 | tf_op jit(solution)/shard_map/ppermute | solution.py:295
  93.3 39.7 %collective-permute-start.5 = (bf16[896,256]{1,0:T(8,128)(2,1)}, bf16[896,256]{1,0:T(8,128)(2,1)}, u32[]{:S(2)}, u32[]{:S(2)}) collective-permute-start(bf16[896,256]{1,0:T(8,128)(2,1)} %copy-done.5), channel_id=1, source_target_pairs={{0,12},{4,8},{8,4},{12,0},{1,13},{5,9},{9,5},{13,1},{2,14},{6,10},... | collective-permute-start | bytes 1376264 | tf_op jit(solution)/shard_map/ppermute | solution.py:295
  133.0 1.0 copy-start.3

commit v2 on v1

v2 whole, which is shorter than its diff:
```python
import functools

import jax
import jax.numpy as jnp
from jax import lax
from jax.experimental import pallas as pl
from jax.experimental.pallas import tpu as pltpu
from jax.sharding import PartitionSpec as P

HEAD_DIM = 256
MIB = 1024 * 1024
CENTRE_ROWS = 16


epsilon = 1e-06
softcap_limit = 50.0


def nn_dot(left, right):
    return lax.dot_general(
        left, right, (((1,), (0,)), ((), ())), preferred_element_type=jnp.float32
    )


def nt_dot(left, right):
    return lax.dot_general(
        left, right, (((1,), (1,)), ((), ())), preferred_element_type=jnp.float32
    )


def tn_dot(left, right):
    return lax.dot_general(
        left, right, (((0,), (0,)), ((), ())), preferred_element_type=jnp.float32
    )


def cost(flops, count):
    return pl.CostEstimate(flops=flops, bytes_accessed=count, transcendentals=0)


def norm_kernel(targets, input_ref, gain_ref, normed_ref, inverse_ref, *rest):
    piece_refs, turned = rest[:-1], rest[-1]
    rows, width = input_ref.shape
    values = input_ref[...].astype(jnp.float32)
    inverse = lax.rsqrt(jnp.mean(values * values, axis=-1, keepdims=True) + epsilon)
    inverse_ref[...] = inverse
    gain = gain_ref[...].reshape(1, width)
    normed = (values * inverse * (1.0 + gain)).astype(jnp.bfloat16)
    normed_ref[...] = normed
    turned[...] = normed.T
    depth = width // len(piece_refs)
    for target, piece_ref in zip(targets(), piece_refs):
        start = pl.multiple_of(target * depth, 16)
        piece_ref[...] = turned[pl.ds(start, depth), :]


def normalize(layer_input, norm_gain, targets, pieces, block):
    rows, width = layer_input.shape
    depth = width // pieces
    out = pl.pallas_call(
        functools.partial(norm_kernel, targets),
        out_shape=(
            jax.ShapeDtypeStruct((rows, width), jnp.bfloat16),
            jax.ShapeDtypeStruct((rows, 1), jnp.float32),
        )
        + (jax.ShapeDtypeStruct((depth, rows), jnp.bfloat16),) * pieces,
        grid=(rows // block,),
        in_specs=[
            pl.BlockSpec((block, width), lambda i: (i, 0)),
            pl.BlockSpec((width,), lambda i: (0,)),
        ],
        out_specs=(
            pl.BlockSpec((block, width), lambda i: (i, 0)),
            pl.BlockSpec((block, 1), lambda i: (i, 0)),
        )
        + (pl.BlockSpec((depth, block), lambda i: (0, i)),) * pieces,
        scratch_shapes=[pltpu.VMEM((width, block), jnp.bfloat16)],
        compiler_params=pltpu.CompilerParams(vmem_limit_bytes=40 * MIB),
        cost_estimate=cost(10 * rows * width, 6 * rows * width),
        name="norm",
    )(layer_input, norm_gain)
    return out[0], out[1], out[2:]


def ancestor_mask(parent_row):
    rows = parent_row.shape[1]
    row = lax.broadcasted_iota(jnp.int32, (rows, rows), 0)
    column = lax.broadcasted_iota(jnp.int32, (rows, rows), 1)
    reached = jnp.where((parent_row == row) | (row == column), 1.0, 0.0)
    for squaring in range(rows.bit_length() - 1):
        halfway = reached.astype(jnp.bfloat16)
        reached = jnp.minimum(nn_dot(halfway, halfway), 1.0)
    return reached.T


def attention_kernel(
    slots,
    kv_local,
    cuts,
    count_ref,
    parent_ref,
    normed_hbm,
    query_hbm,
    key_hbm,
    value_hbm,
    grad_hbm,
    *rest,
):
    delta_hbm = rest[:kv_local]
    turned_hbm, centre_ref, normed_ref, query_ref, key_ref, value_ref, grad_ref = rest[
        kv_local : kv_local + 7
    ]
    delta_ref, turned_ref, load_sem, weight_sem, store_sem = rest[kv_local + 7 :]
    head_dim = HEAD_DIM
    rows, width = normed_ref.shape
    block = rows // slots
    group = query_ref.shape[2] // head_dim
    span = (group + 2) * head_dim
    depth = width // cuts

    def fetch(h, cut, which):
        source, kept = ((query_hbm, query_ref), (key_hbm, key_ref), (value_hbm, value_ref))[which]
        wide = kept.shape[2]
        lines = pl.ds(cut * depth, depth)
        return pltpu.make_async_copy(
            source.at[lines, pl.ds(h * wide, wide)],
            kept.at[h, lines, :],
            weight_sem.at[h, cut, which],
        )

    loads = [
        pltpu.make_async_copy(normed_hbm, normed_ref, load_sem.at[0]),
        pltpu.make_async_copy(grad_hbm, grad_ref, load_sem.at[1]),
    ]
    loads[0].start()
    for cut in range(cuts):
        for which in range(3):
            fetch(0, cut, which).start()
    loads[1].start()
    for h in range(1, kv_local):
        for cut in range(cuts):
            for which in range(3):
                fetch(h, cut, which).start()

    first_count = lax.axis_index("branch") * slots
    parents = parent_ref[...].reshape(1, rows)
    allowed_slots = [
        ancestor_mask(parents[:, slot * block : (slot + 1) * block]) for slot in range(slots)
    ]
    scale = head_dim ** (-0.5)
    centre_parts = [jnp.zeros((block, 1), jnp.float32) for _ in range(slots)]
    stores = []
    for h in range(kv_local):
        sums = [None, None, None]
        for cut in range(cuts):
            if h == 0 and cut == 0:
                loads[0].wait()
            lines = slice(cut * depth, (cut + 1) * depth)
            for which, kept in enumerate((query_ref, key_ref, value_ref)):
                fetch(h, cut, which).wait()
                term = nn_dot(normed_ref[:, lines], kept[h, lines, :])
                sums[which] = term if sums[which] is None else sums[which] + term
        query_sum, key_sum, value_sum = sums
        if h == 0:
            loads[1].wait()
        for slot in range(slots):
            lines = slice(slot * block, (slot + 1) * block)
            query_parts = [
                query_sum[lines, g * head_dim : (g + 1) * head_dim] for g in range(group)
            ]
            queries = jnp.concatenate(query_parts, axis=0).astype(jnp.bfloat16)
            keys = key_sum[lines].astype(jnp.bfloat16)
            values = value_sum[lines].astype(jnp.bfloat16)
            live = (
                lax.broadcasted_iota(jnp.int32, (block, head_dim), 0)
                < count_ref[first_count + slot]
            )
            base = h * group * head_dim
            grads = jnp.concatenate(
                [
                    jnp.where(
                        live,
                        grad_ref[
                            lines, base + g * head_dim : base + (g + 1) * head_dim
                        ].astype(jnp.float32),
                        0.0,
                    )
                    for g in range(group)
                ],
                axis=0,
            ).astype(jnp.bfloat16)
            allowed = jnp.concatenate([allowed_slots[slot]] * group, axis=0)
            bounded = jnp.tanh(nt_dot(queries, keys) * (scale / softcap_limit))
            weights = allowed * jnp.exp(softcap_limit * bounded)
            probabilities = weights * (1.0 / jnp.sum(weights, axis=-1, keepdims=True))
            d_probs = nt_dot(grads, values)
            d_scores = probabilities * (
                d_probs - jnp.sum(probabilities * d_probs, axis=-1, keepdims=True)
            )
            d_raw = (d_scores * (1.0 - bounded * bounded) * scale).astype(jnp.bfloat16)
            prob_half = probabilities.astype(jnp.bfloat16)
            d_query = nn_dot(d_raw, keys).astype(jnp.bfloat16)
            d_key = tn_dot(d_raw, queries).astype(jnp.bfloat16)
            d_value = tn_dot(prob_half, grads).astype(jnp.bfloat16)
            product = d_key.astype(jnp.float32) * key_sum[lines]
            product += d_value.astype(jnp.float32) * value_sum[lines]
            for g in range(group):
                part = d_query[g * block : (g + 1) * block]
                delta_ref[h, lines, g * head_dim : (g + 1) * head_dim] = part
                product += part.astype(jnp.float32) * query_parts[g]
            delta_ref[h, lines, group * head_dim : (group + 1) * head_dim] = d_key
            delta_ref[h, lines, (group + 1) * head_dim :] = d_value
            centre_parts[slot] += jnp.sum(product, axis=-1, keepdims=True)
        stores.append(pltpu.make_async_copy(delta_ref.at[h], delta_hbm[h], store_sem.at[h, 0]))
        stores[-1].start()
        turned_ref[h] = delta_ref[h].T
        stores.append(
            pltpu.make_async_copy(
                turned_ref.at[h], turned_hbm.at[pl.ds(h * span, span), :], store_sem.at[h, 1]
            )
        )
        stores[-1].start()
    centre = jnp.concatenate(centre_parts, axis=0)
    centre_ref[...] = jnp.broadcast_to(centre, (rows, 128)).T[:CENTRE_ROWS]
    for store in stores:
        store.wait()


def attention_backward(normed, w_query, w_key, w_value, head_grad, parents, counts, slots):
    rows, width = normed.shape
    kv_local = w_key.shape[1] // HEAD_DIM
    group = w_query.shape[1] // w_key.shape[1]
    span = (group + 2) * HEAD_DIM
    cuts = 2 if width % 512 == 0 else 1
    hbm = pl.BlockSpec(memory_space=pl.ANY)
    vmem = pl.BlockSpec(memory_space=pltpu.VMEM)
    out = pl.pallas_call(
        functools.partial(attention_kernel, slots, kv_local, cuts),
        out_shape=(jax.ShapeDtypeStruct((rows, span), jnp.bfloat16),) * kv_local
        + (
            jax.ShapeDtypeStruct((kv_local * span, rows), jnp.bfloat16),
            jax.ShapeDtypeStruct((CENTRE_ROWS, rows), jnp.float32),
        ),
        in_specs=[pl.BlockSpec(memory_space=pltpu.SMEM), vmem] + [hbm] * 5,
        out_specs=(hbm,) * (kv_local + 1) + (vmem,),
        scratch_shapes=[
            pltpu.VMEM((rows, width), jnp.bfloat16),
            pltpu.VMEM((kv_local, width, group * HEAD_DIM), jnp.bfloat16),
            pltpu.VMEM((kv_local, width, HEAD_DIM), jnp.bfloat16),
            pltpu.VMEM((kv_local, width, HEAD_DIM), jnp.bfloat16),
            pltpu.VMEM(head_grad.shape, jnp.bfloat16),
            pltpu.VMEM((kv_local, rows, span), jnp.bfloat16),
            pltpu.VMEM((kv_local, span, rows), jnp.bfloat16),
            pltpu.SemaphoreType.DMA((2,)),
            pltpu.SemaphoreType.DMA((kv_local, cuts, 3)),
            pltpu.SemaphoreType.DMA((kv_local, 2)),
        ],
        compiler_params=pltpu.CompilerParams(vmem_limit_bytes=48 * MIB),
        cost_estimate=cost(
            2 * rows * width * kv_local * span, 2 * width * (kv_local * span + rows)
        ),
        name="attention",
    )(counts, parents, normed, w_query, w_key, w_value, head_grad)
    return out[:kv_local], out[kv_local], out[kv_local + 1]


def back_kernel(
    cuts, order_ref, turned_ref, centre_ref, query_ref, key_ref, value_ref, *rest
):
    del order_ref
    pieces = (len(rest) - 2) // 1
    out_hbm, kept, store_sem = rest[:pieces], rest[pieces], rest[pieces + 1]
    piece, cut = pl.program_id(0), pl.program_id(1)
    head_dim = HEAD_DIM
    kv_local = key_ref.shape[1] // head_dim
    group = query_ref.shape[1] // key_ref.shape[1]
    span = (group + 2) * head_dim
    lines = query_ref.shape[0]
    total = None
    for h in range(kv_local):
        base = h * span
        mid = base + group * head_dim
        term = nn_dot(
            query_ref[:, h * group * head_dim : (h + 1) * group * head_dim],
            turned_ref[base:mid, :],
        )
        term += nn_dot(
            key_ref[:, h * head_dim : (h + 1) * head_dim], turned_ref[mid : mid + head_dim, :]
        )
        term += nn_dot(
            value_ref[:, h * head_dim : (h + 1) * head_dim],
            turned_ref[mid + head_dim : mid + 2 * head_dim, :],
        )
        total = term if total is None else total + term
    start = pl.multiple_of(cut * lines, 16)
    kept[piece, pl.ds(start, lines), :] = total.astype(jnp.bfloat16)

    copies = [
        pltpu.make_async_copy(kept.at[place], out_hbm[place], store_sem.at[place])
        for place in range(pieces)
    ]
    for place, copy in enumerate(copies):

        @pl.when((piece == place) & (cut == cuts - 1))
        def _():
            kept[place, cuts * lines :, :] = centre_ref[...].astype(jnp.bfloat16)
            copy.start()

    @pl.when((piece == pieces - 1) & (cut == cuts - 1))
    def _():
        for copy in copies:
            copy.wait()


def back_project(order, turned, centre, w_query, w_key, w_value, blocks):
    rows = turned.shape[1]
    pieces = order.shape[0]
    depth = w_query.shape[0] // blocks
    cuts = 2
    cut = depth // cuts
    picked = lambda i, j, order: (order[i] * cuts + j, 0)
    whole = lambda i, j, order: (0, 0)
    return pl.pallas_call(
        functools.partial(back_kernel, cuts),
        out_shape=(jax.ShapeDtypeStruct((depth + CENTRE_ROWS, rows), jnp.bfloat16),) * pieces,
        grid_spec=pltpu.PrefetchScalarGridSpec(
            num_scalar_prefetch=1,
            grid=(pieces, cuts),
            in_specs=[
                pl.BlockSpec(turned.shape, whole),
                pl.BlockSpec(centre.shape, whole),
                pl.BlockSpec((cut, w_query.shape[1]), picked),
                pl.BlockSpec((cut, w_key.shape[1]), picked),
                pl.BlockSpec((cut, w_value.shape[1]), picked),
            ],
            out_specs=(pl.BlockSpec(memory_space=pl.ANY),) * pieces,
            scratch_shapes=[
                pltpu.VMEM((pieces, depth + CENTRE_ROWS, rows), jnp.bfloat16),
                pltpu.SemaphoreType.DMA((pieces,)),
            ],
        ),
        compiler_params=pltpu.CompilerParams(vmem_limit_bytes=48 * MIB),
        cost_estimate=cost(
            2 * pieces * depth * turned.shape[0] * rows, 2 * pieces * depth * turned.shape[0]
        ),
        name="back",
    )(order, turned, centre, w_query, w_key, w_value)


def weight_kernel(group, sources, *refs):
    turned_refs, delta_refs = refs[:sources], refs[sources : 2 * sources]
    query_ref, key_ref, value_ref = refs[-3:]
    total = None
    for turned_ref, delta_ref in zip(turned_refs, delta_refs):
        term = nn_dot(turned_ref[...], delta_ref[...])
        total = term if total is None else total + term
    mid = group * HEAD_DIM
    query_ref[...] = total[:, :mid]
    key_ref[...] = total[:, mid : mid + HEAD_DIM]
    value_ref[...] = total[:, mid + HEAD_DIM :]


def weight_gradients(turned, deltas, head, kv_local, group, before):
    depth, rows = turned[0].shape
    span = (group + 2) * HEAD_DIM
    cuts = 4 if depth % 64 == 0 else 2
    cut = depth // cuts
    sources = len(turned)
    out_block = lambda i: (i, head)
    kept = list(before) if before is not None else []
    return pl.pallas_call(
        functools.partial(weight_kernel, group, sources),
        out_shape=(
            jax.ShapeDtypeStruct((depth, kv_local * group * HEAD_DIM), jnp.float32),
            jax.ShapeDtypeStruct((depth, kv_local * HEAD_DIM), jnp.float32),
            jax.ShapeDtypeStruct((depth, kv_local * HEAD_DIM), jnp.float32),
        ),
        grid=(cuts,),
        in_specs=[pl.BlockSpec((cut, rows), lambda i: (i, 0))] * sources
        + [pl.BlockSpec((rows, span), lambda i: (0, 0))] * sources
        + [pl.BlockSpec(memory_space=pl.ANY)] * len(kept),
        out_specs=(
            pl.BlockSpec((cut, group * HEAD_DIM), out_block),
            pl.BlockSpec((cut, HEAD_DIM), out_block),
            pl.BlockSpec((cut, HEAD_DIM), out_block),
        ),
        input_output_aliases={2 * sources + i: i for i in range(len(kept))},
        compiler_params=pltpu.CompilerParams(vmem_limit_bytes=48 * MIB),
        cost_estimate=cost(
            2 * sources * rows * depth * span,
            4 * depth * span + 2 * sources * rows * (depth + span),
        ),
        name="weights",
    )(*turned, *deltas, *kept)


def finish_kernel(flag_ref, input_ref, gain_ref, inverse_ref, *refs):
    part_refs, (out_ref, sum_ref) = refs[:-2], refs[-2:]
    rows, wide = out_ref.shape
    total = part_refs[0][...].astype(jnp.float32)
    for place, part_ref in enumerate(part_refs[1:]):
        total += part_ref[...].astype(jnp.float32) * flag_ref[place].astype(jnp.float32)
    total = total.T
    d_normed = total[:, :wide]
    centre = (total[:, wide : wide + 1]) * (1.0 / flag_ref[len(part_refs) - 1].astype(jnp.float32))
    inverse = inverse_ref[...]
    scaled = input_ref[...].astype(jnp.float32) * inverse
    gain = gain_ref[...].reshape(1, wide)
    out_ref[...] = (inverse * ((1.0 + gain) * d_normed - scaled * centre)).astype(jnp.bfloat16)
    sum_ref[...] = jnp.sum(d_normed * scaled, axis=0, keepdims=True)


def finish(flags, input_columns, gain_columns, inverse, parts):
    rows, wide = input_columns.shape
    return pl.pallas_call(
        finish_kernel,
        out_shape=(
            jax.ShapeDtypeStruct((rows, wide), jnp.bfloat16),
            jax.ShapeDtypeStruct((1, wide), jnp.float32),
        ),
        grid=(1,),
        in_specs=[
            pl.BlockSpec(memory_space=pltpu.SMEM),
            pl.BlockSpec((rows, wide), lambda i: (0, 0)),
            pl.BlockSpec((wide,), lambda i: (0,)),
            pl.BlockSpec((rows, 1), lambda i: (0, 0)),
        ]
        + [pl.BlockSpec(part.shape, lambda i: (0, 0)) for part in parts],
        out_specs=(
            pl.BlockSpec((rows, wide), lambda i: (0, 0)),
            pl.BlockSpec((1, wide), lambda i: (0, 0)),
        ),
        compiler_params=pltpu.CompilerParams(vmem_limit_bytes=40 * MIB),
        cost_estimate=cost(20 * rows * wide, 2 * rows * wide * (len(parts) + 2)),
        name="finish",
    )(flags, input_columns, gain_columns, inverse, *parts)


def branch_send(array, chips, shift, swap):
    pairs = [
        (c * 2 + k, ((c + shift) % chips) * 2 + (k ^ swap)) for c in range(chips) for k in range(2)
    ]
    return lax.ppermute(array, "branch", pairs)


def tensor_scatter(project, index, total):
    if total != 4:
        shifts = list(range(1, total)) + [0]
        parts = project(lax.rem(index + jnp.array(shifts, jnp.int32), total))
        arrived = [
            lax.ppermute(part, "tensor", [(t, (t + shift) % total) for t in range(total)])
            for shift, part in zip(shifts, parts[:-1])
        ]
        return parts[-1], arrived, jnp.ones((total - 1,), jnp.int32)
    order = jnp.array([[3, 2, 1, 0], [0, 2, 3, 1], [3, 1, 0, 2], [0, 1, 2, 3]], jnp.int32)[index]
    first, second = project(order[:2])
    third, own = project(order[2:])
    inner = (index == 1) | (index == 2)
    from_first = lax.ppermute(first, "tensor", [(0, 1), (1, 0), (2, 3), (3, 2)])
    from_inner = lax.ppermute(second, "tensor", [(1, 2), (2, 1)])
    from_ends = lax.ppermute(second, "tensor", [(0, 2), (3, 1)])
    kept = jnp.where(inner, from_first.astype(jnp.float32), 0.0)
    joined = (third.astype(jnp.float32) + kept).astype(jnp.bfloat16)
    from_joined = lax.ppermute(joined, "tensor", [(1, 3), (2, 0), (0, 1), (3, 2)])
    flags = jnp.stack([jnp.where(inner, 0, 1), 1, 1, 1]).astype(jnp.int32)
    return own, [from_first, from_inner, from_ends, from_joined], flags


def local(layer_input, norm_gain, w_query, w_key, w_value, head_grad, parents, row_counts):
    branch_total = lax.axis_size("branch")
    tensor_total = lax.axis_size("tensor")
    tensor_index = lax.axis_index("tensor")
    slots = row_counts.shape[0] // branch_total
    rows, width = layer_input.shape
    column_width = width // tensor_total
    chips = branch_total // 2
    group = w_query.shape[1] // w_key.shape[1]
    kv_local = w_key.shape[1] // HEAD_DIM
    offsets = [(shift, swap) for shift in range(chips) for swap in range(2)]

    def targets():
        index = lax.axis_index("branch")
        chip, core = index // 2, index % 2
        return [lax.rem(chip + s, chips) * 2 + lax.rem(core + e, 2) for s, e in offsets]

    normed, inverse, pieces = normalize(
        layer_input, norm_gain, targets, branch_total, rows // slots
    )
    turned = [
        piece if (s, e) == (0, 0) else branch_send(piece, chips, s, e)
        for piece, (s, e) in zip(pieces, offsets)
    ]
    deltas, delta_turned, centre = attention_backward(
        normed, w_query, w_key, w_value, head_grad, parents, row_counts, slots
    )

    def project(order):
        return back_project(
            order, delta_turned, centre, w_query, w_key, w_value, tensor_total
        )

    own, arrived, flags = tensor_scatter(project, tensor_index, tensor_total)

    weights = None
    for head, delta in enumerate(deltas):
        direct = [delta] + [branch_send(delta, chips, s, 0) for s in range(1, chips)]
        gathered = []
        for part in direct:
            gathered += [part, branch_send(part, chips, 0, 1)]
        weights = weight_gradients(turned, gathered, head, kv_local, group, weights)

    column_start = tensor_index * column_width
    input_columns = lax.dynamic_slice_in_dim(layer_input, column_start, column_width, 1)
    gain_columns = lax.dynamic_slice_in_dim(norm_gain, column_start, column_width, 0)
    flags = jnp.concatenate([flags, jnp.array([width], jnp.int32)])
    grad_input, gain_sum = finish(flags, input_columns, gain_columns, inverse, [own] + arrived)
    if chips == 2:
        here = gain_sum + branch_send(gain_sum, chips, 0, 1)
        there = branch_send(gain_sum, chips, 1, 0) + branch_send(gain_sum, chips, 1, 1)
        grad_gain = here + there
    else:
        grad_gain = lax.psum(gain_sum, "branch")
    return (grad_input, *weights, grad_gain.reshape(column_width))


def solution(mesh):
    placed = (
        P(("parts", "branch"), None),
        P(),
        P(None, "tensor"),
        P(None, "tensor"),
        P(None, "tensor"),
        P(("parts", "branch"), "tensor"),
        P(("parts", "branch")),
        P("parts"),
    )
    return jax.shard_map(
        local,
        mesh=mesh,
        in_specs=placed,
        out_specs=(
            P(("parts", "branch"), "tensor"),
            P(("parts", "branch"), "tensor"),
            P(("parts", "branch"), "tensor"),
            P(("parts", "branch"), "tensor"),
            P(("parts", "tensor")),
        ),
        check_vma=False,
    )
```

time: 142 us -> 94.8 us (0.67)
  blocking collectives: 35.8 us -> 0 us
  waiting for transfers between devices: 52.5 us -> 28.5 us
  Pallas kernels: 30 us -> 41 us
  starting transfers between devices: 10.3 us -> 15.8 us
  other arithmetic: 3.82 us -> 1.6 us
  local copies, waits for them, and re-layouts: 8.65 us -> 6.48 us
    psum x2 -> x0, blocking collectives: 35.8 us -> none  [the longest x1 29.6 us: local(): centre = lax.psum(centre_part, 'tensor') * (1.0 / width)]
    ppermute x3 -> x4, waiting for transfers between devices: 29.4 us -> 15 us  [the longest x1 11.3 us: tensor_scatter(): lax.ppermute(joined, 'tensor', [(1, 3), (2, 0), (0, 1), (3, 2)])]
    pallas_call x3 -> x6, Pallas kernels: 28.9 us -> 38.8 us  [the longest x1 13.6 us: attention_backward(): pl.pallas_call(functools.partial(attention_kernel, slots, kv_local, cuts)...]
    ppermute x6 -> x12, waiting for transfers between devices: 23.2 us -> 13.5 us  [branch_send(): return lax.ppermute(array, 'branch', pairs)]
    ppermute x3 -> x4, starting transfers between devices: 5.76 us -> 9.52 us  [the longest x1 5.75 us: tensor_scatter(): from_ends = lax.ppermute(second, 'tensor', [(0, 2), (3, 1)])]
    reduce_sum x1 -> x0, other arithmetic: 2.84 us -> none  [local(): grad_gain = lax.psum(jnp.sum(d_normed * scaled, axis=0), 'branch')]
    unnamed x18 -> x24, local copies, waits for them, and re-layouts: 6.38 us -> 3.79 us
    dynamic_slice x1 -> x3, local copies, waits for them, and re-layouts: 0.74 us -> 2.61 us  [the longest x1 1.05 us: local(): lax.dynamic_slice_in_dim(layer_input, column_start, column_width, 1)]
  transfers between devices with their start and end apart: 9 -> 16, of which waited for: 3 -> 6; matrix products, arithmetic and copies ran while one was open for 3% -> 4% of each run, Pallas kernels for 7% -> 15%
where the time goes in v2:
time: 94.8 us; the launch traced here: 94.1 us
  Pallas kernels  41 us (43%)
  waiting for transfers between devices  28.5 us (30%)
  starting transfers between devices  15.8 us (17%)
  local copies, waits for them, and re-layouts  6.48 us (7%)
  other arithmetic  1.6 us (2%)
    pallas_call x1, Pallas kernels, attention_backward(): pl.pallas_call(functools.partial(attention_kernel, slots, kv_local, cuts)...  13.6 us
    ppermute x12, waiting for transfers between devices, branch_send(): return lax.ppermute(array, 'branch', pairs)  13.5 us
    pallas_call x2, Pallas kernels, back_project(): pl.pallas_call(functools.partial(back_kernel, cuts), out_shape=(jax.Shape...  12.1 us
    ppermute x1, waiting for transfers between devices, tensor_scatter(): lax.ppermute(joined, 'tensor', [(1, 3), (2, 0), (0, 1), (3, 2)])  11.3 us
    pallas_call x2, Pallas kernels, weight_gradients(): pl.pallas_call(functools.partial(weight_kernel, group, sources), out_shap...  10.5 us
    ppermute x12, starting transfers between devices, branch_send(): return lax.ppermute(array, 'branch', pairs)  6.24 us
    ppermute x1, starting transfers between devices, tensor_scatter(): from_ends = lax.ppermute(second, 'tensor', [(0, 2), (3, 1)])  5.75 us
    unnamed x24, local copies, waits for them, and re-layouts  3.79 us
  transfers between devices with their start and end apart: 16, of which 6 were waited for; matrix products, arithmetic and copies ran while one was open for 4% of the time, Pallas kernels for 15%

profile of v2, /device:TPU:0, one launch (start us, length us, event | category | flops | bytes accessed | tf_op | source)
XLA Modules:
  0.0 94.1 jit_solution(15970008132263750100)
XLA Ops:
  0.7 0.7 constant_dynamic-slice_fusion
  1.4 0.1 slice_bitcast_fusion
  1.4 1.5 %copy-done.1 = bf16[256,3584]{1,0:T(8,128)(2,1)S(1)} copy-done((bf16[256,3584]{1,0:T(8,128)(2,1)S(1)}, bf16[256,3584]{1,0:T(8,128)(2,1)}, u32[]{:S(2)}) %copy-start.1) | copy-done | bytes 1835032
  2.9 0.7 copy-done.7
  3.6 2.2 %norm.1 = (bf16[256,3584]{1,0:T(8,128)(2,1)S(1)}, f32[256,1]{1,0:T(8,128)S(1)}, bf16[896,256]{1,0:T(8,128)(2,1)S(1)}, bf16[896,256]{1,0:T(8,128)(2,1)}, bf16[896...) custom-call(bf16[256,3584]{1,0:T(8,128)(2,1)S(1)} %copy-done.1, f32[3584]{0:T(1024)S(1)} %copy-done.7), custom_call_target="tpu_custom_call" | custom-call | flops 9175040 | bytes 5505024 | tf_op jit(solution)/shard_map/norm/pallas_call | solution.py:60
  5.8 0.8 copy-done.3
  6.6 0.0 copy-start
  6.6 13.6 %attention.1 = (bf16[256,1024]{1,0:T(8,128)(2,1)}, bf16[256,1024]{1,0:T(8,128)(2,1)S(1)}, bf16[2048,256]{1,0:T(8,128)(2,1)S(1)}, f32[16,256]{1,0:T(8,128)S(1)}) custom-call(s32[8]{0:T(128)S(1)} %copy-done.9, s32[256]{0:T(256)S(1)} %copy-done.8, bf16[256,3584]{1,0:T(8,128)(2,1)S(1)} %get-tuple-element.28.normed_hbm, bf16[3584,1024]{1,0:T(8,128)(2,1)} %query_ref.3, ...), custom_call_target="tpu_custom_call" | custom-call | flops 3758096384 | bytes 16515072 | tf_op jit(solution)/shard_map/attention/pallas_call | solution.py:237
  20.3 6.2 %back.3 = (bf16[912,256]{1,0:T(8,128)(2,1)}, bf16[912,256]{1,0:T(8,128)(2,1)}) custom-call(s32[2]{0:T(128)S(1)} %get-tuple-element.49.order_ref, bf16[2048,256]{1,0:T(8,128)(2,1)S(1)} %get-tuple-element.29.turned_ref, f32[16,256]{1,0:T(8,128)S(1)} %get-tuple-element.30.centre_ref, bf16[3584,1024]{1,0:T(8,128)(2,1)} %query_ref.3, ...), custom_call_target="tpu_custom_call" | custom-call | flops 1879048192 | bytes 7340032 | tf_op jit(solution)/shard_map/back/pallas_call | solution.py:323
  26.5 3.1 %collective-permute-start = (bf16[912,256]{1,0:T(8,128)(2,1)}, bf16[912,256]{1,0:T(8,128)(2,1)S(1)}, u32[]{:S(2)}, u32[]{:S(2)}) collective-permute-start(bf16[912,256]{1,0:T(8,128)(2,1)} %get-tuple-element.32), channel_id=1, source_target_pairs={{0,1},{1,0},{2,3},{3,2},{4,5},{5,4},{6,7},{7,6},{8,9},{9,8},{10,11... | collective-permute-start | bytes 1400840 | tf_op jit(solution)/shard_map/ppermute | solution.py:459
  29.6 0.7 collective-permute-start.1
  30.2 5.8 %collective-permute-start.2 = (bf16[912,256]{1,0:T(8,128)(2,1)}, bf16[912,256]{1,0:T(8,128)(2,1)S(1)}, u32[]{:S(2)}, u32[]{:S(2)}) collective-permute-start(bf16[912,256]{1,0:T(8,128)(2,1)} %get-tuple-element.33), channel_id=1, source_target_pairs={{0,2},{3,1},{4,6},{7,5},{8,10},{11,9},{12,14},{15,13},{16,18},{19,... | collective-permute-start | bytes 1400840 | tf_op jit(solution)/shard_map/ppermute | solution.py:461
  36.0 0.1 collective-permute-start.4
  36.1 1.6 %collective-permute-start.11 = (bf16[256,1024]{1,0:T(8,128)(2,1)}, bf16[256,1024]{1,0:T(8,128)(2,1)}, u32[]{:S(2)}, u32[]{:S(2)}) collective-permute-start(bf16[256,1024]{1,0:T(8,128)(2,1)} %get-tuple-element.41.refs_4_), channel_id=1, source_target_pairs={{0,8},{4,12},{8,0},{12,4},{1,9},{5,13},{9,1},{13,5},{2,10},{6,14},... | collective-permute-start | bytes 1572872 | tf_op jit(solution)/shard_map/ppermute | solution.py:443
  37.6 5.9 %back.2 = (bf16[912,256]{1,0:T(8,128)(2,1)S(1)}, bf16[912,256]{1,0:T(8,128)(2,1)S(1)}) custom-call(s32[2]{0:T(128)S(1)} %get-tuple-element.50.order_ref, bf16[2048,256]{1,0:T(8,128)(2,1)S(1)} %get-tuple-element.29.turned_ref, f32[16,256]{1,0:T(8,128)S(1)} %get-tuple-element.30.centre_ref, bf16[3584,1024]{1,0:T(8,128)(2,1)} %query_ref.3, ...), custom_call_target="tpu_custom_call" | custom-call | flops 1879048192 | bytes 7340032 | tf_op jit(solution)/shard_map/back/pallas_call | solution.py:323
  43.6 0.0 collective-permute-done.refs_1_
  43.6 0.9 add_convert_fusion
  44.5 0.0 collective-permute-start.3
  44.5 0.0 collective-permute-done.4.refs_1_
  44.5 0.8 copy-done.5
  45.3 1.3 %collective-permute-start.8 = (bf16[256,1024]{1,0:T(8,128)(2,1)S(1)}, bf16[256,1024]{1,0:T(8,128)(2,1)S(1)}, u32[]{:S(2)}, u32[]{:S(2)}) collective-permute-start(bf16[256,1024]{1,0:T(8,128)(2,1)S(1)} %get-tuple-element.40.refs_4_), channel_id=1, source_target_pairs={{0,8},{4,12},{8,0},{12,4},{1,9},{5,13},{9,1},{13,5},{2,10},{6,14},... | collective-permute-start | bytes 1572872 | tf_op jit(solution)/shard_map/ppermute | solution.py:443
  46.5 0.0 collective-permute-done.1.refs_2_
  46.5 0.8 collective-permute-start.5
  47.3 3.7 %collective-permute-done.2.refs_3_ = bf16[912,256]{1,0:T(8,128)(2,1)S(1)} collective-permute-done((bf16[912,256]{1,0:T(8,128)(2,1)}, bf16[912,256]{1,0:T(8,128)(2,1)S(1)}, u32[]{:S(2)}, u32[]{:S(2)}) %collective-permute-start.2) | collective-permute-done | bytes 466976 | tf_op jit(solution)/shard_map/ppermute | solution.py:461
  51.0 0.0 collective-permute-start.10
  51.0 0.2 collective-permute-done.11.refs_6_
  51.2 0.4 collective-permute-start.12
  51.5 1.1 %constant_dynamic-slice_fusion.1.input_ref = bf16[256,896]{1,0:T(8,128)(2,1)S(1)} fusion(bf16[256,3584]{1,0:T(8,128)(2,1)} %input_ref.1, s32[]{:T(128)S(6)} %select_n.20), kind=kLoop, calls=%fused_computation.6 | loop fusion | bytes 917508 | tf_op jit(solution)/shard_map/dynamic_slice | solution.py:513
  52.6 0.0 copy-start.4
  52.6 0.9 dynamic_slice.10.gain_ref
  53.5 11.3 %collective-permute-done.3.refs_4_ = bf16[912,256]{1,0:T(8,128)(2,1)} collective-permute-done((bf16[912,256]{1,0:T(8,128)(2,1)}, bf16[912,256]{1,0:T(8,128)(2,1)}, u32[]{:S(2)}, u32[]{:S(2)}) %collective-permute-start.3) | collective-permute-done | bytes 466976 | tf_op jit(solution)/shard_map/ppermute | solution.py:464
  64.8 0.1 collective-permute-start.6
  64.8 0.1 pad_add_fusion.flag_ref
  64.9 2.6 %finish.1 = (bf16[256,896]{1,0:T(8,128)(2,1)}, f32[1,896]{1,0:T(1,128)S(1)}) custom-call(s32[5]{0:T(128)S(1)} %pad_add_fusion.flag_ref, bf16[256,896]{1,0:T(8,128)(2,1)S(1)} %constant_dynamic-slice_fusion.1.input_ref, f32[896]{0:T(1024)S(1)} %dynamic_slice.10.gain_ref, f32[256,1]{1,0:T(8,128)S(1)} %get-tuple-element.27.inverse_ref, ...), custom_call_target="tpu_custom_call" | custom-call | flops 4587520 | bytes 3211264 | tf_op jit(solution)/shard_map/finish/pallas_call | solution.py:415
  67.5 4.7 %collective-permute-done.5.refs_2_ = bf16[896,256]{1,0:T(8,128)(2,1)} collective-permute-done((bf16[896,256]{1,0:T(8,128)(2,1)}, bf16[896,256]{1,0:T(8,128)(2,1)}, u32[]{:S(2)}, u32[]{:S(2)}) %collective-permute-start.5) | collective-permute-done | bytes 458784 | tf_op jit(solution)/shard_map/ppermute | solution.py:443
  72.3 1.5 %collective-permute-start.14 = (f32[1,896]{1,0:T(1,128)S(1)}, f32[1,896]{1,0:T(1,128)S(1)}, u32[]{:S(2)}, u32[]{:S(2)}) collective-permute-start(f32[1,896]{1,0:T(1,128)S(1)} %get-tuple-element.48), channel_id=1, source_target_pairs={{0,8},{4,12},{8,0},{12,4},{1,9},{5,13},{9,1},{13,5},{2,10},{6,14},... | collective-permute-start | bytes 10760 | tf_op jit(solution)/shard_map/ppermute | solution.py:443
  73.7 0.0 collective-permute-done.8.refs_6_
  73.8 0.0 collective-permute-start.15
  73.8 7.9 %collective-permute-done.14 = f32[1,896]{1,0:T(1,128)S(1)} collective-permute-done((f32[1,896]{1,0:T(1,128)S(1)}, f32[1,896]{1,0:T(1,128)S(1)}, u32[]{:S(2)}, u32[]{:S(2)}) %collective-permute-start.14) | collective-permute-done | bytes 3616 | tf_op jit(solution)/shard_map/ppermute | solution.py:443
  81.6 0.0 collective-permute-start.13
  81.7 0.0 collective-permute-done.15
  81.7 0.5 collective-permute-start.7
  82.2 0.7 collective-permute-done.13
  82.8 0.2 collective-permute-start.9
  83.0 0.6 add_reduce_fusion
  83.6 0.0 collective-permute-done.6.refs_3_
  83.6 5.6 %weights.2 = (f32[896,1024]{1,0:T(8,128)}, f32[896,512]{1,0:T(8,128)}, f32[896,512]{1,0:T(8,128)}) custom-call(bf16[896,256]{1,0:T(8,128)(2,1)S(1)} %copy-done.4, bf16[896,256]{1,0:T(8,128)(2,1)S(1)} %copy-done.6, bf16[896,256]{1,0:T(8,128)(2,1)} %collective-permute-done.5.refs_2_, bf16[896,256]{1,0:T(8,128)(2,1)S(1)} %collective-permute-done.6.refs_3_, ...), custom_call_target="tpu_custom_call" | custom-call | flops 1879048192 | bytes 7602176 | tf_op jit(solution)/shard_map/weights/pallas_call | solution.py:371
  89.2 4.9 %weights.3 = (f32[896,1024]{1,0:T(8,128)}, f32[896,512]{1,0:T(8,128)}, f32[896,512]{1,0:T(8,128)}) custom-call(bf16[896,256]{1,0:T(8,128)(2,1)S(1)} %copy-done.4, bf16[896,256]{1,0:T(8,128)(2,1)S(1)} %copy-done.6, bf16[896,256]{1,0:T(8,128)(2,1)} %collective-permute-done.5.refs_2_, ...), custom_call_target="tpu_custom_call", output_to_operand_aliasing={{0}: (8, {}), {1}: (9, {}), {2}: (10, {})} | custom-call | flops 1879048192 | bytes 7602176 | tf_op jit(solution)/shard_map/weights/pallas_call | solution.py:371
  (23 shorter events, 0.0 us)
Async XLA Ops:
  0.6 6.0 %copy-start.9 = (s32[8]{0:T(128)S(1)}, s32[8]{0:T(128)}, u32[]{:S(2)}) copy-start(s32[8]{0:T(128)} %count_ref.1) | copy-start | bytes 100
  0.6 6.0 %copy-start.8 = (s32[256]{0:T(256)S(1)}, s32[256]{0:T(256)}, u32[]{:S(2)}) copy-start(s32[256]{0:T(256)} %parent_ref.1) | copy-start | bytes 3076
  1.4 1.5 %copy-start.1 = (bf16[256,3584]{1,0:T(8,128)(2,1)S(1)}, bf16[256,3584]{1,0:T(8,128)(2,1)}, u32[]{:S(2)}) copy-start(bf16[256,3584]{1,0:T(8,128)(2,1)} %input_ref.1) | copy-start | bytes 5505028
  2.9 0.7 copy-start.7
  3.6 3.0 %copy-start.2 = (bf16[256,1024]{1,0:T(8,128)(2,1)S(1)}, bf16[256,1024]{1,0:T(8,128)(2,1)}, u32[]{:S(2)}) copy-start(bf16[256,1024]{1,0:T(8,128)(2,1)} %grad_hbm.1) | copy-start | bytes 1572868
  5.8 0.8 copy-start.3
  6.6 13.6 %copy-start.10 = (bf16[896,256]{1,0:T(8,128)(2,1)}, bf16[896,256]{1,0:T(8,128)(2,1)S(1)}, u32[]{:S(2)}) copy-start(bf16[896,256]{1,0:T(8,128)(2,1)S(1)} %get-tuple-element.39) | copy-start | bytes 1376260
  6.6 13.6 %copy-start.11 = (bf16[896,256]{1,0:T(8,128)(2,1)}, bf16[896,256]{1,0:T(8,128)(2,1)S(1)}, u32[]{:S(2)}) copy-start(bf16[896,256]{1,0:T(8,128)(2,1)S(1)} %get-tuple-element.38) | copy-start | bytes 1376260
  6.6 13.6 %copy-start = (bf16[3584,512]{1,0:T(8,128)(2,1)S(1)}, bf16[3584,512]{1,0:T(8,128)(2,1)}, u32[]{:S(2)}) copy-start(bf16[3584,512]{1,0:T(8,128)(2,1)} %key_ref.3) | copy-start | bytes 11010052
  26.5 17.1 %collective-permute-start = (bf16[912,256]{1,0:T(8,128)(2,1)}, bf16[912,256]{1,0:T(8,128)(2,1)S(1)}, u32[]{:S(2)}, u32[]{:S(2)}) collective-permute-start(bf16[912,256]{1,0:T(8,128)(2,1)} %get-tuple-element.32), channel_id=1, source_target_pairs={{0,1},{1,0},{2,3},{3,2},{4,5},{5,4},{6,7},{7,6},{8,9},{9,8},{10,11... | collective-permute-start | bytes 1400840 | tf_op jit(solution)/shard_map/ppermute | solution.py:459
  29.6 17.0 %collective-permute-start.1 = (bf16[912,256]{1,0:T(8,128)(2,1)}, bf16[912,256]{1,0:T(8,128)(2,1)S(1)}, u32[]{:S(2)}, u32[]{:S(2)}) collective-permute-start(bf16[912,256]{1,0:T(8,128)(2,1)} %get-tuple-element.33), channel_id=1, source_target_pairs={{1,2},{2,1},{5,6},{6,5},{9,10},{10,9},{13,14},{14,13},{17,18},{18,... | collective-permute-start | bytes 1400840 | tf_op jit(solution)/shard_map/ppermute | solution.py:460
  30.2 20.8 %collective-permute-start.2 = (bf16[912,256]{1,0:T(8,128)(2,1)}, bf16[912,256]{1,0:T(8,128)(2,1)S(1)}, u32[]{:S(2)}, u32[]{:S(2)}) collective-permute-start(bf16[912,256]{1,0:T(8,128)(2,1)} %get-tuple-element.33), channel_id=1, source_target_pairs={{0,2},{3,1},{4,6},{7,5},{8,10},{11,9},{12,14},{15,13},{16,18},{19,... | collective-permute-start | bytes 1400840 | tf_op jit(solution)/shard_map/ppermute | solution.py:461
  36.0 8.5 %collective-permute-start.4 = (bf16[896,256]{1,0:T(8,128)(2,1)}, bf16[896,256]{1,0:T(8,128)(2,1)S(1)}, u32[]{:S(2)}, u32[]{:S(2)}) collective-permute-start(bf16[896,256]{1,0:T(8,128)(2,1)} %get-tuple-element.37), channel_id=1, source_target_pairs={{0,4},{4,0},{8,12},{12,8},{1,5},{5,1},{9,13},{13,9},{2,6},{6,2},{1... | collective-permute-start | bytes 1376264 | tf_op jit(solution)/shard_map/ppermute | solution.py:443
  36.1 15.1 %collective-permute-start.11 = (bf16[256,1024]{1,0:T(8,128)(2,1)}, bf16[256,1024]{1,0:T(8,128)(2,1)}, u32[]{:S(2)}, u32[]{:S(2)}) collective-permute-start(bf16[256,1024]{1,0:T(8,128)(2,1)} %get-tuple-element.41.refs_4_), channel_id=1, source_target_pairs={{0,8},{4,12},{8,0},{12,4},{1,9},{5,13},{9,1},{13,5},{2,10},{6,14},... | collective-permute-start | bytes 1572872 | tf_op jit(solution)/shard_map/ppermute | solution.py:443
  44.5 20.3 %collective-permute-start.3 = (bf16[912,256]{1,0:T(8,128)(2,1)}, bf16[912,256]{1,0:T(8,128)(2,1)}, u32[]{:S(2)}, u32[]{:S(2)}) collective-permute-start(bf16[912,256]{1,0:T(8,128)(2,1)} %add_convert_fusion), channel_id=1, source_target_pairs={{1,3},{2,0},{0,1},{3,2},{5,7},{6,4},{4,5},{7,6},{9,11},{10,8},{8,9... | collective-permute-start | bytes 1400840 | tf_op jit(solution)/shard_map/ppermute | solution.py:464
  44.5 0.8 copy-start.5
  45.3 28.5 %collective-permute-start.8 = (bf16[256,1024]{1,0:T(8,128)(2,1)S(1)}, bf16[256,1024]{1,0:T(8,128)(2,1)S(1)}, u32[]{:S(2)}, u32[]{:S(2)}) collective-permute-start(bf16[256,1024]{1,0:T(8,128)(2,1)S(1)} %get-tuple-element.40.refs_4_), channel_id=1, source_target_pairs={{0,8},{4,12},{8,0},{12,4},{1,9},{5,13},{9,1},{13,5},{2,10},{6,14},... | collective-permute-start | bytes 1572872 | tf_op jit(solution)/shard_map/ppermute | solution.py:443
  46.5 25.7 %collective-permute-start.5 = (bf16[896,256]{1,0:T(8,128)(2,1)}, bf16[896,256]{1,0:T(8,128)(2,1)}, u32[]{:S(2)}, u32[]{:S(2)}) collective-permute-start(bf16[896,256]{1,0:T(8,128)(2,1)} %copy-done.11), channel_id=1, source_target_pairs={{0,8},{4,12},{8,0},{12,4},{1,9},{5,13},{9,1},{13,5},{2,10},{6,14},... | collective-permute-start | bytes 1376264 | tf_op jit(solution)/shard_map/ppermute | solution.py:443
  51.0 32.6 %collective-permute-start.10 = (bf16[256,1024]{1,0:T(8,128)(2,1)}, bf16[256,1024]{1,0:T(8,128)(2,1)}, u32[]{:S(2)}, u32[]{:S(2)}) collective-permute-start(bf16[256,1024]{1,0:T(8,128)(2,1)} %get-tuple-element.41.refs_4_), channel_id=1, source_target_pairs={{0,4},{4,0},{8,12},{12,8},{1,5},{5,1},{9,13},{13,9},{2,6},{6,2},{1... | collective-permute-start | bytes 1572872 | tf_op jit(solution)/shard_map/ppermute | solution.py:443
  51.2 32.4 %collective-permute-start.12 = (bf16[256,1024]{1,0:T(8,128)(2,1)}, bf16[256,1024]{1,0:T(8,128)(2,1)}, u32[]{:S(2)}, u32[]{:S(2)}) collective-permute-start(bf16[256,1024]{1,0:T(8,128)(2,1)} %collective-permute-done.11.refs_6_), channel_id=1, source_target_pairs={{0,4},{4,0},{8,12},{12,8},{1,5},{5,1},{9,13},{13,9},{2,6},{6,2},{1... | collective-permute-start | bytes 1572872 | tf_op jit(solution)/shard_map/ppermute | solution.py:443
  52.6 31.0 %copy-start.4 = (bf16[896,256]{1,0:T(8,128)(2,1)S(1)}, bf16[896,256]{1,0:T(8,128)(2,1)}, u32[]{:S(2)}) copy-start(bf16[896,256]{1,0:T(8,128)(2,1)} %copy-done.3) | copy-start | bytes 1376260
  52.6 31.0 %copy-start.6 = (bf16[896,256]{1,0:T(8,128)(2,1)S(1)}, bf16[896,256]{1,0:T(8,128)(2,1)}, u32[]{:S(2)}) copy-start(bf16[896,256]{1,0:T(8,128)(2,1)} %copy-done.5) | copy-start | bytes 1376260
  64.8 18.8 %collective-permute-start.6 = (bf16[896,256]{1,0:T(8,128)(2,1)}, bf16[896,256]{1,0:T(8,128)(2,1)S(1)}, u32[]{:S(2)}, u32[]{:S(2)}) collective-permute-start(bf16[896,256]{1,0:T(8,128)(2,1)} %copy-done.10), channel_id=1, source_target_pairs={{0,12},{4,8},{8,4},{12,0},{1,13},{5,9},{9,5},{13,1},{2,14},{6,10},... | collective-permute-start | bytes 1376264 | tf_op jit(solution)/shard_map/ppermute | solution.py:443
  72.3 9.4 %collective-permute-start.14 = (f32[1,896]{1,0:T(1,128)S(1)}, f32[1,896]{1,0:T(1,128)S(1)}, u32[]{:S(2)}, u32[]{:S(2)}) collective-permute-start(f32[1,896]{1,0:T(1,128)S(1)} %get-tuple-element.48), channel_id=1, source_target_pairs={{0,8},{4,12},{8,0},{12,4},{1,9},{5,13},{9,1},{13,5},{2,10},{6,14},... | collective-permute-start | bytes 10760 | tf_op jit(solution)/shard_map/ppermute | solution.py:443
  73.8 7.9 %collective-permute-start.15 = (f32[1,896]{1,0:T(1,128)S(1)}, f32[1,896]{1,0:T(1,128)S(1)}, u32[]{:S(2)}, u32[]{:S(2)}) collective-permute-start(f32[1,896]{1,0:T(1,128)S(1)} %get-tuple-element.48), channel_id=1, source_target_pairs={{0,12},{4,8},{8,4},{12,0},{1,13},{5,9},{9,5},{13,1},{2,14},{6,10},... | collective-permute-start | bytes 10760 | tf_op jit(solution)/shard_map/ppermute | solution.py:443
  81.6 1.2 %collective-permute-start.13 = (f32[1,896]{1,0:T(1,128)S(1)}, f32[1,896]{1,0:T(1,128)S(1)}, u32[]{:S(2)}, u32[]{:S(2)}) collective-permute-start(f32[1,896]{1,0:T(1,128)S(1)} %get-tuple-element.48), channel_id=1, source_target_pairs={{0,4},{4,0},{8,12},{12,8},{1,5},{5,1},{9,13},{13,9},{2,6},{6,2},{1... | collective-permute-start | bytes 10760 | tf_op jit(solution)/shard_map/ppermute | solution.py:443
  81.7 7.6 %collective-permute-start.7 = (bf16[256,1024]{1,0:T(8,128)(2,1)S(1)}, bf16[256,1024]{1,0:T(8,128)(2,1)S(1)}, u32[]{:S(2)}, u32[]{:S(2)}) collective-permute-start(bf16[256,1024]{1,0:T(8,128)(2,1)S(1)} %get-tuple-element.40.refs_4_), channel_id=1, source_target_pairs={{0,4},{4,0},{8,12},{12,8},{1,5},{5,1},{9,13},{13,9},{2,6},{6,2},{1... | collective-permute-start | bytes 1572872 | tf_op jit(solution)/shard_map/ppermute | solution.py:443
  82.8 6.4 %collective-permute-start.9 = (bf16[256,1024]{1,0:T(8,128)(2,1)S(1)}, bf16[256,1024]{1,0:T(8,128)(2,1)S(1)}, u32[]{:S(2)}, u32[]{:S(2)}) collective-permute-start(bf16[256,1024]{1,0:T(8,128)(2,1)S(1)} %collective-permute-done.8.refs_6_), channel_id=1, source_target_pairs={{0,4},{4,0},{8,12},{12,8},{1,5},{5,1},{9,13},{13,9},{2,6},{6,2},{1... | collective-permute-start | bytes 1572872 | tf_op jit(solution)/shard_map/ppermute | solution.py:443

commit v3 on v1

v3 whole, which is shorter than its diff:
```python
import functools

import jax
import jax.numpy as jnp
from jax import lax
from jax.experimental import pallas as pl
from jax.experimental.pallas import tpu as pltpu
from jax.sharding import PartitionSpec as P

HEAD_DIM = 256
MIB = 1024 * 1024
CENTRE_ROWS = 16
VMEM_LIMIT = 64 * MIB


epsilon = 1e-06
softcap_limit = 50.0


def nn_dot(left, right):
    return lax.dot_general(
        left, right, (((1,), (0,)), ((), ())), preferred_element_type=jnp.float32
    )


def nt_dot(left, right):
    return lax.dot_general(
        left, right, (((1,), (1,)), ((), ())), preferred_element_type=jnp.float32
    )


def tn_dot(left, right):
    return lax.dot_general(
        left, right, (((0,), (0,)), ((), ())), preferred_element_type=jnp.float32
    )


def small_cost():
    return pl.CostEstimate(flops=1000000, bytes_accessed=100000, transcendentals=0)


def norm_kernel(targets, cut, input_ref, gain_ref, normed_ref, inverse_ref, *rest):
    input_cut_ref, gain_cut_ref = rest[:2]
    piece_refs, (turned, gain_row) = rest[2:-2], rest[-2:]
    rows, width = input_ref.shape
    values = input_ref[...].astype(jnp.float32)
    inverse = lax.rsqrt(jnp.mean(values * values, axis=-1, keepdims=True) + epsilon)
    inverse_ref[...] = inverse
    gain = gain_ref[...].reshape(1, width)
    normed = (values * inverse * (1.0 + gain)).astype(jnp.bfloat16)
    normed_ref[...] = normed
    turned[...] = normed.T
    depth = width // len(piece_refs)
    for target, piece_ref in zip(targets(), piece_refs):
        start = pl.multiple_of(target * depth, 16)
        piece_ref[...] = turned[pl.ds(start, depth), :]
    wide = input_cut_ref.shape[1]
    if cut:
        gain_row[...] = gain
        start = pl.multiple_of(lax.axis_index("tensor") * wide, 128)
        input_cut_ref[...] = input_ref[:, pl.ds(start, wide)]
        gain_cut_ref[...] = gain_row[:, pl.ds(start, wide)]
    else:
        input_cut_ref[...] = jnp.zeros_like(input_cut_ref)
        gain_cut_ref[...] = jnp.zeros_like(gain_cut_ref)


def normalize(layer_input, norm_gain, targets, pieces, block, column_width):
    rows, width = layer_input.shape
    depth = width // pieces
    cut = column_width % 128 == 0
    wide = column_width if cut else 128
    out = pl.pallas_call(
        functools.partial(norm_kernel, targets, cut),
        out_shape=(
            jax.ShapeDtypeStruct((rows, width), jnp.bfloat16),
            jax.ShapeDtypeStruct((rows, 1), jnp.float32),
            jax.ShapeDtypeStruct((rows, wide), jnp.bfloat16),
            jax.ShapeDtypeStruct((1, wide), jnp.float32),
        )
        + (jax.ShapeDtypeStruct((depth, rows), jnp.bfloat16),) * pieces,
        grid=(rows // block,),
        in_specs=[
            pl.BlockSpec((block, width), lambda i: (i, 0)),
            pl.BlockSpec((width,), lambda i: (0,)),
        ],
        out_specs=(
            pl.BlockSpec((block, width), lambda i: (i, 0)),
            pl.BlockSpec((block, 1), lambda i: (i, 0)),
            pl.BlockSpec((block, wide), lambda i: (i, 0)),
            pl.BlockSpec((1, wide), lambda i: (0, 0)),
        )
        + (pl.BlockSpec((depth, block), lambda i: (0, i)),) * pieces,
        scratch_shapes=[
            pltpu.VMEM((width, block), jnp.bfloat16),
            pltpu.VMEM((1, width), jnp.float32),
        ],
        compiler_params=pltpu.CompilerParams(vmem_limit_bytes=VMEM_LIMIT),
        cost_estimate=small_cost(),
        name="norm",
    )(layer_input, norm_gain)
    if cut:
        input_cut, gain_cut = out[2], out[3]
    else:
        start = lax.axis_index("tensor") * column_width
        input_cut = lax.dynamic_slice_in_dim(layer_input, start, column_width, 1)
        gain_cut = lax.dynamic_slice_in_dim(norm_gain, start, column_width, 0)
        gain_cut = gain_cut.reshape(1, column_width)
    return out[0], out[1], input_cut, gain_cut, out[4:]


def ancestor_mask(parent_row):
    rows = parent_row.shape[1]
    row = lax.broadcasted_iota(jnp.int32, (rows, rows), 0)
    column = lax.broadcasted_iota(jnp.int32, (rows, rows), 1)
    reached = jnp.where((parent_row == row) | (row == column), 1.0, 0.0)
    for squaring in range(rows.bit_length() - 1):
        halfway = reached.astype(jnp.bfloat16)
        reached = jnp.minimum(nn_dot(halfway, halfway), 1.0)
    return reached.T


def attention_kernel(
    slots,
    kv_local,
    group,
    packs,
    count_ref,
    parent_ref,
    normed_hbm,
    query_hbm,
    key_hbm,
    value_hbm,
    grad_hbm,
    *rest,
):
    piece_hbm, rest = rest[:packs], rest[packs:]
    pack_hbm, rest = rest[:packs], rest[packs:]
    delta_hbm, rest = rest[: kv_local - 1], rest[kv_local - 1 :]
    turned_hbm, centre_ref, normed_ref, weight_ref, grad_ref = rest[:5]
    sum_ref, delta_ref, turned_ref, load_sem, weight_sem, pack_sem, store_sem = rest[5:]
    head_dim = HEAD_DIM
    rows, width = normed_ref.shape
    block = rows // slots
    span = (group + 2) * head_dim
    mid = group * head_dim

    def fetch(h):
        places = ((query_hbm, 0, mid), (key_hbm, mid, head_dim), (value_hbm, mid + head_dim, head_dim))
        return [
            pltpu.make_async_copy(
                source.at[:, pl.ds(h * wide, wide)],
                weight_ref.at[h, :, pl.ds(start, wide)],
                weight_sem.at[h, which],
            )
            for which, (source, start, wide) in enumerate(places)
        ]

    loads = [
        pltpu.make_async_copy(normed_hbm, normed_ref, load_sem.at[0]),
        pltpu.make_async_copy(grad_hbm, grad_ref, load_sem.at[1]),
    ]
    fetches = [fetch(h) for h in range(kv_local)]
    loads[0].start()
    for copy in sum(fetches, []) + loads[1:]:
        copy.start()
    depth = piece_hbm[0].shape[0]
    stores = [
        pltpu.make_async_copy(piece, pack.at[pl.ds(0, depth), :], pack_sem.at[place])
        for place, (piece, pack) in enumerate(zip(piece_hbm, pack_hbm))
    ]
    for store in stores:
        store.start()

    first_count = lax.axis_index("branch") * slots
    parents = parent_ref[...].reshape(1, rows)
    allowed_slots = [
        ancestor_mask(parents[:, slot * block : (slot + 1) * block]) for slot in range(slots)
    ]
    loads[0].wait()
    for h in range(kv_local):
        for copy in fetches[h]:
            copy.wait()
        sum_ref[h] = nn_dot(normed_ref[...], weight_ref[h])
    loads[1].wait()

    scale = head_dim ** (-0.5)
    pairs = [(h, slot) for h in range(kv_local) for slot in range(slots)]
    queries, keys, values, grads = {}, {}, {}, {}
    for h, slot in pairs:
        lines = slice(slot * block, (slot + 1) * block)
        base = h * mid
        live = (
            lax.broadcasted_iota(jnp.int32, (block, head_dim), 0) < count_ref[first_count + slot]
        )
        queries[h, slot] = jnp.concatenate(
            [sum_ref[h, lines, g * head_dim : (g + 1) * head_dim] for g in range(group)], axis=0
        ).astype(jnp.bfloat16)
        keys[h, slot] = sum_ref[h, lines, mid : mid + head_dim].astype(jnp.bfloat16)
        values[h, slot] = sum_ref[h, lines, mid + head_dim :].astype(jnp.bfloat16)
        grads[h, slot] = jnp.concatenate(
            [
                jnp.where(
                    live,
                    grad_ref[lines, base + g * head_dim : base + (g + 1) * head_dim].astype(
                        jnp.float32
                    ),
                    0.0,
                )
                for g in range(group)
            ],
            axis=0,
        ).astype(jnp.bfloat16)
    scores = jnp.concatenate([nt_dot(queries[p], keys[p]) for p in pairs], axis=0)
    d_probs = jnp.concatenate([nt_dot(grads[p], values[p]) for p in pairs], axis=0)
    allowed = jnp.concatenate([allowed_slots[slot] for h, slot in pairs for g in range(group)], axis=0)
    bounded = jnp.tanh(scores * (scale / softcap_limit))
    weights = allowed * jnp.exp(softcap_limit * bounded)
    probabilities = weights * (1.0 / jnp.sum(weights, axis=-1, keepdims=True))
    d_scores = probabilities * (
        d_probs - jnp.sum(probabilities * d_probs, axis=-1, keepdims=True)
    )
    d_raw_all = (d_scores * (1.0 - bounded * bounded) * scale).astype(jnp.bfloat16)
    prob_half_all = probabilities.astype(jnp.bfloat16)
    centre_parts = [jnp.zeros((block, 1), jnp.float32) for _ in range(slots)]
    for place, (h, slot) in enumerate(pairs):
        lines = slice(slot * block, (slot + 1) * block)
        taken = slice(place * group * block, (place + 1) * group * block)
        d_raw, prob_half = d_raw_all[taken], prob_half_all[taken]
        d_query = nn_dot(d_raw, keys[h, slot]).astype(jnp.bfloat16)
        d_key = tn_dot(d_raw, queries[h, slot]).astype(jnp.bfloat16)
        d_value = tn_dot(prob_half, grads[h, slot]).astype(jnp.bfloat16)
        parts = [d_query[g * block : (g + 1) * block] for g in range(group)] + [d_key, d_value]
        product = None
        for which, part in enumerate(parts):
            columns = slice(which * head_dim, (which + 1) * head_dim)
            delta_ref[h, which * rows + slot * block : which * rows + (slot + 1) * block] = part
            turned_ref[h, columns, lines] = part.T
            term = part.astype(jnp.float32) * sum_ref[h, lines, columns]
            product = term if product is None else product + term
        centre_parts[slot] += jnp.sum(product, axis=-1, keepdims=True)
    lasts = []
    for h in range(kv_local):
        lasts.append(
            pltpu.make_async_copy(
                turned_ref.at[h], turned_hbm.at[pl.ds(h * span, span), :], store_sem.at[h]
            )
        )
    lasts += [
        pltpu.make_async_copy(
            delta_ref.at[0],
            pack.at[pl.ds(depth, (group + 2) * rows), :],
            store_sem.at[kv_local + place],
        )
        for place, pack in enumerate(pack_hbm)
    ]
    lasts += [
        pltpu.make_async_copy(delta_ref.at[h + 1], out, store_sem.at[kv_local + packs + h])
        for h, out in enumerate(delta_hbm)
    ]
    for store in lasts:
        store.start()
    centre = jnp.concatenate(centre_parts, axis=0)
    centre_ref[...] = jnp.broadcast_to(centre, (rows, 128)).T[:CENTRE_ROWS]
    for store in stores + lasts:
        store.wait()


def attention_backward(
    normed, w_query, w_key, w_value, head_grad, parents, counts, pieces, slots
):
    rows, width = normed.shape
    kv_local = w_key.shape[1] // HEAD_DIM
    group = w_query.shape[1] // w_key.shape[1]
    span = (group + 2) * HEAD_DIM
    stack = (group + 2) * rows
    packs = len(pieces)
    depth = pieces[0].shape[0]
    hbm = pl.BlockSpec(memory_space=pl.ANY)
    vmem = pl.BlockSpec(memory_space=pltpu.VMEM)
    out = pl.pallas_call(
        functools.partial(attention_kernel, slots, kv_local, group, packs),
        out_shape=(jax.ShapeDtypeStruct((depth + stack, HEAD_DIM), jnp.bfloat16),) * packs
        + (jax.ShapeDtypeStruct((stack, HEAD_DIM), jnp.bfloat16),) * (kv_local - 1)
        + (
            jax.ShapeDtypeStruct((kv_local * span, rows), jnp.bfloat16),
            jax.ShapeDtypeStruct((CENTRE_ROWS, rows), jnp.float32),
        ),
        in_specs=[pl.BlockSpec(memory_space=pltpu.SMEM), vmem] + [hbm] * (5 + packs),
        out_specs=(hbm,) * (packs + kv_local) + (vmem,),
        scratch_shapes=[
            pltpu.VMEM((rows, width), jnp.bfloat16),
            pltpu.VMEM((kv_local, width, span), jnp.bfloat16),
            pltpu.VMEM(head_grad.shape, jnp.bfloat16),
            pltpu.VMEM((kv_local, rows, span), jnp.float32),
            pltpu.VMEM((kv_local, stack, HEAD_DIM), jnp.bfloat16),
            pltpu.VMEM((kv_local, span, rows), jnp.bfloat16),
            pltpu.SemaphoreType.DMA((2,)),
            pltpu.SemaphoreType.DMA((kv_local, 3)),
            pltpu.SemaphoreType.DMA((packs,)),
            pltpu.SemaphoreType.DMA((packs + 2 * kv_local - 1,)),
        ],
        compiler_params=pltpu.CompilerParams(vmem_limit_bytes=VMEM_LIMIT),
        cost_estimate=small_cost(),
        name="attention",
    )(counts, parents, normed, w_query, w_key, w_value, head_grad, *pieces)
    return out[:packs], out[packs:-2], out[-2], out[-1]


def back_kernel(order, cuts, blocks, *refs):
    turned_ref, centre_ref, query_hbm, key_hbm, value_hbm = refs[:5]
    rest = refs[5:]
    pieces = len(rest) - 4
    out_hbm = rest[:pieces]
    weight_ref, kept, load_sem, store_sem = rest[pieces:]
    head_dim = HEAD_DIM
    kv_local = key_hbm.shape[1] // head_dim
    group = query_hbm.shape[1] // key_hbm.shape[1]
    span = (group + 2) * head_dim
    mid = group * head_dim
    depth = query_hbm.shape[0] // blocks
    lines = depth // cuts
    steps = [(piece, cut) for piece in range(pieces) for cut in range(cuts)]
    picked = order()

    def fetch(step):
        piece, cut = steps[step]
        start = pl.multiple_of(picked[piece] * depth + cut * lines, 16)
        copies = []
        for h in range(kv_local):
            base = h * span
            for source, place, wide in (
                (query_hbm, base, mid),
                (key_hbm, base + mid, head_dim),
                (value_hbm, base + mid + head_dim, head_dim),
            ):
                copies.append(
                    pltpu.make_async_copy(
                        source.at[pl.ds(start, lines), pl.ds(h * wide, wide)],
                        weight_ref.at[step, :, pl.ds(place, wide)],
                        load_sem.at[step, len(copies)],
                    )
                )
        return copies

    fetches = [fetch(step) for step in range(len(steps))]
    for copy in sum(fetches, []):
        copy.start()
    stores = []
    for step, (piece, cut) in enumerate(steps):
        for copy in fetches[step]:
            copy.wait()
        total = nn_dot(weight_ref[step], turned_ref[...])
        kept[piece, cut * lines : (cut + 1) * lines, :] = total.astype(jnp.bfloat16)
        if cut == cuts - 1:
            kept[piece, depth:, :] = centre_ref[...].astype(jnp.bfloat16)
            stores.append(pltpu.make_async_copy(kept.at[piece], out_hbm[piece], store_sem.at[piece]))
            stores[-1].start()
    for store in stores:
        store.wait()


def back_project(order, pieces, turned, centre, w_query, w_key, w_value, blocks):
    total, rows = turned.shape
    depth = w_query.shape[0] // blocks
    cuts = 2
    kv_local = w_key.shape[1] // HEAD_DIM
    hbm = pl.BlockSpec(memory_space=pl.ANY)
    vmem = pl.BlockSpec(memory_space=pltpu.VMEM)
    return pl.pallas_call(
        functools.partial(back_kernel, order, cuts, blocks),
        out_shape=(jax.ShapeDtypeStruct((depth + CENTRE_ROWS, rows), jnp.bfloat16),) * pieces,
        in_specs=[vmem, vmem] + [hbm] * 3,
        out_specs=(hbm,) * pieces,
        scratch_shapes=[
            pltpu.VMEM((pieces * cuts, depth // cuts, total), jnp.bfloat16),
            pltpu.VMEM((pieces, depth + CENTRE_ROWS, rows), jnp.bfloat16),
            pltpu.SemaphoreType.DMA((pieces * cuts, 3 * kv_local)),
            pltpu.SemaphoreType.DMA((pieces,)),
        ],
        compiler_params=pltpu.CompilerParams(vmem_limit_bytes=VMEM_LIMIT),
        cost_estimate=small_cost(),
        name="back",
    )(turned, centre, w_query, w_key, w_value)


def weight_kernel(group, head, sources, skips, cuts, *refs):
    turned_hbm, delta_hbm = refs[:sources], refs[sources : 2 * sources]
    query_hbm, key_hbm, value_hbm, token_ref = refs[-10:-6]
    turned_ref, delta_ref, kept, turned_sem, delta_sem, store_sem = refs[-6:]
    token_ref[...] = jnp.zeros_like(token_ref)
    depth = turned_ref.shape[0]
    rows = turned_ref.shape[1] // sources
    cut = depth // cuts
    mid = group * HEAD_DIM
    loads = []
    for place in range(sources):
        spot = pl.ds(place * rows, rows)
        for block in range(group + 2):
            loads.append(
                pltpu.make_async_copy(
                    delta_hbm[place].at[pl.ds(skips[place] + block * rows, rows), :],
                    delta_ref.at[spot, pl.ds(block * HEAD_DIM, HEAD_DIM)],
                    delta_sem.at[place, block],
                )
            )
        loads.append(
            pltpu.make_async_copy(
                turned_hbm[place].at[pl.ds(0, depth), :],
                turned_ref.at[:, spot],
                turned_sem.at[place],
            )
        )
    for load in loads:
        load.start()
    for load in loads:
        load.wait()
    stores = []
    for step in range(cuts):
        lines = pl.ds(step * cut, cut)
        kept[lines, :] = nn_dot(turned_ref[lines, :], delta_ref[...])
        for which, (out_hbm, start, wide) in enumerate(
            (
                (query_hbm, 0, mid),
                (key_hbm, mid, HEAD_DIM),
                (value_hbm, mid + HEAD_DIM, HEAD_DIM),
            )
        ):
            stores.append(
                pltpu.make_async_copy(
                    kept.at[lines, pl.ds(start, wide)],
                    out_hbm.at[lines, pl.ds(head * wide, wide)],
                    store_sem.at[step, which],
                )
            )
            stores[-1].start()
    for store in stores:
        store.wait()


def weight_gradients(depth, rows, turned, deltas, skips, head, kv_local, group, before):
    span = (group + 2) * HEAD_DIM
    cuts = 4 if depth % 64 == 0 else 2
    sources = len(turned)
    kept = list(before) if before is not None else []
    hbm = pl.BlockSpec(memory_space=pl.ANY)
    return pl.pallas_call(
        functools.partial(weight_kernel, group, head, sources, skips, cuts),
        out_shape=(
            jax.ShapeDtypeStruct((depth, kv_local * group * HEAD_DIM), jnp.float32),
            jax.ShapeDtypeStruct((depth, kv_local * HEAD_DIM), jnp.float32),
            jax.ShapeDtypeStruct((depth, kv_local * HEAD_DIM), jnp.float32),
            jax.ShapeDtypeStruct((8, 128), jnp.float32),
        ),
        in_specs=[hbm] * (2 * sources + len(kept)),
        out_specs=(hbm,) * 3 + (pl.BlockSpec(memory_space=pltpu.VMEM),),
        input_output_aliases={2 * sources + i: i for i in range(len(kept))},
        scratch_shapes=[
            pltpu.VMEM((depth, sources * rows), jnp.bfloat16),
            pltpu.VMEM((sources * rows, span), jnp.bfloat16),
            pltpu.VMEM((depth, span), jnp.float32),
            pltpu.SemaphoreType.DMA((sources,)),
            pltpu.SemaphoreType.DMA((sources, group + 2)),
            pltpu.SemaphoreType.DMA((cuts, 3)),
        ],
        compiler_params=pltpu.CompilerParams(vmem_limit_bytes=VMEM_LIMIT),
        cost_estimate=small_cost(),
        name="weights",
    )(*turned, *deltas, *kept)


def gate_kernel(*refs):
    del refs


def gate(arrays, tokens):
    hbm = pl.BlockSpec(memory_space=pl.ANY)
    return pl.pallas_call(
        gate_kernel,
        out_shape=tuple(jax.ShapeDtypeStruct(x.shape, x.dtype) for x in arrays),
        in_specs=[hbm] * (len(arrays) + len(tokens)),
        out_specs=(hbm,) * len(arrays),
        input_output_aliases={i: i for i in range(len(arrays))},
        compiler_params=pltpu.CompilerParams(vmem_limit_bytes=VMEM_LIMIT),
        cost_estimate=small_cost(),
        name="gate",
    )(*arrays, *tokens)


def join_kernel(inner_ref, other_ref, end_ref, out_ref, token_ref):
    token_ref[...] = jnp.zeros_like(token_ref)
    index = lax.axis_index("tensor")
    inner = (index > 0) & (index < lax.axis_size("tensor") - 1)

    @pl.when(inner)
    def _():
        out_ref[...] = (
            inner_ref[...].astype(jnp.float32) + other_ref[...].astype(jnp.float32)
        ).astype(jnp.bfloat16)

    @pl.when(jnp.logical_not(inner))
    def _():
        out_ref[...] = end_ref[...]


def join(inner_part, other, end_part):
    vmem = pl.BlockSpec(memory_space=pltpu.VMEM)
    return pl.pallas_call(
        join_kernel,
        out_shape=(
            jax.ShapeDtypeStruct(end_part.shape, end_part.dtype),
            jax.ShapeDtypeStruct((8, 128), jnp.float32),
        ),
        in_specs=[vmem] * 3,
        out_specs=(vmem, vmem),
        compiler_params=pltpu.CompilerParams(vmem_limit_bytes=VMEM_LIMIT),
        cost_estimate=small_cost(),
        name="join",
    )(inner_part, other, end_part)


def finish_kernel(width, for_ends, for_inner, input_ref, gain_ref, inverse_ref, *refs):
    part_refs, (out_ref, sum_ref) = refs[:-3], refs[-2:]
    rows, wide = out_ref.shape
    index = lax.axis_index("tensor")
    ends = ((index == 0) | (index == lax.axis_size("tensor") - 1)).astype(jnp.float32)
    total = None
    for place, part_ref in enumerate(part_refs):
        part = part_ref[...].astype(jnp.float32)
        if place < for_ends:
            part = part * ends
        elif place < for_ends + for_inner:
            part = part * (1.0 - ends)
        total = part if total is None else total + part
    total = total.T
    d_normed = total[:, :wide]
    centre = total[:, wide : wide + 1] * (1.0 / width)
    inverse = inverse_ref[...]
    scaled = input_ref[...].astype(jnp.float32) * inverse
    out_ref[...] = (
        inverse * ((1.0 + gain_ref[...]) * d_normed - scaled * centre)
    ).astype(jnp.bfloat16)
    sum_ref[...] = jnp.sum(d_normed * scaled, axis=0, keepdims=True)


def finish(width, for_ends, for_inner, input_columns, gain_columns, inverse, parts, token):
    rows, wide = input_columns.shape
    whole = lambda array: pl.BlockSpec(array.shape, lambda i: (0, 0))
    return pl.pallas_call(
        functools.partial(finish_kernel, width, for_ends, for_inner),
        out_shape=(
            jax.ShapeDtypeStruct((rows, wide), jnp.bfloat16),
            jax.ShapeDtypeStruct((1, wide), jnp.float32),
        ),
        grid=(1,),
        in_specs=[whole(x) for x in (input_columns, gain_columns, inverse, *parts)]
        + [pl.BlockSpec(memory_space=pl.ANY)],
        out_specs=(
            pl.BlockSpec((rows, wide), lambda i: (0, 0)),
            pl.BlockSpec((1, wide), lambda i: (0, 0)),
        ),
        compiler_params=pltpu.CompilerParams(vmem_limit_bytes=VMEM_LIMIT),
        cost_estimate=small_cost(),
        name="finish",
    )(input_columns, gain_columns, inverse, *parts, token)


def branch_send(array, chips, shift, swap):
    pairs = [
        (c * 2 + k, ((c + shift) % chips) * 2 + (k ^ swap)) for c in range(chips) for k in range(2)
    ]
    return lax.ppermute(array, "branch", pairs)


def pick(table, index):
    chosen = table[-1]
    for place in range(len(table) - 2, -1, -1):
        chosen = jnp.where(index == place, table[place], chosen)
    return chosen


def tensor_scatter(project, total):
    index = lambda: lax.axis_index("tensor")
    if total != 4:
        shifts = list(range(1, total)) + [0]
        parts = project(lambda: [lax.rem(index() + shift, total) for shift in shifts], total)
        arrived = [
            lax.ppermute(part, "tensor", [(t, (t + shift) % total) for t in range(total)])
            for shift, part in zip(shifts, parts[:-1])
        ]
        return [parts[-1]] + arrived, 0, 0, (parts[0],), (arrived[-1],)
    table = [[3, 0, 3, 0], [0, 2, 1, 3], [2, 3, 0, 1], [1, 1, 2, 2]]
    order = lambda rows: lambda: [pick(table[row], index()) for row in rows]
    first, second = project(order((0, 1)), 2)
    from_first = lax.ppermute(first, "tensor", [(0, 1), (1, 0), (2, 3), (3, 2)])
    from_inner = lax.ppermute(second, "tensor", [(1, 2), (2, 1)])
    third, fourth = project(order((2, 3)), 2)
    from_ends = lax.ppermute(third, "tensor", [(0, 2), (3, 1)])
    joined, token = join(third, from_first, fourth)
    from_joined = lax.ppermute(joined, "tensor", [(1, 3), (2, 0), (0, 1), (3, 2)])
    parts = [from_first, second, fourth, from_inner, from_ends, from_joined]
    return parts, 2, 1, (token, from_inner, from_ends), (from_joined,)


def local(layer_input, norm_gain, w_query, w_key, w_value, head_grad, parents, row_counts):
    branch_total = lax.axis_size("branch")
    tensor_total = lax.axis_size("tensor")
    slots = row_counts.shape[0] // branch_total
    rows, width = layer_input.shape
    column_width = width // tensor_total
    chips = branch_total // 2
    group = w_query.shape[1] // w_key.shape[1]
    kv_local = w_key.shape[1] // HEAD_DIM
    offsets = [(shift, swap) for shift in range(chips) for swap in range(2)]

    def targets():
        index = lax.axis_index("branch")
        chip, core = index // 2, index % 2
        return [lax.rem(chip + s, chips) * 2 + lax.rem(core + e, 2) for s, e in offsets]

    normed, inverse, input_columns, gain_columns, pieces = normalize(
        layer_input, norm_gain, targets, branch_total, rows // slots, column_width
    )
    direct = [branch_send(pieces[2 * s], chips, s, 0) for s in range(1, chips)]
    packs, deltas, delta_turned, centre = attention_backward(
        normed, w_query, w_key, w_value, head_grad, parents, row_counts, pieces[1::2], slots
    )

    held = gate(packs[1:], direct)

    def project(order, pieces):
        return back_project(
            order, pieces, delta_turned, centre, w_query, w_key, w_value, tensor_total
        )

    parts, for_ends, for_inner, met, arrived = tensor_scatter(project, tensor_total)

    depth = width // branch_total
    sent = [branch_send(pack, chips, s + 1, 0) for s, pack in enumerate(held)]
    *sent, first_pack = gate((*sent, packs[0]), met)
    deltas = gate(deltas, (sent[0],)) if deltas else deltas
    sent = [first_pack] + sent
    handed = [branch_send(pack, chips, 0, 1) for pack in sent]
    turned = [pieces[0]] + direct + handed
    sources = len(turned)
    *weights, token = weight_gradients(
        depth, rows, turned, sent + handed, [depth] * sources, 0, kv_local, group, None
    )
    grad_input, gain_sum = finish(
        width, for_ends, for_inner, input_columns, gain_columns, inverse, parts, token
    )
    for head, delta in enumerate(deltas):
        sent = [delta] + [branch_send(delta, chips, s, 0) for s in range(1, chips)]
        sent = list(gate(sent, (*arrived, token)))
        handed = [branch_send(part, chips, 0, 1) for part in sent]
        *weights, token = weight_gradients(
            depth, rows, turned, sent + handed, [0] * sources, head + 1, kv_local, group, weights
        )
    if chips == 2:
        here = gain_sum + branch_send(gain_sum, chips, 0, 1)
        there = branch_send(gain_sum, chips, 1, 0) + branch_send(gain_sum, chips, 1, 1)
        grad_gain = here + there
    else:
        grad_gain = lax.psum(gain_sum, "branch")
    return (grad_input, *weights, grad_gain.reshape(column_width))


def solution(mesh):
    placed = (
        P(("parts", "branch"), None),
        P(),
        P(None, "tensor"),
        P(None, "tensor"),
        P(None, "tensor"),
        P(("parts", "branch"), "tensor"),
        P(("parts", "branch")),
        P("parts"),
    )
    return jax.shard_map(
        local,
        mesh=mesh,
        in_specs=placed,
        out_specs=(
            P(("parts", "branch"), "tensor"),
            P(("parts", "branch"), "tensor"),
            P(("parts", "branch"), "tensor"),
            P(("parts", "branch"), "tensor"),
            P(("parts", "tensor")),
        ),
        check_vma=False,
    )
```

time: 142 us -> 104 us (0.73)
  waiting for transfers between devices: 52.5 us -> 12.8 us
  Pallas kernels: 30 us -> 67.9 us
  blocking collectives: 35.8 us -> 0 us
  starting transfers between devices: 10.3 us -> 20.7 us
  local copies, waits for them, and re-layouts: 8.65 us -> 0 us
  other arithmetic: 3.82 us -> 1.29 us
    pallas_call x4 -> x12, Pallas kernels: 30 us -> 67.9 us  [the longest x1 30.3 us: attention_backward(): pl.pallas_call(functools.partial(attention_kernel, slots, kv_local, group...]
    psum x2 -> x0, blocking collectives: 35.8 us -> none  [the longest x1 29.6 us: local(): centre = lax.psum(centre_part, 'tensor') * (1.0 / width)]
    ppermute x6 -> x10, waiting for transfers between devices: 23.2 us -> 1.69 us  [branch_send(): return lax.ppermute(array, 'branch', pairs)]
    ppermute x3 -> x4, waiting for transfers between devices: 29.4 us -> 11.1 us  [the longest x1 6.45 us: tensor_scatter(): from_ends = lax.ppermute(third, 'tensor', [(0, 2), (3, 1)])]
    ppermute x3 -> x4, starting transfers between devices: 5.76 us -> 13 us  [the longest x1 5.76 us: tensor_scatter(): from_ends = lax.ppermute(third, 'tensor', [(0, 2), (3, 1)])]
    unnamed x18 -> x0, local copies, waits for them, and re-layouts: 6.38 us -> none
    ppermute x6 -> x10, starting transfers between devices: 4.5 us -> 7.67 us  [branch_send(): return lax.ppermute(array, 'branch', pairs)]
    reduce_sum x1 -> x0, other arithmetic: 2.84 us -> none  [local(): grad_gain = lax.psum(jnp.sum(d_normed * scaled, axis=0), 'branch')]
  transfers between devices with their start and end apart: 9 -> 14, of which waited for: 3 -> 3; matrix products, arithmetic and copies ran while one was open for 3% -> 1% of each run, Pallas kernels for 7% -> 56%
where the time goes in v3:
time: 104 us
  Pallas kernels  67.9 us (65%)
  starting transfers between devices  20.7 us (20%)
  waiting for transfers between devices  12.8 us (12%)
  other arithmetic  1.29 us (1%)
    pallas_call x1, Pallas kernels, attention_backward(): pl.pallas_call(functools.partial(attention_kernel, slots, kv_local, group...  30.3 us
    pallas_call x2, Pallas kernels, back_project(): pl.pallas_call(functools.partial(back_kernel, order, cuts, blocks), out_s...  16.2 us
    pallas_call x2, Pallas kernels, weight_gradients(): pl.pallas_call(functools.partial(weight_kernel, group, head, sources, ski...  12 us
    ppermute x10, starting transfers between devices, branch_send(): return lax.ppermute(array, 'branch', pairs)  7.67 us
    ppermute x1, waiting for transfers between devices, tensor_scatter(): from_ends = lax.ppermute(third, 'tensor', [(0, 2), (3, 1)])  6.45 us
    ppermute x1, starting transfers between devices, tensor_scatter(): from_ends = lax.ppermute(third, 'tensor', [(0, 2), (3, 1)])  5.76 us
    ppermute x1, waiting for transfers between devices, tensor_scatter(): lax.ppermute(joined, 'tensor', [(1, 3), (2, 0), (0, 1), (3, 2)])  4.65 us
    pallas_call x1, Pallas kernels, normalize(): pl.pallas_call(functools.partial(norm_kernel, targets, cut), out_shape=(j...  3.67 us
  transfers between devices with their start and end apart: 14, of which 3 were waited for; matrix products, arithmetic and copies ran while one was open for 1% of the time, Pallas kernels for 56%

profile of v3, /device:TPU:0, one launch (start us, length us, event | category | flops | bytes accessed | tf_op | source)
XLA Modules:
  0.0 103.6 jit_solution(9445897477062611862)
XLA Ops:
  0.6 3.7 %norm.1 = (bf16[256,3584]{1,0:T(8,128)(2,1)}, f32[256,1]{1,0:T(8,128)}, bf16[256,896]{1,0:T(8,128)(2,1)}, f32[1,896]{1,0:T(1,128)}, bf16[896,256]{1,0:T(8,128)(2...) custom-call(bf16[256,3584]{1,0:T(8,128)(2,1)} %input_ref.1, f32[3584]{0:T(1024)} %gain_ref.1), custom_call_target="tpu_custom_call" | custom-call | flops 1000000 | bytes 100000 | tf_op jit(solution)/shard_map/norm/pallas_call | solution.py:73
  4.3 2.9 %collective-permute-start.4 = (bf16[896,256]{1,0:T(8,128)(2,1)}, bf16[896,256]{1,0:T(8,128)(2,1)}, u32[]{:S(2)}, u32[]{:S(2)}) collective-permute-start(bf16[896,256]{1,0:T(8,128)(2,1)} %get-tuple-element.51), channel_id=1, source_target_pairs={{0,8},{4,12},{8,0},{12,4},{1,9},{5,13},{9,1},{13,5},{2,10},{6,14},... | collective-permute-start | bytes 1376264 | tf_op jit(solution)/shard_map/ppermute | solution.py:572
  7.2 30.3 %attention.1 = (bf16[1920,256]{1,0:T(8,128)(2,1)}, bf16[1920,256]{1,0:T(8,128)(2,1)}, bf16[1024,256]{1,0:T(8,128)(2,1)}, bf16[2048,256]{1,0:T(8,128)(2,1)}, f32[16,256]{1,0:T(8,128)}) custom-call(s32[8]{0:T(128)} %count_ref.1, s32[256]{0:T(256)} %parent_ref.1, bf16[256,3584]{1,0:T(8,128)(2,1)} %get-tuple-element.40.normed_hbm, bf16[3584,1024]{1,0:T(8,128)(2,1)} %refs_2_.3, ...), custom_call_target="tpu_custom_call" | custom-call | flops 1000000 | bytes 100000 | tf_op jit(solution)/shard_map/attention/pallas_call | solution.py:281
  37.6 0.0 collective-permute-done.4.refs_1_
  37.6 0.1 collective-permute-start.5
  37.7 8.1 %back.2 = (bf16[912,256]{1,0:T(8,128)(2,1)}, bf16[912,256]{1,0:T(8,128)(2,1)}) custom-call(bf16[2048,256]{1,0:T(8,128)(2,1)} %get-tuple-element.43.refs_0_, f32[16,256]{1,0:T(8,128)} %get-tuple-element.44.refs_1_, bf16[3584,1024]{1,0:T(8,128)(2,1)} %refs_2_.3, bf16[3584,512]{1,0:T(8,128)(2,1)} %refs_3_.3, bf16[3584,512]{1,0:T(8,128)(2,1)} %refs_4_.3), custom_call_target="tpu_custom_call" | custom-call | flops 1000000 | bytes 100000 | tf_op jit(solution)/shard_map/back/pallas_call | solution.py:370
  45.8 2.2 %collective-permute-start = (bf16[912,256]{1,0:T(8,128)(2,1)}, bf16[912,256]{1,0:T(8,128)(2,1)}, u32[]{:S(2)}, u32[]{:S(2)}) collective-permute-start(bf16[912,256]{1,0:T(8,128)(2,1)} %get-tuple-element.45), channel_id=1, source_target_pairs={{0,1},{1,0},{2,3},{3,2},{4,5},{5,4},{6,7},{7,6},{8,9},{9,8},{10,11... | collective-permute-start | bytes 1400840 | tf_op jit(solution)/shard_map/ppermute | solution.py:595
  48.0 1.4 %collective-permute-start.1 = (bf16[912,256]{1,0:T(8,128)(2,1)}, bf16[912,256]{1,0:T(8,128)(2,1)}, u32[]{:S(2)}, u32[]{:S(2)}) collective-permute-start(bf16[912,256]{1,0:T(8,128)(2,1)} %get-tuple-element.46.refs_1_), channel_id=1, source_target_pairs={{1,2},{2,1},{5,6},{6,5},{9,10},{10,9},{13,14},{14,13},{17,18},{18,... | collective-permute-start | bytes 1400840 | tf_op jit(solution)/shard_map/ppermute | solution.py:596
  49.4 8.1 %back.3 = (bf16[912,256]{1,0:T(8,128)(2,1)}, bf16[912,256]{1,0:T(8,128)(2,1)}) custom-call(bf16[2048,256]{1,0:T(8,128)(2,1)} %get-tuple-element.43.refs_0_, f32[16,256]{1,0:T(8,128)} %get-tuple-element.44.refs_1_, bf16[3584,1024]{1,0:T(8,128)(2,1)} %refs_2_.3, bf16[3584,512]{1,0:T(8,128)(2,1)} %refs_3_.3, bf16[3584,512]{1,0:T(8,128)(2,1)} %refs_4_.3), custom_call_target="tpu_custom_call" | custom-call | flops 1000000 | bytes 100000 | tf_op jit(solution)/shard_map/back/pallas_call | solution.py:370
  57.5 5.8 %collective-permute-start.2 = (bf16[912,256]{1,0:T(8,128)(2,1)}, bf16[912,256]{1,0:T(8,128)(2,1)}, u32[]{:S(2)}, u32[]{:S(2)}) collective-permute-start(bf16[912,256]{1,0:T(8,128)(2,1)} %get-tuple-element.48.inner_ref), channel_id=1, source_target_pairs={{0,2},{3,1},{4,6},{7,5},{8,10},{11,9},{12,14},{15,13},{16,18},{19,... | collective-permute-start | bytes 1400840 | tf_op jit(solution)/shard_map/ppermute | solution.py:598
  63.3 0.0 collective-permute-done.other_ref.refs_0_
  63.3 2.2 %join.1 = (bf16[912,256]{1,0:T(8,128)(2,1)}, f32[8,128]{1,0:T(8,128)}) custom-call(bf16[912,256]{1,0:T(8,128)(2,1)} %get-tuple-element.48.inner_ref, bf16[912,256]{1,0:T(8,128)(2,1)} %collective-permute-done.other_ref.refs_0_, bf16[912,256]{1,0:T(8,128)(2,1)} %get-tuple-element.47.end_ref.refs_2_), custom_call_target="tpu_custom_call" | custom-call | flops 1000000 | bytes 100000 | tf_op jit(solution)/shard_map/join/pallas_call | solution.py:508
  65.5 0.0 collective-permute-done.1.refs_3_
  65.5 6.5 %collective-permute-done.2.refs_4_ = bf16[912,256]{1,0:T(8,128)(2,1)} collective-permute-done((bf16[912,256]{1,0:T(8,128)(2,1)}, bf16[912,256]{1,0:T(8,128)(2,1)}, u32[]{:S(2)}, u32[]{:S(2)}) %collective-permute-start.2) | collective-permute-done | bytes 466976 | tf_op jit(solution)/shard_map/ppermute | solution.py:598
  71.9 0.0 collective-permute-done.5.refs_0_
  71.9 0.0 collective-permute-start.6
  71.9 0.5 collective-permute-start.7
  72.4 1.5 %collective-permute-start.8 = (bf16[1024,256]{1,0:T(8,128)(2,1)}, bf16[1024,256]{1,0:T(8,128)(2,1)}, u32[]{:S(2)}, u32[]{:S(2)}) collective-permute-start(bf16[1024,256]{1,0:T(8,128)(2,1)} %gate.6.refs_0_), channel_id=1, source_target_pairs={{0,8},{4,12},{8,0},{12,4},{1,9},{5,13},{9,1},{13,5},{2,10},{6,14},... | collective-permute-start | bytes 1572872 | tf_op jit(solution)/shard_map/ppermute | solution.py:572
  73.9 3.7 %collective-permute-start.3 = (bf16[912,256]{1,0:T(8,128)(2,1)}, bf16[912,256]{1,0:T(8,128)(2,1)}, u32[]{:S(2)}, u32[]{:S(2)}) collective-permute-start(bf16[912,256]{1,0:T(8,128)(2,1)} %get-tuple-element.49), channel_id=1, source_target_pairs={{1,3},{2,0},{0,1},{3,2},{5,7},{6,4},{4,5},{7,6},{9,11},{10,8},{8,9... | collective-permute-start | bytes 1400840 | tf_op jit(solution)/shard_map/ppermute | solution.py:600
  77.6 0.0 collective-permute-done.6.refs_2_.refs_6_
  77.6 0.0 collective-permute-done.7.refs_3_.refs_7_
  77.6 6.0 %weights.2 = (f32[896,1024]{1,0:T(8,128)}, f32[896,512]{1,0:T(8,128)}, f32[896,512]{1,0:T(8,128)}, f32[8,128]{1,0:T(8,128)}) custom-call(bf16[896,256]{1,0:T(8,128)(2,1)} %get-tuple-element.50.refs_0_, bf16[896,256]{1,0:T(8,128)(2,1)} %collective-permute-done.4.refs_1_, bf16[1920,256]{1,0:T(8,128)(2,1)} %collective-permute-done.6.refs_2_.refs_6_, ...), custom_call_target="tpu_custom_call" | custom-call | flops 1000000 | bytes 100000 | tf_op jit(solution)/shard_map/weights/pallas_call | solution.py:447
  83.6 4.6 %collective-permute-done.3.refs_5_.refs_2_ = bf16[912,256]{1,0:T(8,128)(2,1)} collective-permute-done((bf16[912,256]{1,0:T(8,128)(2,1)}, bf16[912,256]{1,0:T(8,128)(2,1)}, u32[]{:S(2)}, u32[]{:S(2)}) %collective-permute-start.3) | collective-permute-done | bytes 466976 | tf_op jit(solution)/shard_map/ppermute | solution.py:600
  88.3 0.0 collective-permute-done.8.refs_1_
  88.3 0.0 collective-permute-start.9
  88.3 0.5 collective-permute-start.10
  88.8 3.5 %finish.1 = (bf16[256,896]{1,0:T(8,128)(2,1)}, f32[1,896]{1,0:T(1,128)}) custom-call(bf16[256,896]{1,0:T(8,128)(2,1)} %get-tuple-element.37.input_ref, f32[1,896]{1,0:T(1,128)} %get-tuple-element.38.gain_ref, f32[256,1]{1,0:T(8,128)} %get-tuple-element.39.inverse_ref, bf16[912,256]{1,0:T(8,128)(2,1)} %collective-permute-done.other_ref.refs_0_, ...), custom_call_target="tpu_custom_call" | custom-call | flops 1000000 | bytes 100000 | tf_op jit(solution)/shard_map/finish/pallas_call | solution.py:549
  92.3 0.5 collective-permute-start.12
  92.8 0.9 collective-permute-start.13
  93.7 0.7 collective-permute-start.11
  94.4 1.7 %collective-permute-done.12 = f32[1,896]{1,0:T(1,128)S(1)} collective-permute-done((f32[1,896]{1,0:T(1,128)}, f32[1,896]{1,0:T(1,128)S(1)}, u32[]{:S(2)}, u32[]{:S(2)}) %collective-permute-start.12) | collective-permute-done | bytes 3616 | tf_op jit(solution)/shard_map/ppermute | solution.py:572
  96.1 0.0 collective-permute-done.13
  96.1 0.0 collective-permute-done.11
  96.1 1.3 %add_reduce_fusion = f32[896]{0:T(1024)} fusion(f32[1,896]{1,0:T(1,128)S(1)} %collective-permute-done.12, f32[1,896]{1,0:T(1,128)S(1)} %collective-permute-done.13, f32[1,896]{1,0:T(1,128)} %get-tuple-element.68, f32[1,896]{1,0:T(1,128)S(1)} %collective-permute-done.11), kind=kLoop, calls=%fused_computation | loop fusion | flops 2688 | bytes 17920 | tf_op jit(solution)/shard_map/add | solution.py:662
  97.4 0.0 collective-permute-done.9.refs_6_
  97.4 0.0 collective-permute-done.10.refs_7_
  97.4 6.0 %weights.3 = (f32[896,1024]{1,0:T(8,128)}, f32[896,512]{1,0:T(8,128)}, f32[896,512]{1,0:T(8,128)}, f32[8,128]{1,0:T(8,128)}) custom-call(bf16[896,256]{1,0:T(8,128)(2,1)} %get-tuple-element.50.refs_0_, bf16[896,256]{1,0:T(8,128)(2,1)} %collective-permute-done.4.refs_1_, ...), custom_call_target="tpu_custom_call", output_to_operand_aliasing={{0}: (8, {}), {1}: (9, {}), {2}: (10, {})} | custom-call | flops 1000000 | bytes 100000 | tf_op jit(solution)/shard_map/weights/pallas_call | solution.py:447
  (4 shorter events, 0.0 us)
Async XLA Ops:
  4.3 33.3 %collective-permute-start.4 = (bf16[896,256]{1,0:T(8,128)(2,1)}, bf16[896,256]{1,0:T(8,128)(2,1)}, u32[]{:S(2)}, u32[]{:S(2)}) collective-permute-start(bf16[896,256]{1,0:T(8,128)(2,1)} %get-tuple-element.51), channel_id=1, source_target_pairs={{0,8},{4,12},{8,0},{12,4},{1,9},{5,13},{9,1},{13,5},{2,10},{6,14},... | collective-permute-start | bytes 1376264 | tf_op jit(solution)/shard_map/ppermute | solution.py:572
  37.6 34.3 %collective-permute-start.5 = (bf16[1920,256]{1,0:T(8,128)(2,1)}, bf16[1920,256]{1,0:T(8,128)(2,1)}, u32[]{:S(2)}, u32[]{:S(2)}) collective-permute-start(bf16[1920,256]{1,0:T(8,128)(2,1)} %gate.4), channel_id=1, source_target_pairs={{0,8},{4,12},{8,0},{12,4},{1,9},{5,13},{9,1},{13,5},{2,10},{6,14},... | collective-permute-start | bytes 2949128 | tf_op jit(solution)/shard_map/ppermute | solution.py:572
  45.8 17.5 %collective-permute-start = (bf16[912,256]{1,0:T(8,128)(2,1)}, bf16[912,256]{1,0:T(8,128)(2,1)}, u32[]{:S(2)}, u32[]{:S(2)}) collective-permute-start(bf16[912,256]{1,0:T(8,128)(2,1)} %get-tuple-element.45), channel_id=1, source_target_pairs={{0,1},{1,0},{2,3},{3,2},{4,5},{5,4},{6,7},{7,6},{8,9},{9,8},{10,11... | collective-permute-start | bytes 1400840 | tf_op jit(solution)/shard_map/ppermute | solution.py:595
  48.0 17.5 %collective-permute-start.1 = (bf16[912,256]{1,0:T(8,128)(2,1)}, bf16[912,256]{1,0:T(8,128)(2,1)}, u32[]{:S(2)}, u32[]{:S(2)}) collective-permute-start(bf16[912,256]{1,0:T(8,128)(2,1)} %get-tuple-element.46.refs_1_), channel_id=1, source_target_pairs={{1,2},{2,1},{5,6},{6,5},{9,10},{10,9},{13,14},{14,13},{17,18},{18,... | collective-permute-start | bytes 1400840 | tf_op jit(solution)/shard_map/ppermute | solution.py:596
  57.5 14.4 %collective-permute-start.2 = (bf16[912,256]{1,0:T(8,128)(2,1)}, bf16[912,256]{1,0:T(8,128)(2,1)}, u32[]{:S(2)}, u32[]{:S(2)}) collective-permute-start(bf16[912,256]{1,0:T(8,128)(2,1)} %get-tuple-element.48.inner_ref), channel_id=1, source_target_pairs={{0,2},{3,1},{4,6},{7,5},{8,10},{11,9},{12,14},{15,13},{16,18},{19,... | collective-permute-start | bytes 1400840 | tf_op jit(solution)/shard_map/ppermute | solution.py:598
  71.9 5.7 %collective-permute-start.6 = (bf16[1920,256]{1,0:T(8,128)(2,1)}, bf16[1920,256]{1,0:T(8,128)(2,1)}, u32[]{:S(2)}, u32[]{:S(2)}) collective-permute-start(bf16[1920,256]{1,0:T(8,128)(2,1)} %get-tuple-element.55.refs_4_), channel_id=1, source_target_pairs={{0,4},{4,0},{8,12},{12,8},{1,5},{5,1},{9,13},{13,9},{2,6},{6,2},{1... | collective-permute-start | bytes 2949128 | tf_op jit(solution)/shard_map/ppermute | solution.py:572
  71.9 5.7 %collective-permute-start.7 = (bf16[1920,256]{1,0:T(8,128)(2,1)}, bf16[1920,256]{1,0:T(8,128)(2,1)}, u32[]{:S(2)}, u32[]{:S(2)}) collective-permute-start(bf16[1920,256]{1,0:T(8,128)(2,1)} %get-tuple-element.56.refs_5_.refs_1_), channel_id=1, source_target_pairs={{0,4},{4,0},{8,12},{12,8},{1,5},{5,1},{9,13},{13,9},{2,6},{6,2},{1... | collective-permute-start | bytes 2949128 | tf_op jit(solution)/shard_map/ppermute | solution.py:572
  72.4 15.8 %collective-permute-start.8 = (bf16[1024,256]{1,0:T(8,128)(2,1)}, bf16[1024,256]{1,0:T(8,128)(2,1)}, u32[]{:S(2)}, u32[]{:S(2)}) collective-permute-start(bf16[1024,256]{1,0:T(8,128)(2,1)} %gate.6.refs_0_), channel_id=1, source_target_pairs={{0,8},{4,12},{8,0},{12,4},{1,9},{5,13},{9,1},{13,5},{2,10},{6,14},... | collective-permute-start | bytes 1572872 | tf_op jit(solution)/shard_map/ppermute | solution.py:572
  73.9 14.3 %collective-permute-start.3 = (bf16[912,256]{1,0:T(8,128)(2,1)}, bf16[912,256]{1,0:T(8,128)(2,1)}, u32[]{:S(2)}, u32[]{:S(2)}) collective-permute-start(bf16[912,256]{1,0:T(8,128)(2,1)} %get-tuple-element.49), channel_id=1, source_target_pairs={{1,3},{2,0},{0,1},{3,2},{5,7},{6,4},{4,5},{7,6},{9,11},{10,8},{8,9... | collective-permute-start | bytes 1400840 | tf_op jit(solution)/shard_map/ppermute | solution.py:600
  88.3 9.1 %collective-permute-start.9 = (bf16[1024,256]{1,0:T(8,128)(2,1)}, bf16[1024,256]{1,0:T(8,128)(2,1)}, u32[]{:S(2)}, u32[]{:S(2)}) collective-permute-start(bf16[1024,256]{1,0:T(8,128)(2,1)} %get-tuple-element.60.refs_4_), channel_id=1, source_target_pairs={{0,4},{4,0},{8,12},{12,8},{1,5},{5,1},{9,13},{13,9},{2,6},{6,2},{1... | collective-permute-start | bytes 1572872 | tf_op jit(solution)/shard_map/ppermute | solution.py:572
  88.3 9.1 %collective-permute-start.10 = (bf16[1024,256]{1,0:T(8,128)(2,1)}, bf16[1024,256]{1,0:T(8,128)(2,1)}, u32[]{:S(2)}, u32[]{:S(2)}) collective-permute-start(bf16[1024,256]{1,0:T(8,128)(2,1)} %get-tuple-element.61.refs_5_), channel_id=1, source_target_pairs={{0,4},{4,0},{8,12},{12,8},{1,5},{5,1},{9,13},{13,9},{2,6},{6,2},{1... | collective-permute-start | bytes 1572872 | tf_op jit(solution)/shard_map/ppermute | solution.py:572
  92.3 3.8 %collective-permute-start.12 = (f32[1,896]{1,0:T(1,128)}, f32[1,896]{1,0:T(1,128)S(1)}, u32[]{:S(2)}, u32[]{:S(2)}) collective-permute-start(f32[1,896]{1,0:T(1,128)} %get-tuple-element.68), channel_id=1, source_target_pairs={{0,8},{4,12},{8,0},{12,4},{1,9},{5,13},{9,1},{13,5},{2,10},{6,14},... | collective-permute-start | bytes 10760 | tf_op jit(solution)/shard_map/ppermute | solution.py:572
  92.8 3.3 %collective-permute-start.13 = (f32[1,896]{1,0:T(1,128)}, f32[1,896]{1,0:T(1,128)S(1)}, u32[]{:S(2)}, u32[]{:S(2)}) collective-permute-start(f32[1,896]{1,0:T(1,128)} %get-tuple-element.68), channel_id=1, source_target_pairs={{0,12},{4,8},{8,4},{12,0},{1,13},{5,9},{9,5},{13,1},{2,14},{6,10},... | collective-permute-start | bytes 10760 | tf_op jit(solution)/shard_map/ppermute | solution.py:572
  93.7 2.4 %collective-permute-start.11 = (f32[1,896]{1,0:T(1,128)}, f32[1,896]{1,0:T(1,128)S(1)}, u32[]{:S(2)}, u32[]{:S(2)}) collective-permute-start(f32[1,896]{1,0:T(1,128)} %get-tuple-element.68), channel_id=1, source_target_pairs={{0,4},{4,0},{8,12},{12,8},{1,5},{5,1},{9,13},{13,9},{2,6},{6,2},{1... | collective-permute-start | bytes 10760 | tf_op jit(solution)/shard_map/ppermute | solution.py:572

commit v4 on v1

v4 whole, which is shorter than its diff:
```python
import functools

import jax
import jax.numpy as jnp
from jax import lax
from jax.experimental import pallas as pl
from jax.experimental.pallas import tpu as pltpu
from jax.sharding import PartitionSpec as P

HEAD_DIM = 256
MIB = 1024 * 1024
CENTRE_ROWS = 16
VMEM_LIMIT = 64 * MIB


epsilon = 1e-06
softcap_limit = 50.0


def nn_dot(left, right):
    return lax.dot_general(
        left, right, (((1,), (0,)), ((), ())), preferred_element_type=jnp.float32
    )


def nt_dot(left, right):
    return lax.dot_general(
        left, right, (((1,), (1,)), ((), ())), preferred_element_type=jnp.float32
    )


def tn_dot(left, right):
    return lax.dot_general(
        left, right, (((0,), (0,)), ((), ())), preferred_element_type=jnp.float32
    )


def small_cost():
    return pl.CostEstimate(flops=1000000, bytes_accessed=100000, transcendentals=0)


def cut_kernel(targets, input_hbm, *rest):
    piece_hbm, sem = rest[:-1], rest[-1]
    depth = piece_hbm[0].shape[1]
    copies = [
        pltpu.make_async_copy(
            input_hbm.at[:, pl.ds(pl.multiple_of(target * depth, 128), depth)],
            piece,
            sem.at[place],
        )
        for place, (target, piece) in enumerate(zip(targets(), piece_hbm))
    ]
    for copy in copies:
        copy.start()
    for copy in copies:
        copy.wait()


def cut_columns(layer_input, targets, pieces):
    rows, width = layer_input.shape
    depth = width // pieces
    if depth % 128:
        return [
            lax.dynamic_slice_in_dim(layer_input, target * depth, depth, 1) for target in targets()
        ]
    hbm = pl.BlockSpec(memory_space=pl.ANY)
    return pl.pallas_call(
        functools.partial(cut_kernel, targets),
        out_shape=(jax.ShapeDtypeStruct((rows, depth), jnp.bfloat16),) * pieces,
        in_specs=[hbm],
        out_specs=(hbm,) * pieces,
        scratch_shapes=[pltpu.SemaphoreType.DMA((pieces,))],
        compiler_params=pltpu.CompilerParams(vmem_limit_bytes=VMEM_LIMIT),
        cost_estimate=small_cost(),
        name="cut",
    )(layer_input)


def turn_kernel(gain_ref, *refs):
    pieces = len(refs) // 2
    gain = 1.0 + gain_ref[...]
    for piece_ref, out_ref in zip(refs[:pieces], refs[pieces:]):
        out_ref[...] = (piece_ref[...].astype(jnp.float32) * gain).astype(jnp.bfloat16).T


def turn(pieces, gain):
    rows, depth = pieces[0].shape
    return pl.pallas_call(
        turn_kernel,
        out_shape=(jax.ShapeDtypeStruct((depth, rows), jnp.bfloat16),) * len(pieces),
        grid=(1,),
        in_specs=[pl.BlockSpec((1, depth), lambda i: (0, 0))]
        + [pl.BlockSpec((rows, depth), lambda i: (0, 0))] * len(pieces),
        out_specs=(pl.BlockSpec((depth, rows), lambda i: (0, 0)),) * len(pieces),
        compiler_params=pltpu.CompilerParams(vmem_limit_bytes=VMEM_LIMIT),
        cost_estimate=small_cost(),
        name="turn",
    )(gain, *pieces)


def ancestor_mask(parent_row):
    rows = parent_row.shape[1]
    row = lax.broadcasted_iota(jnp.int32, (rows, rows), 0)
    column = lax.broadcasted_iota(jnp.int32, (rows, rows), 1)
    reached = jnp.where((parent_row == row) | (row == column), 1.0, 0.0)
    for squaring in range(rows.bit_length() - 1):
        halfway = reached.astype(jnp.bfloat16)
        reached = jnp.minimum(nn_dot(halfway, halfway), 1.0)
    return reached.T


def attention_kernel(
    slots,
    count_ref,
    parent_ref,
    gain_ref,
    input_ref,
    query_ref,
    key_ref,
    value_ref,
    grad_ref,
    delta_ref,
    centre_ref,
    inverse_ref,
    *rest,
):
    scaled_refs, (normed_ref, allowed_ref) = rest[:-2], rest[-2:]
    head_dim = HEAD_DIM
    rows, width = input_ref.shape
    block = rows // slots
    group = query_ref.shape[1] // head_dim
    step = pl.program_id(0)

    @pl.when(step == 0)
    def _():
        values = input_ref[...].astype(jnp.float32)
        inverse = lax.rsqrt(jnp.mean(values * values, axis=-1, keepdims=True) + epsilon)
        inverse_ref[...] = inverse
        gain = gain_ref[...].reshape(1, width)
        normed_ref[...] = (values * inverse * (1.0 + gain)).astype(jnp.bfloat16)
        centre_ref[...] = jnp.zeros_like(centre_ref)
        parents = parent_ref[...].reshape(1, rows)
        for slot in range(slots):
            allowed_ref[slot] = ancestor_mask(parents[:, slot * block : (slot + 1) * block])

    first_count = lax.axis_index("branch") * slots
    normed = normed_ref[...]
    query_sum = nn_dot(normed, query_ref[...])
    key_sum = nn_dot(normed, key_ref[...])
    value_sum = nn_dot(normed, value_ref[...])
    scale = head_dim ** (-0.5)
    for slot in range(slots):
        lines = slice(slot * block, (slot + 1) * block)
        query_parts = [
            query_sum[lines, g * head_dim : (g + 1) * head_dim] for g in range(group)
        ]
        queries = jnp.concatenate(query_parts, axis=0).astype(jnp.bfloat16)
        keys = key_sum[lines].astype(jnp.bfloat16)
        values = value_sum[lines].astype(jnp.bfloat16)
        live = (
            lax.broadcasted_iota(jnp.int32, (block, head_dim), 0) < count_ref[first_count + slot]
        )
        grads = jnp.concatenate(
            [
                jnp.where(
                    live,
                    grad_ref[lines, g * head_dim : (g + 1) * head_dim].astype(jnp.float32),
                    0.0,
                )
                for g in range(group)
            ],
            axis=0,
        ).astype(jnp.bfloat16)
        allowed = jnp.concatenate([allowed_ref[slot]] * group, axis=0)
        bounded = jnp.tanh(nt_dot(queries, keys) * (scale / softcap_limit))
        weights = allowed * jnp.exp(softcap_limit * bounded)
        probabilities = weights * (1.0 / jnp.sum(weights, axis=-1, keepdims=True))
        d_probs = nt_dot(grads, values)
        d_scores = probabilities * (
            d_probs - jnp.sum(probabilities * d_probs, axis=-1, keepdims=True)
        )
        d_raw = (d_scores * (1.0 - bounded * bounded) * scale).astype(jnp.bfloat16)
        prob_half = probabilities.astype(jnp.bfloat16)
        d_query = nn_dot(d_raw, keys)
        parts = [d_query[g * block : (g + 1) * block] for g in range(group)]
        parts += [tn_dot(d_raw, queries), tn_dot(prob_half, grads)]
        whole = query_parts + [key_sum[lines], value_sum[lines]]
        inverse = inverse_ref[lines, :]
        product = None
        for which, (part, sums) in enumerate(zip(parts, whole)):
            columns = slice(which * head_dim, (which + 1) * head_dim)
            half = part.astype(jnp.bfloat16)
            delta_ref[lines, columns] = half
            term = half.astype(jnp.float32) * sums
            product = term if product is None else product + term
            scaled = (part * inverse).astype(jnp.bfloat16)
            for place, scaled_ref in enumerate(scaled_refs):

                @pl.when(step == place)
                def _():
                    scaled_ref[lines, columns] = scaled

        centre_ref[lines, :] += jnp.sum(product, axis=-1, keepdims=True)


def attention_backward(
    layer_input, norm_gain, w_query, w_key, w_value, head_grad, parents, counts, slots
):
    rows, width = layer_input.shape
    kv_local = w_key.shape[1] // HEAD_DIM
    group = w_query.shape[1] // w_key.shape[1]
    span = (group + 2) * HEAD_DIM
    block = rows // slots
    whole = lambda h: (0, 0)
    by_head = lambda h: (0, h)
    out = pl.pallas_call(
        functools.partial(attention_kernel, slots),
        out_shape=(
            jax.ShapeDtypeStruct((rows, kv_local * span), jnp.bfloat16),
            jax.ShapeDtypeStruct((rows, 1), jnp.float32),
            jax.ShapeDtypeStruct((rows, 1), jnp.float32),
        )
        + (jax.ShapeDtypeStruct((rows, span), jnp.bfloat16),) * kv_local,
        grid=(kv_local,),
        in_specs=[
            pl.BlockSpec(memory_space=pltpu.SMEM),
            pl.BlockSpec((rows,), lambda h: (0,)),
            pl.BlockSpec((width,), lambda h: (0,)),
            pl.BlockSpec((rows, width), whole),
            pl.BlockSpec((width, group * HEAD_DIM), by_head),
            pl.BlockSpec((width, HEAD_DIM), by_head),
            pl.BlockSpec((width, HEAD_DIM), by_head),
            pl.BlockSpec((rows, group * HEAD_DIM), by_head),
        ],
        out_specs=(
            pl.BlockSpec((rows, span), by_head),
            pl.BlockSpec((rows, 1), whole),
            pl.BlockSpec((rows, 1), whole),
        )
        + (pl.BlockSpec((rows, span), whole),) * kv_local,
        scratch_shapes=[
            pltpu.VMEM((rows, width), jnp.bfloat16),
            pltpu.VMEM((slots, block, block), jnp.float32),
        ],
        compiler_params=pltpu.CompilerParams(vmem_limit_bytes=VMEM_LIMIT),
        cost_estimate=small_cost(),
        name="attention",
    )(counts, parents, norm_gain, layer_input, w_query, w_key, w_value, head_grad)
    return out[0], out[1], out[2], out[3:]


def back_kernel(delta_ref, centre_ref, query_ref, key_ref, value_ref, *out_refs):
    step = pl.program_id(0)
    head_dim = HEAD_DIM
    kv_local = key_ref.shape[1] // head_dim
    group = query_ref.shape[1] // key_ref.shape[1]
    span = (group + 2) * head_dim
    rows = delta_ref.shape[0]
    total = None
    for h in range(kv_local):
        base = h * span
        mid = base + group * head_dim
        term = nt_dot(
            delta_ref[:, base:mid],
            query_ref[:, h * group * head_dim : (h + 1) * group * head_dim],
        )
        term += nt_dot(
            delta_ref[:, mid : mid + head_dim], key_ref[:, h * head_dim : (h + 1) * head_dim]
        )
        term += nt_dot(
            delta_ref[:, mid + head_dim : mid + 2 * head_dim],
            value_ref[:, h * head_dim : (h + 1) * head_dim],
        )
        total = term if total is None else total + term
    total = total.astype(jnp.bfloat16)
    centre = jnp.broadcast_to(centre_ref[...], (rows, 128)).T[:CENTRE_ROWS].astype(jnp.bfloat16)
    for place, out_ref in enumerate(out_refs):

        @pl.when(step == place)
        def _():
            out_ref[:rows, :] = total
            out_ref[rows:, :] = jnp.zeros((CENTRE_ROWS, out_ref.shape[1]), jnp.bfloat16)
            out_ref[rows:, :rows] = centre


def back_project(order, pieces, delta, centre, w_query, w_key, w_value, blocks):
    rows = delta.shape[0]
    depth = w_query.shape[0] // blocks
    picked = lambda i: (order(i), 0)
    whole = lambda i: (0, 0)
    return pl.pallas_call(
        back_kernel,
        out_shape=(jax.ShapeDtypeStruct((rows + CENTRE_ROWS, depth), jnp.bfloat16),) * pieces,
        grid=(pieces,),
        in_specs=[
            pl.BlockSpec(delta.shape, whole),
            pl.BlockSpec(centre.shape, whole),
            pl.BlockSpec((depth, w_query.shape[1]), picked),
            pl.BlockSpec((depth, w_key.shape[1]), picked),
            pl.BlockSpec((depth, w_value.shape[1]), picked),
        ],
        out_specs=(pl.BlockSpec((rows + CENTRE_ROWS, depth), whole),) * pieces,
        compiler_params=pltpu.CompilerParams(vmem_limit_bytes=VMEM_LIMIT),
        cost_estimate=small_cost(),
        name="back",
    )(delta, centre, w_query, w_key, w_value)


def weight_kernel(group, sources, *refs):
    turned_refs, delta_refs = refs[:sources], refs[sources : 2 * sources]
    query_ref, key_ref, value_ref, token_ref = refs[-4:]
    token_ref[...] = jnp.zeros_like(token_ref)
    total = None
    for turned_ref, delta_ref in zip(turned_refs, delta_refs):
        term = nn_dot(turned_ref[...], delta_ref[...])
        total = term if total is None else total + term
    mid = group * HEAD_DIM
    query_ref[...] = total[:, :mid]
    key_ref[...] = total[:, mid : mid + HEAD_DIM]
    value_ref[...] = total[:, mid + HEAD_DIM :]


def weight_gradients(turned, deltas, head, kv_local, group, before):
    depth, rows = turned[0].shape
    span = (group + 2) * HEAD_DIM
    cuts = 4 if depth % 64 == 0 else 2
    cut = depth // cuts
    sources = len(turned)
    out_block = lambda i: (i, head)
    kept = list(before) if before is not None else []
    estimate = small_cost()
    if kept:
        estimate = pl.CostEstimate(
            flops=2 * sources * rows * depth * span,
            bytes_accessed=4 * depth * span + 2 * sources * rows * (depth + span),
            transcendentals=0,
        )
    return pl.pallas_call(
        functools.partial(weight_kernel, group, sources),
        out_shape=(
            jax.ShapeDtypeStruct((depth, kv_local * group * HEAD_DIM), jnp.float32),
            jax.ShapeDtypeStruct((depth, kv_local * HEAD_DIM), jnp.float32),
            jax.ShapeDtypeStruct((depth, kv_local * HEAD_DIM), jnp.float32),
            jax.ShapeDtypeStruct((8, 128), jnp.float32),
        ),
        grid=(cuts,),
        in_specs=[pl.BlockSpec((cut, rows), lambda i: (i, 0))] * sources
        + [pl.BlockSpec((rows, span), lambda i: (0, 0))] * sources
        + [pl.BlockSpec(memory_space=pl.ANY)] * len(kept),
        out_specs=(
            pl.BlockSpec((cut, group * HEAD_DIM), out_block),
            pl.BlockSpec((cut, HEAD_DIM), out_block),
            pl.BlockSpec((cut, HEAD_DIM), out_block),
            pl.BlockSpec((8, 128), lambda i: (0, 0)),
        ),
        input_output_aliases={2 * sources + i: i for i in range(len(kept))},
        compiler_params=pltpu.CompilerParams(vmem_limit_bytes=VMEM_LIMIT),
        cost_estimate=estimate,
        name="weights",
    )(*turned, *deltas, *kept)


def gate_kernel(*refs):
    del refs


def gate(arrays, tokens):
    hbm = pl.BlockSpec(memory_space=pl.ANY)
    return pl.pallas_call(
        gate_kernel,
        out_shape=tuple(jax.ShapeDtypeStruct(x.shape, x.dtype) for x in arrays),
        in_specs=[hbm] * (len(arrays) + len(tokens)),
        out_specs=(hbm,) * len(arrays),
        input_output_aliases={i: i for i in range(len(arrays))},
        compiler_params=pltpu.CompilerParams(vmem_limit_bytes=VMEM_LIMIT),
        cost_estimate=small_cost(),
        name="gate",
    )(*arrays, *tokens)


def join_kernel(inner_ref, other_ref, end_ref, *rest):
    out_ref, token_ref = rest[-2:]
    token_ref[...] = jnp.zeros_like(token_ref)
    index = lax.axis_index("tensor")
    inner = (index > 0) & (index < lax.axis_size("tensor") - 1)

    @pl.when(inner)
    def _():
        out_ref[...] = (
            inner_ref[...].astype(jnp.float32) + other_ref[...].astype(jnp.float32)
        ).astype(jnp.bfloat16)

    @pl.when(jnp.logical_not(inner))
    def _():
        out_ref[...] = end_ref[...]


def join(inner_part, other, end_part, tokens):
    vmem = pl.BlockSpec(memory_space=pltpu.VMEM)
    return pl.pallas_call(
        join_kernel,
        out_shape=(
            jax.ShapeDtypeStruct(end_part.shape, end_part.dtype),
            jax.ShapeDtypeStruct((8, 128), jnp.float32),
        ),
        in_specs=[vmem] * 3 + [pl.BlockSpec(memory_space=pl.ANY)] * len(tokens),
        out_specs=(vmem, vmem),
        compiler_params=pltpu.CompilerParams(vmem_limit_bytes=VMEM_LIMIT),
        cost_estimate=small_cost(),
        name="join",
    )(inner_part, other, end_part, *tokens)


def finish_kernel(width, for_ends, for_inner, input_ref, gain_ref, inverse_ref, *refs):
    part_refs, (out_ref, sum_ref) = refs[:-3], refs[-2:]
    rows, wide = out_ref.shape
    index = lax.axis_index("tensor")
    ends = ((index == 0) | (index == lax.axis_size("tensor") - 1)).astype(jnp.float32)
    total = None
    for place, part_ref in enumerate(part_refs):
        part = part_ref[...].astype(jnp.float32)
        if place < for_ends:
            part = part * ends
        elif place < for_ends + for_inner:
            part = part * (1.0 - ends)
        total = part if total is None else total + part
    d_normed = total[:rows]
    centre = total[rows:, :rows].T[:, :1] * (1.0 / width)
    inverse = inverse_ref[...]
    scaled = input_ref[...].astype(jnp.float32) * inverse
    out_ref[...] = (
        inverse * ((1.0 + gain_ref[...]) * d_normed - scaled * centre)
    ).astype(jnp.bfloat16)
    sum_ref[...] = jnp.sum(d_normed * scaled, axis=0, keepdims=True)


def finish(width, for_ends, for_inner, input_columns, gain_columns, inverse, parts, token):
    rows, wide = input_columns.shape
    whole = lambda array: pl.BlockSpec(array.shape, lambda i: (0, 0))
    return pl.pallas_call(
        functools.partial(finish_kernel, width, for_ends, for_inner),
        out_shape=(
            jax.ShapeDtypeStruct((rows, wide), jnp.bfloat16),
            jax.ShapeDtypeStruct((1, wide), jnp.float32),
        ),
        grid=(1,),
        in_specs=[whole(x) for x in (input_columns, gain_columns, inverse, *parts)]
        + [pl.BlockSpec(memory_space=pl.ANY)],
        out_specs=(
            pl.BlockSpec((rows, wide), lambda i: (0, 0)),
            pl.BlockSpec((1, wide), lambda i: (0, 0)),
        ),
        compiler_params=pltpu.CompilerParams(vmem_limit_bytes=VMEM_LIMIT),
        cost_estimate=small_cost(),
        name="finish",
    )(input_columns, gain_columns, inverse, *parts, token)


def total_kernel(*refs):
    refs[-1][...] = (refs[0][...] + refs[1][...]) + (refs[2][...] + refs[3][...])


def total_of_four(arrays, token):
    whole = pl.BlockSpec(arrays[0].shape, lambda i: (0, 0))
    return pl.pallas_call(
        total_kernel,
        out_shape=jax.ShapeDtypeStruct(arrays[0].shape, arrays[0].dtype),
        grid=(1,),
        in_specs=[whole] * 4 + [pl.BlockSpec(memory_space=pl.ANY)],
        out_specs=whole,
        compiler_params=pltpu.CompilerParams(vmem_limit_bytes=VMEM_LIMIT),
        cost_estimate=small_cost(),
        name="total",
    )(*arrays, token)


def branch_send(array, chips, shift, swap):
    pairs = [
        (c * 2 + k, ((c + shift) % chips) * 2 + (k ^ swap)) for c in range(chips) for k in range(2)
    ]
    return lax.ppermute(array, "branch", pairs)


def pick(table, index):
    chosen = table[-1]
    for place in range(len(table) - 2, -1, -1):
        chosen = jnp.where(index == place, table[place], chosen)
    return chosen


def scatter_begin(project, total):
    index = lambda: lax.axis_index("tensor")
    if total != 4:
        parts = project(lambda i: lax.rem(index() + i + 1, total), total)
        arrived = [
            lax.ppermute(part, "tensor", [(t, (t + shift) % total) for t in range(total)])
            for shift, part in zip(range(1, total), parts[:-1])
        ]
        return parts, arrived
    table = [[3, 0, 3, 0], [0, 2, 1, 3], [2, 3, 0, 1], [1, 1, 2, 2]]
    order = lambda base: lambda i: pick([pick(row, index()) for row in table[base : base + 2]], i)
    first, second = project(order(0), 2)
    from_first = lax.ppermute(first, "tensor", [(0, 1), (1, 0), (2, 3), (3, 2)])
    from_inner = lax.ppermute(second, "tensor", [(1, 2), (2, 1)])
    third, fourth = project(order(2), 2)
    return (first, second, third, fourth), (from_first, from_inner)


def scatter_end(parts, arrived, total, tokens):
    if total != 4:
        return [parts[-1], *arrived], 0, 0, arrived[0], arrived
    _, second, third, fourth = parts
    from_first, from_inner = arrived
    joined, token = join(third, from_first, fourth, (from_inner, *tokens))
    (held,) = gate((third,), (token,))
    from_ends = lax.ppermute(held, "tensor", [(0, 2), (3, 1)])
    from_joined = lax.ppermute(joined, "tensor", [(1, 3), (2, 0), (0, 1), (3, 2)])
    return [from_first, second, fourth, from_inner, from_ends, from_joined], 2, 1, token, (from_ends, from_joined)


def local(layer_input, norm_gain, w_query, w_key, w_value, head_grad, parents, row_counts):
    branch_total = lax.axis_size("branch")
    tensor_total = lax.axis_size("tensor")
    slots = row_counts.shape[0] // branch_total
    rows, width = layer_input.shape
    column_width = width // tensor_total
    depth = width // branch_total
    chips = branch_total // 2
    group = w_query.shape[1] // w_key.shape[1]
    kv_local = w_key.shape[1] // HEAD_DIM
    offsets = [(shift, swap) for shift in range(chips) for swap in range(2)]

    def targets():
        index = lax.axis_index("branch")
        chip, core = index // 2, index % 2
        return [lax.rem(chip + s, chips) * 2 + lax.rem(core + e, 2) for s, e in offsets]

    pieces = cut_columns(layer_input, targets, branch_total)
    shared = [branch_send(piece, chips, s, e) for piece, (s, e) in zip(pieces[1:], offsets[1:])]
    delta, centre, inverse, scaled = attention_backward(
        layer_input, norm_gain, w_query, w_key, w_value, head_grad, parents, row_counts, slots
    )

    def project(order, pieces):
        return back_project(
            order, pieces, delta, centre, w_query, w_key, w_value, tensor_total
        )

    parts, arrived = scatter_begin(project, tensor_total)

    (first,) = gate(scaled[:1], (*shared, parts[1]))
    sent = [branch_send(first, chips, s, 0) for s in range(1, chips)]
    gain_own = lax.dynamic_slice_in_dim(norm_gain, lax.axis_index("branch") * depth, depth)
    turned = turn([pieces[0]] + shared, gain_own.reshape(1, depth))
    parts, for_ends, for_inner, met, late = scatter_end(parts, arrived, tensor_total, turned[:1])
    *sent, first = gate((*sent, first), (met,))
    others = gate(scaled[1:], (sent[0],)) if kv_local > 1 else ()
    weights, tokens = None, []
    for head, scaled_delta in enumerate((first, *others)):
        if head > 0:
            sent = [branch_send(scaled_delta, chips, s, 0) for s in range(1, chips)]
            scaled_delta, *sent = gate((scaled_delta, *sent), (*late, tokens[0]))
        gathered = []
        for part in [scaled_delta] + sent:
            gathered += [part, branch_send(part, chips, 0, 1)]
        *weights, token = weight_gradients(turned, gathered, head, kv_local, group, weights)
        tokens.append(token)

    column_start = lax.axis_index("tensor") * column_width
    input_columns = lax.dynamic_slice_in_dim(layer_input, column_start, column_width, 1)
    gain_columns = lax.dynamic_slice_in_dim(norm_gain, column_start, column_width, 0)
    grad_input, gain_sum = finish(
        width,
        for_ends,
        for_inner,
        input_columns,
        gain_columns.reshape(1, column_width),
        inverse,
        parts,
        tokens[0],
    )
    if chips == 2:
        sums = [gain_sum] + [branch_send(gain_sum, chips, s, e) for s, e in offsets[1:]]
        grad_gain = total_of_four(sums, tokens[-1])
    else:
        grad_gain = lax.psum(gain_sum, "branch")
    return (grad_input, *weights, grad_gain.reshape(column_width))


def solution(mesh):
    placed = (
        P(("parts", "branch"), None),
        P(),
        P(None, "tensor"),
        P(None, "tensor"),
        P(None, "tensor"),
        P(("parts", "branch"), "tensor"),
        P(("parts", "branch")),
        P("parts"),
    )
    return jax.shard_map(
        local,
        mesh=mesh,
        in_specs=placed,
        out_specs=(
            P(("parts", "branch"), "tensor"),
            P(("parts", "branch"), "tensor"),
            P(("parts", "branch"), "tensor"),
            P(("parts", "branch"), "tensor"),
            P(("parts", "tensor")),
        ),
        check_vma=False,
    )
```

time: 142 us -> 148 us (1.042)
  Pallas kernels: 30 us -> 105 us
  waiting for transfers between devices: 52.5 us -> 16.1 us
  blocking collectives: 35.8 us -> 0 us
  starting transfers between devices: 10.3 us -> 19.2 us
  local copies, waits for them, and re-layouts: 8.65 us -> 5.15 us
  other arithmetic: 3.82 us -> 1.29 us
    pallas_call x3 -> x14, Pallas kernels: 18.8 us -> 90.7 us  [the longest x1 56.7 us: cut_columns(): pl.pallas_call(functools.partial(cut_kernel, targets), out_shape=(jax.Sha...]
    psum x2 -> x0, blocking collectives: 35.8 us -> none  [the longest x1 29.6 us: local(): centre = lax.psum(centre_part, 'tensor') * (1.0 / width)]
    ppermute x6 -> x12, waiting for transfers between devices: 23.2 us -> 0.14 us  [branch_send(): return lax.ppermute(array, 'branch', pairs)]
    ppermute x3 -> x4, waiting for transfers between devices: 29.4 us -> 15.9 us  [the longest x1 10.9 us: scatter_end(): lax.ppermute(joined, 'tensor', [(1, 3), (2, 0), (0, 1), (3, 2)])]
    unnamed x18 -> x0, local copies, waits for them, and re-layouts: 6.38 us -> none
    ppermute x3 -> x4, starting transfers between devices: 5.76 us -> 11 us  [the longest x1 7.96 us: scatter_end(): from_ends = lax.ppermute(held, 'tensor', [(0, 2), (3, 1)])]
    ppermute x6 -> x12, starting transfers between devices: 4.5 us -> 8.27 us  [branch_send(): return lax.ppermute(array, 'branch', pairs)]
    pallas_call x1, Pallas kernels: 11.2 us -> 14.7 us  [attention_backward(): pl.pallas_call(functools.partial(attention_kernel, slots), out_shape=(jax...]
  transfers between devices with their start and end apart: 9 -> 16, of which waited for: 3 -> 3; matrix products, arithmetic and copies ran while one was open for 3% -> 3% of each run, Pallas kernels for 7% -> 32%
where the time goes in v4:
time: 148 us
  Pallas kernels  105 us (71%)
  starting transfers between devices  19.2 us (13%)
  waiting for transfers between devices  16.1 us (11%)
  local copies, waits for them, and re-layouts  5.15 us (3%)
    pallas_call x1, Pallas kernels, cut_columns(): pl.pallas_call(functools.partial(cut_kernel, targets), out_shape=(jax.Sha...  56.7 us
    pallas_call x1, Pallas kernels, attention_backward(): pl.pallas_call(functools.partial(attention_kernel, slots), out_shape=(jax...  14.7 us
    pallas_call x2, Pallas kernels, back_project(): pl.pallas_call(back_kernel, out_shape=(jax.ShapeDtypeStruct((rows + CENTR...  12.1 us
    pallas_call x2, Pallas kernels, weight_gradients(): pl.pallas_call(functools.partial(weight_kernel, group, sources), out_shap...  12 us
    ppermute x1, waiting for transfers between devices, scatter_end(): lax.ppermute(joined, 'tensor', [(1, 3), (2, 0), (0, 1), (3, 2)])  10.9 us
    ppermute x12, starting transfers between devices, branch_send(): return lax.ppermute(array, 'branch', pairs)  8.27 us
    ppermute x1, starting transfers between devices, scatter_end(): from_ends = lax.ppermute(held, 'tensor', [(0, 2), (3, 1)])  7.96 us
    ppermute x1, waiting for transfers between devices, scatter_end(): from_ends = lax.ppermute(held, 'tensor', [(0, 2), (3, 1)])  5.07 us
  transfers between devices with their start and end apart: 16, of which 3 were waited for; matrix products, arithmetic and copies ran while one was open for 3% of the time, Pallas kernels for 32%

profile of v4, /device:TPU:0, one launch (start us, length us, event | category | flops | bytes accessed | tf_op | source)
XLA Modules:
  0.0 147.8 jit_solution(17582443312364347273)
XLA Ops:
  0.6 56.7 %cut.1 = (bf16[256,896]{1,0:T(8,128)(2,1)}, bf16[256,896]{1,0:T(8,128)(2,1)}, bf16[256,896]{1,0:T(8,128)(2,1)}, bf16[256,896]{1,0:T(8,128)(2,1)}) custom-call(bf16[256,3584]{1,0:T(8,128)(2,1)} %input_hbm.1), custom_call_target="tpu_custom_call" | custom-call | flops 1000000 | bytes 100000 | tf_op jit(solution)/shard_map/cut/pallas_call | solution.py:67
  57.4 0.5 collective-permute-start.2
  57.9 2.6 %collective-permute-start.3 = (bf16[256,896]{1,0:T(8,128)(2,1)}, bf16[256,896]{1,0:T(8,128)(2,1)}, u32[]{:S(2)}, u32[]{:S(2)}) collective-permute-start(bf16[256,896]{1,0:T(8,128)(2,1)} %get-tuple-element.47), channel_id=1, source_target_pairs={{0,8},{4,12},{8,0},{12,4},{1,9},{5,13},{9,1},{13,5},{2,10},{6,14},... | collective-permute-start | bytes 1376264 | tf_op jit(solution)/shard_map/ppermute | solution.py:481
  60.5 0.1 collective-permute-start.4
  60.5 14.7 %attention.1 = (bf16[256,2048]{1,0:T(8,128)(2,1)}, f32[256,1]{1,0:T(8,128)}, f32[256,1]{1,0:T(8,128)}, bf16[256,1024]{1,0:T(8,128)(2,1)}, bf16[256,1024]{1,0:T(8,128)(2,1)}) custom-call(s32[8]{0:T(128)} %count_ref.1, s32[256]{0:T(256)} %parent_ref.1, f32[3584]{0:T(1024)} %gain_ref.1, bf16[256,3584]{1,0:T(8,128)(2,1)} %input_hbm.1, ...), custom_call_target="tpu_custom_call" | custom-call | flops 1000000 | bytes 100000 | tf_op jit(solution)/shard_map/attention/pallas_call | solution.py:216
  75.3 6.1 %back.2 = (bf16[272,896]{1,0:T(8,128)(2,1)}, bf16[272,896]{1,0:T(8,128)(2,1)}) custom-call(bf16[256,2048]{1,0:T(8,128)(2,1)} %get-tuple-element.39.delta_ref, f32[256,1]{1,0:T(8,128)} %get-tuple-element.40.centre_ref, bf16[3584,1024]{1,0:T(8,128)(2,1)} %query_ref.5, bf16[3584,512]{1,0:T(8,128)(2,1)} %key_ref.5, bf16[3584,512]{1,0:T(8,128)(2,1)} %value_ref.5), custom_call_target="tpu_custom_call" | custom-call | flops 1000000 | bytes 100000 | tf_op jit(solution)/shard_map/back/pallas_call | solution.py:291
  81.3 0.0 collective-permute-done.2.refs_1_
  81.3 0.0 collective-permute-done.3.refs_2_
  81.3 0.1 collective-permute-done.4.refs_3_
  81.5 1.7 %collective-permute-start.7 = (bf16[256,1024]{1,0:T(8,128)(2,1)}, bf16[256,1024]{1,0:T(8,128)(2,1)}, u32[]{:S(2)}, u32[]{:S(2)}) collective-permute-start(bf16[256,1024]{1,0:T(8,128)(2,1)} %gate.6.refs_1_), channel_id=1, source_target_pairs={{0,8},{4,12},{8,0},{12,4},{1,9},{5,13},{9,1},{13,5},{2,10},{6,14},... | collective-permute-start | bytes 1572872 | tf_op jit(solution)/shard_map/ppermute | solution.py:481
  83.2 1.6 %collective-permute-start = (bf16[272,896]{1,0:T(8,128)(2,1)}, bf16[272,896]{1,0:T(8,128)(2,1)}, u32[]{:S(2)}, u32[]{:S(2)}) collective-permute-start(bf16[272,896]{1,0:T(8,128)(2,1)} %get-tuple-element.41), channel_id=1, source_target_pairs={{0,1},{1,0},{2,3},{3,2},{4,5},{5,4},{6,7},{7,6},{8,9},{9,8},{10,11... | collective-permute-start | bytes 1462280 | tf_op jit(solution)/shard_map/ppermute | solution.py:503
  84.7 1.4 collective-permute-start.1
  86.2 1.4 fusion
  87.6 0.6 reshape.20.gain_ref
  88.2 6.1 %back.3 = (bf16[272,896]{1,0:T(8,128)(2,1)}, bf16[272,896]{1,0:T(8,128)(2,1)}) custom-call(bf16[256,2048]{1,0:T(8,128)(2,1)} %get-tuple-element.39.delta_ref, f32[256,1]{1,0:T(8,128)} %get-tuple-element.40.centre_ref, bf16[3584,1024]{1,0:T(8,128)(2,1)} %query_ref.5, bf16[3584,512]{1,0:T(8,128)(2,1)} %key_ref.5, bf16[3584,512]{1,0:T(8,128)(2,1)} %value_ref.5), custom_call_target="tpu_custom_call" | custom-call | flops 1000000 | bytes 100000 | tf_op jit(solution)/shard_map/back/pallas_call | solution.py:291
  94.2 2.9 %turn.1 = (bf16[896,256]{1,0:T(8,128)(2,1)}, bf16[896,256]{1,0:T(8,128)(2,1)}, bf16[896,256]{1,0:T(8,128)(2,1)}, bf16[896,256]{1,0:T(8,128)(2,1)}) custom-call(f32[1,896]{1,0:T(1,128)} %reshape.20.gain_ref, bf16[256,896]{1,0:T(8,128)(2,1)} %get-tuple-element.45.refs_0_, bf16[256,896]{1,0:T(8,128)(2,1)} %collective-permute-done.2.refs_1_, ...), custom_call_target="tpu_custom_call" | custom-call | flops 1000000 | bytes 100000 | tf_op jit(solution)/shard_map/turn/pallas_call | solution.py:88
  97.2 0.0 collective-permute-done.other_ref.refs_0_
  97.2 0.0 collective-permute-done.1.rest_0_.refs_3_
  97.2 2.2 %join.1 = (bf16[272,896]{1,0:T(8,128)(2,1)}, f32[8,128]{1,0:T(8,128)}) custom-call(bf16[272,896]{1,0:T(8,128)(2,1)} %get-tuple-element.44.inner_ref.refs_0_, bf16[272,896]{1,0:T(8,128)(2,1)} %collective-permute-done.other_ref.refs_0_, bf16[272,896]{1,0:T(8,128)(2,1)} %get-tuple-element.43.end_ref.refs_2_, ...), custom_call_target="tpu_custom_call" | custom-call | flops 1000000 | bytes 100000 | tf_op jit(solution)/shard_map/join/pallas_call | solution.py:400
  99.3 0.0 collective-permute-done.7.refs_0_
  99.3 0.0 collective-permute-start.8
  99.3 0.5 collective-permute-start.9
  99.8 0.5 collective-permute-start.10
  100.4 8.0 %collective-permute-start.5 = (bf16[272,896]{1,0:T(8,128)(2,1)}, bf16[272,896]{1,0:T(8,128)(2,1)}, u32[]{:S(2)}, u32[]{:S(2)}) collective-permute-start(bf16[272,896]{1,0:T(8,128)(2,1)} %gate.5), channel_id=1, source_target_pairs={{0,2},{3,1},{4,6},{7,5},{8,10},{11,9},{12,14},{15,13},{16,18},{19,... | collective-permute-start | bytes 1462280 | tf_op jit(solution)/shard_map/ppermute | solution.py:516
  108.4 0.0 collective-permute-start.6
  108.4 0.0 collective-permute-done.8.refs_5_
  108.4 0.0 collective-permute-done.9.refs_7_
  108.4 6.0 %weights.2 = (f32[896,1024]{1,0:T(8,128)}, f32[896,512]{1,0:T(8,128)}, f32[896,512]{1,0:T(8,128)}, f32[8,128]{1,0:T(8,128)}) custom-call(bf16[896,256]{1,0:T(8,128)(2,1)} %get-tuple-element.49.rest_1_.refs_0_, bf16[896,256]{1,0:T(8,128)(2,1)} %get-tuple-element.52.refs_1_, bf16[896,256]{1,0:T(8,128)(2,1)} %get-tuple-element.53.refs_2_, ...), custom_call_target="tpu_custom_call" | custom-call | flops 1000000 | bytes 100000 | tf_op jit(solution)/shard_map/weights/pallas_call | solution.py:338
  114.4 5.1 %collective-permute-done.5.refs_4_.refs_2_ = bf16[272,896]{1,0:T(8,128)(2,1)} collective-permute-done((bf16[272,896]{1,0:T(8,128)(2,1)}, bf16[272,896]{1,0:T(8,128)(2,1)}, u32[]{:S(2)}, u32[]{:S(2)}) %collective-permute-start.5) | collective-permute-done | bytes 487456 | tf_op jit(solution)/shard_map/ppermute | solution.py:516
  119.4 10.9 %collective-permute-done.6.refs_5_.refs_3_ = bf16[272,896]{1,0:T(8,128)(2,1)} collective-permute-done((bf16[272,896]{1,0:T(8,128)(2,1)}, bf16[272,896]{1,0:T(8,128)(2,1)}, u32[]{:S(2)}, u32[]{:S(2)}) %collective-permute-start.6) | collective-permute-done | bytes 487456 | tf_op jit(solution)/shard_map/ppermute | solution.py:517
  130.3 0.0 collective-permute-done.10.refs_1_
  130.3 0.0 collective-permute-start.11
  130.3 0.5 collective-permute-start.12
  130.8 1.3 reshape.19.gain_ref
  132.1 1.9 %constant_dynamic-slice_fusion.input_ref = bf16[256,896]{1,0:T(8,128)(2,1)} fusion(bf16[256,3584]{1,0:T(8,128)(2,1)} %input_hbm.1, s32[]{:T(128)S(6)} %select_n.7), kind=kLoop, calls=%fused_computation | loop fusion | bytes 917508 | tf_op jit(solution)/shard_map/dynamic_slice | solution.py:570
  133.9 3.5 %finish.1 = (bf16[256,896]{1,0:T(8,128)(2,1)}, f32[1,896]{1,0:T(1,128)}) custom-call(bf16[256,896]{1,0:T(8,128)(2,1)} %constant_dynamic-slice_fusion.input_ref, f32[1,896]{1,0:T(1,128)} %reshape.19.gain_ref, f32[256,1]{1,0:T(8,128)} %get-tuple-element.38.inverse_ref, bf16[272,896]{1,0:T(8,128)(2,1)} %collective-permute-done.other_ref.refs_0_, ...), custom_call_target="tpu_custom_call" | custom-call | flops 1000000 | bytes 100000 | tf_op jit(solution)/shard_map/finish/pallas_call | solution.py:440
  137.4 0.1 collective-permute-start.13
  137.4 1.5 %collective-permute-start.14 = (f32[1,896]{1,0:T(1,128)}, f32[1,896]{1,0:T(1,128)}, u32[]{:S(2)}, u32[]{:S(2)}) collective-permute-start(f32[1,896]{1,0:T(1,128)} %get-tuple-element.69.refs_0_), channel_id=1, source_target_pairs={{0,8},{4,12},{8,0},{12,4},{1,9},{5,13},{9,1},{13,5},{2,10},{6,14},... | collective-permute-start | bytes 10760 | tf_op jit(solution)/shard_map/ppermute | solution.py:481
  138.9 0.3 collective-permute-start.15
  139.2 0.0 collective-permute-done.11.refs_5_
  139.2 0.0 collective-permute-done.12.refs_7_
  139.2 6.0 %weights.3 = (f32[896,1024]{1,0:T(8,128)}, f32[896,512]{1,0:T(8,128)}, f32[896,512]{1,0:T(8,128)}, f32[8,128]{1,0:T(8,128)}) custom-call(bf16[896,256]{1,0:T(8,128)(2,1)} %get-tuple-element.49.rest_1_.refs_0_, bf16[896,256]{1,0:T(8,128)(2,1)} %get-tuple-element.52.refs_1_, ...), custom_call_target="tpu_custom_call", output_to_operand_aliasing={{0}: (8, {}), {1}: (9, {}), {2}: (10, {})} | custom-call | flops 1879048192 | bytes 7602176 | tf_op jit(solution)/shard_map/weights/pallas_call | solution.py:338
  145.2 0.0 collective-permute-done.13.refs_1_
  145.2 0.0 collective-permute-done.14.refs_2_
  145.2 0.0 collective-permute-done.15.refs_3_
  145.3 1.3 total.1
  146.6 1.3 reduce
  (5 shorter events, 0.0 us)
Async XLA Ops:
  57.4 24.0 %collective-permute-start.2 = (bf16[256,896]{1,0:T(8,128)(2,1)}, bf16[256,896]{1,0:T(8,128)(2,1)}, u32[]{:S(2)}, u32[]{:S(2)}) collective-permute-start(bf16[256,896]{1,0:T(8,128)(2,1)} %get-tuple-element.46), channel_id=1, source_target_pairs={{0,4},{4,0},{8,12},{12,8},{1,5},{5,1},{9,13},{13,9},{2,6},{6,2},{1... | collective-permute-start | bytes 1376264 | tf_op jit(solution)/shard_map/ppermute | solution.py:481
  57.9 23.4 %collective-permute-start.3 = (bf16[256,896]{1,0:T(8,128)(2,1)}, bf16[256,896]{1,0:T(8,128)(2,1)}, u32[]{:S(2)}, u32[]{:S(2)}) collective-permute-start(bf16[256,896]{1,0:T(8,128)(2,1)} %get-tuple-element.47), channel_id=1, source_target_pairs={{0,8},{4,12},{8,0},{12,4},{1,9},{5,13},{9,1},{13,5},{2,10},{6,14},... | collective-permute-start | bytes 1376264 | tf_op jit(solution)/shard_map/ppermute | solution.py:481
  60.5 21.0 %collective-permute-start.4 = (bf16[256,896]{1,0:T(8,128)(2,1)}, bf16[256,896]{1,0:T(8,128)(2,1)}, u32[]{:S(2)}, u32[]{:S(2)}) collective-permute-start(bf16[256,896]{1,0:T(8,128)(2,1)} %get-tuple-element.48), channel_id=1, source_target_pairs={{0,12},{4,8},{8,4},{12,0},{1,13},{5,9},{9,5},{13,1},{2,14},{6,10},... | collective-permute-start | bytes 1376264 | tf_op jit(solution)/shard_map/ppermute | solution.py:481
  81.5 17.9 %collective-permute-start.7 = (bf16[256,1024]{1,0:T(8,128)(2,1)}, bf16[256,1024]{1,0:T(8,128)(2,1)}, u32[]{:S(2)}, u32[]{:S(2)}) collective-permute-start(bf16[256,1024]{1,0:T(8,128)(2,1)} %gate.6.refs_1_), channel_id=1, source_target_pairs={{0,8},{4,12},{8,0},{12,4},{1,9},{5,13},{9,1},{13,5},{2,10},{6,14},... | collective-permute-start | bytes 1572872 | tf_op jit(solution)/shard_map/ppermute | solution.py:481
  83.2 14.0 %collective-permute-start = (bf16[272,896]{1,0:T(8,128)(2,1)}, bf16[272,896]{1,0:T(8,128)(2,1)}, u32[]{:S(2)}, u32[]{:S(2)}) collective-permute-start(bf16[272,896]{1,0:T(8,128)(2,1)} %get-tuple-element.41), channel_id=1, source_target_pairs={{0,1},{1,0},{2,3},{3,2},{4,5},{5,4},{6,7},{7,6},{8,9},{9,8},{10,11... | collective-permute-start | bytes 1462280 | tf_op jit(solution)/shard_map/ppermute | solution.py:503
  84.7 12.4 %collective-permute-start.1 = (bf16[272,896]{1,0:T(8,128)(2,1)}, bf16[272,896]{1,0:T(8,128)(2,1)}, u32[]{:S(2)}, u32[]{:S(2)}) collective-permute-start(bf16[272,896]{1,0:T(8,128)(2,1)} %get-tuple-element.42.refs_4_.refs_1_), channel_id=1, source_target_pairs={{1,2},{2,1},{5,6},{6,5},{9,10},{10,9},{13,14},{14,13},{17,18},{18,... | collective-permute-start | bytes 1462280 | tf_op jit(solution)/shard_map/ppermute | solution.py:504
  99.3 9.0 %collective-permute-start.8 = (bf16[256,1024]{1,0:T(8,128)(2,1)}, bf16[256,1024]{1,0:T(8,128)(2,1)}, u32[]{:S(2)}, u32[]{:S(2)}) collective-permute-start(bf16[256,1024]{1,0:T(8,128)(2,1)} %get-tuple-element.56.refs_4_), channel_id=1, source_target_pairs={{0,4},{4,0},{8,12},{12,8},{1,5},{5,1},{9,13},{13,9},{2,6},{6,2},{1... | collective-permute-start | bytes 1572872 | tf_op jit(solution)/shard_map/ppermute | solution.py:481
  99.3 9.0 %collective-permute-start.9 = (bf16[256,1024]{1,0:T(8,128)(2,1)}, bf16[256,1024]{1,0:T(8,128)(2,1)}, u32[]{:S(2)}, u32[]{:S(2)}) collective-permute-start(bf16[256,1024]{1,0:T(8,128)(2,1)} %get-tuple-element.57.refs_6_.refs_1_), channel_id=1, source_target_pairs={{0,4},{4,0},{8,12},{12,8},{1,5},{5,1},{9,13},{13,9},{2,6},{6,2},{1... | collective-permute-start | bytes 1572872 | tf_op jit(solution)/shard_map/ppermute | solution.py:481
  99.8 30.4 %collective-permute-start.10 = (bf16[256,1024]{1,0:T(8,128)(2,1)}, bf16[256,1024]{1,0:T(8,128)(2,1)}, u32[]{:S(2)}, u32[]{:S(2)}) collective-permute-start(bf16[256,1024]{1,0:T(8,128)(2,1)} %gate.8.refs_0_), channel_id=1, source_target_pairs={{0,8},{4,12},{8,0},{12,4},{1,9},{5,13},{9,1},{13,5},{2,10},{6,14},... | collective-permute-start | bytes 1572872 | tf_op jit(solution)/shard_map/ppermute | solution.py:481
  100.4 19.0 %collective-permute-start.5 = (bf16[272,896]{1,0:T(8,128)(2,1)}, bf16[272,896]{1,0:T(8,128)(2,1)}, u32[]{:S(2)}, u32[]{:S(2)}) collective-permute-start(bf16[272,896]{1,0:T(8,128)(2,1)} %gate.5), channel_id=1, source_target_pairs={{0,2},{3,1},{4,6},{7,5},{8,10},{11,9},{12,14},{15,13},{16,18},{19,... | collective-permute-start | bytes 1462280 | tf_op jit(solution)/shard_map/ppermute | solution.py:516
  108.4 21.9 %collective-permute-start.6 = (bf16[272,896]{1,0:T(8,128)(2,1)}, bf16[272,896]{1,0:T(8,128)(2,1)}, u32[]{:S(2)}, u32[]{:S(2)}) collective-permute-start(bf16[272,896]{1,0:T(8,128)(2,1)} %get-tuple-element.51), channel_id=1, source_target_pairs={{1,3},{2,0},{0,1},{3,2},{5,7},{6,4},{4,5},{7,6},{9,11},{10,8},{8,9... | collective-permute-start | bytes 1462280 | tf_op jit(solution)/shard_map/ppermute | solution.py:517
  130.3 9.0 %collective-permute-start.11 = (bf16[256,1024]{1,0:T(8,128)(2,1)}, bf16[256,1024]{1,0:T(8,128)(2,1)}, u32[]{:S(2)}, u32[]{:S(2)}) collective-permute-start(bf16[256,1024]{1,0:T(8,128)(2,1)} %get-tuple-element.61.refs_4_), channel_id=1, source_target_pairs={{0,4},{4,0},{8,12},{12,8},{1,5},{5,1},{9,13},{13,9},{2,6},{6,2},{1... | collective-permute-start | bytes 1572872 | tf_op jit(solution)/shard_map/ppermute | solution.py:481
  130.3 9.0 %collective-permute-start.12 = (bf16[256,1024]{1,0:T(8,128)(2,1)}, bf16[256,1024]{1,0:T(8,128)(2,1)}, u32[]{:S(2)}, u32[]{:S(2)}) collective-permute-start(bf16[256,1024]{1,0:T(8,128)(2,1)} %get-tuple-element.62.refs_6_), channel_id=1, source_target_pairs={{0,4},{4,0},{8,12},{12,8},{1,5},{5,1},{9,13},{13,9},{2,6},{6,2},{1... | collective-permute-start | bytes 1572872 | tf_op jit(solution)/shard_map/ppermute | solution.py:481
  137.4 7.9 %collective-permute-start.13 = (f32[1,896]{1,0:T(1,128)}, f32[1,896]{1,0:T(1,128)}, u32[]{:S(2)}, u32[]{:S(2)}) collective-permute-start(f32[1,896]{1,0:T(1,128)} %get-tuple-element.69.refs_0_), channel_id=1, source_target_pairs={{0,4},{4,0},{8,12},{12,8},{1,5},{5,1},{9,13},{13,9},{2,6},{6,2},{1... | collective-permute-start | bytes 10760 | tf_op jit(solution)/shard_map/ppermute | solution.py:481
  137.4 7.8 %collective-permute-start.14 = (f32[1,896]{1,0:T(1,128)}, f32[1,896]{1,0:T(1,128)}, u32[]{:S(2)}, u32[]{:S(2)}) collective-permute-start(f32[1,896]{1,0:T(1,128)} %get-tuple-element.69.refs_0_), channel_id=1, source_target_pairs={{0,8},{4,12},{8,0},{12,4},{1,9},{5,13},{9,1},{13,5},{2,10},{6,14},... | collective-permute-start | bytes 10760 | tf_op jit(solution)/shard_map/ppermute | solution.py:481
  138.9 6.3 %collective-permute-start.15 = (f32[1,896]{1,0:T(1,128)}, f32[1,896]{1,0:T(1,128)}, u32[]{:S(2)}, u32[]{:S(2)}) collective-permute-start(f32[1,896]{1,0:T(1,128)} %get-tuple-element.69.refs_0_), channel_id=1, source_target_pairs={{0,12},{4,8},{8,4},{12,0},{1,13},{5,9},{9,5},{13,1},{2,14},{6,10},... | collective-permute-start | bytes 10760 | tf_op jit(solution)/shard_map/ppermute | solution.py:481

commit v5 on v0

v5 whole, which is shorter than its diff:
```python
import functools

import jax
import jax.numpy as jnp
from jax import lax
from jax.experimental import pallas as pl
from jax.experimental.pallas import tpu as pltpu
from jax.sharding import PartitionSpec as P

HEAD_DIM = 256
MIB = 1024 * 1024
CENTRE_ROWS = 16
VMEM_LIMIT = 64 * MIB


epsilon = 1e-06
softcap_limit = 50.0


def nn_dot(left, right):
    return lax.dot_general(
        left, right, (((1,), (0,)), ((), ())), preferred_element_type=jnp.float32
    )


def nt_dot(left, right):
    return lax.dot_general(
        left, right, (((1,), (1,)), ((), ())), preferred_element_type=jnp.float32
    )


def tn_dot(left, right):
    return lax.dot_general(
        left, right, (((0,), (0,)), ((), ())), preferred_element_type=jnp.float32
    )


def small_cost():
    return pl.CostEstimate(flops=1000000, bytes_accessed=100000, transcendentals=0)


def norm_kernel(targets, input_ref, gain_ref, inverse_ref, *rest):
    piece_refs, turned = rest[:-1], rest[-1]
    rows, width = input_ref.shape
    values = input_ref[...].astype(jnp.float32)
    inverse = lax.rsqrt(jnp.mean(values * values, axis=-1, keepdims=True) + epsilon)
    inverse_ref[...] = inverse
    gain = gain_ref[...].reshape(1, width)
    turned[...] = (values * inverse * (1.0 + gain)).astype(jnp.bfloat16).T
    depth = width // len(piece_refs)
    for target, piece_ref in zip(targets(), piece_refs):
        start = pl.multiple_of(target * depth, 16)
        piece_ref[...] = turned[pl.ds(start, depth), :]


def normalize(layer_input, norm_gain, targets, pieces, block):
    rows, width = layer_input.shape
    depth = width // pieces
    out = pl.pallas_call(
        functools.partial(norm_kernel, targets),
        out_shape=(jax.ShapeDtypeStruct((rows, 1), jnp.float32),)
        + (jax.ShapeDtypeStruct((depth, rows), jnp.bfloat16),) * pieces,
        grid=(rows // block,),
        in_specs=[
            pl.BlockSpec((block, width), lambda i: (i, 0)),
            pl.BlockSpec((width,), lambda i: (0,)),
        ],
        out_specs=(pl.BlockSpec((block, 1), lambda i: (i, 0)),)
        + (pl.BlockSpec((depth, block), lambda i: (0, i)),) * pieces,
        scratch_shapes=[pltpu.VMEM((width, block), jnp.bfloat16)],
        compiler_params=pltpu.CompilerParams(vmem_limit_bytes=VMEM_LIMIT),
        cost_estimate=small_cost(),
        name="norm",
    )(layer_input, norm_gain)
    return out[0], out[1:]


def ancestor_mask(parent_row):
    rows = parent_row.shape[1]
    row = lax.broadcasted_iota(jnp.int32, (rows, rows), 0)
    column = lax.broadcasted_iota(jnp.int32, (rows, rows), 1)
    reached = jnp.where((parent_row == row) | (row == column), 1.0, 0.0)
    for squaring in range(rows.bit_length() - 1):
        halfway = reached.astype(jnp.bfloat16)
        reached = jnp.minimum(nn_dot(halfway, halfway), 1.0)
    return reached.T


def attention_kernel(
    slots,
    group,
    kv_local,
    order,
    blocks,
    columns,
    shares,
    count_ref,
    parent_ref,
    inverse_ref,
    gain_ref,
    input_hbm,
    query_hbm,
    key_hbm,
    value_hbm,
    grad_hbm,
    *rest,
):
    delta_hbm, rest = rest[: len(shares)], rest[len(shares) :]
    part_hbm, rest = rest[:blocks], rest[blocks:]
    column_hbm, column_gain_ref, rest = rest[0], rest[1], rest[2:]
    (
        input_ref,
        gain_row,
        query_ref,
        key_ref,
        value_ref,
        grad_ref,
        sum_ref,
        delta_ref,
        query_turned,
        key_turned,
        value_turned,
        allowed_ref,
        centre_ref,
        kept,
        load_sem,
        weight_sem,
        store_sem,
        part_sem,
    ) = rest
    head_dim = HEAD_DIM
    rows, width = input_ref.shape
    block = rows // slots
    mid = group * head_dim
    steps = weight_sem.shape[0]
    chunk = width // steps
    weights = ((query_hbm, query_ref, mid, 0), (key_hbm, key_ref, head_dim, mid))
    weights += ((value_hbm, value_ref, head_dim, mid + head_dim),)

    def fetch(step, which):
        lines = pl.ds(pl.multiple_of(step * chunk, chunk), chunk)
        source, kept_ref = weights[which][:2]
        return pltpu.make_async_copy(
            source.at[lines, :], kept_ref.at[lines, :], weight_sem.at[step, which]
        )

    input_load = pltpu.make_async_copy(input_hbm, input_ref, load_sem.at[0])
    grad_load = pltpu.make_async_copy(grad_hbm, grad_ref, load_sem.at[1])
    input_load.start()
    for step in range(steps):
        for which in range(3):
            fetch(step, which).start()
    grad_load.start()
    gain_row[...] = gain_ref[...].reshape(1, width)

    first_count = lax.axis_index("branch") * slots
    parents = parent_ref[...].reshape(1, rows)
    for slot in range(slots):
        allowed_ref[slot] = ancestor_mask(parents[:, slot * block : (slot + 1) * block])
    sum_ref[...] = jnp.zeros_like(sum_ref)
    inverse = inverse_ref[...]
    input_load.wait()
    stores = []
    if columns:
        start = pl.multiple_of(lax.axis_index("tensor") * columns, 128)
        stores.append(
            pltpu.make_async_copy(
                input_ref.at[:, pl.ds(start, columns)], column_hbm, store_sem.at[0]
            )
        )
        stores[0].start()
        column_gain_ref[...] = gain_row[:, pl.ds(start, columns)]
    else:
        column_gain_ref[...] = jnp.zeros_like(column_gain_ref)

    def project(step, carry):
        lines = pl.ds(pl.multiple_of(step * chunk, chunk), chunk)
        gain = 1.0 + gain_row[:, lines]
        normed = (input_ref[:, lines].astype(jnp.float32) * inverse * gain).astype(jnp.bfloat16)
        for which, (_, kept_ref, wide, place) in enumerate(weights):
            fetch(step, which).wait()
            term = nn_dot(normed, kept_ref[lines, :])
            for h in range(kv_local):
                sum_ref[h, :, place : place + wide] += term[:, h * wide : (h + 1) * wide]
        return carry

    lax.fori_loop(0, steps, project, 0)
    grad_load.wait()
    scale = head_dim ** (-0.5)
    centre_ref[...] = jnp.zeros_like(centre_ref)

    def attend(h, carry):
        for slot in range(slots):
            lines = slice(slot * block, (slot + 1) * block)
            live = (
                lax.broadcasted_iota(jnp.int32, (block, mid), 0) < count_ref[first_count + slot]
            )
            columns = pl.ds(pl.multiple_of(h * mid, mid), mid)
            grad_rows = jnp.where(live, grad_ref[lines, columns].astype(jnp.float32), 0.0)
            pair = [slice(g * head_dim, (g + 1) * head_dim) for g in range(group)]
            grads = jnp.concatenate([grad_rows[:, p] for p in pair], axis=0).astype(jnp.bfloat16)
            queries = jnp.concatenate([sum_ref[h, lines, p] for p in pair], axis=0)
            queries = queries.astype(jnp.bfloat16)
            keys = sum_ref[h, lines, mid : mid + head_dim].astype(jnp.bfloat16)
            values = sum_ref[h, lines, mid + head_dim :].astype(jnp.bfloat16)
            allowed = jnp.concatenate([allowed_ref[slot]] * group, axis=0)
            bounded = jnp.tanh(nt_dot(queries, keys) * (scale / softcap_limit))
            weighted = allowed * jnp.exp(softcap_limit * bounded)
            probabilities = weighted * (1.0 / jnp.sum(weighted, axis=-1, keepdims=True))
            d_probs = nt_dot(grads, values)
            d_scores = probabilities * (
                d_probs - jnp.sum(probabilities * d_probs, axis=-1, keepdims=True)
            )
            d_raw = (d_scores * (1.0 - bounded * bounded) * scale).astype(jnp.bfloat16)
            prob_half = probabilities.astype(jnp.bfloat16)
            d_query = nn_dot(d_raw, keys)
            d_key = tn_dot(d_raw, queries)
            d_value = tn_dot(prob_half, grads)
            places = [
                (d_query[g * block : (g + 1) * block], query_turned, h * mid + g * head_dim)
                for g in range(group)
            ]
            places += [(d_key, key_turned, h * head_dim), (d_value, value_turned, h * head_dim)]
            product = None
            for which, (part, turned_ref, start) in enumerate(places):
                half = part.astype(jnp.bfloat16)
                line = which * rows + slot * block
                delta_ref[h, line : line + block, :] = half
                spot = pl.ds(pl.multiple_of(start, head_dim), head_dim)
                turned_ref[spot, lines] = half.T
                term = half.astype(jnp.float32) * sum_ref[
                    h, lines, which * head_dim : (which + 1) * head_dim
                ]
                product = term if product is None else product + term
            centre_ref[lines, :] += jnp.sum(product, axis=-1, keepdims=True)
        return carry

    lax.fori_loop(0, kv_local, attend, 0)
    lasts = []
    for share, out in zip(shares, delta_hbm):
        for place, block_index in enumerate(share):
            h, which = divmod(block_index, group + 2)
            lasts.append(
                pltpu.make_async_copy(
                    delta_ref.at[h, pl.ds(which * rows, rows), :],
                    out.at[pl.ds(place * rows, rows), :],
                    store_sem.at[1 + len(lasts)],
                )
            )
    for store in lasts:
        store.start()

    centre = jnp.broadcast_to(centre_ref[...], (rows, 128)).T[:CENTRE_ROWS].astype(jnp.bfloat16)
    span = width // blocks
    cuts = 2
    cut_lines = span // cuts
    parts = [
        pltpu.make_async_copy(kept.at[place], part_hbm[place], part_sem.at[place])
        for place in range(blocks)
    ]

    def project_back(step, carry):
        place, cut = step // cuts, lax.rem(step, cuts)
        lines = pl.ds(pl.multiple_of(order(place) * span + cut * cut_lines, 16), cut_lines)
        total = nn_dot(query_ref[lines, :], query_turned[...])
        total += nn_dot(key_ref[lines, :], key_turned[...])
        total += nn_dot(value_ref[lines, :], value_turned[...])
        spot = pl.ds(pl.multiple_of(cut * cut_lines, 16), cut_lines)
        kept[place, spot, :] = total.astype(jnp.bfloat16)
        for which, part in enumerate(parts):

            @pl.when((place == which) & (cut == cuts - 1))
            def _():
                kept[which, span:, :] = centre
                part.start()

        return carry

    lax.fori_loop(0, blocks * cuts, project_back, 0)
    for store in stores + lasts + parts:
        store.wait()


def attention_backward(
    layer_input,
    inverse,
    norm_gain,
    w_query,
    w_key,
    w_value,
    head_grad,
    parents,
    counts,
    slots,
    order,
    blocks,
    shares,
):
    rows, width = layer_input.shape
    kv_local = w_key.shape[1] // HEAD_DIM
    group = w_query.shape[1] // w_key.shape[1]
    span = (group + 2) * HEAD_DIM
    stack = (group + 2) * rows
    column_width = width // blocks
    cut = column_width % 128 == 0
    wide = column_width if cut else 128
    steps = width // 512 if width % 512 == 0 else 1
    part_shape = (column_width + CENTRE_ROWS, rows)
    hbm = pl.BlockSpec(memory_space=pl.ANY)
    vmem = pl.BlockSpec(memory_space=pltpu.VMEM)
    half = lambda *shape: jax.ShapeDtypeStruct(shape, jnp.bfloat16)
    out = pl.pallas_call(
        functools.partial(
            attention_kernel, slots, group, kv_local, order, blocks, wide if cut else 0, shares
        ),
        out_shape=tuple(half(len(share) * rows, HEAD_DIM) for share in shares)
        + (half(*part_shape),) * blocks
        + (half(rows, wide), jax.ShapeDtypeStruct((1, wide), jnp.float32)),
        in_specs=[pl.BlockSpec(memory_space=pltpu.SMEM), vmem, vmem, vmem] + [hbm] * 5,
        out_specs=(hbm,) * (1 + len(shares) + blocks) + (vmem,),
        scratch_shapes=[
            pltpu.VMEM((rows, width), jnp.bfloat16),
            pltpu.VMEM((1, width), jnp.float32),
            pltpu.VMEM(w_query.shape, jnp.bfloat16),
            pltpu.VMEM(w_key.shape, jnp.bfloat16),
            pltpu.VMEM(w_value.shape, jnp.bfloat16),
            pltpu.VMEM(head_grad.shape, jnp.bfloat16),
            pltpu.VMEM((kv_local, rows, span), jnp.float32),
            pltpu.VMEM((kv_local, stack, HEAD_DIM), jnp.bfloat16),
            pltpu.VMEM((w_query.shape[1], rows), jnp.bfloat16),
            pltpu.VMEM((w_key.shape[1], rows), jnp.bfloat16),
            pltpu.VMEM((w_value.shape[1], rows), jnp.bfloat16),
            pltpu.VMEM((slots, rows // slots, rows // slots), jnp.float32),
            pltpu.VMEM((rows, 1), jnp.float32),
            pltpu.VMEM((blocks, *part_shape), jnp.bfloat16),
            pltpu.SemaphoreType.DMA((2,)),
            pltpu.SemaphoreType.DMA((steps, 3)),
            pltpu.SemaphoreType.DMA((1 + kv_local * (group + 2),)),
            pltpu.SemaphoreType.DMA((blocks,)),
        ],
        compiler_params=pltpu.CompilerParams(vmem_limit_bytes=VMEM_LIMIT),
        cost_estimate=small_cost(),
        name="attention",
    )(counts, parents, inverse, norm_gain, layer_input, w_query, w_key, w_value, head_grad)
    deltas, parts = out[: len(shares)], out[len(shares) : len(shares) + blocks]
    if cut:
        input_cut, gain_cut = out[-2], out[-1]
    else:
        start = lax.axis_index("tensor") * column_width
        input_cut = lax.dynamic_slice_in_dim(layer_input, start, column_width, 1)
        gain_cut = lax.dynamic_slice_in_dim(norm_gain, start, column_width, 0)
        gain_cut = gain_cut.reshape(1, column_width)
    return deltas, parts, input_cut, gain_cut


def weight_kernel(outs, sources, *refs):
    turned_hbm, delta_hbm = refs[:sources], refs[sources : 2 * sources]
    out_hbm, token_ref = refs[-10:-7], refs[-7]
    turned_ref, delta_ref, kept, turned_sem, delta_sem, store_sem = refs[-6:]
    token_ref[...] = jnp.zeros_like(token_ref)
    rows = turned_ref.shape[2]
    loads = []
    for place in range(sources):
        loads.append(
            pltpu.make_async_copy(
                turned_hbm[place], turned_ref.at[place], turned_sem.at[place]
            )
        )
        loads.append(
            pltpu.make_async_copy(delta_hbm[place], delta_ref.at[place], delta_sem.at[place])
        )
    for load in loads:
        load.start()
    for load in loads:
        load.wait()
    stores = [
        pltpu.make_async_copy(
            kept.at[block],
            out_hbm[which].at[:, pl.ds(column * HEAD_DIM, HEAD_DIM)],
            store_sem.at[block],
        )
        for block, (which, column) in enumerate(outs)
    ]

    def fill(block, carry):
        lines = pl.ds(pl.multiple_of(block * rows, rows), rows)
        total = None
        for place in range(sources):
            term = nn_dot(turned_ref[place], delta_ref[place, lines, :])
            total = term if total is None else total + term
        kept[block] = total
        for which, store in enumerate(stores):

            @pl.when(block == which)
            def _():
                store.start()

        return carry

    lax.fori_loop(0, len(outs), fill, 0)
    for store in stores:
        store.wait()


def weight_gradients(turned, deltas, share, kv_local, group, before):
    depth, rows = turned[0].shape
    sources = len(turned)
    outs = []
    for block in share:
        h, which = divmod(block, group + 2)
        outs.append((0, h * group + which) if which < group else (which - group + 1, h))
    kept = list(before) if before is not None else []
    hbm = pl.BlockSpec(memory_space=pl.ANY)
    return pl.pallas_call(
        functools.partial(weight_kernel, outs, sources),
        out_shape=(
            jax.ShapeDtypeStruct((depth, kv_local * group * HEAD_DIM), jnp.float32),
            jax.ShapeDtypeStruct((depth, kv_local * HEAD_DIM), jnp.float32),
            jax.ShapeDtypeStruct((depth, kv_local * HEAD_DIM), jnp.float32),
            jax.ShapeDtypeStruct((8, 128), jnp.float32),
        ),
        in_specs=[hbm] * (2 * sources + len(kept)),
        out_specs=(hbm,) * 3 + (pl.BlockSpec(memory_space=pltpu.VMEM),),
        input_output_aliases={2 * sources + i: i for i in range(len(kept))},
        scratch_shapes=[
            pltpu.VMEM((sources, depth, rows), jnp.bfloat16),
            pltpu.VMEM((sources, len(share) * rows, HEAD_DIM), jnp.bfloat16),
            pltpu.VMEM((len(share), depth, HEAD_DIM), jnp.float32),
            pltpu.SemaphoreType.DMA((sources,)),
            pltpu.SemaphoreType.DMA((sources,)),
            pltpu.SemaphoreType.DMA((len(share),)),
        ],
        compiler_params=pltpu.CompilerParams(vmem_limit_bytes=VMEM_LIMIT),
        cost_estimate=small_cost(),
        name="weights",
    )(*turned, *deltas, *kept)


def gate_kernel(*refs):
    del refs


def gate(arrays, tokens):
    hbm = pl.BlockSpec(memory_space=pl.ANY)
    return pl.pallas_call(
        gate_kernel,
        out_shape=tuple(jax.ShapeDtypeStruct(x.shape, x.dtype) for x in arrays),
        in_specs=[hbm] * (len(arrays) + len(tokens)),
        out_specs=(hbm,) * len(arrays),
        input_output_aliases={i: i for i in range(len(arrays))},
        compiler_params=pltpu.CompilerParams(vmem_limit_bytes=VMEM_LIMIT),
        cost_estimate=small_cost(),
        name="gate",
    )(*arrays, *tokens)


def join_kernel(inner_ref, other_ref, end_ref, *rest):
    out_ref, token_ref = rest[-2:]
    token_ref[...] = jnp.zeros_like(token_ref)
    index = lax.axis_index("tensor")
    inner = (index > 0) & (index < lax.axis_size("tensor") - 1)

    @pl.when(inner)
    def _():
        out_ref[...] = (
            inner_ref[...].astype(jnp.float32) + other_ref[...].astype(jnp.float32)
        ).astype(jnp.bfloat16)

    @pl.when(jnp.logical_not(inner))
    def _():
        out_ref[...] = end_ref[...]


def join(inner_part, other, end_part, tokens):
    vmem = pl.BlockSpec(memory_space=pltpu.VMEM)
    return pl.pallas_call(
        join_kernel,
        out_shape=(
            jax.ShapeDtypeStruct(end_part.shape, end_part.dtype),
            jax.ShapeDtypeStruct((8, 128), jnp.float32),
        ),
        in_specs=[vmem] * 3 + [pl.BlockSpec(memory_space=pl.ANY)] * len(tokens),
        out_specs=(vmem, vmem),
        compiler_params=pltpu.CompilerParams(vmem_limit_bytes=VMEM_LIMIT),
        cost_estimate=small_cost(),
        name="join",
    )(inner_part, other, end_part, *tokens)


def finish_kernel(width, for_ends, for_inner, count, input_ref, gain_ref, inverse_ref, *refs):
    part_refs, centre_refs, (out_ref, sum_ref) = refs[:count], refs[count : 2 * count], refs[-2:]
    step = pl.program_id(0)
    index = lax.axis_index("tensor")
    ends = ((index == 0) | (index == lax.axis_size("tensor") - 1)).astype(jnp.float32)

    def total_of(part_refs):
        total = None
        for place, part_ref in enumerate(part_refs):
            part = part_ref[...].astype(jnp.float32)
            if place < for_ends:
                part = part * ends
            elif place < for_ends + for_inner:
                part = part * (1.0 - ends)
            total = part if total is None else total + part
        return total

    d_normed = total_of(part_refs).T
    centre = total_of(centre_refs).T[:, :1] * (1.0 / width)
    inverse = inverse_ref[...]
    scaled = input_ref[...].astype(jnp.float32) * inverse
    out_ref[...] = (
        inverse * ((1.0 + gain_ref[...]) * d_normed - scaled * centre)
    ).astype(jnp.bfloat16)

    @pl.when(step == 0)
    def _():
        sum_ref[...] = jnp.zeros_like(sum_ref)

    sum_ref[...] += jnp.sum(d_normed * scaled, axis=0, keepdims=True)


def finish(width, for_ends, for_inner, input_columns, gain_columns, inverse, parts, token):
    rows, wide = input_columns.shape
    some = 128
    whole = pl.BlockSpec((1, wide), lambda i: (0, 0))
    return pl.pallas_call(
        functools.partial(finish_kernel, width, for_ends, for_inner, len(parts)),
        out_shape=(
            jax.ShapeDtypeStruct((rows, wide), jnp.bfloat16),
            jax.ShapeDtypeStruct((1, wide), jnp.float32),
        ),
        grid=(rows // some,),
        in_specs=[
            pl.BlockSpec((some, wide), lambda i: (i, 0)),
            whole,
            pl.BlockSpec((some, 1), lambda i: (i, 0)),
        ]
        + [pl.BlockSpec((wide, some), lambda i: (0, i))] * len(parts)
        + [pl.BlockSpec((CENTRE_ROWS, some), lambda i: (wide // CENTRE_ROWS, i))] * len(parts)
        + [pl.BlockSpec(memory_space=pl.ANY)],
        out_specs=(pl.BlockSpec((some, wide), lambda i: (i, 0)), whole),
        compiler_params=pltpu.CompilerParams(vmem_limit_bytes=VMEM_LIMIT),
        cost_estimate=small_cost(),
        name="finish",
    )(input_columns, gain_columns, inverse, *parts, *parts, token)


def total_kernel(*refs):
    total = (refs[0][...] + refs[1][...]) + (refs[2][...] + refs[3][...])
    refs[-1][...] = total.reshape(refs[-1].shape)


def total_of_four(arrays):
    whole = pl.BlockSpec(arrays[0].shape, lambda i: (0, 0))
    wide = arrays[0].shape[1]
    return pl.pallas_call(
        total_kernel,
        out_shape=jax.ShapeDtypeStruct((wide,), arrays[0].dtype),
        grid=(1,),
        in_specs=[whole] * 4,
        out_specs=pl.BlockSpec((wide,), lambda i: (0,)),
        compiler_params=pltpu.CompilerParams(vmem_limit_bytes=VMEM_LIMIT),
        cost_estimate=small_cost(),
        name="total",
    )(*arrays)


def branch_send(array, chips, shift, swap):
    pairs = [
        (c * 2 + k, ((c + shift) % chips) * 2 + (k ^ swap)) for c in range(chips) for k in range(2)
    ]
    return lax.ppermute(array, "branch", pairs)


def pick(table, index):
    chosen = table[-1]
    for place in range(len(table) - 2, -1, -1):
        chosen = jnp.where(index == place, table[place], chosen)
    return chosen


def scatter_order(total):
    index = lax.axis_index("tensor")
    if total != 4:
        return lambda place: lax.rem(index + place + 1, total)
    table = [[3, 0, 3, 0], [0, 2, 1, 3], [2, 3, 0, 1], [1, 1, 2, 2]]
    here = [pick(row, index) for row in table]
    return lambda place: pick(here, place)


def scatter_begin(parts, total):
    if total != 4:
        return [
            lax.ppermute(part, "tensor", [(t, (t + shift) % total) for t in range(total)])
            for shift, part in zip(range(1, total), parts[:-1])
        ]
    from_first = lax.ppermute(parts[0], "tensor", [(0, 1), (1, 0), (2, 3), (3, 2)])
    from_inner = lax.ppermute(parts[1], "tensor", [(1, 2), (2, 1)])
    return from_first, from_inner


def scatter_end(parts, arrived, total, tokens):
    if total != 4:
        return [parts[-1], *arrived], 0, 0, arrived[0], arrived
    _, second, third, fourth = parts
    from_first, from_inner = arrived
    joined, token = join(third, from_first, fourth, (from_inner, *tokens))
    (held,) = gate((third,), (token,))
    from_ends = lax.ppermute(held, "tensor", [(0, 2), (3, 1)])
    from_joined = lax.ppermute(joined, "tensor", [(1, 3), (2, 0), (0, 1), (3, 2)])
    return [from_first, second, fourth, from_inner, from_ends, from_joined], 2, 1, token, (from_ends, from_joined)


def local(layer_input, norm_gain, w_query, w_key, w_value, head_grad, parents, row_counts):
    branch_total = lax.axis_size("branch")
    tensor_total = lax.axis_size("tensor")
    slots = row_counts.shape[0] // branch_total
    rows, width = layer_input.shape
    column_width = width // tensor_total
    chips = branch_total // 2
    group = w_query.shape[1] // w_key.shape[1]
    kv_local = w_key.shape[1] // HEAD_DIM
    offsets = [(shift, swap) for shift in range(chips) for swap in range(2)]
    blocks = list(range(kv_local * (group + 2)))
    early = blocks[: group + 2] + [h * (group + 2) + group for h in range(1, kv_local)]
    shares = [early, [block for block in blocks if block not in early]]
    shares = [share for share in shares if share]

    def targets():
        index = lax.axis_index("branch")
        chip, core = index // 2, index % 2
        return [lax.rem(chip + s, chips) * 2 + lax.rem(core + e, 2) for s, e in offsets]

    inverse, pieces = normalize(layer_input, norm_gain, targets, branch_total, rows // slots)
    shared = [branch_send(piece, chips, s, e) for piece, (s, e) in zip(pieces[1:], offsets[1:])]
    deltas, parts, input_columns, gain_columns = attention_backward(
        layer_input,
        inverse,
        norm_gain,
        w_query,
        w_key,
        w_value,
        head_grad,
        parents,
        row_counts,
        slots,
        lambda place: scatter_order(tensor_total)(place),
        tensor_total,
        shares,
    )
    arrived = scatter_begin(parts, tensor_total)

    (first,) = gate(deltas[:1], shared)
    sent = [branch_send(first, chips, s, 0) for s in range(1, chips)]
    parts, for_ends, for_inner, met, _ = scatter_end(parts, arrived, tensor_total, ())
    *sent, first = gate((*sent, first), (met,))
    others = gate(deltas[1:], (sent[0],)) if deltas[1:] else ()
    turned = [pieces[0]] + shared
    weights, token = None, None
    for share, delta in zip(shares, (first, *others)):
        if token is not None:
            sent = [branch_send(delta, chips, s, 0) for s in range(1, chips)]
            delta, *sent = gate((delta, *sent), (token,))
        gathered = []
        for part in [delta] + sent:
            gathered += [part, branch_send(part, chips, 0, 1)]
        *weights, token = weight_gradients(turned, gathered, share, kv_local, group, weights)

    grad_input, gain_sum = finish(
        width, for_ends, for_inner, input_columns, gain_columns, inverse, parts, token
    )
    if chips == 2:
        sums = [gain_sum] + [branch_send(gain_sum, chips, s, e) for s, e in offsets[1:]]
        grad_gain = total_of_four(sums)
    else:
        grad_gain = lax.psum(gain_sum, "branch").reshape(column_width)
    return (grad_input, *weights, grad_gain)


def solution(mesh):
    placed = (
        P(("parts", "branch"), None),
        P(),
        P(None, "tensor"),
        P(None, "tensor"),
        P(None, "tensor"),
        P(("parts", "branch"), "tensor"),
        P(("parts", "branch")),
        P("parts"),
    )
    return jax.shard_map(
        local,
        mesh=mesh,
        in_specs=placed,
        out_specs=(
            P(("parts", "branch"), "tensor"),
            P(("parts", "branch"), "tensor"),
            P(("parts", "branch"), "tensor"),
            P(("parts", "branch"), "tensor"),
            P(("parts", "tensor")),
        ),
        check_vma=False,
    )
```

time: 498 us -> 88.5 us (0.18)
  waiting for transfers between devices: 357 us -> 21.5 us
  matrix products: 92.2 us -> 0 us
  Pallas kernels: 0 us -> 46.5 us
  starting transfers between devices: 0.13 us -> 19.5 us
  between operations: 15.7 us -> 0.74 us
  other arithmetic: 13.3 us -> 0 us
  local copies, waits for them, and re-layouts: 8.91 us -> 0 us
  blocking collectives: 6.22 us -> 0 us
    reduce_scatter x3 -> x0, waiting for transfers between devices: 243 us -> none  [the longest x1 116 us: local(): lax.psum_scatter(acc_query, 'branch', scatter_dimension=0, tiled=True)]
    psum x2 -> x0, waiting for transfers between devices: 113 us -> none  [one_tree(): d_normed = lax.psum(partial_rows, 'tensor')]
    dot_general x36 -> x0, matrix products: 92.2 us -> none  [the longest x6 42.9 us: transpose_dot(): lax.dot_general(left, right, (((0,), (0,)), ((), ())), preferred_element_...]
    pallas_call x0 -> x12, Pallas kernels: none -> 46.5 us  [the longest x1 24 us: attention_backward(): pl.pallas_call(functools.partial(attention_kernel, slots, group, kv_local...]
    ppermute x0 -> x16, waiting for transfers between devices: none -> 21.5 us  [the longest x1 9.93 us: scatter_begin(): lax.ppermute(parts[0], 'tensor', [(0, 1), (1, 0), (2, 3), (3, 2)])]
    ppermute x0 -> x16, starting transfers between devices: none -> 19.5 us  [the longest x12 9.61 us: branch_send(): return lax.ppermute(array, 'branch', pairs)]
    reduce_sum x5 -> x0, other arithmetic: 7.44 us -> none  [the longest x2 4.43 us: one_tree(): centred = jnp.mean(scaled * adjusted, axis=-1, keepdims=True)]
    psum x1 -> x0, blocking collectives: 6.22 us -> none  [local(): grad_gain = lax.psum(acc_gain, 'branch')]
  transfers between devices with their start and end apart: 5 -> 16, of which waited for: 5 -> 7; matrix products, arithmetic and copies ran while one was open for 9% -> 0% of each run, Pallas kernels for 0% -> 44%
where the time goes in v5:
time: 88.5 us; the launch traced here: 88.2 us
  Pallas kernels  46.5 us (53%)
  waiting for transfers between devices  21.5 us (24%)
  starting transfers between devices  19.5 us (22%)
    pallas_call x1, Pallas kernels, attention_backward(): pl.pallas_call(functools.partial(attention_kernel, slots, group, kv_local...  24 us
    pallas_call x2, Pallas kernels, weight_gradients(): pl.pallas_call(functools.partial(weight_kernel, outs, sources), out_shape...  12.5 us
    ppermute x1, waiting for transfers between devices, scatter_begin(): lax.ppermute(parts[0], 'tensor', [(0, 1), (1, 0), (2, 3), (3, 2)])  9.93 us
    ppermute x12, starting transfers between devices, branch_send(): return lax.ppermute(array, 'branch', pairs)  9.61 us
    ppermute x1, starting transfers between devices, scatter_end(): from_ends = lax.ppermute(held, 'tensor', [(0, 2), (3, 1)])  6.86 us
    ppermute x1, waiting for transfers between devices, scatter_end(): lax.ppermute(joined, 'tensor', [(1, 3), (2, 0), (0, 1), (3, 2)])  5.8 us
    ppermute x12, waiting for transfers between devices, branch_send(): return lax.ppermute(array, 'branch', pairs)  5.78 us
    pallas_call x1, Pallas kernels, normalize(): pl.pallas_call(functools.partial(norm_kernel, targets), out_shape=(jax.Sh...  3.45 us
  transfers between devices with their start and end apart: 16, of which 7 were waited for; matrix products, arithmetic and copies ran while one was open for 0% of the time, Pallas kernels for 44%

profile of v5, /device:TPU:0, one launch (start us, length us, event | category | flops | bytes accessed | tf_op | source)
XLA Modules:
  0.0 88.2 jit_solution(8644881999074224332)
XLA Ops:
  0.6 3.5 %norm.1 = (f32[256,1]{1,0:T(8,128)}, bf16[896,256]{1,0:T(8,128)(2,1)}, bf16[896,256]{1,0:T(8,128)(2,1)}, bf16[896,256]{1,0:T(8,128)(2,1)}, bf16[896,256]{1,0:T(8,128)(2,1)}) custom-call(bf16[256,3584]{1,0:T(8,128)(2,1)} %input_hbm.1, f32[3584]{0:T(1024)} %gain_ref.3), custom_call_target="tpu_custom_call" | custom-call | flops 1000000 | bytes 100000 | tf_op jit(solution)/shard_map/norm/pallas_call | solution.py:59
  4.1 0.5 collective-permute-start.4
  4.5 2.5 %collective-permute-start.5 = (bf16[896,256]{1,0:T(8,128)(2,1)}, bf16[896,256]{1,0:T(8,128)(2,1)}, u32[]{:S(2)}, u32[]{:S(2)}) collective-permute-start(bf16[896,256]{1,0:T(8,128)(2,1)} %get-tuple-element.45), channel_id=1, source_target_pairs={{0,8},{4,12},{8,0},{12,4},{1,9},{5,13},{9,1},{13,5},{2,10},{6,14},... | collective-permute-start | bytes 1376264 | tf_op jit(solution)/shard_map/ppermute | solution.py:572
  7.1 0.1 collective-permute-start.6
  7.2 24.0 %attention.1 = (bf16[1280,256]{1,0:T(8,128)(2,1)}, bf16[768,256]{1,0:T(8,128)(2,1)}, bf16[912,256]{1,0:T(8,128)(2,1)}, bf16[912,256]{1,0:T(8,128)(2,1)}, bf16[91...) custom-call(s32[8]{0:T(128)} %count_ref.1, s32[256]{0:T(256)} %parent_ref.1, ...), custom_call_target="tpu_custom_call" | custom-call | flops 1000000 | bytes 100000 | tf_op jit(solution)/shard_map/attention/pallas_call | solution.py:312
  31.1 0.0 collective-permute-done.4.refs_1_
  31.1 0.0 collective-permute-done.5.refs_2_
  31.2 0.0 collective-permute-done.6.refs_3_
  31.2 1.8 %collective-permute-start.7 = (bf16[1280,256]{1,0:T(8,128)(2,1)}, bf16[1280,256]{1,0:T(8,128)(2,1)}, u32[]{:S(2)}, u32[]{:S(2)}) collective-permute-start(bf16[1280,256]{1,0:T(8,128)(2,1)} %gate.6.refs_1_), channel_id=1, source_target_pairs={{0,8},{4,12},{8,0},{12,4},{1,9},{5,13},{9,1},{13,5},{2,10},{6,14},... | collective-permute-start | bytes 1966088 | tf_op jit(solution)/shard_map/ppermute | solution.py:572
  33.0 1.6 %collective-permute-start = (bf16[912,256]{1,0:T(8,128)(2,1)}, bf16[912,256]{1,0:T(8,128)(2,1)}, u32[]{:S(2)}, u32[]{:S(2)}) collective-permute-start(bf16[912,256]{1,0:T(8,128)(2,1)} %get-tuple-element.37), channel_id=1, source_target_pairs={{0,1},{1,0},{2,3},{3,2},{4,5},{5,4},{6,7},{7,6},{8,9},{9,8},{10,11... | collective-permute-start | bytes 1400840 | tf_op jit(solution)/shard_map/ppermute | solution.py:597
  34.5 1.4 %collective-permute-start.1 = (bf16[912,256]{1,0:T(8,128)(2,1)}, bf16[912,256]{1,0:T(8,128)(2,1)}, u32[]{:S(2)}, u32[]{:S(2)}) collective-permute-start(bf16[912,256]{1,0:T(8,128)(2,1)} %get-tuple-element.38.refs_1_.refs_7_), channel_id=1, source_target_pairs={{1,2},{2,1},{5,6},{6,5},{9,10},{10,9},{13,14},{14,13},{17,18},{18,... | collective-permute-start | bytes 1400840 | tf_op jit(solution)/shard_map/ppermute | solution.py:598
  36.0 9.9 %collective-permute-done.other_ref.refs_0_.refs_6_ = bf16[912,256]{1,0:T(8,128)(2,1)} collective-permute-done((bf16[912,256]{1,0:T(8,128)(2,1)}, bf16[912,256]{1,0:T(8,128)(2,1)}, u32[]{:S(2)}, u32[]{:S(2)}) %collective-permute-start) | collective-permute-done | bytes 466976 | tf_op jit(solution)/shard_map/ppermute | solution.py:597
  45.9 0.0 collective-permute-done.1.rest_0_.refs_3_.refs_9_
  45.9 2.1 %join.1 = (bf16[912,256]{1,0:T(8,128)(2,1)}, f32[8,128]{1,0:T(8,128)}) custom-call(bf16[912,256]{1,0:T(8,128)(2,1)} %get-tuple-element.40.inner_ref.refs_0_, bf16[912,256]{1,0:T(8,128)(2,1)} %collective-permute-done.other_ref.refs_0_.refs_6_, bf16[912,256]{1,0:T(8,128)(2,1)} %get-tuple-element.39.end_ref.refs_2_.refs_8_, ...), custom_call_target="tpu_custom_call" | custom-call | flops 1000000 | bytes 100000 | tf_op jit(solution)/shard_map/join/pallas_call | solution.py:476
  48.0 0.5 collective-permute-done.7.refs_0_
  48.5 0.0 collective-permute-start.9
  48.5 0.5 collective-permute-start.10
  49.0 1.7 %collective-permute-start.8 = (bf16[768,256]{1,0:T(8,128)(2,1)}, bf16[768,256]{1,0:T(8,128)(2,1)}, u32[]{:S(2)}, u32[]{:S(2)}) collective-permute-start(bf16[768,256]{1,0:T(8,128)(2,1)} %gate.8.refs_0_), channel_id=1, source_target_pairs={{0,8},{4,12},{8,0},{12,4},{1,9},{5,13},{9,1},{13,5},{2,10},{6,14},... | collective-permute-start | bytes 1179656 | tf_op jit(solution)/shard_map/ppermute | solution.py:572
  50.7 6.9 %collective-permute-start.2 = (bf16[912,256]{1,0:T(8,128)(2,1)}, bf16[912,256]{1,0:T(8,128)(2,1)}, u32[]{:S(2)}, u32[]{:S(2)}) collective-permute-start(bf16[912,256]{1,0:T(8,128)(2,1)} %gate.5), channel_id=1, source_target_pairs={{0,2},{3,1},{4,6},{7,5},{8,10},{11,9},{12,14},{15,13},{16,18},{19,... | collective-permute-start | bytes 1400840 | tf_op jit(solution)/shard_map/ppermute | solution.py:609
  57.6 0.0 collective-permute-start.3
  57.6 0.0 collective-permute-done.9.refs_5_
  57.6 0.0 collective-permute-done.10.refs_7_
  57.6 7.1 %weights.2 = (f32[896,1024]{1,0:T(8,128)}, f32[896,512]{1,0:T(8,128)}, f32[896,512]{1,0:T(8,128)}, f32[8,128]{1,0:T(8,128)}) custom-call(bf16[896,256]{1,0:T(8,128)(2,1)} %get-tuple-element.43.refs_0_, bf16[896,256]{1,0:T(8,128)(2,1)} %collective-permute-done.4.refs_1_, bf16[896,256]{1,0:T(8,128)(2,1)} %collective-permute-done.5.refs_2_, ...), custom_call_target="tpu_custom_call" | custom-call | flops 1000000 | bytes 100000 | tf_op jit(solution)/shard_map/weights/pallas_call | solution.py:414
  64.7 0.0 collective-permute-done.8.refs_1_
  64.7 0.1 collective-permute-start.11
  64.8 0.5 collective-permute-start.12
  65.3 1.6 %collective-permute-done.11.refs_5_ = bf16[768,256]{1,0:T(8,128)(2,1)} collective-permute-done((bf16[768,256]{1,0:T(8,128)(2,1)}, bf16[768,256]{1,0:T(8,128)(2,1)}, u32[]{:S(2)}, u32[]{:S(2)}) %collective-permute-start.11) | collective-permute-done | bytes 393248 | tf_op jit(solution)/shard_map/ppermute | solution.py:572
  66.9 0.6 collective-permute-done.12.refs_7_
  67.4 5.4 %weights.3 = (f32[896,1024]{1,0:T(8,128)}, f32[896,512]{1,0:T(8,128)}, f32[896,512]{1,0:T(8,128)}, f32[8,128]{1,0:T(8,128)}) custom-call(bf16[896,256]{1,0:T(8,128)(2,1)} %get-tuple-element.43.refs_0_, bf16[896,256]{1,0:T(8,128)(2,1)} %collective-permute-done.4.refs_1_, ...), custom_call_target="tpu_custom_call", output_to_operand_aliasing={{0}: (8, {}), {1}: (9, {}), {2}: (10, {})} | custom-call | flops 1000000 | bytes 100000 | tf_op jit(solution)/shard_map/weights/pallas_call | solution.py:414
  72.9 0.0 collective-permute-done.2.refs_4_.refs_10_
  72.9 5.8 %collective-permute-done.3.refs_5_.refs_11_ = bf16[912,256]{1,0:T(8,128)(2,1)} collective-permute-done((bf16[912,256]{1,0:T(8,128)(2,1)}, bf16[912,256]{1,0:T(8,128)(2,1)}, u32[]{:S(2)}, u32[]{:S(2)}) %collective-permute-start.3) | collective-permute-done | bytes 466976 | tf_op jit(solution)/shard_map/ppermute | solution.py:610
  78.7 3.2 %finish.1 = (bf16[256,896]{1,0:T(8,128)(2,1)}, f32[1,896]{1,0:T(1,128)}) custom-call(bf16[256,896]{1,0:T(8,128)(2,1)} %get-tuple-element.35.input_ref, f32[1,896]{1,0:T(1,128)} %get-tuple-element.36.gain_ref, f32[256,1]{1,0:T(8,128)} %get-tuple-element.34.inverse_ref, bf16[912,256]{1,0:T(8,128)(2,1)} %collective-permute-done.other_ref.refs_0_.refs_6_, ...), custom_call_target="tpu_custom_call" | custom-call | flops 1000000 | bytes 100000 | tf_op jit(solution)/shard_map/finish/pallas_call | solution.py:526
  81.9 1.2 %collective-permute-start.15 = (f32[1,896]{1,0:T(1,128)}, f32[1,896]{1,0:T(1,128)}, u32[]{:S(2)}, u32[]{:S(2)}) collective-permute-start(f32[1,896]{1,0:T(1,128)} %get-tuple-element.62.refs_0_), channel_id=1, source_target_pairs={{0,12},{4,8},{8,4},{12,0},{1,13},{5,9},{9,5},{13,1},{2,14},{6,10},... | collective-permute-start | bytes 10760 | tf_op jit(solution)/shard_map/ppermute | solution.py:572
  83.0 0.5 collective-permute-start.14
  83.6 0.2 collective-permute-start.13
  83.8 1.5 %collective-permute-done.15.refs_3_ = f32[1,896]{1,0:T(1,128)} collective-permute-done((f32[1,896]{1,0:T(1,128)}, f32[1,896]{1,0:T(1,128)}, u32[]{:S(2)}, u32[]{:S(2)}) %collective-permute-start.15) | collective-permute-done | bytes 3616 | tf_op jit(solution)/shard_map/ppermute | solution.py:572
  85.3 1.7 %collective-permute-done.14.refs_2_ = f32[1,896]{1,0:T(1,128)} collective-permute-done((f32[1,896]{1,0:T(1,128)}, f32[1,896]{1,0:T(1,128)}, u32[]{:S(2)}, u32[]{:S(2)}) %collective-permute-start.14) | collective-permute-done | bytes 3616 | tf_op jit(solution)/shard_map/ppermute | solution.py:572
  87.0 0.0 collective-permute-done.13.refs_1_
  87.0 1.3 %total.1 = f32[896]{0:T(1024)} custom-call(f32[1,896]{1,0:T(1,128)} %get-tuple-element.62.refs_0_, f32[1,896]{1,0:T(1,128)} %collective-permute-done.13.refs_1_, f32[1,896]{1,0:T(1,128)} %collective-permute-done.14.refs_2_, f32[1,896]{1,0:T(1,128)} %collective-permute-done.15.refs_3_), custom_call_target="tpu_custom_call" | custom-call | flops 1000000 | bytes 100000 | tf_op jit(solution)/shard_map/total/pallas_call | solution.py:556
  (5 shorter events, 0.0 us)
Async XLA Ops:
  4.1 27.1 %collective-permute-start.4 = (bf16[896,256]{1,0:T(8,128)(2,1)}, bf16[896,256]{1,0:T(8,128)(2,1)}, u32[]{:S(2)}, u32[]{:S(2)}) collective-permute-start(bf16[896,256]{1,0:T(8,128)(2,1)} %get-tuple-element.44), channel_id=1, source_target_pairs={{0,4},{4,0},{8,12},{12,8},{1,5},{5,1},{9,13},{13,9},{2,6},{6,2},{1... | collective-permute-start | bytes 1376264 | tf_op jit(solution)/shard_map/ppermute | solution.py:572
  4.5 26.6 %collective-permute-start.5 = (bf16[896,256]{1,0:T(8,128)(2,1)}, bf16[896,256]{1,0:T(8,128)(2,1)}, u32[]{:S(2)}, u32[]{:S(2)}) collective-permute-start(bf16[896,256]{1,0:T(8,128)(2,1)} %get-tuple-element.45), channel_id=1, source_target_pairs={{0,8},{4,12},{8,0},{12,4},{1,9},{5,13},{9,1},{13,5},{2,10},{6,14},... | collective-permute-start | bytes 1376264 | tf_op jit(solution)/shard_map/ppermute | solution.py:572
  7.1 24.1 %collective-permute-start.6 = (bf16[896,256]{1,0:T(8,128)(2,1)}, bf16[896,256]{1,0:T(8,128)(2,1)}, u32[]{:S(2)}, u32[]{:S(2)}) collective-permute-start(bf16[896,256]{1,0:T(8,128)(2,1)} %get-tuple-element.46), channel_id=1, source_target_pairs={{0,12},{4,8},{8,4},{12,0},{1,13},{5,9},{9,5},{13,1},{2,14},{6,10},... | collective-permute-start | bytes 1376264 | tf_op jit(solution)/shard_map/ppermute | solution.py:572
  31.2 17.3 %collective-permute-start.7 = (bf16[1280,256]{1,0:T(8,128)(2,1)}, bf16[1280,256]{1,0:T(8,128)(2,1)}, u32[]{:S(2)}, u32[]{:S(2)}) collective-permute-start(bf16[1280,256]{1,0:T(8,128)(2,1)} %gate.6.refs_1_), channel_id=1, source_target_pairs={{0,8},{4,12},{8,0},{12,4},{1,9},{5,13},{9,1},{13,5},{2,10},{6,14},... | collective-permute-start | bytes 1966088 | tf_op jit(solution)/shard_map/ppermute | solution.py:572
  33.0 13.0 %collective-permute-start = (bf16[912,256]{1,0:T(8,128)(2,1)}, bf16[912,256]{1,0:T(8,128)(2,1)}, u32[]{:S(2)}, u32[]{:S(2)}) collective-permute-start(bf16[912,256]{1,0:T(8,128)(2,1)} %get-tuple-element.37), channel_id=1, source_target_pairs={{0,1},{1,0},{2,3},{3,2},{4,5},{5,4},{6,7},{7,6},{8,9},{9,8},{10,11... | collective-permute-start | bytes 1400840 | tf_op jit(solution)/shard_map/ppermute | solution.py:597
  34.5 11.4 %collective-permute-start.1 = (bf16[912,256]{1,0:T(8,128)(2,1)}, bf16[912,256]{1,0:T(8,128)(2,1)}, u32[]{:S(2)}, u32[]{:S(2)}) collective-permute-start(bf16[912,256]{1,0:T(8,128)(2,1)} %get-tuple-element.38.refs_1_.refs_7_), channel_id=1, source_target_pairs={{1,2},{2,1},{5,6},{6,5},{9,10},{10,9},{13,14},{14,13},{17,18},{18,... | collective-permute-start | bytes 1400840 | tf_op jit(solution)/shard_map/ppermute | solution.py:598
  48.5 9.1 %collective-permute-start.9 = (bf16[1280,256]{1,0:T(8,128)(2,1)}, bf16[1280,256]{1,0:T(8,128)(2,1)}, u32[]{:S(2)}, u32[]{:S(2)}) collective-permute-start(bf16[1280,256]{1,0:T(8,128)(2,1)} %get-tuple-element.50.refs_4_), channel_id=1, source_target_pairs={{0,4},{4,0},{8,12},{12,8},{1,5},{5,1},{9,13},{13,9},{2,6},{6,2},{1... | collective-permute-start | bytes 1966088 | tf_op jit(solution)/shard_map/ppermute | solution.py:572
  48.5 9.1 %collective-permute-start.10 = (bf16[1280,256]{1,0:T(8,128)(2,1)}, bf16[1280,256]{1,0:T(8,128)(2,1)}, u32[]{:S(2)}, u32[]{:S(2)}) collective-permute-start(bf16[1280,256]{1,0:T(8,128)(2,1)} %get-tuple-element.49.refs_1_.refs_6_), channel_id=1, source_target_pairs={{0,4},{4,0},{8,12},{12,8},{1,5},{5,1},{9,13},{13,9},{2,6},{6,2},{1... | collective-permute-start | bytes 1966088 | tf_op jit(solution)/shard_map/ppermute | solution.py:572
  49.0 15.7 %collective-permute-start.8 = (bf16[768,256]{1,0:T(8,128)(2,1)}, bf16[768,256]{1,0:T(8,128)(2,1)}, u32[]{:S(2)}, u32[]{:S(2)}) collective-permute-start(bf16[768,256]{1,0:T(8,128)(2,1)} %gate.8.refs_0_), channel_id=1, source_target_pairs={{0,8},{4,12},{8,0},{12,4},{1,9},{5,13},{9,1},{13,5},{2,10},{6,14},... | collective-permute-start | bytes 1179656 | tf_op jit(solution)/shard_map/ppermute | solution.py:572
  50.7 22.1 %collective-permute-start.2 = (bf16[912,256]{1,0:T(8,128)(2,1)}, bf16[912,256]{1,0:T(8,128)(2,1)}, u32[]{:S(2)}, u32[]{:S(2)}) collective-permute-start(bf16[912,256]{1,0:T(8,128)(2,1)} %gate.5), channel_id=1, source_target_pairs={{0,2},{3,1},{4,6},{7,5},{8,10},{11,9},{12,14},{15,13},{16,18},{19,... | collective-permute-start | bytes 1400840 | tf_op jit(solution)/shard_map/ppermute | solution.py:609
  57.6 21.1 %collective-permute-start.3 = (bf16[912,256]{1,0:T(8,128)(2,1)}, bf16[912,256]{1,0:T(8,128)(2,1)}, u32[]{:S(2)}, u32[]{:S(2)}) collective-permute-start(bf16[912,256]{1,0:T(8,128)(2,1)} %get-tuple-element.42), channel_id=1, source_target_pairs={{1,3},{2,0},{0,1},{3,2},{5,7},{6,4},{4,5},{7,6},{9,11},{10,8},{8,9... | collective-permute-start | bytes 1400840 | tf_op jit(solution)/shard_map/ppermute | solution.py:610
  64.7 2.1 %collective-permute-start.11 = (bf16[768,256]{1,0:T(8,128)(2,1)}, bf16[768,256]{1,0:T(8,128)(2,1)}, u32[]{:S(2)}, u32[]{:S(2)}) collective-permute-start(bf16[768,256]{1,0:T(8,128)(2,1)} %get-tuple-element.52.refs_4_), channel_id=1, source_target_pairs={{0,4},{4,0},{8,12},{12,8},{1,5},{5,1},{9,13},{13,9},{2,6},{6,2},{1... | collective-permute-start | bytes 1179656 | tf_op jit(solution)/shard_map/ppermute | solution.py:572
  64.8 2.6 %collective-permute-start.12 = (bf16[768,256]{1,0:T(8,128)(2,1)}, bf16[768,256]{1,0:T(8,128)(2,1)}, u32[]{:S(2)}, u32[]{:S(2)}) collective-permute-start(bf16[768,256]{1,0:T(8,128)(2,1)} %get-tuple-element.53.refs_6_), channel_id=1, source_target_pairs={{0,4},{4,0},{8,12},{12,8},{1,5},{5,1},{9,13},{13,9},{2,6},{6,2},{1... | collective-permute-start | bytes 1179656 | tf_op jit(solution)/shard_map/ppermute | solution.py:572
  81.9 3.4 %collective-permute-start.15 = (f32[1,896]{1,0:T(1,128)}, f32[1,896]{1,0:T(1,128)}, u32[]{:S(2)}, u32[]{:S(2)}) collective-permute-start(f32[1,896]{1,0:T(1,128)} %get-tuple-element.62.refs_0_), channel_id=1, source_target_pairs={{0,12},{4,8},{8,4},{12,0},{1,13},{5,9},{9,5},{13,1},{2,14},{6,10},... | collective-permute-start | bytes 10760 | tf_op jit(solution)/shard_map/ppermute | solution.py:572
  83.0 3.9 %collective-permute-start.14 = (f32[1,896]{1,0:T(1,128)}, f32[1,896]{1,0:T(1,128)}, u32[]{:S(2)}, u32[]{:S(2)}) collective-permute-start(f32[1,896]{1,0:T(1,128)} %get-tuple-element.62.refs_0_), channel_id=1, source_target_pairs={{0,8},{4,12},{8,0},{12,4},{1,9},{5,13},{9,1},{13,5},{2,10},{6,14},... | collective-permute-start | bytes 10760 | tf_op jit(solution)/shard_map/ppermute | solution.py:572
  83.6 3.4 %collective-permute-start.13 = (f32[1,896]{1,0:T(1,128)}, f32[1,896]{1,0:T(1,128)}, u32[]{:S(2)}, u32[]{:S(2)}) collective-permute-start(f32[1,896]{1,0:T(1,128)} %get-tuple-element.62.refs_0_), channel_id=1, source_target_pairs={{0,4},{4,0},{8,12},{12,8},{1,5},{5,1},{9,13},{13,9},{2,6},{6,2},{1... | collective-permute-start | bytes 10760 | tf_op jit(solution)/shard_map/ppermute | solution.py:572

commit v6 on v5

--- a/solution.py
+++ b/solution.py
@@ -92,6 +92,7 @@
     kv_local,
     order,
     blocks,
+    ready,
     columns,
     shares,
     count_ref,
@@ -106,7 +107,8 @@
     *rest,
 ):
     delta_hbm, rest = rest[: len(shares)], rest[len(shares) :]
-    part_hbm, rest = rest[:blocks], rest[blocks:]
+    part_hbm, rest = rest[:ready], rest[ready:]
+    turned_hbm, centre_out, rest = rest[:3], rest[3], rest[4:]
     column_hbm, column_gain_ref, rest = rest[0], rest[1], rest[2:]
     (
         input_ref,
@@ -247,16 +249,21 @@
                     store_sem.at[1 + len(lasts)],
                 )
             )
+    for which, turned_ref in enumerate((query_turned, key_turned, value_turned)):
+        lasts.append(
+            pltpu.make_async_copy(turned_ref, turned_hbm[which], store_sem.at[1 + len(lasts)])
+        )
     for store in lasts:
         store.start()
 
     centre = jnp.broadcast_to(centre_ref[...], (rows, 128)).T[:CENTRE_ROWS].astype(jnp.bfloat16)
+    centre_out[...] = centre
     span = width // blocks
     cuts = 2
     cut_lines = span // cuts
     parts = [
         pltpu.make_async_copy(kept.at[place], part_hbm[place], part_sem.at[place])
-        for place in range(blocks)
+        for place in range(ready)
     ]
 
     def project_back(step, carry):
@@ -276,7 +283,7 @@
 
         return carry
 
-    lax.fori_loop(0, blocks * cuts, project_back, 0)
+    lax.fori_loop(0, ready * cuts, project_back, 0)
     for store in stores + lasts + parts:
         store.wait()
 
@@ -294,6 +301,7 @@
     slots,
     order,
     blocks,
+    ready,
     shares,
 ):
     rows, width = layer_input.shape
@@ -304,20 +312,30 @@
     column_width = width // blocks
     cut = column_width % 128 == 0
     wide = column_width if cut else 128
-    steps = width // 512 if width % 512 == 0 else 1
+    steps = 2 if width % 512 == 0 else 1
     part_shape = (column_width + CENTRE_ROWS, rows)
     hbm = pl.BlockSpec(memory_space=pl.ANY)
     vmem = pl.BlockSpec(memory_space=pltpu.VMEM)
     half = lambda *shape: jax.ShapeDtypeStruct(shape, jnp.bfloat16)
     out = pl.pallas_call(
         functools.partial(
-            attention_kernel, slots, group, kv_local, order, blocks, wide if cut else 0, shares
+            attention_kernel,
+            slots,
+            group,
+            kv_local,
+            order,
+            blocks,
+            ready,
+            wide if cut else 0,
+            shares,
         ),
         out_shape=tuple(half(len(share) * rows, HEAD_DIM) for share in shares)
-        + (half(*part_shape),) * blocks
+        + (half(*part_shape),) * ready
+        + tuple(half(w.shape[1], rows) for w in (w_query, w_key, w_value))
+        + (half(CENTRE_ROWS, rows),)
         + (half(rows, wide), jax.ShapeDtypeStruct((1, wide), jnp.float32)),
         in_specs=[pl.BlockSpec(memory_space=pltpu.SMEM), vmem, vmem, vmem] + [hbm] * 5,
-        out_specs=(hbm,) * (1 + len(shares) + blocks) + (vmem,),
+        out_specs=(hbm,) * (len(shares) + ready + 3) + (vmem, hbm, vmem),
         scratch_shapes=[
             pltpu.VMEM((rows, width), jnp.bfloat16),
             pltpu.VMEM((1, width), jnp.float32),
@@ -332,17 +350,18 @@
             pltpu.VMEM((w_value.shape[1], rows), jnp.bfloat16),
             pltpu.VMEM((slots, rows // slots, rows // slots), jnp.float32),
             pltpu.VMEM((rows, 1), jnp.float32),
-            pltpu.VMEM((blocks, *part_shape), jnp.bfloat16),
+            pltpu.VMEM((ready, *part_shape), jnp.bfloat16),
             pltpu.SemaphoreType.DMA((2,)),
             pltpu.SemaphoreType.DMA((steps, 3)),
-            pltpu.SemaphoreType.DMA((1 + kv_local * (group + 2),)),
-            pltpu.SemaphoreType.DMA((blocks,)),
+            pltpu.SemaphoreType.DMA((4 + kv_local * (group + 2),)),
+            pltpu.SemaphoreType.DMA((ready,)),
         ],
         compiler_params=pltpu.CompilerParams(vmem_limit_bytes=VMEM_LIMIT),
         cost_estimate=small_cost(),
         name="attention",
     )(counts, parents, inverse, norm_gain, layer_input, w_query, w_key, w_value, head_grad)
-    deltas, parts = out[: len(shares)], out[len(shares) : len(shares) + blocks]
+    deltas, out = out[: len(shares)], out[len(shares) :]
+    parts, turned, centre = out[:ready], out[ready : ready + 3], out[ready + 3]
     if cut:
         input_cut, gain_cut = out[-2], out[-1]
     else:
@@ -350,7 +369,47 @@
         input_cut = lax.dynamic_slice_in_dim(layer_input, start, column_width, 1)
         gain_cut = lax.dynamic_slice_in_dim(norm_gain, start, column_width, 0)
         gain_cut = gain_cut.reshape(1, column_width)
-    return deltas, parts, input_cut, gain_cut
+    return deltas, parts, turned, centre, input_cut, gain_cut
+
+
+def back_kernel(centre_ref, *refs):
+    turned_refs, weight_refs, out_refs = refs[:3], refs[3:6], refs[6:]
+    piece, cut = pl.program_id(0), pl.program_id(1)
+    lines = weight_refs[0].shape[0]
+    total = None
+    for weight_ref, turned_ref in zip(weight_refs, turned_refs):
+        term = nn_dot(weight_ref[...], turned_ref[...])
+        total = term if total is None else total + term
+    total = total.astype(jnp.bfloat16)
+    start = pl.multiple_of(cut * lines, 16)
+    depth = out_refs[0].shape[0] - CENTRE_ROWS
+    for place, out_ref in enumerate(out_refs):
+
+        @pl.when(piece == place)
+        def _():
+            out_ref[pl.ds(start, lines), :] = total
+            out_ref[depth:, :] = centre_ref[...]
+
+
+def back_project(order, first, pieces, turned, centre, weights, blocks):
+    rows = centre.shape[1]
+    depth = weights[0].shape[0] // blocks
+    cuts = 2
+    whole = lambda i, j: (0, 0)
+    return pl.pallas_call(
+        back_kernel,
+        out_shape=(jax.ShapeDtypeStruct((depth + CENTRE_ROWS, rows), jnp.bfloat16),) * pieces,
+        grid=(pieces, cuts),
+        in_specs=[pl.BlockSpec(x.shape, whole) for x in (centre, *turned)]
+        + [
+            pl.BlockSpec((depth // cuts, w.shape[1]), lambda i, j: (order(first + i) * cuts + j, 0))
+            for w in weights
+        ],
+        out_specs=(pl.BlockSpec((depth + CENTRE_ROWS, rows), whole),) * pieces,
+        compiler_params=pltpu.CompilerParams(vmem_limit_bytes=VMEM_LIMIT),
+        cost_estimate=small_cost(),
+        name="back",
+    )(centre, *turned, *weights)
 
 
 def weight_kernel(outs, sources, *refs):
@@ -487,62 +546,89 @@
     )(inner_part, other, end_part, *tokens)
 
 
-def finish_kernel(width, for_ends, for_inner, count, input_ref, gain_ref, inverse_ref, *refs):
-    part_refs, centre_refs, (out_ref, sum_ref) = refs[:count], refs[count : 2 * count], refs[-2:]
-    step = pl.program_id(0)
+def add_parts(for_ends, for_inner, part_refs):
     index = lax.axis_index("tensor")
     ends = ((index == 0) | (index == lax.axis_size("tensor") - 1)).astype(jnp.float32)
-
-    def total_of(part_refs):
-        total = None
-        for place, part_ref in enumerate(part_refs):
-            part = part_ref[...].astype(jnp.float32)
-            if place < for_ends:
-                part = part * ends
-            elif place < for_ends + for_inner:
-                part = part * (1.0 - ends)
-            total = part if total is None else total + part
-        return total
-
-    d_normed = total_of(part_refs).T
-    centre = total_of(centre_refs).T[:, :1] * (1.0 / width)
-    inverse = inverse_ref[...]
-    scaled = input_ref[...].astype(jnp.float32) * inverse
-    out_ref[...] = (
-        inverse * ((1.0 + gain_ref[...]) * d_normed - scaled * centre)
-    ).astype(jnp.bfloat16)
-
-    @pl.when(step == 0)
+    total = None
+    for place, part_ref in enumerate(part_refs):
+        part = part_ref[...].astype(jnp.float32)
+        if place < for_ends:
+            part = part * ends
+        elif place < for_ends + for_inner:
+            part = part * (1.0 - ends)
+        total = part if total is None else total + part
+    return total
+
+
+def gain_kernel(add, count, input_ref, inverse_ref, *refs):
+    part_refs, (sum_ref, total_ref) = refs[:count], refs[-2:]
+
+    @pl.when(pl.program_id(0) == 0)
     def _():
         sum_ref[...] = jnp.zeros_like(sum_ref)
 
+    d_normed = add(part_refs).T
+    total_ref[...] = d_normed
+    scaled = input_ref[...].astype(jnp.float32) * inverse_ref[...]
     sum_ref[...] += jnp.sum(d_normed * scaled, axis=0, keepdims=True)
 
 
-def finish(width, for_ends, for_inner, input_columns, gain_columns, inverse, parts, token):
+def gain_sums(add, input_columns, inverse, parts, token):
     rows, wide = input_columns.shape
     some = 128
-    whole = pl.BlockSpec((1, wide), lambda i: (0, 0))
     return pl.pallas_call(
-        functools.partial(finish_kernel, width, for_ends, for_inner, len(parts)),
+        functools.partial(gain_kernel, add, len(parts)),
         out_shape=(
-            jax.ShapeDtypeStruct((rows, wide), jnp.bfloat16),
             jax.ShapeDtypeStruct((1, wide), jnp.float32),
+            jax.ShapeDtypeStruct((rows, wide), jnp.float32),
         ),
         grid=(rows // some,),
         in_specs=[
             pl.BlockSpec((some, wide), lambda i: (i, 0)),
-            whole,
             pl.BlockSpec((some, 1), lambda i: (i, 0)),
         ]
         + [pl.BlockSpec((wide, some), lambda i: (0, i))] * len(parts)
-        + [pl.BlockSpec((CENTRE_ROWS, some), lambda i: (wide // CENTRE_ROWS, i))] * len(parts)
         + [pl.BlockSpec(memory_space=pl.ANY)],
-        out_specs=(pl.BlockSpec((some, wide), lambda i: (i, 0)), whole),
+        out_specs=(
+            pl.BlockSpec((1, wide), lambda i: (0, 0)),
+            pl.BlockSpec((some, wide), lambda i: (i, 0)),
+        ),
+        compiler_params=pltpu.CompilerParams(vmem_limit_bytes=VMEM_LIMIT),
+        cost_estimate=small_cost(),
+        name="gains",
+    )(input_columns, inverse, *parts, token)
+
+
+def finish_kernel(width, add, total_ref, input_ref, gain_ref, inverse_ref, *refs):
+    centre_refs, out_ref = refs[:-1], refs[-1]
+    centre = add(centre_refs).T[:, :1] * (1.0 / width)
+    inverse = inverse_ref[...]
+    scaled = input_ref[...].astype(jnp.float32) * inverse
+    out_ref[...] = (
+        inverse * ((1.0 + gain_ref[...]) * total_ref[...] - scaled * centre)
+    ).astype(jnp.bfloat16)
+
+
+def finish(width, add, total, input_columns, gain_columns, inverse, parts):
+    rows, wide = input_columns.shape
+    some = 128
+    row_block = pl.BlockSpec((some, wide), lambda i: (i, 0))
+    return pl.pallas_call(
+        functools.partial(finish_kernel, width, add),
+        out_shape=jax.ShapeDtypeStruct((rows, wide), jnp.bfloat16),
+        grid=(rows // some,),
+        in_specs=[
+            row_block,
+            row_block,
+            pl.BlockSpec((1, wide), lambda i: (0, 0)),
+            pl.BlockSpec((some, 1), lambda i: (i, 0)),
+        ]
+        + [pl.BlockSpec((CENTRE_ROWS, some), lambda i: (wide // CENTRE_ROWS, i))] * len(parts),
+        out_specs=row_block,
         compiler_params=pltpu.CompilerParams(vmem_limit_bytes=VMEM_LIMIT),
         cost_estimate=small_cost(),
         name="finish",
-    )(input_columns, gain_columns, inverse, *parts, *parts, token)
+    )(total, input_columns, gain_columns, inverse, *parts)
 
 
 def total_kernel(*refs):
@@ -550,19 +636,19 @@
     refs[-1][...] = total.reshape(refs[-1].shape)
 
 
-def total_of_four(arrays):
+def total_of_four(arrays, token):
     whole = pl.BlockSpec(arrays[0].shape, lambda i: (0, 0))
     wide = arrays[0].shape[1]
     return pl.pallas_call(
         total_kernel,
         out_shape=jax.ShapeDtypeStruct((wide,), arrays[0].dtype),
         grid=(1,),
-        in_specs=[whole] * 4,
+        in_specs=[whole] * 4 + [pl.BlockSpec(memory_space=pl.ANY)],
         out_specs=pl.BlockSpec((wide,), lambda i: (0,)),
         compiler_params=pltpu.CompilerParams(vmem_limit_bytes=VMEM_LIMIT),
         cost_estimate=small_cost(),
         name="total",
-    )(*arrays)
+    )(*arrays, token)
 
 
 def branch_send(array, chips, shift, swap):
@@ -599,16 +685,22 @@
     return from_first, from_inner
 
 
-def scatter_end(parts, arrived, total, tokens):
+def scatter_middle(parts, arrived, total):
     if total != 4:
-        return [parts[-1], *arrived], 0, 0, arrived[0], arrived
-    _, second, third, fourth = parts
-    from_first, from_inner = arrived
-    joined, token = join(third, from_first, fourth, (from_inner, *tokens))
-    (held,) = gate((third,), (token,))
+        return arrived, None, arrived[0]
+    (held,) = gate((parts[2],), (arrived[0],))
     from_ends = lax.ppermute(held, "tensor", [(0, 2), (3, 1)])
+    joined, token = join(held, arrived[0], parts[3], (arrived[1],))
+    return (*arrived, from_ends), joined, token
+
+
+def scatter_end(parts, arrived, joined, total, token):
+    if total != 4:
+        return [parts[-1], *arrived], 0, 0
+    from_first, from_inner, from_ends = arrived
+    (joined,) = gate((joined,), (from_ends, token))
     from_joined = lax.ppermute(joined, "tensor", [(1, 3), (2, 0), (0, 1), (3, 2)])
-    return [from_first, second, fourth, from_inner, from_ends, from_joined], 2, 1, token, (from_ends, from_joined)
+    return [from_first, parts[1], parts[3], from_inner, from_ends, from_joined], 2, 1
 
 
 def local(layer_input, norm_gain, w_query, w_key, w_value, head_grad, parents, row_counts):
@@ -633,7 +725,9 @@
 
     inverse, pieces = normalize(layer_input, norm_gain, targets, branch_total, rows // slots)
     shared = [branch_send(piece, chips, s, e) for piece, (s, e) in zip(pieces[1:], offsets[1:])]
-    deltas, parts, input_columns, gain_columns = attention_backward(
+    order = lambda place: scatter_order(tensor_total)(place)
+    ready = min(2, tensor_total)
+    deltas, parts, delta_turned, centre, input_columns, gain_columns = attention_backward(
         layer_input,
         inverse,
         norm_gain,
@@ -644,15 +738,21 @@
         parents,
         row_counts,
         slots,
-        lambda place: scatter_order(tensor_total)(place),
+        order,
         tensor_total,
+        ready,
         shares,
     )
+    if ready < tensor_total:
+        weights = (w_query, w_key, w_value)
+        parts += back_project(
+            order, ready, tensor_total - ready, delta_turned, centre, weights, tensor_total
+        )
     arrived = scatter_begin(parts, tensor_total)
 
     (first,) = gate(deltas[:1], shared)
     sent = [branch_send(first, chips, s, 0) for s in range(1, chips)]
-    parts, for_ends, for_inner, met, _ = scatter_end(parts, arrived, tensor_total, ())
+    arrived, joined, met = scatter_middle(parts, arrived, tensor_total)
     *sent, first = gate((*sent, first), (met,))
     others = gate(deltas[1:], (sent[0],)) if deltas[1:] else ()
     turned = [pieces[0]] + shared
@@ -664,14 +764,17 @@
         gathered = []
         for part in [delta] + sent:
             gathered += [part, branch_send(part, chips, 0, 1)]
+        first_share = weights is None
         *weights, token = weight_gradients(turned, gathered, share, kv_local, group, weights)
-
-    grad_input, gain_sum = finish(
-        width, for_ends, for_inner, input_columns, gain_columns, inverse, parts, token
-    )
+        if first_share:
+            parts, for_ends, for_inner = scatter_end(parts, arrived, joined, tensor_total, token)
+
+    add = functools.partial(add_parts, for_ends, for_inner)
+    gain_sum, total = gain_sums(add, input_columns, inverse, parts, token)
+    grad_input = finish(width, add, total, input_columns, gain_columns, inverse, parts)
     if chips == 2:
         sums = [gain_sum] + [branch_send(gain_sum, chips, s, e) for s, e in offsets[1:]]
-        grad_gain = total_of_four(sums)
+        grad_gain = total_of_four(sums, grad_input)
     else:
         grad_gain = lax.psum(gain_sum, "branch").reshape(column_width)
     return (grad_input, *weights, grad_gain)

time: 88.5 us -> 86.3 us (0.975)
  waiting for transfers between devices: 21.5 us -> 15.1 us
  Pallas kernels: 46.5 us -> 48.8 us
  starting transfers between devices: 19.5 us -> 21.3 us
    pallas_call x1 -> x3, Pallas kernels: 3.17 us -> 11.9 us  [the longest x1 6.45 us: back_project(): pl.pallas_call(back_kernel, out_shape=(jax.ShapeDtypeStruct((depth + CENT...]
    ppermute x1, waiting for transfers between devices: 9.93 us -> 3.43 us  [scatter_begin(): lax.ppermute(parts[0], 'tensor', [(0, 1), (1, 0), (2, 3), (3, 2)])]
    pallas_call x1, Pallas kernels: 24 us -> 17.5 us  [attention_backward(): pl.pallas_call(functools.partial(attention_kernel, slots, group, kv_local...]
    ppermute x1, waiting for transfers between devices: 5.8 us -> 3.49 us  [scatter_end(): lax.ppermute(joined, 'tensor', [(1, 3), (2, 0), (0, 1), (3, 2)])]
    ppermute x1, starting transfers between devices: 0.01 us -> 2.21 us  [scatter_end(): lax.ppermute(joined, 'tensor', [(1, 3), (2, 0), (0, 1), (3, 2)])]
    ppermute x1, waiting for transfers between devices: 0.01 us -> 2.09 us  [scatter_middle(): from_ends = lax.ppermute(held, 'tensor', [(0, 2), (3, 1)])]
    ppermute x12, starting transfers between devices: 9.61 us -> 8.06 us  [branch_send(): return lax.ppermute(array, 'branch', pairs)]
    ppermute x1, starting transfers between devices: 6.86 us -> 8.01 us  [scatter_middle(): from_ends = lax.ppermute(held, 'tensor', [(0, 2), (3, 1)])]
  transfers between devices with their start and end apart: 16 -> 16, of which waited for: 7 -> 7; matrix products, arithmetic and copies ran while one was open for 0% -> 0% of each run, Pallas kernels for 44% -> 48%
where the time goes in v6:
time: 86.3 us; the launch traced here: 85.9 us
  Pallas kernels  48.8 us (57%)
  starting transfers between devices  21.3 us (25%)
  waiting for transfers between devices  15.1 us (17%)
    pallas_call x1, Pallas kernels, attention_backward(): pl.pallas_call(functools.partial(attention_kernel, slots, group, kv_local...  17.5 us
    pallas_call x2, Pallas kernels, weight_gradients(): pl.pallas_call(functools.partial(weight_kernel, outs, sources), out_shape...  12.5 us
    ppermute x12, starting transfers between devices, branch_send(): return lax.ppermute(array, 'branch', pairs)  8.06 us
    ppermute x1, starting transfers between devices, scatter_middle(): from_ends = lax.ppermute(held, 'tensor', [(0, 2), (3, 1)])  8.01 us
    pallas_call x1, Pallas kernels, back_project(): pl.pallas_call(back_kernel, out_shape=(jax.ShapeDtypeStruct((depth + CENT...  6.45 us
    ppermute x12, waiting for transfers between devices, branch_send(): return lax.ppermute(array, 'branch', pairs)  6.03 us
    ppermute x1, waiting for transfers between devices, scatter_end(): lax.ppermute(joined, 'tensor', [(1, 3), (2, 0), (0, 1), (3, 2)])  3.49 us
    pallas_call x1, Pallas kernels, normalize(): pl.pallas_call(functools.partial(norm_kernel, targets), out_shape=(jax.Sh...  3.44 us
  transfers between devices with their start and end apart: 16, of which 7 were waited for; matrix products, arithmetic and copies ran while one was open for 0% of the time, Pallas kernels for 48%

profile of v6, /device:TPU:0, one launch (start us, length us, event | category | flops | bytes accessed | tf_op | source)
XLA Modules:
  0.0 85.9 jit_solution(16755010880807043290)
XLA Ops:
  0.6 3.4 %norm.1 = (f32[256,1]{1,0:T(8,128)}, bf16[896,256]{1,0:T(8,128)(2,1)}, bf16[896,256]{1,0:T(8,128)(2,1)}, bf16[896,256]{1,0:T(8,128)(2,1)}, bf16[896,256]{1,0:T(8,128)(2,1)}) custom-call(bf16[256,3584]{1,0:T(8,128)(2,1)} %input_hbm.1, f32[3584]{0:T(1024)} %gain_ref.3), custom_call_target="tpu_custom_call" | custom-call | flops 1000000 | bytes 100000 | tf_op jit(solution)/shard_map/norm/pallas_call | solution.py:59
  4.1 0.5 collective-permute-start.3
  4.5 2.5 %collective-permute-start.4 = (bf16[896,256]{1,0:T(8,128)(2,1)}, bf16[896,256]{1,0:T(8,128)(2,1)}, u32[]{:S(2)}, u32[]{:S(2)}) collective-permute-start(bf16[896,256]{1,0:T(8,128)(2,1)} %get-tuple-element.51), channel_id=1, source_target_pairs={{0,8},{4,12},{8,0},{12,4},{1,9},{5,13},{9,1},{13,5},{2,10},{6,14},... | collective-permute-start | bytes 1376264 | tf_op jit(solution)/shard_map/ppermute | solution.py:658
  7.1 0.1 collective-permute-start.5
  7.2 17.5 %attention.1 = (bf16[1280,256]{1,0:T(8,128)(2,1)}, bf16[768,256]{1,0:T(8,128)(2,1)}, bf16[912,256]{1,0:T(8,128)(2,1)}, bf16[912,256]{1,0:T(8,128)(2,1)}, bf16[10...) custom-call(s32[8]{0:T(128)} %count_ref.1, ...), custom_call_target="tpu_custom_call" | custom-call | flops 1000000 | bytes 100000 | tf_op jit(solution)/shard_map/attention/pallas_call | solution.py:320
  24.7 0.0 collective-permute-done.3.refs_1_
  24.7 0.0 collective-permute-done.4.refs_2_
  24.7 3.4 %collective-permute-done.5.refs_3_ = bf16[896,256]{1,0:T(8,128)(2,1)} collective-permute-done((bf16[896,256]{1,0:T(8,128)(2,1)}, bf16[896,256]{1,0:T(8,128)(2,1)}, u32[]{:S(2)}, u32[]{:S(2)}) %collective-permute-start.5) | collective-permute-done | bytes 458784 | tf_op jit(solution)/shard_map/ppermute | solution.py:658
  28.1 1.5 %collective-permute-start.6 = (bf16[1280,256]{1,0:T(8,128)(2,1)}, bf16[1280,256]{1,0:T(8,128)(2,1)}, u32[]{:S(2)}, u32[]{:S(2)}) collective-permute-start(bf16[1280,256]{1,0:T(8,128)(2,1)} %gate.7.refs_1_), channel_id=1, source_target_pairs={{0,8},{4,12},{8,0},{12,4},{1,9},{5,13},{9,1},{13,5},{2,10},{6,14},... | collective-permute-start | bytes 1966088 | tf_op jit(solution)/shard_map/ppermute | solution.py:658
  29.7 1.6 %collective-permute-start = (bf16[912,256]{1,0:T(8,128)(2,1)}, bf16[912,256]{1,0:T(8,128)(2,1)}, u32[]{:S(2)}, u32[]{:S(2)}) collective-permute-start(bf16[912,256]{1,0:T(8,128)(2,1)} %get-tuple-element.40), channel_id=1, source_target_pairs={{0,1},{1,0},{2,3},{3,2},{4,5},{5,4},{6,7},{7,6},{8,9},{9,8},{10,11... | collective-permute-start | bytes 1400840 | tf_op jit(solution)/shard_map/ppermute | solution.py:683
  31.2 1.4 %collective-permute-start.1 = (bf16[912,256]{1,0:T(8,128)(2,1)}, bf16[912,256]{1,0:T(8,128)(2,1)}, u32[]{:S(2)}, u32[]{:S(2)}) collective-permute-start(bf16[912,256]{1,0:T(8,128)(2,1)} %get-tuple-element.41.refs_1_), channel_id=1, source_target_pairs={{1,2},{2,1},{5,6},{6,5},{9,10},{10,9},{13,14},{14,13},{17,18},{18,... | collective-permute-start | bytes 1400840 | tf_op jit(solution)/shard_map/ppermute | solution.py:684
  32.7 6.4 %back.1 = (bf16[912,256]{1,0:T(8,128)(2,1)}, bf16[912,256]{1,0:T(8,128)(2,1)}) custom-call(bf16[16,256]{1,0:T(8,128)(2,1)} %get-tuple-element.42.centre_ref, bf16[1024,256]{1,0:T(8,128)(2,1)} %get-tuple-element.43.refs_0_, bf16[512,256]{1,0:T(8,128)(2,1)} %get-tuple-element.44.refs_1_, bf16[512,256]{1,0:T(8,128)(2,1)} %get-tuple-element.45.refs_2_, ...), custom_call_target="tpu_custom_call" | custom-call | flops 1000000 | bytes 100000 | tf_op jit(solution)/shard_map/back/pallas_call | solution.py:399
  39.1 3.4 %collective-permute-done.refs_1_.other_ref.refs_0_ = bf16[912,256]{1,0:T(8,128)(2,1)} collective-permute-done((bf16[912,256]{1,0:T(8,128)(2,1)}, bf16[912,256]{1,0:T(8,128)(2,1)}, u32[]{:S(2)}, u32[]{:S(2)}) %collective-permute-start) | collective-permute-done | bytes 466976 | tf_op jit(solution)/shard_map/ppermute | solution.py:683
  42.6 0.0 collective-permute-done.1.rest_0_.refs_3_
  42.6 2.1 %join.1 = (bf16[912,256]{1,0:T(8,128)(2,1)}, f32[8,128]{1,0:T(8,128)}) custom-call(bf16[912,256]{1,0:T(8,128)(2,1)} %gate.6.inner_ref, bf16[912,256]{1,0:T(8,128)(2,1)} %collective-permute-done.refs_1_.other_ref.refs_0_, bf16[912,256]{1,0:T(8,128)(2,1)} %get-tuple-element.46.end_ref.refs_2_, bf16[912,256]{1,0:T(8,128)(2,1)} %collective-permute-done.1.rest_0_.refs_3_), custom_call_target="tpu_custom_call" | custom-call | flops 1000000 | bytes 100000 | tf_op jit(solution)/shard_map/join/pallas_call | solution.py:535
  44.7 0.5 collective-permute-done.6.refs_0_
  45.2 0.0 collective-permute-start.7
  45.2 0.5 collective-permute-start.8
  45.7 8.0 %collective-permute-start.2 = (bf16[912,256]{1,0:T(8,128)(2,1)}, bf16[912,256]{1,0:T(8,128)(2,1)}, u32[]{:S(2)}, u32[]{:S(2)}) collective-permute-start(bf16[912,256]{1,0:T(8,128)(2,1)} %gate.6.inner_ref), channel_id=1, source_target_pairs={{0,2},{3,1},{4,6},{7,5},{8,10},{11,9},{12,14},{15,13},{16,18},{19,... | collective-permute-start | bytes 1400840 | tf_op jit(solution)/shard_map/ppermute | solution.py:692
  53.7 0.5 collective-permute-start.10
  54.3 0.0 collective-permute-done.7.refs_5_
  54.3 0.0 collective-permute-done.8.refs_7_
  54.3 7.1 %weights.2 = (f32[896,1024]{1,0:T(8,128)}, f32[896,512]{1,0:T(8,128)}, f32[896,512]{1,0:T(8,128)}, f32[8,128]{1,0:T(8,128)}) custom-call(bf16[896,256]{1,0:T(8,128)(2,1)} %get-tuple-element.49.refs_0_, bf16[896,256]{1,0:T(8,128)(2,1)} %collective-permute-done.3.refs_1_, bf16[896,256]{1,0:T(8,128)(2,1)} %collective-permute-done.4.refs_2_, ...), custom_call_target="tpu_custom_call" | custom-call | flops 1000000 | bytes 100000 | tf_op jit(solution)/shard_map/weights/pallas_call | solution.py:473
  61.3 2.1 %collective-permute-done.2.refs_1_.refs_4_ = bf16[912,256]{1,0:T(8,128)(2,1)} collective-permute-done((bf16[912,256]{1,0:T(8,128)(2,1)}, bf16[912,256]{1,0:T(8,128)(2,1)}, u32[]{:S(2)}, u32[]{:S(2)}) %collective-permute-start.2) | collective-permute-done | bytes 466976 | tf_op jit(solution)/shard_map/ppermute | solution.py:692
  63.4 2.2 %collective-permute-start.9 = (bf16[912,256]{1,0:T(8,128)(2,1)}, bf16[912,256]{1,0:T(8,128)(2,1)}, u32[]{:S(2)}, u32[]{:S(2)}) collective-permute-start(bf16[912,256]{1,0:T(8,128)(2,1)} %gate.9), channel_id=1, source_target_pairs={{1,3},{2,0},{0,1},{3,2},{5,7},{6,4},{4,5},{7,6},{9,11},{10,8},{8,9... | collective-permute-start | bytes 1400840 | tf_op jit(solution)/shard_map/ppermute | solution.py:702
  65.6 0.0 collective-permute-done.10.refs_1_
  65.6 0.0 collective-permute-start.11
  65.7 0.5 collective-permute-start.12
  66.2 1.6 %collective-permute-done.11.refs_5_ = bf16[768,256]{1,0:T(8,128)(2,1)} collective-permute-done((bf16[768,256]{1,0:T(8,128)(2,1)}, bf16[768,256]{1,0:T(8,128)(2,1)}, u32[]{:S(2)}, u32[]{:S(2)}) %collective-permute-start.11) | collective-permute-done | bytes 393248 | tf_op jit(solution)/shard_map/ppermute | solution.py:658
  67.7 0.6 collective-permute-done.12.refs_7_
  68.3 5.4 %weights.3 = (f32[896,1024]{1,0:T(8,128)}, f32[896,512]{1,0:T(8,128)}, f32[896,512]{1,0:T(8,128)}, f32[8,128]{1,0:T(8,128)}) custom-call(bf16[896,256]{1,0:T(8,128)(2,1)} %get-tuple-element.49.refs_0_, bf16[896,256]{1,0:T(8,128)(2,1)} %collective-permute-done.3.refs_1_, ...), custom_call_target="tpu_custom_call", output_to_operand_aliasing={{0}: (8, {}), {1}: (9, {}), {2}: (10, {})} | custom-call | flops 1000000 | bytes 100000 | tf_op jit(solution)/shard_map/weights/pallas_call | solution.py:473
  73.7 3.5 %collective-permute-done.9.refs_5_ = bf16[912,256]{1,0:T(8,128)(2,1)} collective-permute-done((bf16[912,256]{1,0:T(8,128)(2,1)}, bf16[912,256]{1,0:T(8,128)(2,1)}, u32[]{:S(2)}, u32[]{:S(2)}) %collective-permute-start.9) | collective-permute-done | bytes 466976 | tf_op jit(solution)/shard_map/ppermute | solution.py:702
  77.2 3.1 %gains.1 = (f32[1,896]{1,0:T(1,128)}, f32[256,896]{1,0:T(8,128)}) custom-call(bf16[256,896]{1,0:T(8,128)(2,1)} %get-tuple-element.39.input_ref, f32[256,1]{1,0:T(8,128)} %get-tuple-element.38.inverse_ref, bf16[912,256]{1,0:T(8,128)(2,1)} %collective-permute-done.refs_1_.other_ref.refs_0_, bf16[912,256]{1,0:T(8,128)(2,1)} %get-tuple-element.41.refs_1_, ...), custom_call_target="tpu_custom_call" | custom-call | flops 1000000 | bytes 100000 | tf_op jit(solution)/shard_map/gains/pallas_call | solution.py:579
  80.3 0.0 collective-permute-start.15
  80.3 0.6 collective-permute-start.14
  80.9 1.2 %collective-permute-start.13 = (f32[1,896]{1,0:T(1,128)}, f32[1,896]{1,0:T(1,128)}, u32[]{:S(2)}, u32[]{:S(2)}) collective-permute-start(f32[1,896]{1,0:T(1,128)} %get-tuple-element.70.refs_0_), channel_id=1, source_target_pairs={{0,4},{4,0},{8,12},{12,8},{1,5},{5,1},{9,13},{13,9},{2,6},{6,2},{1... | collective-permute-start | bytes 10760 | tf_op jit(solution)/shard_map/ppermute | solution.py:658
  82.2 2.4 %finish.1.refs_4_ = bf16[256,896]{1,0:T(8,128)(2,1)} custom-call(f32[256,896]{1,0:T(8,128)} %get-tuple-element.65.total_ref, bf16[256,896]{1,0:T(8,128)(2,1)} %get-tuple-element.39.input_ref, f32[1,896]{1,0:T(1,128)} %get-tuple-element.66.gain_ref, f32[256,1]{1,0:T(8,128)} %get-tuple-element.38.inverse_ref, ...), custom_call_target="tpu_custom_call" | custom-call | flops 1000000 | bytes 100000 | tf_op jit(solution)/shard_map/finish/pallas_call | solution.py:616
  84.6 0.0 collective-permute-done.15.refs_3_
  84.6 0.0 collective-permute-done.14.refs_2_
  84.6 0.0 collective-permute-done.13.refs_1_
  84.6 1.3 %total.1 = f32[896]{0:T(1024)} custom-call(f32[1,896]{1,0:T(1,128)} %get-tuple-element.70.refs_0_, f32[1,896]{1,0:T(1,128)} %collective-permute-done.13.refs_1_, f32[1,896]{1,0:T(1,128)} %collective-permute-done.14.refs_2_, f32[1,896]{1,0:T(1,128)} %collective-permute-done.15.refs_3_, bf16[256,896]{1,0:T(8,128)(2,1)} %finish.1.refs_4_), custom_call_target="tpu_custom_call" | custom-call | flops 1000000 | bytes 100000 | tf_op jit(solution)/shard_map/total/pallas_call | solution.py:642
  (6 shorter events, 0.0 us)
Async XLA Ops:
  4.1 20.6 %collective-permute-start.3 = (bf16[896,256]{1,0:T(8,128)(2,1)}, bf16[896,256]{1,0:T(8,128)(2,1)}, u32[]{:S(2)}, u32[]{:S(2)}) collective-permute-start(bf16[896,256]{1,0:T(8,128)(2,1)} %get-tuple-element.50), channel_id=1, source_target_pairs={{0,4},{4,0},{8,12},{12,8},{1,5},{5,1},{9,13},{13,9},{2,6},{6,2},{1... | collective-permute-start | bytes 1376264 | tf_op jit(solution)/shard_map/ppermute | solution.py:658
  4.5 20.2 %collective-permute-start.4 = (bf16[896,256]{1,0:T(8,128)(2,1)}, bf16[896,256]{1,0:T(8,128)(2,1)}, u32[]{:S(2)}, u32[]{:S(2)}) collective-permute-start(bf16[896,256]{1,0:T(8,128)(2,1)} %get-tuple-element.51), channel_id=1, source_target_pairs={{0,8},{4,12},{8,0},{12,4},{1,9},{5,13},{9,1},{13,5},{2,10},{6,14},... | collective-permute-start | bytes 1376264 | tf_op jit(solution)/shard_map/ppermute | solution.py:658
  7.1 21.1 %collective-permute-start.5 = (bf16[896,256]{1,0:T(8,128)(2,1)}, bf16[896,256]{1,0:T(8,128)(2,1)}, u32[]{:S(2)}, u32[]{:S(2)}) collective-permute-start(bf16[896,256]{1,0:T(8,128)(2,1)} %get-tuple-element.52), channel_id=1, source_target_pairs={{0,12},{4,8},{8,4},{12,0},{1,13},{5,9},{9,5},{13,1},{2,14},{6,10},... | collective-permute-start | bytes 1376264 | tf_op jit(solution)/shard_map/ppermute | solution.py:658
  28.1 17.1 %collective-permute-start.6 = (bf16[1280,256]{1,0:T(8,128)(2,1)}, bf16[1280,256]{1,0:T(8,128)(2,1)}, u32[]{:S(2)}, u32[]{:S(2)}) collective-permute-start(bf16[1280,256]{1,0:T(8,128)(2,1)} %gate.7.refs_1_), channel_id=1, source_target_pairs={{0,8},{4,12},{8,0},{12,4},{1,9},{5,13},{9,1},{13,5},{2,10},{6,14},... | collective-permute-start | bytes 1966088 | tf_op jit(solution)/shard_map/ppermute | solution.py:658
  29.7 12.9 %collective-permute-start = (bf16[912,256]{1,0:T(8,128)(2,1)}, bf16[912,256]{1,0:T(8,128)(2,1)}, u32[]{:S(2)}, u32[]{:S(2)}) collective-permute-start(bf16[912,256]{1,0:T(8,128)(2,1)} %get-tuple-element.40), channel_id=1, source_target_pairs={{0,1},{1,0},{2,3},{3,2},{4,5},{5,4},{6,7},{7,6},{8,9},{9,8},{10,11... | collective-permute-start | bytes 1400840 | tf_op jit(solution)/shard_map/ppermute | solution.py:683
  31.2 11.3 %collective-permute-start.1 = (bf16[912,256]{1,0:T(8,128)(2,1)}, bf16[912,256]{1,0:T(8,128)(2,1)}, u32[]{:S(2)}, u32[]{:S(2)}) collective-permute-start(bf16[912,256]{1,0:T(8,128)(2,1)} %get-tuple-element.41.refs_1_), channel_id=1, source_target_pairs={{1,2},{2,1},{5,6},{6,5},{9,10},{10,9},{13,14},{14,13},{17,18},{18,... | collective-permute-start | bytes 1400840 | tf_op jit(solution)/shard_map/ppermute | solution.py:684
  45.2 9.1 %collective-permute-start.7 = (bf16[1280,256]{1,0:T(8,128)(2,1)}, bf16[1280,256]{1,0:T(8,128)(2,1)}, u32[]{:S(2)}, u32[]{:S(2)}) collective-permute-start(bf16[1280,256]{1,0:T(8,128)(2,1)} %get-tuple-element.55.refs_4_), channel_id=1, source_target_pairs={{0,4},{4,0},{8,12},{12,8},{1,5},{5,1},{9,13},{13,9},{2,6},{6,2},{1... | collective-permute-start | bytes 1966088 | tf_op jit(solution)/shard_map/ppermute | solution.py:658
  45.2 9.1 %collective-permute-start.8 = (bf16[1280,256]{1,0:T(8,128)(2,1)}, bf16[1280,256]{1,0:T(8,128)(2,1)}, u32[]{:S(2)}, u32[]{:S(2)}) collective-permute-start(bf16[1280,256]{1,0:T(8,128)(2,1)} %get-tuple-element.56.refs_6_.refs_1_), channel_id=1, source_target_pairs={{0,4},{4,0},{8,12},{12,8},{1,5},{5,1},{9,13},{13,9},{2,6},{6,2},{1... | collective-permute-start | bytes 1966088 | tf_op jit(solution)/shard_map/ppermute | solution.py:658
  45.7 17.7 %collective-permute-start.2 = (bf16[912,256]{1,0:T(8,128)(2,1)}, bf16[912,256]{1,0:T(8,128)(2,1)}, u32[]{:S(2)}, u32[]{:S(2)}) collective-permute-start(bf16[912,256]{1,0:T(8,128)(2,1)} %gate.6.inner_ref), channel_id=1, source_target_pairs={{0,2},{3,1},{4,6},{7,5},{8,10},{11,9},{12,14},{15,13},{16,18},{19,... | collective-permute-start | bytes 1400840 | tf_op jit(solution)/shard_map/ppermute | solution.py:692
  53.7 11.9 %collective-permute-start.10 = (bf16[768,256]{1,0:T(8,128)(2,1)}, bf16[768,256]{1,0:T(8,128)(2,1)}, u32[]{:S(2)}, u32[]{:S(2)}) collective-permute-start(bf16[768,256]{1,0:T(8,128)(2,1)} %gate.10.refs_0_), channel_id=1, source_target_pairs={{0,8},{4,12},{8,0},{12,4},{1,9},{5,13},{9,1},{13,5},{2,10},{6,14},... | collective-permute-start | bytes 1179656 | tf_op jit(solution)/shard_map/ppermute | solution.py:658
  63.4 13.8 %collective-permute-start.9 = (bf16[912,256]{1,0:T(8,128)(2,1)}, bf16[912,256]{1,0:T(8,128)(2,1)}, u32[]{:S(2)}, u32[]{:S(2)}) collective-permute-start(bf16[912,256]{1,0:T(8,128)(2,1)} %gate.9), channel_id=1, source_target_pairs={{1,3},{2,0},{0,1},{3,2},{5,7},{6,4},{4,5},{7,6},{9,11},{10,8},{8,9... | collective-permute-start | bytes 1400840 | tf_op jit(solution)/shard_map/ppermute | solution.py:702
  65.6 2.1 %collective-permute-start.11 = (bf16[768,256]{1,0:T(8,128)(2,1)}, bf16[768,256]{1,0:T(8,128)(2,1)}, u32[]{:S(2)}, u32[]{:S(2)}) collective-permute-start(bf16[768,256]{1,0:T(8,128)(2,1)} %get-tuple-element.59.refs_4_), channel_id=1, source_target_pairs={{0,4},{4,0},{8,12},{12,8},{1,5},{5,1},{9,13},{13,9},{2,6},{6,2},{1... | collective-permute-start | bytes 1179656 | tf_op jit(solution)/shard_map/ppermute | solution.py:658
  65.7 2.6 %collective-permute-start.12 = (bf16[768,256]{1,0:T(8,128)(2,1)}, bf16[768,256]{1,0:T(8,128)(2,1)}, u32[]{:S(2)}, u32[]{:S(2)}) collective-permute-start(bf16[768,256]{1,0:T(8,128)(2,1)} %get-tuple-element.60.refs_6_), channel_id=1, source_target_pairs={{0,4},{4,0},{8,12},{12,8},{1,5},{5,1},{9,13},{13,9},{2,6},{6,2},{1... | collective-permute-start | bytes 1179656 | tf_op jit(solution)/shard_map/ppermute | solution.py:658
  80.3 4.3 %collective-permute-start.15 = (f32[1,896]{1,0:T(1,128)}, f32[1,896]{1,0:T(1,128)}, u32[]{:S(2)}, u32[]{:S(2)}) collective-permute-start(f32[1,896]{1,0:T(1,128)} %get-tuple-element.70.refs_0_), channel_id=1, source_target_pairs={{0,12},{4,8},{8,4},{12,0},{1,13},{5,9},{9,5},{13,1},{2,14},{6,10},... | collective-permute-start | bytes 10760 | tf_op jit(solution)/shard_map/ppermute | solution.py:658
  80.3 4.3 %collective-permute-start.14 = (f32[1,896]{1,0:T(1,128)}, f32[1,896]{1,0:T(1,128)}, u32[]{:S(2)}, u32[]{:S(2)}) collective-permute-start(f32[1,896]{1,0:T(1,128)} %get-tuple-element.70.refs_0_), channel_id=1, source_target_pairs={{0,8},{4,12},{8,0},{12,4},{1,9},{5,13},{9,1},{13,5},{2,10},{6,14},... | collective-permute-start | bytes 10760 | tf_op jit(solution)/shard_map/ppermute | solution.py:658
  80.9 3.7 %collective-permute-start.13 = (f32[1,896]{1,0:T(1,128)}, f32[1,896]{1,0:T(1,128)}, u32[]{:S(2)}, u32[]{:S(2)}) collective-permute-start(f32[1,896]{1,0:T(1,128)} %get-tuple-element.70.refs_0_), channel_id=1, source_target_pairs={{0,4},{4,0},{8,12},{12,8},{1,5},{5,1},{9,13},{13,9},{2,6},{6,2},{1... | collective-permute-start | bytes 10760 | tf_op jit(solution)/shard_map/ppermute | solution.py:658

commit v7 on v6

--- a/solution.py
+++ b/solution.py
@@ -412,21 +412,21 @@
     )(centre, *turned, *weights)
 
 
-def weight_kernel(outs, sources, *refs):
-    turned_hbm, delta_hbm = refs[:sources], refs[sources : 2 * sources]
+def weight_kernel(outs, owners, sources, *refs):
+    turned_hbm, delta_hbm = refs[:sources], refs[sources]
     out_hbm, token_ref = refs[-10:-7], refs[-7]
+    token_ref[...] = jnp.zeros_like(token_ref)
     turned_ref, delta_ref, kept, turned_sem, delta_sem, store_sem = refs[-6:]
-    token_ref[...] = jnp.zeros_like(token_ref)
     rows = turned_ref.shape[2]
     loads = []
-    for place in range(sources):
+    for place, owner in enumerate(owners()):
         loads.append(
             pltpu.make_async_copy(
                 turned_hbm[place], turned_ref.at[place], turned_sem.at[place]
             )
         )
         loads.append(
-            pltpu.make_async_copy(delta_hbm[place], delta_ref.at[place], delta_sem.at[place])
+            pltpu.make_async_copy(delta_hbm.at[owner], delta_ref.at[place], delta_sem.at[place])
         )
     for load in loads:
         load.start()
@@ -461,38 +461,41 @@
         store.wait()
 
 
-def weight_gradients(turned, deltas, share, kv_local, group, before):
+def weight_gradients(turned, gathered, owners, kv_local, group, tokens):
     depth, rows = turned[0].shape
     sources = len(turned)
+    stack = gathered.shape[1]
     outs = []
-    for block in share:
+    for block in range(kv_local * (group + 2)):
         h, which = divmod(block, group + 2)
         outs.append((0, h * group + which) if which < group else (which - group + 1, h))
-    kept = list(before) if before is not None else []
     hbm = pl.BlockSpec(memory_space=pl.ANY)
     return pl.pallas_call(
-        functools.partial(weight_kernel, outs, sources),
+        functools.partial(weight_kernel, outs, owners, sources),
         out_shape=(
             jax.ShapeDtypeStruct((depth, kv_local * group * HEAD_DIM), jnp.float32),
             jax.ShapeDtypeStruct((depth, kv_local * HEAD_DIM), jnp.float32),
             jax.ShapeDtypeStruct((depth, kv_local * HEAD_DIM), jnp.float32),
             jax.ShapeDtypeStruct((8, 128), jnp.float32),
         ),
-        in_specs=[hbm] * (2 * sources + len(kept)),
+        in_specs=[hbm] * (sources + 1 + len(tokens)),
         out_specs=(hbm,) * 3 + (pl.BlockSpec(memory_space=pltpu.VMEM),),
-        input_output_aliases={2 * sources + i: i for i in range(len(kept))},
         scratch_shapes=[
             pltpu.VMEM((sources, depth, rows), jnp.bfloat16),
-            pltpu.VMEM((sources, len(share) * rows, HEAD_DIM), jnp.bfloat16),
-            pltpu.VMEM((len(share), depth, HEAD_DIM), jnp.float32),
+            pltpu.VMEM((sources, stack, HEAD_DIM), jnp.bfloat16),
+            pltpu.VMEM((len(outs), depth, HEAD_DIM), jnp.float32),
             pltpu.SemaphoreType.DMA((sources,)),
             pltpu.SemaphoreType.DMA((sources,)),
-            pltpu.SemaphoreType.DMA((len(share),)),
+            pltpu.SemaphoreType.DMA((len(outs),)),
         ],
         compiler_params=pltpu.CompilerParams(vmem_limit_bytes=VMEM_LIMIT),
-        cost_estimate=small_cost(),
+        cost_estimate=pl.CostEstimate(
+            flops=2 * sources * rows * depth * stack,
+            bytes_accessed=4 * depth * stack + 2 * sources * rows * (depth + stack),
+            transcendentals=0,
+        ),
         name="weights",
-    )(*turned, *deltas, *kept)
+    )(*turned, gathered, *tokens)
 
 
 def gate_kernel(*refs):
@@ -513,71 +516,31 @@
     )(*arrays, *tokens)
 
 
-def join_kernel(inner_ref, other_ref, end_ref, *rest):
-    out_ref, token_ref = rest[-2:]
-    token_ref[...] = jnp.zeros_like(token_ref)
-    index = lax.axis_index("tensor")
-    inner = (index > 0) & (index < lax.axis_size("tensor") - 1)
-
-    @pl.when(inner)
-    def _():
-        out_ref[...] = (
-            inner_ref[...].astype(jnp.float32) + other_ref[...].astype(jnp.float32)
-        ).astype(jnp.bfloat16)
-
-    @pl.when(jnp.logical_not(inner))
-    def _():
-        out_ref[...] = end_ref[...]
-
-
-def join(inner_part, other, end_part, tokens):
-    vmem = pl.BlockSpec(memory_space=pltpu.VMEM)
-    return pl.pallas_call(
-        join_kernel,
-        out_shape=(
-            jax.ShapeDtypeStruct(end_part.shape, end_part.dtype),
-            jax.ShapeDtypeStruct((8, 128), jnp.float32),
-        ),
-        in_specs=[vmem] * 3 + [pl.BlockSpec(memory_space=pl.ANY)] * len(tokens),
-        out_specs=(vmem, vmem),
-        compiler_params=pltpu.CompilerParams(vmem_limit_bytes=VMEM_LIMIT),
-        cost_estimate=small_cost(),
-        name="join",
-    )(inner_part, other, end_part, *tokens)
-
-
-def add_parts(for_ends, for_inner, part_refs):
-    index = lax.axis_index("tensor")
-    ends = ((index == 0) | (index == lax.axis_size("tensor") - 1)).astype(jnp.float32)
-    total = None
-    for place, part_ref in enumerate(part_refs):
-        part = part_ref[...].astype(jnp.float32)
-        if place < for_ends:
-            part = part * ends
-        elif place < for_ends + for_inner:
-            part = part * (1.0 - ends)
-        total = part if total is None else total + part
+def add_parts(part_refs):
+    total = part_refs[0][...].astype(jnp.float32)
+    for part_ref in part_refs[1:]:
+        total += part_ref[...].astype(jnp.float32)
     return total
 
 
-def gain_kernel(add, count, input_ref, inverse_ref, *refs):
+def gain_kernel(count, input_ref, inverse_ref, *refs):
     part_refs, (sum_ref, total_ref) = refs[:count], refs[-2:]
 
     @pl.when(pl.program_id(0) == 0)
     def _():
         sum_ref[...] = jnp.zeros_like(sum_ref)
 
-    d_normed = add(part_refs).T
+    d_normed = add_parts(part_refs).T
     total_ref[...] = d_normed
     scaled = input_ref[...].astype(jnp.float32) * inverse_ref[...]
     sum_ref[...] += jnp.sum(d_normed * scaled, axis=0, keepdims=True)
 
 
-def gain_sums(add, input_columns, inverse, parts, token):
+def gain_sums(input_columns, inverse, parts, token):
     rows, wide = input_columns.shape
     some = 128
     return pl.pallas_call(
-        functools.partial(gain_kernel, add, len(parts)),
+        functools.partial(gain_kernel, len(parts)),
         out_shape=(
             jax.ShapeDtypeStruct((1, wide), jnp.float32),
             jax.ShapeDtypeStruct((rows, wide), jnp.float32),
@@ -599,9 +562,9 @@
     )(input_columns, inverse, *parts, token)
 
 
-def finish_kernel(width, add, total_ref, input_ref, gain_ref, inverse_ref, *refs):
+def finish_kernel(width, total_ref, input_ref, gain_ref, inverse_ref, *refs):
     centre_refs, out_ref = refs[:-1], refs[-1]
-    centre = add(centre_refs).T[:, :1] * (1.0 / width)
+    centre = add_parts(centre_refs).T[:, :1] * (1.0 / width)
     inverse = inverse_ref[...]
     scaled = input_ref[...].astype(jnp.float32) * inverse
     out_ref[...] = (
@@ -609,12 +572,12 @@
     ).astype(jnp.bfloat16)
 
 
-def finish(width, add, total, input_columns, gain_columns, inverse, parts):
+def finish(width, total, input_columns, gain_columns, inverse, parts):
     rows, wide = input_columns.shape
     some = 128
     row_block = pl.BlockSpec((some, wide), lambda i: (i, 0))
     return pl.pallas_call(
-        functools.partial(finish_kernel, width, add),
+        functools.partial(finish_kernel, width),
         out_shape=jax.ShapeDtypeStruct((rows, wide), jnp.bfloat16),
         grid=(rows // some,),
         in_specs=[
@@ -658,51 +621,6 @@
     return lax.ppermute(array, "branch", pairs)
 
 
-def pick(table, index):
-    chosen = table[-1]
-    for place in range(len(table) - 2, -1, -1):
-        chosen = jnp.where(index == place, table[place], chosen)
-    return chosen
-
-
-def scatter_order(total):
-    index = lax.axis_index("tensor")
-    if total != 4:
-        return lambda place: lax.rem(index + place + 1, total)
-    table = [[3, 0, 3, 0], [0, 2, 1, 3], [2, 3, 0, 1], [1, 1, 2, 2]]
-    here = [pick(row, index) for row in table]
-    return lambda place: pick(here, place)
-
-
-def scatter_begin(parts, total):
-    if total != 4:
-        return [
-            lax.ppermute(part, "tensor", [(t, (t + shift) % total) for t in range(total)])
-            for shift, part in zip(range(1, total), parts[:-1])
-        ]
-    from_first = lax.ppermute(parts[0], "tensor", [(0, 1), (1, 0), (2, 3), (3, 2)])
-    from_inner = lax.ppermute(parts[1], "tensor", [(1, 2), (2, 1)])
-    return from_first, from_inner
-
-
-def scatter_middle(parts, arrived, total):
-    if total != 4:
-        return arrived, None, arrived[0]
-    (held,) = gate((parts[2],), (arrived[0],))
-    from_ends = lax.ppermute(held, "tensor", [(0, 2), (3, 1)])
-    joined, token = join(held, arrived[0], parts[3], (arrived[1],))
-    return (*arrived, from_ends), joined, token
-
-
-def scatter_end(parts, arrived, joined, total, token):
-    if total != 4:
-        return [parts[-1], *arrived], 0, 0
-    from_first, from_inner, from_ends = arrived
-    (joined,) = gate((joined,), (from_ends, token))
-    from_joined = lax.ppermute(joined, "tensor", [(1, 3), (2, 0), (0, 1), (3, 2)])
-    return [from_first, parts[1], parts[3], from_inner, from_ends, from_joined], 2, 1
-
-
 def local(layer_input, norm_gain, w_query, w_key, w_value, head_grad, parents, row_counts):
     branch_total = lax.axis_size("branch")
     tensor_total = lax.axis_size("tensor")
@@ -713,19 +631,34 @@
     group = w_query.shape[1] // w_key.shape[1]
     kv_local = w_key.shape[1] // HEAD_DIM
     offsets = [(shift, swap) for shift in range(chips) for swap in range(2)]
-    blocks = list(range(kv_local * (group + 2)))
-    early = blocks[: group + 2] + [h * (group + 2) + group for h in range(1, kv_local)]
-    shares = [early, [block for block in blocks if block not in early]]
-    shares = [share for share in shares if share]
+    shares = [list(range(kv_local * (group + 2)))]
 
     def targets():
         index = lax.axis_index("branch")
         chip, core = index // 2, index % 2
         return [lax.rem(chip + s, chips) * 2 + lax.rem(core + e, 2) for s, e in offsets]
 
+    def owners():
+        index = lax.axis_index("branch")
+        chip, core = index // 2, index % 2
+        return [lax.rem(chip + chips - s, chips) * 2 + lax.rem(core + e, 2) for s, e in offsets]
+
     inverse, pieces = normalize(layer_input, norm_gain, targets, branch_total, rows // slots)
-    shared = [branch_send(piece, chips, s, e) for piece, (s, e) in zip(pieces[1:], offsets[1:])]
-    order = lambda place: scatter_order(tensor_total)(place)
+    near = branch_send(pieces[1], chips, 0, 1)
+    direct = [branch_send(pieces[2 * s], chips, s, 0) for s in range(1, chips)]
+    held = gate(pieces[3::2], direct) if chips > 1 else ()
+    across = [branch_send(piece, chips, s + 1, 1) for s, piece in enumerate(held)]
+    turned = [pieces[0], near]
+    for pair in zip(direct, across):
+        turned += pair
+    shifts = list(range(1, tensor_total)) + [0]
+    if tensor_total > 2:
+        shifts = [2, 1] + shifts[2:]
+
+    def order(place):
+        shift = sum(jnp.where(place == i, s, 0) for i, s in enumerate(shifts))
+        return lax.rem(lax.axis_index("tensor") + shift, tensor_total)
+
     ready = min(2, tensor_total)
     deltas, parts, delta_turned, centre, input_columns, gain_columns = attention_backward(
         layer_input,
@@ -748,30 +681,18 @@
         parts += back_project(
             order, ready, tensor_total - ready, delta_turned, centre, weights, tensor_total
         )
-    arrived = scatter_begin(parts, tensor_total)
-
-    (first,) = gate(deltas[:1], shared)
-    sent = [branch_send(first, chips, s, 0) for s in range(1, chips)]
-    arrived, joined, met = scatter_middle(parts, arrived, tensor_total)
-    *sent, first = gate((*sent, first), (met,))
-    others = gate(deltas[1:], (sent[0],)) if deltas[1:] else ()
-    turned = [pieces[0]] + shared
-    weights, token = None, None
-    for share, delta in zip(shares, (first, *others)):
-        if token is not None:
-            sent = [branch_send(delta, chips, s, 0) for s in range(1, chips)]
-            delta, *sent = gate((delta, *sent), (token,))
-        gathered = []
-        for part in [delta] + sent:
-            gathered += [part, branch_send(part, chips, 0, 1)]
-        first_share = weights is None
-        *weights, token = weight_gradients(turned, gathered, share, kv_local, group, weights)
-        if first_share:
-            parts, for_ends, for_inner = scatter_end(parts, arrived, joined, tensor_total, token)
-
-    add = functools.partial(add_parts, for_ends, for_inner)
-    gain_sum, total = gain_sums(add, input_columns, inverse, parts, token)
-    grad_input = finish(width, add, total, input_columns, gain_columns, inverse, parts)
+    (delta,) = gate(deltas[:1], (near, *direct))
+    gathered = lax.all_gather(delta, "branch")
+    arrived = [
+        lax.ppermute(part, "tensor", [(t, (t + shift) % tensor_total) for t in range(tensor_total)])
+        for part, shift in zip(parts, shifts[:-1])
+    ]
+    parts = [parts[-1]] + arrived
+    *weights, token = weight_gradients(
+        turned, gathered, owners, kv_local, group, arrived[:ready]
+    )
+    gain_sum, total = gain_sums(input_columns, inverse, parts, token)
+    grad_input = finish(width, total, input_columns, gain_columns, inverse, parts)
     if chips == 2:
         sums = [gain_sum] + [branch_send(gain_sum, chips, s, e) for s, e in offsets[1:]]
         grad_gain = total_of_four(sums, grad_input)

time: 86.3 us -> 99.4 us (1.15)
  the two profiles are of different devices: /device:TPU:0 before, /device:TPU:17 now
where the time goes in v7:
time: 99.4 us; the launch traced here: 99.1 us
  Pallas kernels  43.5 us (44%)
  waiting for transfers between devices  34.1 us (34%)
  between operations  14.1 us (14%)
  starting transfers between devices  7.36 us (7%)
    ppermute x3, waiting for transfers between devices, local(): lax.ppermute(part, 'tensor', [(t, (t + shift) % tensor_total) for t in ra...  34 us
    pallas_call x1, Pallas kernels, attention_backward(): pl.pallas_call(functools.partial(attention_kernel, slots, group, kv_local...  17.5 us
    pallas_call x1, Pallas kernels, weight_gradients(): pl.pallas_call(functools.partial(weight_kernel, outs, owners, sources), o...  9.54 us
    pallas_call x1, Pallas kernels, back_project(): pl.pallas_call(back_kernel, out_shape=(jax.ShapeDtypeStruct((depth + CENT...  6.59 us
    ppermute x6, starting transfers between devices, branch_send(): return lax.ppermute(array, 'branch', pairs)  5.04 us
    pallas_call x1, Pallas kernels, normalize(): pl.pallas_call(functools.partial(norm_kernel, targets), out_shape=(jax.Sh...  3.47 us
    pallas_call x1, Pallas kernels, gain_sums(): pl.pallas_call(functools.partial(gain_kernel, len(parts)), out_shape=(jax...  2.76 us
    pallas_call x1, Pallas kernels, finish(): pl.pallas_call(functools.partial(finish_kernel, width), out_shape=jax.Sha...  2.34 us
  transfers between devices with their start and end apart: 10, of which 2 were waited for; matrix products, arithmetic and copies ran while one was open for 0% of the time, Pallas kernels for 36%

profile of v7, /device:TPU:17, one launch (start us, length us, event | category | flops | bytes accessed | tf_op | source)
XLA Modules:
  0.0 99.1 jit_solution(16938580766691308062)
XLA Ops:
  7.2 0.0 all-gather.3.cloned.1.call-start
  7.2 3.5 %norm.1 = (f32[256,1]{1,0:T(8,128)}, bf16[896,256]{1,0:T(8,128)(2,1)}, bf16[896,256]{1,0:T(8,128)(2,1)}, bf16[896,256]{1,0:T(8,128)(2,1)}, bf16[896,256]{1,0:T(8,128)(2,1)}) custom-call(bf16[256,3584]{1,0:T(8,128)(2,1)} %input_hbm.1, f32[3584]{0:T(1024)} %gain_ref.3), custom_call_target="tpu_custom_call" | custom-call | flops 1000000 | bytes 100000 | tf_op jit(solution)/shard_map/norm/pallas_call | solution.py:59
  10.7 0.7 collective-permute-start.3
  11.4 1.2 %collective-permute-start.4 = (bf16[896,256]{1,0:T(8,128)(2,1)}, bf16[896,256]{1,0:T(8,128)(2,1)}, u32[]{:S(2)}, u32[]{:S(2)}) collective-permute-start(bf16[896,256]{1,0:T(8,128)(2,1)} %get-tuple-element.39), channel_id=1, source_target_pairs={{0,8},{4,12},{8,0},{12,4},{1,9},{5,13},{9,1},{13,5},{2,10},{6,14},... | collective-permute-start | bytes 1376264 | tf_op jit(solution)/shard_map/ppermute | solution.py:621
  12.6 17.5 %attention.1 = (bf16[2048,256]{1,0:T(8,128)(2,1)}, bf16[912,256]{1,0:T(8,128)(2,1)}, bf16[912,256]{1,0:T(8,128)(2,1)}, bf16[1024,256]{1,0:T(8,128)(2,1)}, bf16[5...) custom-call(s32[8]{0:T(128)} %count_ref.1, ...), custom_call_target="tpu_custom_call" | custom-call | flops 1000000 | bytes 100000 | tf_op jit(solution)/shard_map/attention/pallas_call | solution.py:320
  30.1 0.0 collective-permute-done.3.refs_1_
  30.1 0.0 collective-permute-done.4.refs_1_.refs_2_
  30.2 0.0 all-gather.3.cloned.1.call-update
  30.2 0.1 collective-permute-start
  30.3 1.3 %collective-permute-start.1 = (bf16[912,256]{1,0:T(8,128)(2,1)}, bf16[912,256]{1,0:T(8,128)(2,1)}, u32[]{:S(2)}, u32[]{:S(2)}) collective-permute-start(bf16[912,256]{1,0:T(8,128)(2,1)} %get-tuple-element.35), channel_id=1, source_target_pairs={{0,1},{1,2},{2,3},{3,0},{4,5},{5,6},{6,7},{7,4},{8,9},{9,10},{10,1... | collective-permute-start | bytes 1400840 | tf_op jit(solution)/shard_map/ppermute | solution.py:687
  31.6 1.0 %collective-permute-start.5 = (bf16[896,256]{1,0:T(8,128)(2,1)}, bf16[896,256]{1,0:T(8,128)(2,1)}, u32[]{:S(2)}, u32[]{:S(2)}) collective-permute-start(bf16[896,256]{1,0:T(8,128)(2,1)} %gate.2), channel_id=1, source_target_pairs={{0,12},{4,8},{8,4},{12,0},{1,13},{5,9},{9,5},{13,1},{2,14},{6,10},... | collective-permute-start | bytes 1376264 | tf_op jit(solution)/shard_map/ppermute | solution.py:621
  32.6 6.6 %back.1 = (bf16[912,256]{1,0:T(8,128)(2,1)}, bf16[912,256]{1,0:T(8,128)(2,1)}) custom-call(bf16[16,256]{1,0:T(8,128)(2,1)} %get-tuple-element.29.centre_ref, bf16[1024,256]{1,0:T(8,128)(2,1)} %get-tuple-element.30.refs_0_, bf16[512,256]{1,0:T(8,128)(2,1)} %get-tuple-element.31.refs_1_, bf16[512,256]{1,0:T(8,128)(2,1)} %get-tuple-element.32.refs_2_, ...), custom_call_target="tpu_custom_call" | custom-call | flops 1000000 | bytes 100000 | tf_op jit(solution)/shard_map/back/pallas_call | solution.py:399
  39.2 0.9 collective-permute-start.2
  40.1 20.4 %collective-permute-done.refs_5_.refs_1_ = bf16[912,256]{1,0:T(8,128)(2,1)} collective-permute-done((bf16[912,256]{1,0:T(8,128)(2,1)}, bf16[912,256]{1,0:T(8,128)(2,1)}, u32[]{:S(2)}, u32[]{:S(2)}) %collective-permute-start) | collective-permute-done | bytes 466976 | tf_op jit(solution)/shard_map/ppermute | solution.py:687
  60.4 13.7 %collective-permute-done.1.refs_6_.refs_2_ = bf16[912,256]{1,0:T(8,128)(2,1)} collective-permute-done((bf16[912,256]{1,0:T(8,128)(2,1)}, bf16[912,256]{1,0:T(8,128)(2,1)}, u32[]{:S(2)}, u32[]{:S(2)}) %collective-permute-start.1) | collective-permute-done | bytes 466976 | tf_op jit(solution)/shard_map/ppermute | solution.py:687
  74.1 0.0 collective-permute-done.5.refs_3_
  74.1 0.0 all-gather.3.cloned.1.call-done
  74.1 9.5 %weights.1 = (f32[896,1024]{1,0:T(8,128)}, f32[896,512]{1,0:T(8,128)}, f32[896,512]{1,0:T(8,128)}, f32[8,128]{1,0:T(8,128)}) custom-call(bf16[896,256]{1,0:T(8,128)(2,1)} %get-tuple-element.37.refs_0_, bf16[896,256]{1,0:T(8,128)(2,1)} %collective-permute-done.3.refs_1_, bf16[896,256]{1,0:T(8,128)(2,1)} %collective-permute-done.4.refs_1_.refs_2_, ...), custom_call_target="tpu_custom_call" | custom-call | flops 3758096384 | bytes 13369344 | tf_op jit(solution)/shard_map/weights/pallas_call | solution.py:473
  83.7 0.0 collective-permute-done.2.refs_3_
  83.7 2.8 %gains.1 = (f32[1,896]{1,0:T(1,128)}, f32[256,896]{1,0:T(8,128)}) custom-call(bf16[256,896]{1,0:T(8,128)(2,1)} %get-tuple-element.28.input_ref, f32[256,1]{1,0:T(8,128)} %get-tuple-element.27.inverse_ref, bf16[912,256]{1,0:T(8,128)(2,1)} %get-tuple-element.33.refs_0_, bf16[912,256]{1,0:T(8,128)(2,1)} %collective-permute-done.refs_5_.refs_1_, ...), custom_call_target="tpu_custom_call" | custom-call | flops 1000000 | bytes 100000 | tf_op jit(solution)/shard_map/gains/pallas_call | solution.py:542
  86.4 0.6 collective-permute-start.8
  87.1 1.2 %collective-permute-start.7 = (f32[1,896]{1,0:T(1,128)}, f32[1,896]{1,0:T(1,128)}, u32[]{:S(2)}, u32[]{:S(2)}) collective-permute-start(f32[1,896]{1,0:T(1,128)} %get-tuple-element.48.refs_0_), channel_id=1, source_target_pairs={{0,8},{4,12},{8,0},{12,4},{1,9},{5,13},{9,1},{13,5},{2,10},{6,14},... | collective-permute-start | bytes 10760 | tf_op jit(solution)/shard_map/ppermute | solution.py:621
  88.3 0.3 collective-permute-start.6
  88.6 2.3 %finish.1.refs_4_ = bf16[256,896]{1,0:T(8,128)(2,1)} custom-call(f32[256,896]{1,0:T(8,128)} %get-tuple-element.43.total_ref, bf16[256,896]{1,0:T(8,128)(2,1)} %get-tuple-element.28.input_ref, f32[1,896]{1,0:T(1,128)} %get-tuple-element.44.gain_ref, f32[256,1]{1,0:T(8,128)} %get-tuple-element.27.inverse_ref, bf16[912,256]{1,0:T(8,128)(2,1)} %get-tuple-element.33.refs_0_, ...), custom_call_target="tpu_custom_call" | custom-call | flops 1000000 | bytes 100000 | tf_op jit(solution)/shard_map/finish/pallas_call | solution.py:579
  90.9 0.0 collective-permute-done.8.refs_3_
  90.9 0.0 collective-permute-done.7.refs_2_
  91.0 0.0 collective-permute-done.6.refs_1_
  91.0 1.3 %total.1 = f32[896]{0:T(1024)} custom-call(f32[1,896]{1,0:T(1,128)} %get-tuple-element.48.refs_0_, f32[1,896]{1,0:T(1,128)} %collective-permute-done.6.refs_1_, f32[1,896]{1,0:T(1,128)} %collective-permute-done.7.refs_2_, f32[1,896]{1,0:T(1,128)} %collective-permute-done.8.refs_3_, bf16[256,896]{1,0:T(8,128)(2,1)} %finish.1.refs_4_), custom_call_target="tpu_custom_call" | custom-call | flops 1000000 | bytes 100000 | tf_op jit(solution)/shard_map/total/pallas_call | solution.py:605
  (2 shorter events, 0.0 us)
Async XLA Ops:
  7.2 67.0 %all-gather.3.cloned.1.call-start = ((), (), s32[]{:S(2)}) async-start(), calls=%async_computation | async-start | bytes 5242880 | tf_op jit(solution)/shard_map/all_gather | solution.py:685
  10.7 19.4 %collective-permute-start.3 = (bf16[896,256]{1,0:T(8,128)(2,1)}, bf16[896,256]{1,0:T(8,128)(2,1)}, u32[]{:S(2)}, u32[]{:S(2)}) collective-permute-start(bf16[896,256]{1,0:T(8,128)(2,1)} %get-tuple-element.38), channel_id=1, source_target_pairs={{0,4},{4,0},{8,12},{12,8},{1,5},{5,1},{9,13},{13,9},{2,6},{6,2},{1... | collective-permute-start | bytes 1376264 | tf_op jit(solution)/shard_map/ppermute | solution.py:621
  11.4 18.8 %collective-permute-start.4 = (bf16[896,256]{1,0:T(8,128)(2,1)}, bf16[896,256]{1,0:T(8,128)(2,1)}, u32[]{:S(2)}, u32[]{:S(2)}) collective-permute-start(bf16[896,256]{1,0:T(8,128)(2,1)} %get-tuple-element.39), channel_id=1, source_target_pairs={{0,8},{4,12},{8,0},{12,4},{1,9},{5,13},{9,1},{13,5},{2,10},{6,14},... | collective-permute-start | bytes 1376264 | tf_op jit(solution)/shard_map/ppermute | solution.py:621
  30.2 30.3 %collective-permute-start = (bf16[912,256]{1,0:T(8,128)(2,1)}, bf16[912,256]{1,0:T(8,128)(2,1)}, u32[]{:S(2)}, u32[]{:S(2)}) collective-permute-start(bf16[912,256]{1,0:T(8,128)(2,1)} %get-tuple-element.34), channel_id=1, source_target_pairs={{0,2},{1,3},{2,0},{3,1},{4,6},{5,7},{6,4},{7,5},{8,10},{9,11},{10,... | collective-permute-start | bytes 1400840 | tf_op jit(solution)/shard_map/ppermute | solution.py:687
  30.3 43.8 %collective-permute-start.1 = (bf16[912,256]{1,0:T(8,128)(2,1)}, bf16[912,256]{1,0:T(8,128)(2,1)}, u32[]{:S(2)}, u32[]{:S(2)}) collective-permute-start(bf16[912,256]{1,0:T(8,128)(2,1)} %get-tuple-element.35), channel_id=1, source_target_pairs={{0,1},{1,2},{2,3},{3,0},{4,5},{5,6},{6,7},{7,4},{8,9},{9,10},{10,1... | collective-permute-start | bytes 1400840 | tf_op jit(solution)/shard_map/ppermute | solution.py:687
  31.6 42.5 %collective-permute-start.5 = (bf16[896,256]{1,0:T(8,128)(2,1)}, bf16[896,256]{1,0:T(8,128)(2,1)}, u32[]{:S(2)}, u32[]{:S(2)}) collective-permute-start(bf16[896,256]{1,0:T(8,128)(2,1)} %gate.2), channel_id=1, source_target_pairs={{0,12},{4,8},{8,4},{12,0},{1,13},{5,9},{9,5},{13,1},{2,14},{6,10},... | collective-permute-start | bytes 1376264 | tf_op jit(solution)/shard_map/ppermute | solution.py:621
  39.2 44.5 %collective-permute-start.2 = (bf16[912,256]{1,0:T(8,128)(2,1)}, bf16[912,256]{1,0:T(8,128)(2,1)}, u32[]{:S(2)}, u32[]{:S(2)}) collective-permute-start(bf16[912,256]{1,0:T(8,128)(2,1)} %get-tuple-element.36), channel_id=1, source_target_pairs={{0,3},{1,0},{2,1},{3,2},{4,7},{5,4},{6,5},{7,6},{8,11},{9,8},{10,9... | collective-permute-start | bytes 1400840 | tf_op jit(solution)/shard_map/ppermute | solution.py:687
  86.4 4.5 %collective-permute-start.8 = (f32[1,896]{1,0:T(1,128)}, f32[1,896]{1,0:T(1,128)}, u32[]{:S(2)}, u32[]{:S(2)}) collective-permute-start(f32[1,896]{1,0:T(1,128)} %get-tuple-element.48.refs_0_), channel_id=1, source_target_pairs={{0,12},{4,8},{8,4},{12,0},{1,13},{5,9},{9,5},{13,1},{2,14},{6,10},... | collective-permute-start | bytes 10760 | tf_op jit(solution)/shard_map/ppermute | solution.py:621
  87.1 3.9 %collective-permute-start.7 = (f32[1,896]{1,0:T(1,128)}, f32[1,896]{1,0:T(1,128)}, u32[]{:S(2)}, u32[]{:S(2)}) collective-permute-start(f32[1,896]{1,0:T(1,128)} %get-tuple-element.48.refs_0_), channel_id=1, source_target_pairs={{0,8},{4,12},{8,0},{12,4},{1,9},{5,13},{9,1},{13,5},{2,10},{6,14},... | collective-permute-start | bytes 10760 | tf_op jit(solution)/shard_map/ppermute | solution.py:621
  88.3 2.7 %collective-permute-start.6 = (f32[1,896]{1,0:T(1,128)}, f32[1,896]{1,0:T(1,128)}, u32[]{:S(2)}, u32[]{:S(2)}) collective-permute-start(f32[1,896]{1,0:T(1,128)} %get-tuple-element.48.refs_0_), channel_id=1, source_target_pairs={{0,4},{4,0},{8,12},{12,8},{1,5},{5,1},{9,13},{13,9},{2,6},{6,2},{1... | collective-permute-start | bytes 10760 | tf_op jit(solution)/shard_map/ppermute | solution.py:621
Sparse Core Ops, SparseCore 0:
  30.3 38.8 all-gather.2

commit v8 on v6

--- a/solution.py
+++ b/solution.py
@@ -682,25 +682,17 @@
         ]
     from_first = lax.ppermute(parts[0], "tensor", [(0, 1), (1, 0), (2, 3), (3, 2)])
     from_inner = lax.ppermute(parts[1], "tensor", [(1, 2), (2, 1)])
-    return from_first, from_inner
-
-
-def scatter_middle(parts, arrived, total):
+    from_ends = lax.ppermute(parts[2], "tensor", [(0, 2), (3, 1)])
+    return from_first, from_inner, from_ends
+
+
+def scatter_end(parts, arrived, total):
     if total != 4:
-        return arrived, None, arrived[0]
-    (held,) = gate((parts[2],), (arrived[0],))
-    from_ends = lax.ppermute(held, "tensor", [(0, 2), (3, 1)])
-    joined, token = join(held, arrived[0], parts[3], (arrived[1],))
-    return (*arrived, from_ends), joined, token
-
-
-def scatter_end(parts, arrived, joined, total, token):
-    if total != 4:
-        return [parts[-1], *arrived], 0, 0
+        return [parts[-1], *arrived], 0, 0, arrived[0]
     from_first, from_inner, from_ends = arrived
-    (joined,) = gate((joined,), (from_ends, token))
+    joined, token = join(parts[2], from_first, parts[3], (from_inner, from_ends))
     from_joined = lax.ppermute(joined, "tensor", [(1, 3), (2, 0), (0, 1), (3, 2)])
-    return [from_first, parts[1], parts[3], from_inner, from_ends, from_joined], 2, 1
+    return [from_first, parts[1], parts[3], from_inner, from_ends, from_joined], 2, 1, token
 
 
 def local(layer_input, norm_gain, w_query, w_key, w_value, head_grad, parents, row_counts):
@@ -724,9 +716,13 @@
         return [lax.rem(chip + s, chips) * 2 + lax.rem(core + e, 2) for s, e in offsets]
 
     inverse, pieces = normalize(layer_input, norm_gain, targets, branch_total, rows // slots)
-    shared = [branch_send(piece, chips, s, e) for piece, (s, e) in zip(pieces[1:], offsets[1:])]
+    near = branch_send(pieces[1], chips, 0, 1)
+    direct = [branch_send(pieces[2 * s], chips, s, 0) for s in range(1, chips)]
+    held = gate(pieces[3::2], direct) if chips > 1 else ()
+    across = [branch_send(piece, chips, s + 1, 1) for s, piece in enumerate(held)]
+    turned = [pieces[0]] + direct + [near] + across
     order = lambda place: scatter_order(tensor_total)(place)
-    ready = min(2, tensor_total)
+    ready = min(3, tensor_total)
     deltas, parts, delta_turned, centre, input_columns, gain_columns = attention_backward(
         layer_input,
         inverse,
@@ -750,31 +746,27 @@
         )
     arrived = scatter_begin(parts, tensor_total)
 
-    (first,) = gate(deltas[:1], shared)
+    (first,) = gate(deltas[:1], (near, *direct))
     sent = [branch_send(first, chips, s, 0) for s in range(1, chips)]
-    arrived, joined, met = scatter_middle(parts, arrived, tensor_total)
-    *sent, first = gate((*sent, first), (met,))
+    parts, for_ends, for_inner, met = scatter_end(parts, arrived, tensor_total)
+    *sent, first = gate((*sent, first), parts[2:3])
     others = gate(deltas[1:], (sent[0],)) if deltas[1:] else ()
-    turned = [pieces[0]] + shared
-    weights, token = None, None
+    weights, tokens = None, []
     for share, delta in zip(shares, (first, *others)):
-        if token is not None:
+        if tokens:
             sent = [branch_send(delta, chips, s, 0) for s in range(1, chips)]
-            delta, *sent = gate((delta, *sent), (token,))
-        gathered = []
-        for part in [delta] + sent:
-            gathered += [part, branch_send(part, chips, 0, 1)]
-        first_share = weights is None
+            delta, *sent = gate((delta, *sent), ())
+        gathered = [delta] + sent
+        gathered += [branch_send(part, chips, 0, 1) for part in gathered]
         *weights, token = weight_gradients(turned, gathered, share, kv_local, group, weights)
-        if first_share:
-            parts, for_ends, for_inner = scatter_end(parts, arrived, joined, tensor_total, token)
+        tokens.append(token)
 
     add = functools.partial(add_parts, for_ends, for_inner)
-    gain_sum, total = gain_sums(add, input_columns, inverse, parts, token)
+    gain_sum, total = gain_sums(add, input_columns, inverse, parts, tokens[0])
     grad_input = finish(width, add, total, input_columns, gain_columns, inverse, parts)
     if chips == 2:
         sums = [gain_sum] + [branch_send(gain_sum, chips, s, e) for s, e in offsets[1:]]
-        grad_gain = total_of_four(sums, grad_input)
+        grad_gain = total_of_four(sums, tokens[-1])
     else:
         grad_gain = lax.psum(gain_sum, "branch").reshape(column_width)
     return (grad_input, *weights, grad_gain)

time: 86.3 us -> 83.9 us (0.972)
  waiting for transfers between devices: 15.1 us -> 13.5 us
  Pallas kernels: 48.8 us -> 47.7 us
    ppermute x1, waiting for transfers between devices: 3.49 us -> 0.01 us  [scatter_end(): lax.ppermute(joined, 'tensor', [(1, 3), (2, 0), (0, 1), (3, 2)])]
    ppermute x1, waiting for transfers between devices: 3.43 us -> 0.01 us  [scatter_begin(): lax.ppermute(parts[0], 'tensor', [(0, 1), (1, 0), (2, 3), (3, 2)])]
    ppermute x1, starting transfers between devices: 2.21 us -> 5.54 us  [scatter_end(): lax.ppermute(joined, 'tensor', [(1, 3), (2, 0), (0, 1), (3, 2)])]
    ppermute x12, waiting for transfers between devices: 6.03 us -> 9.14 us  [branch_send(): return lax.ppermute(array, 'branch', pairs)]
    pallas_call x1, Pallas kernels: 6.45 us -> 3.9 us  [back_project(): pl.pallas_call(back_kernel, out_shape=(jax.ShapeDtypeStruct((depth + CENT...]
    ppermute x1, starting transfers between devices: 8.01 us -> 5.79 us  [scatter_begin(): from_ends = lax.ppermute(parts[2], 'tensor', [(0, 2), (3, 1)])]
    ppermute x1, waiting for transfers between devices: 2.09 us -> 4.31 us  [scatter_begin(): from_ends = lax.ppermute(parts[2], 'tensor', [(0, 2), (3, 1)])]
    pallas_call x1, Pallas kernels: 17.5 us -> 18.9 us  [attention_backward(): pl.pallas_call(functools.partial(attention_kernel, slots, group, kv_local...]
  transfers between devices with their start and end apart: 16 -> 16, of which waited for: 7 -> 3; matrix products, arithmetic and copies ran while one was open for 0% -> 0% of each run, Pallas kernels for 48% -> 51%
where the time goes in v8:
time: 83.9 us; the launch traced here: 83.6 us
  Pallas kernels  47.7 us (57%)
  starting transfers between devices  21.7 us (26%)
  waiting for transfers between devices  13.5 us (16%)
    pallas_call x1, Pallas kernels, attention_backward(): pl.pallas_call(functools.partial(attention_kernel, slots, group, kv_local...  18.9 us
    pallas_call x2, Pallas kernels, weight_gradients(): pl.pallas_call(functools.partial(weight_kernel, outs, sources), out_shape...  12.5 us
    ppermute x12, waiting for transfers between devices, branch_send(): return lax.ppermute(array, 'branch', pairs)  9.14 us
    ppermute x12, starting transfers between devices, branch_send(): return lax.ppermute(array, 'branch', pairs)  6.94 us
    ppermute x1, starting transfers between devices, scatter_begin(): from_ends = lax.ppermute(parts[2], 'tensor', [(0, 2), (3, 1)])  5.79 us
    ppermute x1, starting transfers between devices, scatter_end(): lax.ppermute(joined, 'tensor', [(1, 3), (2, 0), (0, 1), (3, 2)])  5.54 us
    ppermute x1, waiting for transfers between devices, scatter_begin(): from_ends = lax.ppermute(parts[2], 'tensor', [(0, 2), (3, 1)])  4.31 us
    pallas_call x1, Pallas kernels, back_project(): pl.pallas_call(back_kernel, out_shape=(jax.ShapeDtypeStruct((depth + CENT...  3.9 us
  transfers between devices with their start and end apart: 16, of which 3 were waited for; matrix products, arithmetic and copies ran while one was open for 0% of the time, Pallas kernels for 51%

profile of v8, /device:TPU:0, one launch (start us, length us, event | category | flops | bytes accessed | tf_op | source)
XLA Modules:
  0.0 83.6 jit_solution(6757917458094700919)
XLA Ops:
  0.6 3.5 %norm.1 = (f32[256,1]{1,0:T(8,128)}, bf16[896,256]{1,0:T(8,128)(2,1)}, bf16[896,256]{1,0:T(8,128)(2,1)}, bf16[896,256]{1,0:T(8,128)(2,1)}, bf16[896,256]{1,0:T(8,128)(2,1)}) custom-call(bf16[256,3584]{1,0:T(8,128)(2,1)} %input_hbm.1, f32[3584]{0:T(1024)} %gain_ref.3), custom_call_target="tpu_custom_call" | custom-call | flops 1000000 | bytes 100000 | tf_op jit(solution)/shard_map/norm/pallas_call | solution.py:59
  4.1 2.9 %collective-permute-start.4 = (bf16[896,256]{1,0:T(8,128)(2,1)}, bf16[896,256]{1,0:T(8,128)(2,1)}, u32[]{:S(2)}, u32[]{:S(2)}) collective-permute-start(bf16[896,256]{1,0:T(8,128)(2,1)} %get-tuple-element.47), channel_id=1, source_target_pairs={{0,8},{4,12},{8,0},{12,4},{1,9},{5,13},{9,1},{13,5},{2,10},{6,14},... | collective-permute-start | bytes 1376264 | tf_op jit(solution)/shard_map/ppermute | solution.py:658
  7.0 0.0 collective-permute-start.5
  7.0 18.9 %attention.1 = (bf16[1280,256]{1,0:T(8,128)(2,1)}, bf16[768,256]{1,0:T(8,128)(2,1)}, bf16[912,256]{1,0:T(8,128)(2,1)}, bf16[912,256]{1,0:T(8,128)(2,1)}, bf16[91...) custom-call(s32[8]{0:T(128)} %count_ref.1, ...), custom_call_target="tpu_custom_call" | custom-call | flops 1000000 | bytes 100000 | tf_op jit(solution)/shard_map/attention/pallas_call | solution.py:320
  25.9 0.0 collective-permute-done.4.refs_1_.refs_2_
  25.9 0.0 collective-permute-done.5.refs_1_.refs_2_
  26.0 0.1 collective-permute-start.7
  26.1 2.0 %collective-permute-start = (bf16[912,256]{1,0:T(8,128)(2,1)}, bf16[912,256]{1,0:T(8,128)(2,1)}, u32[]{:S(2)}, u32[]{:S(2)}) collective-permute-start(bf16[912,256]{1,0:T(8,128)(2,1)} %get-tuple-element.38), channel_id=1, source_target_pairs={{0,1},{1,0},{2,3},{3,2},{4,5},{5,4},{6,7},{7,6},{8,9},{9,8},{10,11... | collective-permute-start | bytes 1400840 | tf_op jit(solution)/shard_map/ppermute | solution.py:683
  28.1 1.4 %collective-permute-start.1 = (bf16[912,256]{1,0:T(8,128)(2,1)}, bf16[912,256]{1,0:T(8,128)(2,1)}, u32[]{:S(2)}, u32[]{:S(2)}) collective-permute-start(bf16[912,256]{1,0:T(8,128)(2,1)} %get-tuple-element.39.refs_1_), channel_id=1, source_target_pairs={{1,2},{2,1},{5,6},{6,5},{9,10},{10,9},{13,14},{14,13},{17,18},{18,... | collective-permute-start | bytes 1400840 | tf_op jit(solution)/shard_map/ppermute | solution.py:684
  29.6 5.8 %collective-permute-start.2 = (bf16[912,256]{1,0:T(8,128)(2,1)}, bf16[912,256]{1,0:T(8,128)(2,1)}, u32[]{:S(2)}, u32[]{:S(2)}) collective-permute-start(bf16[912,256]{1,0:T(8,128)(2,1)} %get-tuple-element.44.inner_ref), channel_id=1, source_target_pairs={{0,2},{3,1},{4,6},{7,5},{8,10},{11,9},{12,14},{15,13},{16,18},{19,... | collective-permute-start | bytes 1400840 | tf_op jit(solution)/shard_map/ppermute | solution.py:685
  35.4 0.8 collective-permute-start.6
  36.1 3.9 %back.1.end_ref.refs_2_ = bf16[912,256]{1,0:T(8,128)(2,1)} custom-call(bf16[16,256]{1,0:T(8,128)(2,1)} %get-tuple-element.40.centre_ref, bf16[1024,256]{1,0:T(8,128)(2,1)} %get-tuple-element.41.refs_0_, bf16[512,256]{1,0:T(8,128)(2,1)} %get-tuple-element.42.refs_1_, bf16[512,256]{1,0:T(8,128)(2,1)} %get-tuple-element.43.refs_2_, bf16[3584,1024]{1,0:T(8,128)(2,1)} %refs_3_.1, ...), custom_call_target="tpu_custom_call" | custom-call | flops 1000000 | bytes 100000 | tf_op jit(solution)/shard_map/back/pallas_call | solution.py:399
  40.0 3.9 %collective-permute-done.7.refs_0_ = bf16[1280,256]{1,0:T(8,128)(2,1)} collective-permute-done((bf16[1280,256]{1,0:T(8,128)(2,1)}, bf16[1280,256]{1,0:T(8,128)(2,1)}, u32[]{:S(2)}, u32[]{:S(2)}) %collective-permute-start.7) | collective-permute-done | bytes 655392 | tf_op jit(solution)/shard_map/ppermute | solution.py:658
  43.9 0.1 collective-permute-start.10
  44.0 0.0 collective-permute-done.other_ref.refs_0_
  44.0 0.0 collective-permute-start.8
  44.0 0.0 collective-permute-done.1.rest_0_.refs_3_
  44.0 0.5 collective-permute-start.9
  44.5 4.3 %collective-permute-done.2.rest_1_.refs_4_ = bf16[912,256]{1,0:T(8,128)(2,1)} collective-permute-done((bf16[912,256]{1,0:T(8,128)(2,1)}, bf16[912,256]{1,0:T(8,128)(2,1)}, u32[]{:S(2)}, u32[]{:S(2)}) %collective-permute-start.2) | collective-permute-done | bytes 466976 | tf_op jit(solution)/shard_map/ppermute | solution.py:685
  48.9 2.1 %join.1 = (bf16[912,256]{1,0:T(8,128)(2,1)}, f32[8,128]{1,0:T(8,128)}) custom-call(bf16[912,256]{1,0:T(8,128)(2,1)} %get-tuple-element.44.inner_ref, bf16[912,256]{1,0:T(8,128)(2,1)} %collective-permute-done.other_ref.refs_0_, bf16[912,256]{1,0:T(8,128)(2,1)} %back.1.end_ref.refs_2_, bf16[912,256]{1,0:T(8,128)(2,1)} %collective-permute-done.1.rest_0_.refs_3_, ...), custom_call_target="tpu_custom_call" | custom-call | flops 1000000 | bytes 100000 | tf_op jit(solution)/shard_map/join/pallas_call | solution.py:535
  51.0 5.5 %collective-permute-start.3 = (bf16[912,256]{1,0:T(8,128)(2,1)}, bf16[912,256]{1,0:T(8,128)(2,1)}, u32[]{:S(2)}, u32[]{:S(2)}) collective-permute-start(bf16[912,256]{1,0:T(8,128)(2,1)} %get-tuple-element.45), channel_id=1, source_target_pairs={{1,3},{2,0},{0,1},{3,2},{5,7},{6,4},{4,5},{7,6},{9,11},{10,8},{8,9... | collective-permute-start | bytes 1400840 | tf_op jit(solution)/shard_map/ppermute | solution.py:694
  56.5 5.2 %collective-permute-done.10.refs_1_ = bf16[768,256]{1,0:T(8,128)(2,1)} collective-permute-done((bf16[768,256]{1,0:T(8,128)(2,1)}, bf16[768,256]{1,0:T(8,128)(2,1)}, u32[]{:S(2)}, u32[]{:S(2)}) %collective-permute-start.10) | collective-permute-done | bytes 393248 | tf_op jit(solution)/shard_map/ppermute | solution.py:658
  61.8 0.0 collective-permute-start.11
  61.8 0.0 collective-permute-done.6.refs_3_
  61.8 0.5 collective-permute-start.12
  62.3 0.0 collective-permute-done.8.refs_6_
  62.3 0.0 collective-permute-done.9.refs_7_
  62.3 7.1 %weights.2 = (f32[896,1024]{1,0:T(8,128)}, f32[896,512]{1,0:T(8,128)}, f32[896,512]{1,0:T(8,128)}, f32[8,128]{1,0:T(8,128)}) custom-call(bf16[896,256]{1,0:T(8,128)(2,1)} %get-tuple-element.46.refs_0_, bf16[896,256]{1,0:T(8,128)(2,1)} %collective-permute-done.4.refs_1_.refs_2_, bf16[896,256]{1,0:T(8,128)(2,1)} %collective-permute-done.5.refs_1_.refs_2_, ...), custom_call_target="tpu_custom_call" | custom-call | flops 1000000 | bytes 100000 | tf_op jit(solution)/shard_map/weights/pallas_call | solution.py:473
  69.4 0.0 collective-permute-done.3.refs_5_
  69.4 3.1 %gains.1 = (f32[1,896]{1,0:T(1,128)}, f32[256,896]{1,0:T(8,128)}) custom-call(bf16[256,896]{1,0:T(8,128)(2,1)} %get-tuple-element.37.input_ref, f32[256,1]{1,0:T(8,128)} %get-tuple-element.36.inverse_ref, bf16[912,256]{1,0:T(8,128)(2,1)} %collective-permute-done.other_ref.refs_0_, bf16[912,256]{1,0:T(8,128)(2,1)} %get-tuple-element.39.refs_1_, ...), custom_call_target="tpu_custom_call" | custom-call | flops 1000000 | bytes 100000 | tf_op jit(solution)/shard_map/gains/pallas_call | solution.py:579
  72.5 0.1 collective-permute-start.13
  72.6 1.5 %collective-permute-start.14 = (f32[1,896]{1,0:T(1,128)}, f32[1,896]{1,0:T(1,128)}, u32[]{:S(2)}, u32[]{:S(2)}) collective-permute-start(f32[1,896]{1,0:T(1,128)} %get-tuple-element.65.refs_0_), channel_id=1, source_target_pairs={{0,8},{4,12},{8,0},{12,4},{1,9},{5,13},{9,1},{13,5},{2,10},{6,14},... | collective-permute-start | bytes 10760 | tf_op jit(solution)/shard_map/ppermute | solution.py:658
  74.1 0.3 collective-permute-start.15
  74.4 2.4 %finish.1 = bf16[256,896]{1,0:T(8,128)(2,1)} custom-call(f32[256,896]{1,0:T(8,128)} %get-tuple-element.54.total_ref, bf16[256,896]{1,0:T(8,128)(2,1)} %get-tuple-element.37.input_ref, f32[1,896]{1,0:T(1,128)} %get-tuple-element.55.gain_ref, f32[256,1]{1,0:T(8,128)} %get-tuple-element.36.inverse_ref, bf16[912,256]{1,0:T(8,128)(2,1)} %collective-permute-done.other_ref.refs_0_, ...), custom_call_target="tpu_custom_call" | custom-call | flops 1000000 | bytes 100000 | tf_op jit(solution)/shard_map/finish/pallas_call | solution.py:616
  76.9 0.0 collective-permute-done.11.refs_6_
  76.9 0.0 collective-permute-done.12.refs_7_
  76.9 5.4 %weights.3 = (f32[896,1024]{1,0:T(8,128)}, f32[896,512]{1,0:T(8,128)}, f32[896,512]{1,0:T(8,128)}, f32[8,128]{1,0:T(8,128)}) custom-call(bf16[896,256]{1,0:T(8,128)(2,1)} %get-tuple-element.46.refs_0_, bf16[896,256]{1,0:T(8,128)(2,1)} %collective-permute-done.4.refs_1_.refs_2_, ...), custom_call_target="tpu_custom_call", output_to_operand_aliasing={{0}: (8, {}), {1}: (9, {}), {2}: (10, {})} | custom-call | flops 1000000 | bytes 100000 | tf_op jit(solution)/shard_map/weights/pallas_call | solution.py:473
  82.3 0.0 collective-permute-done.13.refs_1_
  82.3 0.0 collective-permute-done.14.refs_2_
  82.3 0.0 collective-permute-done.15.refs_3_
  82.4 1.3 %total.1 = f32[896]{0:T(1024)} custom-call(f32[1,896]{1,0:T(1,128)} %get-tuple-element.65.refs_0_, f32[1,896]{1,0:T(1,128)} %collective-permute-done.13.refs_1_, f32[1,896]{1,0:T(1,128)} %collective-permute-done.14.refs_2_, f32[1,896]{1,0:T(1,128)} %collective-permute-done.15.refs_3_, f32[8,128]{1,0:T(8,128)} %get-tuple-element.66.refs_4_), custom_call_target="tpu_custom_call" | custom-call | flops 1000000 | bytes 100000 | tf_op jit(solution)/shard_map/total/pallas_call | solution.py:642
  (5 shorter events, 0.0 us)
Async XLA Ops:
  4.1 21.8 %collective-permute-start.4 = (bf16[896,256]{1,0:T(8,128)(2,1)}, bf16[896,256]{1,0:T(8,128)(2,1)}, u32[]{:S(2)}, u32[]{:S(2)}) collective-permute-start(bf16[896,256]{1,0:T(8,128)(2,1)} %get-tuple-element.47), channel_id=1, source_target_pairs={{0,8},{4,12},{8,0},{12,4},{1,9},{5,13},{9,1},{13,5},{2,10},{6,14},... | collective-permute-start | bytes 1376264 | tf_op jit(solution)/shard_map/ppermute | solution.py:658
  7.0 18.9 %collective-permute-start.5 = (bf16[896,256]{1,0:T(8,128)(2,1)}, bf16[896,256]{1,0:T(8,128)(2,1)}, u32[]{:S(2)}, u32[]{:S(2)}) collective-permute-start(bf16[896,256]{1,0:T(8,128)(2,1)} %get-tuple-element.48), channel_id=1, source_target_pairs={{0,4},{4,0},{8,12},{12,8},{1,5},{5,1},{9,13},{13,9},{2,6},{6,2},{1... | collective-permute-start | bytes 1376264 | tf_op jit(solution)/shard_map/ppermute | solution.py:658
  26.0 17.9 %collective-permute-start.7 = (bf16[1280,256]{1,0:T(8,128)(2,1)}, bf16[1280,256]{1,0:T(8,128)(2,1)}, u32[]{:S(2)}, u32[]{:S(2)}) collective-permute-start(bf16[1280,256]{1,0:T(8,128)(2,1)} %gate.6.refs_1_), channel_id=1, source_target_pairs={{0,8},{4,12},{8,0},{12,4},{1,9},{5,13},{9,1},{13,5},{2,10},{6,14},... | collective-permute-start | bytes 1966088 | tf_op jit(solution)/shard_map/ppermute | solution.py:658
  26.1 17.9 %collective-permute-start = (bf16[912,256]{1,0:T(8,128)(2,1)}, bf16[912,256]{1,0:T(8,128)(2,1)}, u32[]{:S(2)}, u32[]{:S(2)}) collective-permute-start(bf16[912,256]{1,0:T(8,128)(2,1)} %get-tuple-element.38), channel_id=1, source_target_pairs={{0,1},{1,0},{2,3},{3,2},{4,5},{5,4},{6,7},{7,6},{8,9},{9,8},{10,11... | collective-permute-start | bytes 1400840 | tf_op jit(solution)/shard_map/ppermute | solution.py:683
  28.1 15.9 %collective-permute-start.1 = (bf16[912,256]{1,0:T(8,128)(2,1)}, bf16[912,256]{1,0:T(8,128)(2,1)}, u32[]{:S(2)}, u32[]{:S(2)}) collective-permute-start(bf16[912,256]{1,0:T(8,128)(2,1)} %get-tuple-element.39.refs_1_), channel_id=1, source_target_pairs={{1,2},{2,1},{5,6},{6,5},{9,10},{10,9},{13,14},{14,13},{17,18},{18,... | collective-permute-start | bytes 1400840 | tf_op jit(solution)/shard_map/ppermute | solution.py:684
  29.6 19.3 %collective-permute-start.2 = (bf16[912,256]{1,0:T(8,128)(2,1)}, bf16[912,256]{1,0:T(8,128)(2,1)}, u32[]{:S(2)}, u32[]{:S(2)}) collective-permute-start(bf16[912,256]{1,0:T(8,128)(2,1)} %get-tuple-element.44.inner_ref), channel_id=1, source_target_pairs={{0,2},{3,1},{4,6},{7,5},{8,10},{11,9},{12,14},{15,13},{16,18},{19,... | collective-permute-start | bytes 1400840 | tf_op jit(solution)/shard_map/ppermute | solution.py:685
  35.4 26.4 %collective-permute-start.6 = (bf16[896,256]{1,0:T(8,128)(2,1)}, bf16[896,256]{1,0:T(8,128)(2,1)}, u32[]{:S(2)}, u32[]{:S(2)}) collective-permute-start(bf16[896,256]{1,0:T(8,128)(2,1)} %gate.5), channel_id=1, source_target_pairs={{0,12},{4,8},{8,4},{12,0},{1,13},{5,9},{9,5},{13,1},{2,14},{6,10},... | collective-permute-start | bytes 1376264 | tf_op jit(solution)/shard_map/ppermute | solution.py:658
  43.9 17.9 %collective-permute-start.10 = (bf16[768,256]{1,0:T(8,128)(2,1)}, bf16[768,256]{1,0:T(8,128)(2,1)}, u32[]{:S(2)}, u32[]{:S(2)}) collective-permute-start(bf16[768,256]{1,0:T(8,128)(2,1)} %gate.8.refs_0_), channel_id=1, source_target_pairs={{0,8},{4,12},{8,0},{12,4},{1,9},{5,13},{9,1},{13,5},{2,10},{6,14},... | collective-permute-start | bytes 1179656 | tf_op jit(solution)/shard_map/ppermute | solution.py:658
  44.0 18.2 %collective-permute-start.8 = (bf16[1280,256]{1,0:T(8,128)(2,1)}, bf16[1280,256]{1,0:T(8,128)(2,1)}, u32[]{:S(2)}, u32[]{:S(2)}) collective-permute-start(bf16[1280,256]{1,0:T(8,128)(2,1)} %get-tuple-element.51.refs_4_), channel_id=1, source_target_pairs={{0,4},{4,0},{8,12},{12,8},{1,5},{5,1},{9,13},{13,9},{2,6},{6,2},{1... | collective-permute-start | bytes 1966088 | tf_op jit(solution)/shard_map/ppermute | solution.py:658
  44.0 18.2 %collective-permute-start.9 = (bf16[1280,256]{1,0:T(8,128)(2,1)}, bf16[1280,256]{1,0:T(8,128)(2,1)}, u32[]{:S(2)}, u32[]{:S(2)}) collective-permute-start(bf16[1280,256]{1,0:T(8,128)(2,1)} %get-tuple-element.52.refs_5_.refs_1_), channel_id=1, source_target_pairs={{0,4},{4,0},{8,12},{12,8},{1,5},{5,1},{9,13},{13,9},{2,6},{6,2},{1... | collective-permute-start | bytes 1966088 | tf_op jit(solution)/shard_map/ppermute | solution.py:658
  51.0 18.4 %collective-permute-start.3 = (bf16[912,256]{1,0:T(8,128)(2,1)}, bf16[912,256]{1,0:T(8,128)(2,1)}, u32[]{:S(2)}, u32[]{:S(2)}) collective-permute-start(bf16[912,256]{1,0:T(8,128)(2,1)} %get-tuple-element.45), channel_id=1, source_target_pairs={{1,3},{2,0},{0,1},{3,2},{5,7},{6,4},{4,5},{7,6},{9,11},{10,8},{8,9... | collective-permute-start | bytes 1400840 | tf_op jit(solution)/shard_map/ppermute | solution.py:694
  61.8 15.1 %collective-permute-start.11 = (bf16[768,256]{1,0:T(8,128)(2,1)}, bf16[768,256]{1,0:T(8,128)(2,1)}, u32[]{:S(2)}, u32[]{:S(2)}) collective-permute-start(bf16[768,256]{1,0:T(8,128)(2,1)} %get-tuple-element.57.refs_4_), channel_id=1, source_target_pairs={{0,4},{4,0},{8,12},{12,8},{1,5},{5,1},{9,13},{13,9},{2,6},{6,2},{1... | collective-permute-start | bytes 1179656 | tf_op jit(solution)/shard_map/ppermute | solution.py:658
  61.8 15.1 %collective-permute-start.12 = (bf16[768,256]{1,0:T(8,128)(2,1)}, bf16[768,256]{1,0:T(8,128)(2,1)}, u32[]{:S(2)}, u32[]{:S(2)}) collective-permute-start(bf16[768,256]{1,0:T(8,128)(2,1)} %get-tuple-element.58.refs_5_), channel_id=1, source_target_pairs={{0,4},{4,0},{8,12},{12,8},{1,5},{5,1},{9,13},{13,9},{2,6},{6,2},{1... | collective-permute-start | bytes 1179656 | tf_op jit(solution)/shard_map/ppermute | solution.py:658
  72.5 9.8 %collective-permute-start.13 = (f32[1,896]{1,0:T(1,128)}, f32[1,896]{1,0:T(1,128)}, u32[]{:S(2)}, u32[]{:S(2)}) collective-permute-start(f32[1,896]{1,0:T(1,128)} %get-tuple-element.65.refs_0_), channel_id=1, source_target_pairs={{0,4},{4,0},{8,12},{12,8},{1,5},{5,1},{9,13},{13,9},{2,6},{6,2},{1... | collective-permute-start | bytes 10760 | tf_op jit(solution)/shard_map/ppermute | solution.py:658
  72.6 9.7 %collective-permute-start.14 = (f32[1,896]{1,0:T(1,128)}, f32[1,896]{1,0:T(1,128)}, u32[]{:S(2)}, u32[]{:S(2)}) collective-permute-start(f32[1,896]{1,0:T(1,128)} %get-tuple-element.65.refs_0_), channel_id=1, source_target_pairs={{0,8},{4,12},{8,0},{12,4},{1,9},{5,13},{9,1},{13,5},{2,10},{6,14},... | collective-permute-start | bytes 10760 | tf_op jit(solution)/shard_map/ppermute | solution.py:658
  74.1 8.2 %collective-permute-start.15 = (f32[1,896]{1,0:T(1,128)}, f32[1,896]{1,0:T(1,128)}, u32[]{:S(2)}, u32[]{:S(2)}) collective-permute-start(f32[1,896]{1,0:T(1,128)} %get-tuple-element.65.refs_0_), channel_id=1, source_target_pairs={{0,12},{4,8},{8,4},{12,0},{1,13},{5,9},{9,5},{13,1},{2,14},{6,10},... | collective-permute-start | bytes 10760 | tf_op jit(solution)/shard_map/ppermute | solution.py:658

commit v9 on v8

--- a/solution.py
+++ b/solution.py
@@ -140,7 +140,7 @@
     weights += ((value_hbm, value_ref, head_dim, mid + head_dim),)
 
     def fetch(step, which):
-        lines = pl.ds(pl.multiple_of(step * chunk, chunk), chunk)
+        lines = pl.ds(step * chunk, chunk)
         source, kept_ref = weights[which][:2]
         return pltpu.make_async_copy(
             source.at[lines, :], kept_ref.at[lines, :], weight_sem.at[step, which]
@@ -159,7 +159,6 @@
     parents = parent_ref[...].reshape(1, rows)
     for slot in range(slots):
         allowed_ref[slot] = ancestor_mask(parents[:, slot * block : (slot + 1) * block])
-    sum_ref[...] = jnp.zeros_like(sum_ref)
     inverse = inverse_ref[...]
     input_load.wait()
     stores = []
@@ -175,18 +174,18 @@
     else:
         column_gain_ref[...] = jnp.zeros_like(column_gain_ref)
 
-    def project(step, carry):
-        lines = pl.ds(pl.multiple_of(step * chunk, chunk), chunk)
+    for step in range(steps):
+        lines = slice(step * chunk, (step + 1) * chunk)
         gain = 1.0 + gain_row[:, lines]
         normed = (input_ref[:, lines].astype(jnp.float32) * inverse * gain).astype(jnp.bfloat16)
         for which, (_, kept_ref, wide, place) in enumerate(weights):
             fetch(step, which).wait()
             term = nn_dot(normed, kept_ref[lines, :])
             for h in range(kv_local):
-                sum_ref[h, :, place : place + wide] += term[:, h * wide : (h + 1) * wide]
-        return carry
-
-    lax.fori_loop(0, steps, project, 0)
+                part = term[:, h * wide : (h + 1) * wide]
+                if step > 0:
+                    part = part + sum_ref[h, :, place : place + wide]
+                sum_ref[h, :, place : place + wide] = part
     grad_load.wait()
     scale = head_dim ** (-0.5)
     centre_ref[...] = jnp.zeros_like(centre_ref)
@@ -718,8 +717,7 @@
     inverse, pieces = normalize(layer_input, norm_gain, targets, branch_total, rows // slots)
     near = branch_send(pieces[1], chips, 0, 1)
     direct = [branch_send(pieces[2 * s], chips, s, 0) for s in range(1, chips)]
-    held = gate(pieces[3::2], direct) if chips > 1 else ()
-    across = [branch_send(piece, chips, s + 1, 1) for s, piece in enumerate(held)]
+    across = [branch_send(pieces[2 * s + 1], chips, s, 1) for s in range(1, chips)]
     turned = [pieces[0]] + direct + [near] + across
     order = lambda place: scatter_order(tensor_total)(place)
     ready = min(3, tensor_total)
@@ -746,7 +744,7 @@
         )
     arrived = scatter_begin(parts, tensor_total)
 
-    (first,) = gate(deltas[:1], (near, *direct))
+    (first,) = gate(deltas[:1], (near, *direct, *across))
     sent = [branch_send(first, chips, s, 0) for s in range(1, chips)]
     parts, for_ends, for_inner, met = scatter_end(parts, arrived, tensor_total)
     *sent, first = gate((*sent, first), parts[2:3])
@@ -762,7 +760,7 @@
         tokens.append(token)
 
     add = functools.partial(add_parts, for_ends, for_inner)
-    gain_sum, total = gain_sums(add, input_columns, inverse, parts, tokens[0])
+    gain_sum, total = gain_sums(add, input_columns, inverse, parts, tokens[-1])
     grad_input = finish(width, add, total, input_columns, gain_columns, inverse, parts)
     if chips == 2:
         sums = [gain_sum] + [branch_send(gain_sum, chips, s, e) for s, e in offsets[1:]]

time: 83.9 us -> 82.9 us (0.988)
  starting transfers between devices: 21.7 us -> 19.3 us
  waiting for transfers between devices: 13.5 us -> 15.2 us
    ppermute x1, waiting for transfers between devices: 0.01 us -> 9.32 us  [scatter_begin(): lax.ppermute(parts[0], 'tensor', [(0, 1), (1, 0), (2, 3), (3, 2)])]
    ppermute x1, waiting for transfers between devices: 4.31 us -> 0.01 us  [scatter_begin(): from_ends = lax.ppermute(parts[2], 'tensor', [(0, 2), (3, 1)])]
    ppermute x12, waiting for transfers between devices: 9.14 us -> 5.85 us  [branch_send(): return lax.ppermute(array, 'branch', pairs)]
    ppermute x1, starting transfers between devices: 5.54 us -> 2.56 us  [scatter_end(): lax.ppermute(joined, 'tensor', [(1, 3), (2, 0), (0, 1), (3, 2)])]
    ppermute x12, starting transfers between devices: 6.94 us -> 9.12 us  [branch_send(): return lax.ppermute(array, 'branch', pairs)]
    ppermute x1, starting transfers between devices: 2.04 us -> 0.01 us  [scatter_begin(): lax.ppermute(parts[0], 'tensor', [(0, 1), (1, 0), (2, 3), (3, 2)])]
  transfers between devices with their start and end apart: 16 -> 16, of which waited for: 3 -> 3; matrix products, arithmetic and copies ran while one was open for 0% -> 0% of each run, Pallas kernels for 51% -> 48%
where the time goes in v9:
time: 82.9 us; the launch traced here: 82.6 us
  Pallas kernels  47.4 us (57%)
  starting transfers between devices  19.3 us (23%)
  waiting for transfers between devices  15.2 us (18%)
    pallas_call x1, Pallas kernels, attention_backward(): pl.pallas_call(functools.partial(attention_kernel, slots, group, kv_local...  18.6 us
    pallas_call x2, Pallas kernels, weight_gradients(): pl.pallas_call(functools.partial(weight_kernel, outs, sources), out_shape...  12.5 us
    ppermute x1, waiting for transfers between devices, scatter_begin(): lax.ppermute(parts[0], 'tensor', [(0, 1), (1, 0), (2, 3), (3, 2)])  9.32 us
    ppermute x12, starting transfers between devices, branch_send(): return lax.ppermute(array, 'branch', pairs)  9.12 us
    ppermute x1, starting transfers between devices, scatter_begin(): from_ends = lax.ppermute(parts[2], 'tensor', [(0, 2), (3, 1)])  6.18 us
    ppermute x12, waiting for transfers between devices, branch_send(): return lax.ppermute(array, 'branch', pairs)  5.85 us
    pallas_call x1, Pallas kernels, back_project(): pl.pallas_call(back_kernel, out_shape=(jax.ShapeDtypeStruct((depth + CENT...  3.9 us
    pallas_call x1, Pallas kernels, normalize(): pl.pallas_call(functools.partial(norm_kernel, targets), out_shape=(jax.Sh...  3.49 us
  transfers between devices with their start and end apart: 16, of which 3 were waited for; matrix products, arithmetic and copies ran while one was open for 0% of the time, Pallas kernels for 48%

profile of v9, /device:TPU:0, one launch (start us, length us, event | category | flops | bytes accessed | tf_op | source)
XLA Modules:
  0.0 82.6 jit_solution(4012862809332207991)
XLA Ops:
  0.6 3.5 %norm.1 = (f32[256,1]{1,0:T(8,128)}, bf16[896,256]{1,0:T(8,128)(2,1)}, bf16[896,256]{1,0:T(8,128)(2,1)}, bf16[896,256]{1,0:T(8,128)(2,1)}, bf16[896,256]{1,0:T(8,128)(2,1)}) custom-call(bf16[256,3584]{1,0:T(8,128)(2,1)} %input_hbm.1, f32[3584]{0:T(1024)} %gain_ref.3), custom_call_target="tpu_custom_call" | custom-call | flops 1000000 | bytes 100000 | tf_op jit(solution)/shard_map/norm/pallas_call | solution.py:59
  4.1 2.9 %collective-permute-start.4 = (bf16[896,256]{1,0:T(8,128)(2,1)}, bf16[896,256]{1,0:T(8,128)(2,1)}, u32[]{:S(2)}, u32[]{:S(2)}) collective-permute-start(bf16[896,256]{1,0:T(8,128)(2,1)} %get-tuple-element.46), channel_id=1, source_target_pairs={{0,8},{4,12},{8,0},{12,4},{1,9},{5,13},{9,1},{13,5},{2,10},{6,14},... | collective-permute-start | bytes 1376264 | tf_op jit(solution)/shard_map/ppermute | solution.py:657
  7.1 0.0 collective-permute-start.5
  7.1 0.2 collective-permute-start.6
  7.2 18.6 %attention.1 = (bf16[1280,256]{1,0:T(8,128)(2,1)}, bf16[768,256]{1,0:T(8,128)(2,1)}, bf16[912,256]{1,0:T(8,128)(2,1)}, bf16[912,256]{1,0:T(8,128)(2,1)}, bf16[91...) custom-call(s32[8]{0:T(128)} %count_ref.1, ...), custom_call_target="tpu_custom_call" | custom-call | flops 1000000 | bytes 100000 | tf_op jit(solution)/shard_map/attention/pallas_call | solution.py:319
  25.8 0.0 collective-permute-done.4.refs_2_.refs_1_
  25.8 0.0 collective-permute-done.5.refs_1_.refs_2_
  25.8 1.2 %collective-permute-done.6.refs_3_ = bf16[896,256]{1,0:T(8,128)(2,1)} collective-permute-done((bf16[896,256]{1,0:T(8,128)(2,1)}, bf16[896,256]{1,0:T(8,128)(2,1)}, u32[]{:S(2)}, u32[]{:S(2)}) %collective-permute-start.6) | collective-permute-done | bytes 458784 | tf_op jit(solution)/shard_map/ppermute | solution.py:657
  27.0 1.3 %collective-permute-start.7 = (bf16[1280,256]{1,0:T(8,128)(2,1)}, bf16[1280,256]{1,0:T(8,128)(2,1)}, u32[]{:S(2)}, u32[]{:S(2)}) collective-permute-start(bf16[1280,256]{1,0:T(8,128)(2,1)} %gate.4.refs_1_), channel_id=1, source_target_pairs={{0,8},{4,12},{8,0},{12,4},{1,9},{5,13},{9,1},{13,5},{2,10},{6,14},... | collective-permute-start | bytes 1966088 | tf_op jit(solution)/shard_map/ppermute | solution.py:657
  28.3 1.4 %collective-permute-start.1 = (bf16[912,256]{1,0:T(8,128)(2,1)}, bf16[912,256]{1,0:T(8,128)(2,1)}, u32[]{:S(2)}, u32[]{:S(2)}) collective-permute-start(bf16[912,256]{1,0:T(8,128)(2,1)} %get-tuple-element.38.refs_1_), channel_id=1, source_target_pairs={{1,2},{2,1},{5,6},{6,5},{9,10},{10,9},{13,14},{14,13},{17,18},{18,... | collective-permute-start | bytes 1400840 | tf_op jit(solution)/shard_map/ppermute | solution.py:683
  29.8 6.2 %collective-permute-start.2 = (bf16[912,256]{1,0:T(8,128)(2,1)}, bf16[912,256]{1,0:T(8,128)(2,1)}, u32[]{:S(2)}, u32[]{:S(2)}) collective-permute-start(bf16[912,256]{1,0:T(8,128)(2,1)} %get-tuple-element.43.inner_ref), channel_id=1, source_target_pairs={{0,2},{3,1},{4,6},{7,5},{8,10},{11,9},{12,14},{15,13},{16,18},{19,... | collective-permute-start | bytes 1400840 | tf_op jit(solution)/shard_map/ppermute | solution.py:684
  35.9 0.0 collective-permute-start
  35.9 3.9 %back.1.end_ref.refs_2_ = bf16[912,256]{1,0:T(8,128)(2,1)} custom-call(bf16[16,256]{1,0:T(8,128)(2,1)} %get-tuple-element.39.centre_ref, bf16[1024,256]{1,0:T(8,128)(2,1)} %get-tuple-element.40.refs_0_, bf16[512,256]{1,0:T(8,128)(2,1)} %get-tuple-element.41.refs_1_, bf16[512,256]{1,0:T(8,128)(2,1)} %get-tuple-element.42.refs_2_, bf16[3584,1024]{1,0:T(8,128)(2,1)} %refs_3_.1, ...), custom_call_target="tpu_custom_call" | custom-call | flops 1000000 | bytes 100000 | tf_op jit(solution)/shard_map/back/pallas_call | solution.py:398
  39.8 4.7 %collective-permute-done.7.refs_0_ = bf16[1280,256]{1,0:T(8,128)(2,1)} collective-permute-done((bf16[1280,256]{1,0:T(8,128)(2,1)}, bf16[1280,256]{1,0:T(8,128)(2,1)}, u32[]{:S(2)}, u32[]{:S(2)}) %collective-permute-start.7) | collective-permute-done | bytes 655392 | tf_op jit(solution)/shard_map/ppermute | solution.py:657
  44.5 1.7 %collective-permute-start.8 = (bf16[768,256]{1,0:T(8,128)(2,1)}, bf16[768,256]{1,0:T(8,128)(2,1)}, u32[]{:S(2)}, u32[]{:S(2)}) collective-permute-start(bf16[768,256]{1,0:T(8,128)(2,1)} %gate.6.refs_0_), channel_id=1, source_target_pairs={{0,8},{4,12},{8,0},{12,4},{1,9},{5,13},{9,1},{13,5},{2,10},{6,14},... | collective-permute-start | bytes 1179656 | tf_op jit(solution)/shard_map/ppermute | solution.py:657
  46.2 0.0 collective-permute-start.11
  46.2 0.0 collective-permute-done.1.rest_0_.refs_3_
  46.2 0.5 collective-permute-start.12
  46.7 0.0 collective-permute-done.2.rest_1_.refs_4_
  46.8 9.3 %collective-permute-done.other_ref.refs_0_ = bf16[912,256]{1,0:T(8,128)(2,1)} collective-permute-done((bf16[912,256]{1,0:T(8,128)(2,1)}, bf16[912,256]{1,0:T(8,128)(2,1)}, u32[]{:S(2)}, u32[]{:S(2)}) %collective-permute-start) | collective-permute-done | bytes 466976 | tf_op jit(solution)/shard_map/ppermute | solution.py:682
  56.1 2.1 %join.1 = (bf16[912,256]{1,0:T(8,128)(2,1)}, f32[8,128]{1,0:T(8,128)}) custom-call(bf16[912,256]{1,0:T(8,128)(2,1)} %get-tuple-element.43.inner_ref, bf16[912,256]{1,0:T(8,128)(2,1)} %collective-permute-done.other_ref.refs_0_, bf16[912,256]{1,0:T(8,128)(2,1)} %back.1.end_ref.refs_2_, bf16[912,256]{1,0:T(8,128)(2,1)} %collective-permute-done.1.rest_0_.refs_3_, ...), custom_call_target="tpu_custom_call" | custom-call | flops 1000000 | bytes 100000 | tf_op jit(solution)/shard_map/join/pallas_call | solution.py:534
  58.2 2.6 %collective-permute-start.3 = (bf16[912,256]{1,0:T(8,128)(2,1)}, bf16[912,256]{1,0:T(8,128)(2,1)}, u32[]{:S(2)}, u32[]{:S(2)}) collective-permute-start(bf16[912,256]{1,0:T(8,128)(2,1)} %get-tuple-element.44), channel_id=1, source_target_pairs={{1,3},{2,0},{0,1},{3,2},{5,7},{6,4},{4,5},{7,6},{9,11},{10,8},{8,9... | collective-permute-start | bytes 1400840 | tf_op jit(solution)/shard_map/ppermute | solution.py:693
  60.7 0.0 collective-permute-done.8.refs_1_
  60.7 0.0 collective-permute-start.10
  60.7 0.5 collective-permute-start.9
  61.3 0.0 collective-permute-done.11.refs_6_
  61.3 0.0 collective-permute-done.12.refs_7_
  61.3 7.1 %weights.2 = (f32[896,1024]{1,0:T(8,128)}, f32[896,512]{1,0:T(8,128)}, f32[896,512]{1,0:T(8,128)}, f32[8,128]{1,0:T(8,128)}) custom-call(bf16[896,256]{1,0:T(8,128)(2,1)} %get-tuple-element.45.refs_0_, bf16[896,256]{1,0:T(8,128)(2,1)} %collective-permute-done.4.refs_2_.refs_1_, bf16[896,256]{1,0:T(8,128)(2,1)} %collective-permute-done.5.refs_1_.refs_2_, ...), custom_call_target="tpu_custom_call" | custom-call | flops 1000000 | bytes 100000 | tf_op jit(solution)/shard_map/weights/pallas_call | solution.py:472
  68.3 0.0 collective-permute-done.10.refs_7_
  68.4 0.0 collective-permute-done.9.refs_6_
  68.4 5.4 %weights.3 = (f32[896,1024]{1,0:T(8,128)}, f32[896,512]{1,0:T(8,128)}, f32[896,512]{1,0:T(8,128)}, f32[8,128]{1,0:T(8,128)}) custom-call(bf16[896,256]{1,0:T(8,128)(2,1)} %get-tuple-element.45.refs_0_, bf16[896,256]{1,0:T(8,128)(2,1)} %collective-permute-done.4.refs_2_.refs_1_, ...), custom_call_target="tpu_custom_call", output_to_operand_aliasing={{0}: (8, {}), {1}: (9, {}), {2}: (10, {})} | custom-call | flops 1000000 | bytes 100000 | tf_op jit(solution)/shard_map/weights/pallas_call | solution.py:472
  73.8 0.0 collective-permute-done.3.refs_5_
  73.8 3.1 %gains.1 = (f32[1,896]{1,0:T(1,128)}, f32[256,896]{1,0:T(8,128)}) custom-call(bf16[256,896]{1,0:T(8,128)(2,1)} %get-tuple-element.36.input_ref, f32[256,1]{1,0:T(8,128)} %get-tuple-element.35.inverse_ref, bf16[912,256]{1,0:T(8,128)(2,1)} %collective-permute-done.other_ref.refs_0_, bf16[912,256]{1,0:T(8,128)(2,1)} %get-tuple-element.38.refs_1_, ...), custom_call_target="tpu_custom_call" | custom-call | flops 1000000 | bytes 100000 | tf_op jit(solution)/shard_map/gains/pallas_call | solution.py:578
  76.9 0.1 collective-permute-start.13
  77.0 0.6 collective-permute-start.14
  77.6 1.3 %collective-permute-start.15 = (f32[1,896]{1,0:T(1,128)}, f32[1,896]{1,0:T(1,128)}, u32[]{:S(2)}, u32[]{:S(2)}) collective-permute-start(f32[1,896]{1,0:T(1,128)} %get-tuple-element.64.refs_0_), channel_id=1, source_target_pairs={{0,12},{4,8},{8,4},{12,0},{1,13},{5,9},{9,5},{13,1},{2,14},{6,10},... | collective-permute-start | bytes 10760 | tf_op jit(solution)/shard_map/ppermute | solution.py:657
  78.9 2.4 %finish.1 = bf16[256,896]{1,0:T(8,128)(2,1)} custom-call(f32[256,896]{1,0:T(8,128)} %get-tuple-element.59.total_ref, bf16[256,896]{1,0:T(8,128)(2,1)} %get-tuple-element.36.input_ref, f32[1,896]{1,0:T(1,128)} %get-tuple-element.60.gain_ref, f32[256,1]{1,0:T(8,128)} %get-tuple-element.35.inverse_ref, bf16[912,256]{1,0:T(8,128)(2,1)} %collective-permute-done.other_ref.refs_0_, ...), custom_call_target="tpu_custom_call" | custom-call | flops 1000000 | bytes 100000 | tf_op jit(solution)/shard_map/finish/pallas_call | solution.py:615
  81.3 0.0 collective-permute-done.13.refs_1_
  81.3 0.0 collective-permute-done.14.refs_2_
  81.3 0.0 collective-permute-done.15.refs_3_
  81.3 1.3 %total.1 = f32[896]{0:T(1024)} custom-call(f32[1,896]{1,0:T(1,128)} %get-tuple-element.64.refs_0_, f32[1,896]{1,0:T(1,128)} %collective-permute-done.13.refs_1_, f32[1,896]{1,0:T(1,128)} %collective-permute-done.14.refs_2_, f32[1,896]{1,0:T(1,128)} %collective-permute-done.15.refs_3_, f32[8,128]{1,0:T(8,128)} %get-tuple-element.58.refs_6_.refs_4_), custom_call_target="tpu_custom_call" | custom-call | flops 1000000 | bytes 100000 | tf_op jit(solution)/shard_map/total/pallas_call | solution.py:641
  (4 shorter events, 0.0 us)
Async XLA Ops:
  4.1 21.7 %collective-permute-start.4 = (bf16[896,256]{1,0:T(8,128)(2,1)}, bf16[896,256]{1,0:T(8,128)(2,1)}, u32[]{:S(2)}, u32[]{:S(2)}) collective-permute-start(bf16[896,256]{1,0:T(8,128)(2,1)} %get-tuple-element.46), channel_id=1, source_target_pairs={{0,8},{4,12},{8,0},{12,4},{1,9},{5,13},{9,1},{13,5},{2,10},{6,14},... | collective-permute-start | bytes 1376264 | tf_op jit(solution)/shard_map/ppermute | solution.py:657
  7.1 18.7 %collective-permute-start.5 = (bf16[896,256]{1,0:T(8,128)(2,1)}, bf16[896,256]{1,0:T(8,128)(2,1)}, u32[]{:S(2)}, u32[]{:S(2)}) collective-permute-start(bf16[896,256]{1,0:T(8,128)(2,1)} %get-tuple-element.47), channel_id=1, source_target_pairs={{0,4},{4,0},{8,12},{12,8},{1,5},{5,1},{9,13},{13,9},{2,6},{6,2},{1... | collective-permute-start | bytes 1376264 | tf_op jit(solution)/shard_map/ppermute | solution.py:657
  7.1 19.9 %collective-permute-start.6 = (bf16[896,256]{1,0:T(8,128)(2,1)}, bf16[896,256]{1,0:T(8,128)(2,1)}, u32[]{:S(2)}, u32[]{:S(2)}) collective-permute-start(bf16[896,256]{1,0:T(8,128)(2,1)} %get-tuple-element.48), channel_id=1, source_target_pairs={{0,12},{4,8},{8,4},{12,0},{1,13},{5,9},{9,5},{13,1},{2,14},{6,10},... | collective-permute-start | bytes 1376264 | tf_op jit(solution)/shard_map/ppermute | solution.py:657
  27.0 17.5 %collective-permute-start.7 = (bf16[1280,256]{1,0:T(8,128)(2,1)}, bf16[1280,256]{1,0:T(8,128)(2,1)}, u32[]{:S(2)}, u32[]{:S(2)}) collective-permute-start(bf16[1280,256]{1,0:T(8,128)(2,1)} %gate.4.refs_1_), channel_id=1, source_target_pairs={{0,8},{4,12},{8,0},{12,4},{1,9},{5,13},{9,1},{13,5},{2,10},{6,14},... | collective-permute-start | bytes 1966088 | tf_op jit(solution)/shard_map/ppermute | solution.py:657
  28.3 17.9 %collective-permute-start.1 = (bf16[912,256]{1,0:T(8,128)(2,1)}, bf16[912,256]{1,0:T(8,128)(2,1)}, u32[]{:S(2)}, u32[]{:S(2)}) collective-permute-start(bf16[912,256]{1,0:T(8,128)(2,1)} %get-tuple-element.38.refs_1_), channel_id=1, source_target_pairs={{1,2},{2,1},{5,6},{6,5},{9,10},{10,9},{13,14},{14,13},{17,18},{18,... | collective-permute-start | bytes 1400840 | tf_op jit(solution)/shard_map/ppermute | solution.py:683
  29.8 17.0 %collective-permute-start.2 = (bf16[912,256]{1,0:T(8,128)(2,1)}, bf16[912,256]{1,0:T(8,128)(2,1)}, u32[]{:S(2)}, u32[]{:S(2)}) collective-permute-start(bf16[912,256]{1,0:T(8,128)(2,1)} %get-tuple-element.43.inner_ref), channel_id=1, source_target_pairs={{0,2},{3,1},{4,6},{7,5},{8,10},{11,9},{12,14},{15,13},{16,18},{19,... | collective-permute-start | bytes 1400840 | tf_op jit(solution)/shard_map/ppermute | solution.py:684
  35.9 20.1 %collective-permute-start = (bf16[912,256]{1,0:T(8,128)(2,1)}, bf16[912,256]{1,0:T(8,128)(2,1)}, u32[]{:S(2)}, u32[]{:S(2)}) collective-permute-start(bf16[912,256]{1,0:T(8,128)(2,1)} %get-tuple-element.37), channel_id=1, source_target_pairs={{0,1},{1,0},{2,3},{3,2},{4,5},{5,4},{6,7},{7,6},{8,9},{9,8},{10,11... | collective-permute-start | bytes 1400840 | tf_op jit(solution)/shard_map/ppermute | solution.py:682
  44.5 16.2 %collective-permute-start.8 = (bf16[768,256]{1,0:T(8,128)(2,1)}, bf16[768,256]{1,0:T(8,128)(2,1)}, u32[]{:S(2)}, u32[]{:S(2)}) collective-permute-start(bf16[768,256]{1,0:T(8,128)(2,1)} %gate.6.refs_0_), channel_id=1, source_target_pairs={{0,8},{4,12},{8,0},{12,4},{1,9},{5,13},{9,1},{13,5},{2,10},{6,14},... | collective-permute-start | bytes 1179656 | tf_op jit(solution)/shard_map/ppermute | solution.py:657
  46.2 15.0 %collective-permute-start.11 = (bf16[1280,256]{1,0:T(8,128)(2,1)}, bf16[1280,256]{1,0:T(8,128)(2,1)}, u32[]{:S(2)}, u32[]{:S(2)}) collective-permute-start(bf16[1280,256]{1,0:T(8,128)(2,1)} %get-tuple-element.54.refs_4_), channel_id=1, source_target_pairs={{0,4},{4,0},{8,12},{12,8},{1,5},{5,1},{9,13},{13,9},{2,6},{6,2},{1... | collective-permute-start | bytes 1966088 | tf_op jit(solution)/shard_map/ppermute | solution.py:657
  46.2 15.0 %collective-permute-start.12 = (bf16[1280,256]{1,0:T(8,128)(2,1)}, bf16[1280,256]{1,0:T(8,128)(2,1)}, u32[]{:S(2)}, u32[]{:S(2)}) collective-permute-start(bf16[1280,256]{1,0:T(8,128)(2,1)} %get-tuple-element.51.refs_1_.refs_5_), channel_id=1, source_target_pairs={{0,4},{4,0},{8,12},{12,8},{1,5},{5,1},{9,13},{13,9},{2,6},{6,2},{1... | collective-permute-start | bytes 1966088 | tf_op jit(solution)/shard_map/ppermute | solution.py:657
  58.2 15.6 %collective-permute-start.3 = (bf16[912,256]{1,0:T(8,128)(2,1)}, bf16[912,256]{1,0:T(8,128)(2,1)}, u32[]{:S(2)}, u32[]{:S(2)}) collective-permute-start(bf16[912,256]{1,0:T(8,128)(2,1)} %get-tuple-element.44), channel_id=1, source_target_pairs={{1,3},{2,0},{0,1},{3,2},{5,7},{6,4},{4,5},{7,6},{9,11},{10,8},{8,9... | collective-permute-start | bytes 1400840 | tf_op jit(solution)/shard_map/ppermute | solution.py:693
  60.7 7.6 %collective-permute-start.10 = (bf16[768,256]{1,0:T(8,128)(2,1)}, bf16[768,256]{1,0:T(8,128)(2,1)}, u32[]{:S(2)}, u32[]{:S(2)}) collective-permute-start(bf16[768,256]{1,0:T(8,128)(2,1)} %get-tuple-element.53.refs_5_), channel_id=1, source_target_pairs={{0,4},{4,0},{8,12},{12,8},{1,5},{5,1},{9,13},{13,9},{2,6},{6,2},{1... | collective-permute-start | bytes 1179656 | tf_op jit(solution)/shard_map/ppermute | solution.py:657
  60.7 7.6 %collective-permute-start.9 = (bf16[768,256]{1,0:T(8,128)(2,1)}, bf16[768,256]{1,0:T(8,128)(2,1)}, u32[]{:S(2)}, u32[]{:S(2)}) collective-permute-start(bf16[768,256]{1,0:T(8,128)(2,1)} %get-tuple-element.52.refs_4_), channel_id=1, source_target_pairs={{0,4},{4,0},{8,12},{12,8},{1,5},{5,1},{9,13},{13,9},{2,6},{6,2},{1... | collective-permute-start | bytes 1179656 | tf_op jit(solution)/shard_map/ppermute | solution.py:657
  76.9 4.3 %collective-permute-start.13 = (f32[1,896]{1,0:T(1,128)}, f32[1,896]{1,0:T(1,128)}, u32[]{:S(2)}, u32[]{:S(2)}) collective-permute-start(f32[1,896]{1,0:T(1,128)} %get-tuple-element.64.refs_0_), channel_id=1, source_target_pairs={{0,4},{4,0},{8,12},{12,8},{1,5},{5,1},{9,13},{13,9},{2,6},{6,2},{1... | collective-permute-start | bytes 10760 | tf_op jit(solution)/shard_map/ppermute | solution.py:657
  77.0 4.3 %collective-permute-start.14 = (f32[1,896]{1,0:T(1,128)}, f32[1,896]{1,0:T(1,128)}, u32[]{:S(2)}, u32[]{:S(2)}) collective-permute-start(f32[1,896]{1,0:T(1,128)} %get-tuple-element.64.refs_0_), channel_id=1, source_target_pairs={{0,8},{4,12},{8,0},{12,4},{1,9},{5,13},{9,1},{13,5},{2,10},{6,14},... | collective-permute-start | bytes 10760 | tf_op jit(solution)/shard_map/ppermute | solution.py:657
  77.6 3.7 %collective-permute-start.15 = (f32[1,896]{1,0:T(1,128)}, f32[1,896]{1,0:T(1,128)}, u32[]{:S(2)}, u32[]{:S(2)}) collective-permute-start(f32[1,896]{1,0:T(1,128)} %get-tuple-element.64.refs_0_), channel_id=1, source_target_pairs={{0,12},{4,8},{8,4},{12,0},{1,13},{5,9},{9,5},{13,1},{2,14},{6,10},... | collective-permute-start | bytes 10760 | tf_op jit(solution)/shard_map/ppermute | solution.py:657

commit v10 on v9

--- a/solution.py
+++ b/solution.py
@@ -424,11 +424,18 @@
                 turned_hbm[place], turned_ref.at[place], turned_sem.at[place]
             )
         )
-        loads.append(
-            pltpu.make_async_copy(delta_hbm[place], delta_ref.at[place], delta_sem.at[place])
-        )
     for load in loads:
         load.start()
+
+    def fetch(block, place):
+        lines = pl.ds(pl.multiple_of(block * rows, rows), rows)
+        return pltpu.make_async_copy(
+            delta_hbm[place].at[lines, :], delta_ref.at[place, lines, :], delta_sem.at[block, place]
+        )
+
+    for block in range(len(outs)):
+        for place in range(sources):
+            fetch(block, place).start()
     for load in loads:
         load.wait()
     stores = [
@@ -443,6 +450,8 @@
     def fill(block, carry):
         lines = pl.ds(pl.multiple_of(block * rows, rows), rows)
         total = None
+        for place in range(sources):
+            fetch(block, place).wait()
         for place in range(sources):
             term = nn_dot(turned_ref[place], delta_ref[place, lines, :])
             total = term if total is None else total + term
@@ -485,7 +494,7 @@
             pltpu.VMEM((sources, len(share) * rows, HEAD_DIM), jnp.bfloat16),
             pltpu.VMEM((len(share), depth, HEAD_DIM), jnp.float32),
             pltpu.SemaphoreType.DMA((sources,)),
-            pltpu.SemaphoreType.DMA((sources,)),
+            pltpu.SemaphoreType.DMA((len(share), sources)),
             pltpu.SemaphoreType.DMA((len(share),)),
         ],
         compiler_params=pltpu.CompilerParams(vmem_limit_bytes=VMEM_LIMIT),
@@ -513,8 +522,7 @@
 
 
 def join_kernel(inner_ref, other_ref, end_ref, *rest):
-    out_ref, token_ref = rest[-2:]
-    token_ref[...] = jnp.zeros_like(token_ref)
+    out_ref = rest[-1]
     index = lax.axis_index("tensor")
     inner = (index > 0) & (index < lax.axis_size("tensor") - 1)
 
@@ -533,12 +541,9 @@
     vmem = pl.BlockSpec(memory_space=pltpu.VMEM)
     return pl.pallas_call(
         join_kernel,
-        out_shape=(
-            jax.ShapeDtypeStruct(end_part.shape, end_part.dtype),
-            jax.ShapeDtypeStruct((8, 128), jnp.float32),
-        ),
+        out_shape=jax.ShapeDtypeStruct(end_part.shape, end_part.dtype),
         in_specs=[vmem] * 3 + [pl.BlockSpec(memory_space=pl.ANY)] * len(tokens),
-        out_specs=(vmem, vmem),
+        out_specs=vmem,
         compiler_params=pltpu.CompilerParams(vmem_limit_bytes=VMEM_LIMIT),
         cost_estimate=small_cost(),
         name="join",
@@ -685,13 +690,13 @@
     return from_first, from_inner, from_ends
 
 
-def scatter_end(parts, arrived, total):
+def scatter_end(parts, arrived, total, tokens):
     if total != 4:
-        return [parts[-1], *arrived], 0, 0, arrived[0]
+        return [parts[-1], *arrived], 0, 0
     from_first, from_inner, from_ends = arrived
-    joined, token = join(parts[2], from_first, parts[3], (from_inner, from_ends))
+    joined = join(parts[2], from_first, parts[3], (from_inner, from_ends, *tokens))
     from_joined = lax.ppermute(joined, "tensor", [(1, 3), (2, 0), (0, 1), (3, 2)])
-    return [from_first, parts[1], parts[3], from_inner, from_ends, from_joined], 2, 1, token
+    return [from_first, parts[1], parts[3], from_inner, from_ends, from_joined], 2, 1
 
 
 def local(layer_input, norm_gain, w_query, w_key, w_value, head_grad, parents, row_counts):
@@ -705,8 +710,8 @@
     kv_local = w_key.shape[1] // HEAD_DIM
     offsets = [(shift, swap) for shift in range(chips) for swap in range(2)]
     blocks = list(range(kv_local * (group + 2)))
-    early = blocks[: group + 2] + [h * (group + 2) + group for h in range(1, kv_local)]
-    shares = [early, [block for block in blocks if block not in early]]
+    early = len(blocks) * 3 // 8
+    shares = [blocks[:early], blocks[early:]]
     shares = [share for share in shares if share]
 
     def targets():
@@ -744,20 +749,16 @@
         )
     arrived = scatter_begin(parts, tensor_total)
 
-    (first,) = gate(deltas[:1], (near, *direct, *across))
-    sent = [branch_send(first, chips, s, 0) for s in range(1, chips)]
-    parts, for_ends, for_inner, met = scatter_end(parts, arrived, tensor_total)
-    *sent, first = gate((*sent, first), parts[2:3])
-    others = gate(deltas[1:], (sent[0],)) if deltas[1:] else ()
+    deltas = gate(deltas, (near, *direct, *across))
+    sent = [[branch_send(delta, chips, s, 0) for s in range(1, chips)] for delta in deltas]
     weights, tokens = None, []
-    for share, delta in zip(shares, (first, *others)):
-        if tokens:
-            sent = [branch_send(delta, chips, s, 0) for s in range(1, chips)]
-            delta, *sent = gate((delta, *sent), ())
-        gathered = [delta] + sent
+    for share, delta, arrivals in zip(shares, deltas, sent):
+        delta, *arrivals = gate((delta, *arrivals), () if tokens else (*parts[3:4], *arrived[:2]))
+        gathered = [delta] + arrivals
         gathered += [branch_send(part, chips, 0, 1) for part in gathered]
         *weights, token = weight_gradients(turned, gathered, share, kv_local, group, weights)
         tokens.append(token)
+    parts, for_ends, for_inner = scatter_end(parts, arrived, tensor_total, tokens[:1])
 
     add = functools.partial(add_parts, for_ends, for_inner)
     gain_sum, total = gain_sums(add, input_columns, inverse, parts, tokens[-1])

time: 82.9 us -> 90.3 us (1.089)
  waiting for transfers between devices: 15.2 us -> 24.3 us
  starting transfers between devices: 19.3 us -> 17.3 us
    ppermute x12, waiting for transfers between devices: 5.85 us -> 15.7 us  [branch_send(): return lax.ppermute(array, 'branch', pairs)]
    ppermute x1, waiting for transfers between devices: 9.32 us -> 2.27 us  [scatter_begin(): lax.ppermute(parts[0], 'tensor', [(0, 1), (1, 0), (2, 3), (3, 2)])]
    ppermute x1, waiting for transfers between devices: 0.01 us -> 6.26 us  [scatter_end(): lax.ppermute(joined, 'tensor', [(1, 3), (2, 0), (0, 1), (3, 2)])]
    ppermute x1, starting transfers between devices: 0.01 us -> 4.18 us  [scatter_begin(): lax.ppermute(parts[0], 'tensor', [(0, 1), (1, 0), (2, 3), (3, 2)])]
    ppermute x1, starting transfers between devices: 6.18 us -> 3.14 us  [scatter_begin(): from_ends = lax.ppermute(parts[2], 'tensor', [(0, 2), (3, 1)])]
    ppermute x1, starting transfers between devices: 2.56 us -> 0.39 us  [scatter_end(): lax.ppermute(joined, 'tensor', [(1, 3), (2, 0), (0, 1), (3, 2)])]
    ppermute x12, starting transfers between devices: 9.12 us -> 8.14 us  [branch_send(): return lax.ppermute(array, 'branch', pairs)]
  transfers between devices with their start and end apart: 16 -> 16, of which waited for: 3 -> 6; matrix products, arithmetic and copies ran while one was open for 0% -> 0% of each run, Pallas kernels for 48% -> 44%
where the time goes in v10:
time: 90.3 us; the launch traced here: 89.9 us
  Pallas kernels  47.7 us (53%)
  waiting for transfers between devices  24.3 us (27%)
  starting transfers between devices  17.3 us (19%)
    pallas_call x1, Pallas kernels, attention_backward(): pl.pallas_call(functools.partial(attention_kernel, slots, group, kv_local...  18.6 us
    ppermute x12, waiting for transfers between devices, branch_send(): return lax.ppermute(array, 'branch', pairs)  15.7 us
    pallas_call x2, Pallas kernels, weight_gradients(): pl.pallas_call(functools.partial(weight_kernel, outs, sources), out_shape...  12.9 us
    ppermute x12, starting transfers between devices, branch_send(): return lax.ppermute(array, 'branch', pairs)  8.14 us
    ppermute x1, waiting for transfers between devices, scatter_end(): lax.ppermute(joined, 'tensor', [(1, 3), (2, 0), (0, 1), (3, 2)])  6.26 us
    ppermute x1, starting transfers between devices, scatter_begin(): lax.ppermute(parts[0], 'tensor', [(0, 1), (1, 0), (2, 3), (3, 2)])  4.18 us
    pallas_call x1, Pallas kernels, back_project(): pl.pallas_call(back_kernel, out_shape=(jax.ShapeDtypeStruct((depth + CENT...  3.9 us
    pallas_call x1, Pallas kernels, normalize(): pl.pallas_call(functools.partial(norm_kernel, targets), out_shape=(jax.Sh...  3.44 us
  transfers between devices with their start and end apart: 16, of which 6 were waited for; matrix products, arithmetic and copies ran while one was open for 0% of the time, Pallas kernels for 44%

profile of v10, /device:TPU:0, one launch (start us, length us, event | category | flops | bytes accessed | tf_op | source)
XLA Modules:
  0.0 89.9 jit_solution(16051901262122124539)
XLA Ops:
  0.6 3.4 %norm.1 = (f32[256,1]{1,0:T(8,128)}, bf16[896,256]{1,0:T(8,128)(2,1)}, bf16[896,256]{1,0:T(8,128)(2,1)}, bf16[896,256]{1,0:T(8,128)(2,1)}, bf16[896,256]{1,0:T(8,128)(2,1)}) custom-call(bf16[256,3584]{1,0:T(8,128)(2,1)} %input_hbm.1, f32[3584]{0:T(1024)} %gain_ref.3), custom_call_target="tpu_custom_call" | custom-call | flops 1000000 | bytes 100000 | tf_op jit(solution)/shard_map/norm/pallas_call | solution.py:59
  4.1 2.9 %collective-permute-start.3 = (bf16[896,256]{1,0:T(8,128)(2,1)}, bf16[896,256]{1,0:T(8,128)(2,1)}, u32[]{:S(2)}, u32[]{:S(2)}) collective-permute-start(bf16[896,256]{1,0:T(8,128)(2,1)} %get-tuple-element.47), channel_id=1, source_target_pairs={{0,8},{4,12},{8,0},{12,4},{1,9},{5,13},{9,1},{13,5},{2,10},{6,14},... | collective-permute-start | bytes 1376264 | tf_op jit(solution)/shard_map/ppermute | solution.py:662
  7.0 0.0 collective-permute-start.4
  7.0 0.2 collective-permute-start.5
  7.2 18.6 %attention.1 = (bf16[768,256]{1,0:T(8,128)(2,1)}, bf16[1280,256]{1,0:T(8,128)(2,1)}, bf16[912,256]{1,0:T(8,128)(2,1)}, bf16[912,256]{1,0:T(8,128)(2,1)}, bf16[91...) custom-call(s32[8]{0:T(128)} %count_ref.1, ...), custom_call_target="tpu_custom_call" | custom-call | flops 1000000 | bytes 100000 | tf_op jit(solution)/shard_map/attention/pallas_call | solution.py:319
  25.8 1.4 %collective-permute-start.1 = (bf16[912,256]{1,0:T(8,128)(2,1)}, bf16[912,256]{1,0:T(8,128)(2,1)}, u32[]{:S(2)}, u32[]{:S(2)}) collective-permute-start(bf16[912,256]{1,0:T(8,128)(2,1)} %get-tuple-element.40.refs_1_), channel_id=1, source_target_pairs={{1,2},{2,1},{5,6},{6,5},{9,10},{10,9},{13,14},{14,13},{17,18},{18,... | collective-permute-start | bytes 1400840 | tf_op jit(solution)/shard_map/ppermute | solution.py:688
  27.2 4.2 %collective-permute-start = (bf16[912,256]{1,0:T(8,128)(2,1)}, bf16[912,256]{1,0:T(8,128)(2,1)}, u32[]{:S(2)}, u32[]{:S(2)}) collective-permute-start(bf16[912,256]{1,0:T(8,128)(2,1)} %get-tuple-element.39), channel_id=1, source_target_pairs={{0,1},{1,0},{2,3},{3,2},{4,5},{5,4},{6,7},{7,6},{8,9},{9,8},{10,11... | collective-permute-start | bytes 1400840 | tf_op jit(solution)/shard_map/ppermute | solution.py:687
  31.4 0.0 collective-permute-done.3.refs_3_.refs_1_
  31.4 0.0 collective-permute-done.4.refs_2_
  31.4 0.0 collective-permute-done.5.refs_4_.refs_3_
  31.4 1.6 %collective-permute-start.10 = (bf16[1280,256]{1,0:T(8,128)(2,1)}, bf16[1280,256]{1,0:T(8,128)(2,1)}, u32[]{:S(2)}, u32[]{:S(2)}) collective-permute-start(bf16[1280,256]{1,0:T(8,128)(2,1)} %get-tuple-element.56.refs_0_), channel_id=1, source_target_pairs={{0,8},{4,12},{8,0},{12,4},{1,9},{5,13},{9,1},{13,5},{2,10},{6,14},... | collective-permute-start | bytes 1966088 | tf_op jit(solution)/shard_map/ppermute | solution.py:662
  33.0 0.5 collective-permute-start.6
  33.5 3.1 %collective-permute-start.2 = (bf16[912,256]{1,0:T(8,128)(2,1)}, bf16[912,256]{1,0:T(8,128)(2,1)}, u32[]{:S(2)}, u32[]{:S(2)}) collective-permute-start(bf16[912,256]{1,0:T(8,128)(2,1)} %get-tuple-element.45.inner_ref), channel_id=1, source_target_pairs={{0,2},{3,1},{4,6},{7,5},{8,10},{11,9},{12,14},{15,13},{16,18},{19,... | collective-permute-start | bytes 1400840 | tf_op jit(solution)/shard_map/ppermute | solution.py:689
  36.6 3.9 %back.1.refs_2_.end_ref = bf16[912,256]{1,0:T(8,128)(2,1)} custom-call(bf16[16,256]{1,0:T(8,128)(2,1)} %get-tuple-element.41.centre_ref, bf16[1024,256]{1,0:T(8,128)(2,1)} %get-tuple-element.42.refs_0_, bf16[512,256]{1,0:T(8,128)(2,1)} %get-tuple-element.43.refs_1_, bf16[512,256]{1,0:T(8,128)(2,1)} %get-tuple-element.44.refs_2_, bf16[3584,1024]{1,0:T(8,128)(2,1)} %refs_3_.1, ...), custom_call_target="tpu_custom_call" | custom-call | flops 1000000 | bytes 100000 | tf_op jit(solution)/shard_map/back/pallas_call | solution.py:398
  40.5 0.0 collective-permute-done.1.refs_4_.rest_0_.refs_3_
  40.5 2.3 %collective-permute-done.refs_3_.other_ref.refs_0_ = bf16[912,256]{1,0:T(8,128)(2,1)} collective-permute-done((bf16[912,256]{1,0:T(8,128)(2,1)}, bf16[912,256]{1,0:T(8,128)(2,1)}, u32[]{:S(2)}, u32[]{:S(2)}) %collective-permute-start) | collective-permute-done | bytes 466976 | tf_op jit(solution)/shard_map/ppermute | solution.py:687
  42.8 13.5 %collective-permute-done.6.refs_1_ = bf16[768,256]{1,0:T(8,128)(2,1)} collective-permute-done((bf16[768,256]{1,0:T(8,128)(2,1)}, bf16[768,256]{1,0:T(8,128)(2,1)}, u32[]{:S(2)}, u32[]{:S(2)}) %collective-permute-start.6) | collective-permute-done | bytes 393248 | tf_op jit(solution)/shard_map/ppermute | solution.py:662
  56.3 0.0 collective-permute-start.7
  56.3 0.5 collective-permute-start.8
  56.8 0.0 collective-permute-done.10.refs_1_
  56.8 0.0 collective-permute-start.11
  56.8 0.5 collective-permute-start.12
  57.3 1.0 %collective-permute-done.7.refs_6_ = bf16[768,256]{1,0:T(8,128)(2,1)} collective-permute-done((bf16[768,256]{1,0:T(8,128)(2,1)}, bf16[768,256]{1,0:T(8,128)(2,1)}, u32[]{:S(2)}, u32[]{:S(2)}) %collective-permute-start.7) | collective-permute-done | bytes 393248 | tf_op jit(solution)/shard_map/ppermute | solution.py:662
  58.4 0.6 collective-permute-done.8.refs_7_
  58.9 5.6 %weights.2 = (f32[896,1024]{1,0:T(8,128)}, f32[896,512]{1,0:T(8,128)}, f32[896,512]{1,0:T(8,128)}, f32[8,128]{1,0:T(8,128)}) custom-call(bf16[896,256]{1,0:T(8,128)(2,1)} %get-tuple-element.46.refs_0_, bf16[896,256]{1,0:T(8,128)(2,1)} %collective-permute-done.3.refs_3_.refs_1_, bf16[896,256]{1,0:T(8,128)(2,1)} %collective-permute-done.4.refs_2_, ...), custom_call_target="tpu_custom_call" | custom-call | flops 1000000 | bytes 100000 | tf_op jit(solution)/shard_map/weights/pallas_call | solution.py:481
  64.5 0.0 collective-permute-done.2.rest_1_.refs_4_
  64.5 2.1 %join.1 = bf16[912,256]{1,0:T(8,128)(2,1)} custom-call(bf16[912,256]{1,0:T(8,128)(2,1)} %get-tuple-element.45.inner_ref, bf16[912,256]{1,0:T(8,128)(2,1)} %collective-permute-done.refs_3_.other_ref.refs_0_, bf16[912,256]{1,0:T(8,128)(2,1)} %back.1.refs_2_.end_ref, bf16[912,256]{1,0:T(8,128)(2,1)} %collective-permute-done.1.refs_4_.rest_0_.refs_3_, ...), custom_call_target="tpu_custom_call" | custom-call | flops 1000000 | bytes 100000 | tf_op jit(solution)/shard_map/join/pallas_call | solution.py:542
  66.7 0.4 collective-permute-start.9
  67.0 0.0 collective-permute-done.11.refs_6_
  67.1 0.0 collective-permute-done.12.refs_7_
  67.1 7.3 %weights.3 = (f32[896,1024]{1,0:T(8,128)}, f32[896,512]{1,0:T(8,128)}, f32[896,512]{1,0:T(8,128)}, f32[8,128]{1,0:T(8,128)}) custom-call(bf16[896,256]{1,0:T(8,128)(2,1)} %get-tuple-element.46.refs_0_, bf16[896,256]{1,0:T(8,128)(2,1)} %collective-permute-done.3.refs_3_.refs_1_, ...), custom_call_target="tpu_custom_call", output_to_operand_aliasing={{0}: (8, {}), {1}: (9, {}), {2}: (10, {})} | custom-call | flops 1000000 | bytes 100000 | tf_op jit(solution)/shard_map/weights/pallas_call | solution.py:481
  74.4 6.3 %collective-permute-done.9.refs_5_ = bf16[912,256]{1,0:T(8,128)(2,1)} collective-permute-done((bf16[912,256]{1,0:T(8,128)(2,1)}, bf16[912,256]{1,0:T(8,128)(2,1)}, u32[]{:S(2)}, u32[]{:S(2)}) %collective-permute-start.9) | collective-permute-done | bytes 466976 | tf_op jit(solution)/shard_map/ppermute | solution.py:698
  80.6 3.1 %gains.1 = (f32[1,896]{1,0:T(1,128)}, f32[256,896]{1,0:T(8,128)}) custom-call(bf16[256,896]{1,0:T(8,128)(2,1)} %get-tuple-element.38.input_ref, f32[256,1]{1,0:T(8,128)} %get-tuple-element.37.inverse_ref, bf16[912,256]{1,0:T(8,128)(2,1)} %collective-permute-done.refs_3_.other_ref.refs_0_, bf16[912,256]{1,0:T(8,128)(2,1)} %get-tuple-element.40.refs_1_, ...), custom_call_target="tpu_custom_call" | custom-call | flops 1000000 | bytes 100000 | tf_op jit(solution)/shard_map/gains/pallas_call | solution.py:583
  83.7 0.1 collective-permute-start.13
  83.8 1.6 %collective-permute-start.14 = (f32[1,896]{1,0:T(1,128)}, f32[1,896]{1,0:T(1,128)}, u32[]{:S(2)}, u32[]{:S(2)}) collective-permute-start(f32[1,896]{1,0:T(1,128)} %get-tuple-element.68.refs_0_), channel_id=1, source_target_pairs={{0,8},{4,12},{8,0},{12,4},{1,9},{5,13},{9,1},{13,5},{2,10},{6,14},... | collective-permute-start | bytes 10760 | tf_op jit(solution)/shard_map/ppermute | solution.py:662
  85.3 0.3 collective-permute-start.15
  85.6 2.4 %finish.1 = bf16[256,896]{1,0:T(8,128)(2,1)} custom-call(f32[256,896]{1,0:T(8,128)} %get-tuple-element.63.total_ref, bf16[256,896]{1,0:T(8,128)(2,1)} %get-tuple-element.38.input_ref, f32[1,896]{1,0:T(1,128)} %get-tuple-element.64.gain_ref, f32[256,1]{1,0:T(8,128)} %get-tuple-element.37.inverse_ref, ...), custom_call_target="tpu_custom_call" | custom-call | flops 1000000 | bytes 100000 | tf_op jit(solution)/shard_map/finish/pallas_call | solution.py:620
  88.0 0.0 collective-permute-done.13.refs_1_
  88.0 0.0 collective-permute-done.14.refs_2_
  88.0 0.6 collective-permute-done.15.refs_3_
  88.7 1.3 %total.1 = f32[896]{0:T(1024)} custom-call(f32[1,896]{1,0:T(1,128)} %get-tuple-element.68.refs_0_, f32[1,896]{1,0:T(1,128)} %collective-permute-done.13.refs_1_, f32[1,896]{1,0:T(1,128)} %collective-permute-done.14.refs_2_, f32[1,896]{1,0:T(1,128)} %collective-permute-done.15.refs_3_, f32[8,128]{1,0:T(8,128)} %get-tuple-element.62.refs_6_.refs_4_), custom_call_target="tpu_custom_call" | custom-call | flops 1000000 | bytes 100000 | tf_op jit(solution)/shard_map/total/pallas_call | solution.py:646
  (3 shorter events, 0.0 us)
Async XLA Ops:
  4.1 27.3 %collective-permute-start.3 = (bf16[896,256]{1,0:T(8,128)(2,1)}, bf16[896,256]{1,0:T(8,128)(2,1)}, u32[]{:S(2)}, u32[]{:S(2)}) collective-permute-start(bf16[896,256]{1,0:T(8,128)(2,1)} %get-tuple-element.47), channel_id=1, source_target_pairs={{0,8},{4,12},{8,0},{12,4},{1,9},{5,13},{9,1},{13,5},{2,10},{6,14},... | collective-permute-start | bytes 1376264 | tf_op jit(solution)/shard_map/ppermute | solution.py:662
  7.0 24.4 %collective-permute-start.4 = (bf16[896,256]{1,0:T(8,128)(2,1)}, bf16[896,256]{1,0:T(8,128)(2,1)}, u32[]{:S(2)}, u32[]{:S(2)}) collective-permute-start(bf16[896,256]{1,0:T(8,128)(2,1)} %get-tuple-element.48), channel_id=1, source_target_pairs={{0,4},{4,0},{8,12},{12,8},{1,5},{5,1},{9,13},{13,9},{2,6},{6,2},{1... | collective-permute-start | bytes 1376264 | tf_op jit(solution)/shard_map/ppermute | solution.py:662
  7.0 24.4 %collective-permute-start.5 = (bf16[896,256]{1,0:T(8,128)(2,1)}, bf16[896,256]{1,0:T(8,128)(2,1)}, u32[]{:S(2)}, u32[]{:S(2)}) collective-permute-start(bf16[896,256]{1,0:T(8,128)(2,1)} %get-tuple-element.49), channel_id=1, source_target_pairs={{0,12},{4,8},{8,4},{12,0},{1,13},{5,9},{9,5},{13,1},{2,14},{6,10},... | collective-permute-start | bytes 1376264 | tf_op jit(solution)/shard_map/ppermute | solution.py:662
  25.8 14.8 %collective-permute-start.1 = (bf16[912,256]{1,0:T(8,128)(2,1)}, bf16[912,256]{1,0:T(8,128)(2,1)}, u32[]{:S(2)}, u32[]{:S(2)}) collective-permute-start(bf16[912,256]{1,0:T(8,128)(2,1)} %get-tuple-element.40.refs_1_), channel_id=1, source_target_pairs={{1,2},{2,1},{5,6},{6,5},{9,10},{10,9},{13,14},{14,13},{17,18},{18,... | collective-permute-start | bytes 1400840 | tf_op jit(solution)/shard_map/ppermute | solution.py:688
  27.2 15.6 %collective-permute-start = (bf16[912,256]{1,0:T(8,128)(2,1)}, bf16[912,256]{1,0:T(8,128)(2,1)}, u32[]{:S(2)}, u32[]{:S(2)}) collective-permute-start(bf16[912,256]{1,0:T(8,128)(2,1)} %get-tuple-element.39), channel_id=1, source_target_pairs={{0,1},{1,0},{2,3},{3,2},{4,5},{5,4},{6,7},{7,6},{8,9},{9,8},{10,11... | collective-permute-start | bytes 1400840 | tf_op jit(solution)/shard_map/ppermute | solution.py:687
  31.4 25.4 %collective-permute-start.10 = (bf16[1280,256]{1,0:T(8,128)(2,1)}, bf16[1280,256]{1,0:T(8,128)(2,1)}, u32[]{:S(2)}, u32[]{:S(2)}) collective-permute-start(bf16[1280,256]{1,0:T(8,128)(2,1)} %get-tuple-element.56.refs_0_), channel_id=1, source_target_pairs={{0,8},{4,12},{8,0},{12,4},{1,9},{5,13},{9,1},{13,5},{2,10},{6,14},... | collective-permute-start | bytes 1966088 | tf_op jit(solution)/shard_map/ppermute | solution.py:662
  33.0 23.3 %collective-permute-start.6 = (bf16[768,256]{1,0:T(8,128)(2,1)}, bf16[768,256]{1,0:T(8,128)(2,1)}, u32[]{:S(2)}, u32[]{:S(2)}) collective-permute-start(bf16[768,256]{1,0:T(8,128)(2,1)} %get-tuple-element.52.refs_0_), channel_id=1, source_target_pairs={{0,8},{4,12},{8,0},{12,4},{1,9},{5,13},{9,1},{13,5},{2,10},{6,14},... | collective-permute-start | bytes 1179656 | tf_op jit(solution)/shard_map/ppermute | solution.py:662
  33.5 31.0 %collective-permute-start.2 = (bf16[912,256]{1,0:T(8,128)(2,1)}, bf16[912,256]{1,0:T(8,128)(2,1)}, u32[]{:S(2)}, u32[]{:S(2)}) collective-permute-start(bf16[912,256]{1,0:T(8,128)(2,1)} %get-tuple-element.45.inner_ref), channel_id=1, source_target_pairs={{0,2},{3,1},{4,6},{7,5},{8,10},{11,9},{12,14},{15,13},{16,18},{19,... | collective-permute-start | bytes 1400840 | tf_op jit(solution)/shard_map/ppermute | solution.py:689
  56.3 2.1 %collective-permute-start.7 = (bf16[768,256]{1,0:T(8,128)(2,1)}, bf16[768,256]{1,0:T(8,128)(2,1)}, u32[]{:S(2)}, u32[]{:S(2)}) collective-permute-start(bf16[768,256]{1,0:T(8,128)(2,1)} %get-tuple-element.53.refs_4_), channel_id=1, source_target_pairs={{0,4},{4,0},{8,12},{12,8},{1,5},{5,1},{9,13},{13,9},{2,6},{6,2},{1... | collective-permute-start | bytes 1179656 | tf_op jit(solution)/shard_map/ppermute | solution.py:662
  56.3 2.6 %collective-permute-start.8 = (bf16[768,256]{1,0:T(8,128)(2,1)}, bf16[768,256]{1,0:T(8,128)(2,1)}, u32[]{:S(2)}, u32[]{:S(2)}) collective-permute-start(bf16[768,256]{1,0:T(8,128)(2,1)} %get-tuple-element.54.refs_5_), channel_id=1, source_target_pairs={{0,4},{4,0},{8,12},{12,8},{1,5},{5,1},{9,13},{13,9},{2,6},{6,2},{1... | collective-permute-start | bytes 1179656 | tf_op jit(solution)/shard_map/ppermute | solution.py:662
  56.8 10.2 %collective-permute-start.11 = (bf16[1280,256]{1,0:T(8,128)(2,1)}, bf16[1280,256]{1,0:T(8,128)(2,1)}, u32[]{:S(2)}, u32[]{:S(2)}) collective-permute-start(bf16[1280,256]{1,0:T(8,128)(2,1)} %get-tuple-element.57.refs_4_), channel_id=1, source_target_pairs={{0,4},{4,0},{8,12},{12,8},{1,5},{5,1},{9,13},{13,9},{2,6},{6,2},{1... | collective-permute-start | bytes 1966088 | tf_op jit(solution)/shard_map/ppermute | solution.py:662
  56.8 10.2 %collective-permute-start.12 = (bf16[1280,256]{1,0:T(8,128)(2,1)}, bf16[1280,256]{1,0:T(8,128)(2,1)}, u32[]{:S(2)}, u32[]{:S(2)}) collective-permute-start(bf16[1280,256]{1,0:T(8,128)(2,1)} %get-tuple-element.58.refs_5_), channel_id=1, source_target_pairs={{0,4},{4,0},{8,12},{12,8},{1,5},{5,1},{9,13},{13,9},{2,6},{6,2},{1... | collective-permute-start | bytes 1966088 | tf_op jit(solution)/shard_map/ppermute | solution.py:662
  66.7 14.0 %collective-permute-start.9 = (bf16[912,256]{1,0:T(8,128)(2,1)}, bf16[912,256]{1,0:T(8,128)(2,1)}, u32[]{:S(2)}, u32[]{:S(2)}) collective-permute-start(bf16[912,256]{1,0:T(8,128)(2,1)} %join.1), channel_id=1, source_target_pairs={{1,3},{2,0},{0,1},{3,2},{5,7},{6,4},{4,5},{7,6},{9,11},{10,8},{8,9... | collective-permute-start | bytes 1400840 | tf_op jit(solution)/shard_map/ppermute | solution.py:698
  83.7 4.3 %collective-permute-start.13 = (f32[1,896]{1,0:T(1,128)}, f32[1,896]{1,0:T(1,128)}, u32[]{:S(2)}, u32[]{:S(2)}) collective-permute-start(f32[1,896]{1,0:T(1,128)} %get-tuple-element.68.refs_0_), channel_id=1, source_target_pairs={{0,4},{4,0},{8,12},{12,8},{1,5},{5,1},{9,13},{13,9},{2,6},{6,2},{1... | collective-permute-start | bytes 10760 | tf_op jit(solution)/shard_map/ppermute | solution.py:662
  83.8 4.3 %collective-permute-start.14 = (f32[1,896]{1,0:T(1,128)}, f32[1,896]{1,0:T(1,128)}, u32[]{:S(2)}, u32[]{:S(2)}) collective-permute-start(f32[1,896]{1,0:T(1,128)} %get-tuple-element.68.refs_0_), channel_id=1, source_target_pairs={{0,8},{4,12},{8,0},{12,4},{1,9},{5,13},{9,1},{13,5},{2,10},{6,14},... | collective-permute-start | bytes 10760 | tf_op jit(solution)/shard_map/ppermute | solution.py:662
  85.3 3.3 %collective-permute-start.15 = (f32[1,896]{1,0:T(1,128)}, f32[1,896]{1,0:T(1,128)}, u32[]{:S(2)}, u32[]{:S(2)}) collective-permute-start(f32[1,896]{1,0:T(1,128)} %get-tuple-element.68.refs_0_), channel_id=1, source_target_pairs={{0,12},{4,8},{8,4},{12,0},{1,13},{5,9},{9,5},{13,1},{2,14},{6,10},... | collective-permute-start | bytes 10760 | tf_op jit(solution)/shard_map/ppermute | solution.py:662

commit v11 on v9

--- a/solution.py
+++ b/solution.py
@@ -424,11 +424,18 @@
                 turned_hbm[place], turned_ref.at[place], turned_sem.at[place]
             )
         )
-        loads.append(
-            pltpu.make_async_copy(delta_hbm[place], delta_ref.at[place], delta_sem.at[place])
-        )
     for load in loads:
         load.start()
+
+    def fetch(block, place):
+        lines = pl.ds(pl.multiple_of(block * rows, rows), rows)
+        return pltpu.make_async_copy(
+            delta_hbm[place].at[lines, :], delta_ref.at[place, lines, :], delta_sem.at[block, place]
+        )
+
+    for block in range(len(outs)):
+        for place in range(sources):
+            fetch(block, place).start()
     for load in loads:
         load.wait()
     stores = [
@@ -443,6 +450,8 @@
     def fill(block, carry):
         lines = pl.ds(pl.multiple_of(block * rows, rows), rows)
         total = None
+        for place in range(sources):
+            fetch(block, place).wait()
         for place in range(sources):
             term = nn_dot(turned_ref[place], delta_ref[place, lines, :])
             total = term if total is None else total + term
@@ -485,7 +494,7 @@
             pltpu.VMEM((sources, len(share) * rows, HEAD_DIM), jnp.bfloat16),
             pltpu.VMEM((len(share), depth, HEAD_DIM), jnp.float32),
             pltpu.SemaphoreType.DMA((sources,)),
-            pltpu.SemaphoreType.DMA((sources,)),
+            pltpu.SemaphoreType.DMA((len(share), sources)),
             pltpu.SemaphoreType.DMA((len(share),)),
         ],
         compiler_params=pltpu.CompilerParams(vmem_limit_bytes=VMEM_LIMIT),
@@ -753,14 +762,14 @@
     for share, delta in zip(shares, (first, *others)):
         if tokens:
             sent = [branch_send(delta, chips, s, 0) for s in range(1, chips)]
-            delta, *sent = gate((delta, *sent), ())
+            delta, *sent = gate((delta, *sent), (parts[-1], tokens[0]))
         gathered = [delta] + sent
         gathered += [branch_send(part, chips, 0, 1) for part in gathered]
         *weights, token = weight_gradients(turned, gathered, share, kv_local, group, weights)
         tokens.append(token)
 
     add = functools.partial(add_parts, for_ends, for_inner)
-    gain_sum, total = gain_sums(add, input_columns, inverse, parts, tokens[-1])
+    gain_sum, total = gain_sums(add, input_columns, inverse, parts, tokens[0])
     grad_input = finish(width, add, total, input_columns, gain_columns, inverse, parts)
     if chips == 2:
         sums = [gain_sum] + [branch_send(gain_sum, chips, s, e) for s, e in offsets[1:]]

time: 82.9 us -> 85.9 us (1.036)
  starting transfers between devices: 19.3 us -> 22.2 us
    ppermute x1, waiting for transfers between devices: 9.32 us -> 0.01 us  [scatter_begin(): lax.ppermute(parts[0], 'tensor', [(0, 1), (1, 0), (2, 3), (3, 2)])]
    ppermute x1, waiting for transfers between devices: 0.01 us -> 6.05 us  [scatter_begin(): from_ends = lax.ppermute(parts[2], 'tensor', [(0, 2), (3, 1)])]
    ppermute x1, waiting for transfers between devices: 0.01 us -> 4.16 us  [scatter_end(): lax.ppermute(joined, 'tensor', [(1, 3), (2, 0), (0, 1), (3, 2)])]
    ppermute x1, starting transfers between devices: 2.56 us -> 5.54 us  [scatter_end(): lax.ppermute(joined, 'tensor', [(1, 3), (2, 0), (0, 1), (3, 2)])]
    ppermute x1, starting transfers between devices: 0.01 us -> 1.58 us  [scatter_begin(): lax.ppermute(parts[0], 'tensor', [(0, 1), (1, 0), (2, 3), (3, 2)])]
    ppermute x12, starting transfers between devices: 9.12 us -> 7.94 us  [branch_send(): return lax.ppermute(array, 'branch', pairs)]
    ppermute x12, waiting for transfers between devices: 5.85 us -> 4.72 us  [branch_send(): return lax.ppermute(array, 'branch', pairs)]
  transfers between devices with their start and end apart: 16 -> 16, of which waited for: 3 -> 4; matrix products, arithmetic and copies ran while one was open for 0% -> 0% of each run, Pallas kernels for 48% -> 50%
where the time goes in v11:
time: 85.9 us; the launch traced here: 85.6 us
  Pallas kernels  47.7 us (56%)
  starting transfers between devices  22.2 us (26%)
  waiting for transfers between devices  14.9 us (17%)
    pallas_call x1, Pallas kernels, attention_backward(): pl.pallas_call(functools.partial(attention_kernel, slots, group, kv_local...  18.6 us
    pallas_call x2, Pallas kernels, weight_gradients(): pl.pallas_call(functools.partial(weight_kernel, outs, sources), out_shape...  12.9 us
    ppermute x12, starting transfers between devices, branch_send(): return lax.ppermute(array, 'branch', pairs)  7.94 us
    ppermute x1, waiting for transfers between devices, scatter_begin(): from_ends = lax.ppermute(parts[2], 'tensor', [(0, 2), (3, 1)])  6.05 us
    ppermute x1, starting transfers between devices, scatter_begin(): from_ends = lax.ppermute(parts[2], 'tensor', [(0, 2), (3, 1)])  5.74 us
    ppermute x1, starting transfers between devices, scatter_end(): lax.ppermute(joined, 'tensor', [(1, 3), (2, 0), (0, 1), (3, 2)])  5.54 us
    ppermute x12, waiting for transfers between devices, branch_send(): return lax.ppermute(array, 'branch', pairs)  4.72 us
    ppermute x1, waiting for transfers between devices, scatter_end(): lax.ppermute(joined, 'tensor', [(1, 3), (2, 0), (0, 1), (3, 2)])  4.16 us
  transfers between devices with their start and end apart: 16, of which 4 were waited for; matrix products, arithmetic and copies ran while one was open for 0% of the time, Pallas kernels for 50%

profile of v11, /device:TPU:0, one launch (start us, length us, event | category | flops | bytes accessed | tf_op | source)
XLA Modules:
  0.0 85.6 jit_solution(1744466146591882758)
XLA Ops:
  0.6 3.4 %norm.1 = (f32[256,1]{1,0:T(8,128)}, bf16[896,256]{1,0:T(8,128)(2,1)}, bf16[896,256]{1,0:T(8,128)(2,1)}, bf16[896,256]{1,0:T(8,128)(2,1)}, bf16[896,256]{1,0:T(8,128)(2,1)}) custom-call(bf16[256,3584]{1,0:T(8,128)(2,1)} %input_hbm.1, f32[3584]{0:T(1024)} %gain_ref.3), custom_call_target="tpu_custom_call" | custom-call | flops 1000000 | bytes 100000 | tf_op jit(solution)/shard_map/norm/pallas_call | solution.py:59
  4.1 2.9 %collective-permute-start.4 = (bf16[896,256]{1,0:T(8,128)(2,1)}, bf16[896,256]{1,0:T(8,128)(2,1)}, u32[]{:S(2)}, u32[]{:S(2)}) collective-permute-start(bf16[896,256]{1,0:T(8,128)(2,1)} %get-tuple-element.47), channel_id=1, source_target_pairs={{0,8},{4,12},{8,0},{12,4},{1,9},{5,13},{9,1},{13,5},{2,10},{6,14},... | collective-permute-start | bytes 1376264 | tf_op jit(solution)/shard_map/ppermute | solution.py:666
  7.0 0.0 collective-permute-start.5
  7.0 0.2 collective-permute-start.6
  7.2 18.6 %attention.1 = (bf16[1280,256]{1,0:T(8,128)(2,1)}, bf16[768,256]{1,0:T(8,128)(2,1)}, bf16[912,256]{1,0:T(8,128)(2,1)}, bf16[912,256]{1,0:T(8,128)(2,1)}, bf16[91...) custom-call(s32[8]{0:T(128)} %count_ref.1, ...), custom_call_target="tpu_custom_call" | custom-call | flops 1000000 | bytes 100000 | tf_op jit(solution)/shard_map/attention/pallas_call | solution.py:319
  25.7 0.0 collective-permute-done.4.refs_2_.refs_1_
  25.7 0.0 collective-permute-done.5.refs_1_.refs_2_
  25.8 1.2 %collective-permute-done.6.refs_3_ = bf16[896,256]{1,0:T(8,128)(2,1)} collective-permute-done((bf16[896,256]{1,0:T(8,128)(2,1)}, bf16[896,256]{1,0:T(8,128)(2,1)}, u32[]{:S(2)}, u32[]{:S(2)}) %collective-permute-start.6) | collective-permute-done | bytes 458784 | tf_op jit(solution)/shard_map/ppermute | solution.py:666
  26.9 1.3 %collective-permute-start.7 = (bf16[1280,256]{1,0:T(8,128)(2,1)}, bf16[1280,256]{1,0:T(8,128)(2,1)}, u32[]{:S(2)}, u32[]{:S(2)}) collective-permute-start(bf16[1280,256]{1,0:T(8,128)(2,1)} %gate.4.refs_1_), channel_id=1, source_target_pairs={{0,8},{4,12},{8,0},{12,4},{1,9},{5,13},{9,1},{13,5},{2,10},{6,14},... | collective-permute-start | bytes 1966088 | tf_op jit(solution)/shard_map/ppermute | solution.py:666
  28.3 1.6 %collective-permute-start = (bf16[912,256]{1,0:T(8,128)(2,1)}, bf16[912,256]{1,0:T(8,128)(2,1)}, u32[]{:S(2)}, u32[]{:S(2)}) collective-permute-start(bf16[912,256]{1,0:T(8,128)(2,1)} %get-tuple-element.38), channel_id=1, source_target_pairs={{0,1},{1,0},{2,3},{3,2},{4,5},{5,4},{6,7},{7,6},{8,9},{9,8},{10,11... | collective-permute-start | bytes 1400840 | tf_op jit(solution)/shard_map/ppermute | solution.py:691
  29.8 1.4 %collective-permute-start.1 = (bf16[912,256]{1,0:T(8,128)(2,1)}, bf16[912,256]{1,0:T(8,128)(2,1)}, u32[]{:S(2)}, u32[]{:S(2)}) collective-permute-start(bf16[912,256]{1,0:T(8,128)(2,1)} %get-tuple-element.39.refs_1_), channel_id=1, source_target_pairs={{1,2},{2,1},{5,6},{6,5},{9,10},{10,9},{13,14},{14,13},{17,18},{18,... | collective-permute-start | bytes 1400840 | tf_op jit(solution)/shard_map/ppermute | solution.py:692
  31.3 5.7 %collective-permute-start.2 = (bf16[912,256]{1,0:T(8,128)(2,1)}, bf16[912,256]{1,0:T(8,128)(2,1)}, u32[]{:S(2)}, u32[]{:S(2)}) collective-permute-start(bf16[912,256]{1,0:T(8,128)(2,1)} %get-tuple-element.44.inner_ref), channel_id=1, source_target_pairs={{0,2},{3,1},{4,6},{7,5},{8,10},{11,9},{12,14},{15,13},{16,18},{19,... | collective-permute-start | bytes 1400840 | tf_op jit(solution)/shard_map/ppermute | solution.py:693
  37.0 3.9 %back.1.end_ref.refs_2_ = bf16[912,256]{1,0:T(8,128)(2,1)} custom-call(bf16[16,256]{1,0:T(8,128)(2,1)} %get-tuple-element.40.centre_ref, bf16[1024,256]{1,0:T(8,128)(2,1)} %get-tuple-element.41.refs_0_, bf16[512,256]{1,0:T(8,128)(2,1)} %get-tuple-element.42.refs_1_, bf16[512,256]{1,0:T(8,128)(2,1)} %get-tuple-element.43.refs_2_, bf16[3584,1024]{1,0:T(8,128)(2,1)} %refs_3_.1, ...), custom_call_target="tpu_custom_call" | custom-call | flops 1000000 | bytes 100000 | tf_op jit(solution)/shard_map/back/pallas_call | solution.py:398
  40.9 3.5 %collective-permute-done.7.refs_0_ = bf16[1280,256]{1,0:T(8,128)(2,1)} collective-permute-done((bf16[1280,256]{1,0:T(8,128)(2,1)}, bf16[1280,256]{1,0:T(8,128)(2,1)}, u32[]{:S(2)}, u32[]{:S(2)}) %collective-permute-start.7) | collective-permute-done | bytes 655392 | tf_op jit(solution)/shard_map/ppermute | solution.py:666
  44.4 0.0 collective-permute-start.8
  44.4 0.5 collective-permute-start.9
  45.0 0.0 collective-permute-done.other_ref.refs_0_
  45.0 0.0 collective-permute-done.1.rest_0_.refs_3_
  45.0 6.1 %collective-permute-done.2.rest_1_.refs_4_ = bf16[912,256]{1,0:T(8,128)(2,1)} collective-permute-done((bf16[912,256]{1,0:T(8,128)(2,1)}, bf16[912,256]{1,0:T(8,128)(2,1)}, u32[]{:S(2)}, u32[]{:S(2)}) %collective-permute-start.2) | collective-permute-done | bytes 466976 | tf_op jit(solution)/shard_map/ppermute | solution.py:693
  51.0 2.1 %join.1 = (bf16[912,256]{1,0:T(8,128)(2,1)}, f32[8,128]{1,0:T(8,128)}) custom-call(bf16[912,256]{1,0:T(8,128)(2,1)} %get-tuple-element.44.inner_ref, bf16[912,256]{1,0:T(8,128)(2,1)} %collective-permute-done.other_ref.refs_0_, bf16[912,256]{1,0:T(8,128)(2,1)} %back.1.end_ref.refs_2_, bf16[912,256]{1,0:T(8,128)(2,1)} %collective-permute-done.1.rest_0_.refs_3_, ...), custom_call_target="tpu_custom_call" | custom-call | flops 1000000 | bytes 100000 | tf_op jit(solution)/shard_map/join/pallas_call | solution.py:543
  53.1 5.5 %collective-permute-start.3 = (bf16[912,256]{1,0:T(8,128)(2,1)}, bf16[912,256]{1,0:T(8,128)(2,1)}, u32[]{:S(2)}, u32[]{:S(2)}) collective-permute-start(bf16[912,256]{1,0:T(8,128)(2,1)} %get-tuple-element.45), channel_id=1, source_target_pairs={{1,3},{2,0},{0,1},{3,2},{5,7},{6,4},{4,5},{7,6},{9,11},{10,8},{8,9... | collective-permute-start | bytes 1400840 | tf_op jit(solution)/shard_map/ppermute | solution.py:702
  58.7 0.5 collective-permute-start.10
  59.2 0.0 collective-permute-done.8.refs_6_
  59.2 0.0 collective-permute-done.9.refs_7_
  59.2 7.3 %weights.2 = (f32[896,1024]{1,0:T(8,128)}, f32[896,512]{1,0:T(8,128)}, f32[896,512]{1,0:T(8,128)}, f32[8,128]{1,0:T(8,128)}) custom-call(bf16[896,256]{1,0:T(8,128)(2,1)} %get-tuple-element.46.refs_0_, bf16[896,256]{1,0:T(8,128)(2,1)} %collective-permute-done.4.refs_2_.refs_1_, bf16[896,256]{1,0:T(8,128)(2,1)} %collective-permute-done.5.refs_1_.refs_2_, ...), custom_call_target="tpu_custom_call" | custom-call | flops 1000000 | bytes 100000 | tf_op jit(solution)/shard_map/weights/pallas_call | solution.py:481
  66.5 4.2 %collective-permute-done.3.refs_5_.refs_2_ = bf16[912,256]{1,0:T(8,128)(2,1)} collective-permute-done((bf16[912,256]{1,0:T(8,128)(2,1)}, bf16[912,256]{1,0:T(8,128)(2,1)}, u32[]{:S(2)}, u32[]{:S(2)}) %collective-permute-start.3) | collective-permute-done | bytes 466976 | tf_op jit(solution)/shard_map/ppermute | solution.py:702
  70.7 0.0 collective-permute-done.10.refs_1_
  70.7 0.0 collective-permute-start.11
  70.7 0.5 collective-permute-start.12
  71.2 3.1 %gains.1 = (f32[1,896]{1,0:T(1,128)}, f32[256,896]{1,0:T(8,128)}) custom-call(bf16[256,896]{1,0:T(8,128)(2,1)} %get-tuple-element.37.input_ref, f32[256,1]{1,0:T(8,128)} %get-tuple-element.36.inverse_ref, bf16[912,256]{1,0:T(8,128)(2,1)} %collective-permute-done.other_ref.refs_0_, bf16[912,256]{1,0:T(8,128)(2,1)} %get-tuple-element.39.refs_1_, ...), custom_call_target="tpu_custom_call" | custom-call | flops 1000000 | bytes 100000 | tf_op jit(solution)/shard_map/gains/pallas_call | solution.py:587
  74.3 0.1 collective-permute-start.13
  74.4 0.3 collective-permute-start.14
  74.7 1.5 %collective-permute-start.15 = (f32[1,896]{1,0:T(1,128)}, f32[1,896]{1,0:T(1,128)}, u32[]{:S(2)}, u32[]{:S(2)}) collective-permute-start(f32[1,896]{1,0:T(1,128)} %get-tuple-element.65.refs_0_), channel_id=1, source_target_pairs={{0,12},{4,8},{8,4},{12,0},{1,13},{5,9},{9,5},{13,1},{2,14},{6,10},... | collective-permute-start | bytes 10760 | tf_op jit(solution)/shard_map/ppermute | solution.py:666
  76.2 2.4 %finish.1 = bf16[256,896]{1,0:T(8,128)(2,1)} custom-call(f32[256,896]{1,0:T(8,128)} %get-tuple-element.54.total_ref, bf16[256,896]{1,0:T(8,128)(2,1)} %get-tuple-element.37.input_ref, f32[1,896]{1,0:T(1,128)} %get-tuple-element.55.gain_ref, f32[256,1]{1,0:T(8,128)} %get-tuple-element.36.inverse_ref, bf16[912,256]{1,0:T(8,128)(2,1)} %collective-permute-done.other_ref.refs_0_, ...), custom_call_target="tpu_custom_call" | custom-call | flops 1000000 | bytes 100000 | tf_op jit(solution)/shard_map/finish/pallas_call | solution.py:624
  78.6 0.0 collective-permute-done.11.refs_6_
  78.6 0.0 collective-permute-done.12.refs_7_
  78.7 5.6 %weights.3 = (f32[896,1024]{1,0:T(8,128)}, f32[896,512]{1,0:T(8,128)}, f32[896,512]{1,0:T(8,128)}, f32[8,128]{1,0:T(8,128)}) custom-call(bf16[896,256]{1,0:T(8,128)(2,1)} %get-tuple-element.46.refs_0_, bf16[896,256]{1,0:T(8,128)(2,1)} %collective-permute-done.4.refs_2_.refs_1_, ...), custom_call_target="tpu_custom_call", output_to_operand_aliasing={{0}: (8, {}), {1}: (9, {}), {2}: (10, {})} | custom-call | flops 1000000 | bytes 100000 | tf_op jit(solution)/shard_map/weights/pallas_call | solution.py:481
  84.3 0.0 collective-permute-done.13.refs_1_
  84.3 0.0 collective-permute-done.14.refs_2_
  84.3 0.0 collective-permute-done.15.refs_3_
  84.3 1.3 %total.1 = f32[896]{0:T(1024)} custom-call(f32[1,896]{1,0:T(1,128)} %get-tuple-element.65.refs_0_, f32[1,896]{1,0:T(1,128)} %collective-permute-done.13.refs_1_, f32[1,896]{1,0:T(1,128)} %collective-permute-done.14.refs_2_, f32[1,896]{1,0:T(1,128)} %collective-permute-done.15.refs_3_, f32[8,128]{1,0:T(8,128)} %get-tuple-element.66.refs_4_), custom_call_target="tpu_custom_call" | custom-call | flops 1000000 | bytes 100000 | tf_op jit(solution)/shard_map/total/pallas_call | solution.py:650
  (4 shorter events, 0.0 us)
Async XLA Ops:
  4.1 21.7 %collective-permute-start.4 = (bf16[896,256]{1,0:T(8,128)(2,1)}, bf16[896,256]{1,0:T(8,128)(2,1)}, u32[]{:S(2)}, u32[]{:S(2)}) collective-permute-start(bf16[896,256]{1,0:T(8,128)(2,1)} %get-tuple-element.47), channel_id=1, source_target_pairs={{0,8},{4,12},{8,0},{12,4},{1,9},{5,13},{9,1},{13,5},{2,10},{6,14},... | collective-permute-start | bytes 1376264 | tf_op jit(solution)/shard_map/ppermute | solution.py:666
  7.0 18.7 %collective-permute-start.5 = (bf16[896,256]{1,0:T(8,128)(2,1)}, bf16[896,256]{1,0:T(8,128)(2,1)}, u32[]{:S(2)}, u32[]{:S(2)}) collective-permute-start(bf16[896,256]{1,0:T(8,128)(2,1)} %get-tuple-element.48), channel_id=1, source_target_pairs={{0,4},{4,0},{8,12},{12,8},{1,5},{5,1},{9,13},{13,9},{2,6},{6,2},{1... | collective-permute-start | bytes 1376264 | tf_op jit(solution)/shard_map/ppermute | solution.py:666
  7.0 19.9 %collective-permute-start.6 = (bf16[896,256]{1,0:T(8,128)(2,1)}, bf16[896,256]{1,0:T(8,128)(2,1)}, u32[]{:S(2)}, u32[]{:S(2)}) collective-permute-start(bf16[896,256]{1,0:T(8,128)(2,1)} %get-tuple-element.49), channel_id=1, source_target_pairs={{0,12},{4,8},{8,4},{12,0},{1,13},{5,9},{9,5},{13,1},{2,14},{6,10},... | collective-permute-start | bytes 1376264 | tf_op jit(solution)/shard_map/ppermute | solution.py:666
  26.9 17.5 %collective-permute-start.7 = (bf16[1280,256]{1,0:T(8,128)(2,1)}, bf16[1280,256]{1,0:T(8,128)(2,1)}, u32[]{:S(2)}, u32[]{:S(2)}) collective-permute-start(bf16[1280,256]{1,0:T(8,128)(2,1)} %gate.4.refs_1_), channel_id=1, source_target_pairs={{0,8},{4,12},{8,0},{12,4},{1,9},{5,13},{9,1},{13,5},{2,10},{6,14},... | collective-permute-start | bytes 1966088 | tf_op jit(solution)/shard_map/ppermute | solution.py:666
  28.3 16.7 %collective-permute-start = (bf16[912,256]{1,0:T(8,128)(2,1)}, bf16[912,256]{1,0:T(8,128)(2,1)}, u32[]{:S(2)}, u32[]{:S(2)}) collective-permute-start(bf16[912,256]{1,0:T(8,128)(2,1)} %get-tuple-element.38), channel_id=1, source_target_pairs={{0,1},{1,0},{2,3},{3,2},{4,5},{5,4},{6,7},{7,6},{8,9},{9,8},{10,11... | collective-permute-start | bytes 1400840 | tf_op jit(solution)/shard_map/ppermute | solution.py:691
  29.8 15.1 %collective-permute-start.1 = (bf16[912,256]{1,0:T(8,128)(2,1)}, bf16[912,256]{1,0:T(8,128)(2,1)}, u32[]{:S(2)}, u32[]{:S(2)}) collective-permute-start(bf16[912,256]{1,0:T(8,128)(2,1)} %get-tuple-element.39.refs_1_), channel_id=1, source_target_pairs={{1,2},{2,1},{5,6},{6,5},{9,10},{10,9},{13,14},{14,13},{17,18},{18,... | collective-permute-start | bytes 1400840 | tf_op jit(solution)/shard_map/ppermute | solution.py:692
  31.3 19.7 %collective-permute-start.2 = (bf16[912,256]{1,0:T(8,128)(2,1)}, bf16[912,256]{1,0:T(8,128)(2,1)}, u32[]{:S(2)}, u32[]{:S(2)}) collective-permute-start(bf16[912,256]{1,0:T(8,128)(2,1)} %get-tuple-element.44.inner_ref), channel_id=1, source_target_pairs={{0,2},{3,1},{4,6},{7,5},{8,10},{11,9},{12,14},{15,13},{16,18},{19,... | collective-permute-start | bytes 1400840 | tf_op jit(solution)/shard_map/ppermute | solution.py:693
  44.4 14.8 %collective-permute-start.8 = (bf16[1280,256]{1,0:T(8,128)(2,1)}, bf16[1280,256]{1,0:T(8,128)(2,1)}, u32[]{:S(2)}, u32[]{:S(2)}) collective-permute-start(bf16[1280,256]{1,0:T(8,128)(2,1)} %get-tuple-element.51.refs_4_), channel_id=1, source_target_pairs={{0,4},{4,0},{8,12},{12,8},{1,5},{5,1},{9,13},{13,9},{2,6},{6,2},{1... | collective-permute-start | bytes 1966088 | tf_op jit(solution)/shard_map/ppermute | solution.py:666
  44.4 14.8 %collective-permute-start.9 = (bf16[1280,256]{1,0:T(8,128)(2,1)}, bf16[1280,256]{1,0:T(8,128)(2,1)}, u32[]{:S(2)}, u32[]{:S(2)}) collective-permute-start(bf16[1280,256]{1,0:T(8,128)(2,1)} %get-tuple-element.52.refs_5_.refs_1_), channel_id=1, source_target_pairs={{0,4},{4,0},{8,12},{12,8},{1,5},{5,1},{9,13},{13,9},{2,6},{6,2},{1... | collective-permute-start | bytes 1966088 | tf_op jit(solution)/shard_map/ppermute | solution.py:666
  53.1 17.5 %collective-permute-start.3 = (bf16[912,256]{1,0:T(8,128)(2,1)}, bf16[912,256]{1,0:T(8,128)(2,1)}, u32[]{:S(2)}, u32[]{:S(2)}) collective-permute-start(bf16[912,256]{1,0:T(8,128)(2,1)} %get-tuple-element.45), channel_id=1, source_target_pairs={{1,3},{2,0},{0,1},{3,2},{5,7},{6,4},{4,5},{7,6},{9,11},{10,8},{8,9... | collective-permute-start | bytes 1400840 | tf_op jit(solution)/shard_map/ppermute | solution.py:702
  58.7 12.0 %collective-permute-start.10 = (bf16[768,256]{1,0:T(8,128)(2,1)}, bf16[768,256]{1,0:T(8,128)(2,1)}, u32[]{:S(2)}, u32[]{:S(2)}) collective-permute-start(bf16[768,256]{1,0:T(8,128)(2,1)} %gate.6.refs_0_), channel_id=1, source_target_pairs={{0,8},{4,12},{8,0},{12,4},{1,9},{5,13},{9,1},{13,5},{2,10},{6,14},... | collective-permute-start | bytes 1179656 | tf_op jit(solution)/shard_map/ppermute | solution.py:666
  70.7 8.0 %collective-permute-start.11 = (bf16[768,256]{1,0:T(8,128)(2,1)}, bf16[768,256]{1,0:T(8,128)(2,1)}, u32[]{:S(2)}, u32[]{:S(2)}) collective-permute-start(bf16[768,256]{1,0:T(8,128)(2,1)} %get-tuple-element.57.refs_4_), channel_id=1, source_target_pairs={{0,4},{4,0},{8,12},{12,8},{1,5},{5,1},{9,13},{13,9},{2,6},{6,2},{1... | collective-permute-start | bytes 1179656 | tf_op jit(solution)/shard_map/ppermute | solution.py:666
  70.7 8.0 %collective-permute-start.12 = (bf16[768,256]{1,0:T(8,128)(2,1)}, bf16[768,256]{1,0:T(8,128)(2,1)}, u32[]{:S(2)}, u32[]{:S(2)}) collective-permute-start(bf16[768,256]{1,0:T(8,128)(2,1)} %get-tuple-element.58.refs_5_), channel_id=1, source_target_pairs={{0,4},{4,0},{8,12},{12,8},{1,5},{5,1},{9,13},{13,9},{2,6},{6,2},{1... | collective-permute-start | bytes 1179656 | tf_op jit(solution)/shard_map/ppermute | solution.py:666
  74.3 10.0 %collective-permute-start.13 = (f32[1,896]{1,0:T(1,128)}, f32[1,896]{1,0:T(1,128)}, u32[]{:S(2)}, u32[]{:S(2)}) collective-permute-start(f32[1,896]{1,0:T(1,128)} %get-tuple-element.65.refs_0_), channel_id=1, source_target_pairs={{0,4},{4,0},{8,12},{12,8},{1,5},{5,1},{9,13},{13,9},{2,6},{6,2},{1... | collective-permute-start | bytes 10760 | tf_op jit(solution)/shard_map/ppermute | solution.py:666
  74.4 9.9 %collective-permute-start.14 = (f32[1,896]{1,0:T(1,128)}, f32[1,896]{1,0:T(1,128)}, u32[]{:S(2)}, u32[]{:S(2)}) collective-permute-start(f32[1,896]{1,0:T(1,128)} %get-tuple-element.65.refs_0_), channel_id=1, source_target_pairs={{0,8},{4,12},{8,0},{12,4},{1,9},{5,13},{9,1},{13,5},{2,10},{6,14},... | collective-permute-start | bytes 10760 | tf_op jit(solution)/shard_map/ppermute | solution.py:666
  74.7 9.5 %collective-permute-start.15 = (f32[1,896]{1,0:T(1,128)}, f32[1,896]{1,0:T(1,128)}, u32[]{:S(2)}, u32[]{:S(2)}) collective-permute-start(f32[1,896]{1,0:T(1,128)} %get-tuple-element.65.refs_0_), channel_id=1, source_target_pairs={{0,12},{4,8},{8,4},{12,0},{1,13},{5,9},{9,5},{13,1},{2,14},{6,10},... | collective-permute-start | bytes 10760 | tf_op jit(solution)/shard_map/ppermute | solution.py:666

commit v12 on v11

--- a/solution.py
+++ b/solution.py
@@ -713,10 +713,7 @@
     group = w_query.shape[1] // w_key.shape[1]
     kv_local = w_key.shape[1] // HEAD_DIM
     offsets = [(shift, swap) for shift in range(chips) for swap in range(2)]
-    blocks = list(range(kv_local * (group + 2)))
-    early = blocks[: group + 2] + [h * (group + 2) + group for h in range(1, kv_local)]
-    shares = [early, [block for block in blocks if block not in early]]
-    shares = [share for share in shares if share]
+    shares = [list(range(kv_local * (group + 2)))]
 
     def targets():
         index = lax.axis_index("branch")
@@ -753,27 +750,19 @@
         )
     arrived = scatter_begin(parts, tensor_total)
 
-    (first,) = gate(deltas[:1], (near, *direct, *across))
-    sent = [branch_send(first, chips, s, 0) for s in range(1, chips)]
-    parts, for_ends, for_inner, met = scatter_end(parts, arrived, tensor_total)
-    *sent, first = gate((*sent, first), parts[2:3])
-    others = gate(deltas[1:], (sent[0],)) if deltas[1:] else ()
-    weights, tokens = None, []
-    for share, delta in zip(shares, (first, *others)):
-        if tokens:
-            sent = [branch_send(delta, chips, s, 0) for s in range(1, chips)]
-            delta, *sent = gate((delta, *sent), (parts[-1], tokens[0]))
-        gathered = [delta] + sent
-        gathered += [branch_send(part, chips, 0, 1) for part in gathered]
-        *weights, token = weight_gradients(turned, gathered, share, kv_local, group, weights)
-        tokens.append(token)
+    (delta,) = gate(deltas, (near, *direct, *across))
+    sent = [branch_send(delta, chips, s, 0) for s in range(1, chips)]
+    gathered = list(gate((delta, *sent), (parts[-1], *arrived)))
+    parts, for_ends, for_inner, _ = scatter_end(parts, arrived, tensor_total)
+    gathered += [branch_send(part, chips, 0, 1) for part in gathered]
+    *weights, token = weight_gradients(turned, gathered, shares[0], kv_local, group, None)
 
     add = functools.partial(add_parts, for_ends, for_inner)
-    gain_sum, total = gain_sums(add, input_columns, inverse, parts, tokens[0])
+    gain_sum, total = gain_sums(add, input_columns, inverse, parts, token)
     grad_input = finish(width, add, total, input_columns, gain_columns, inverse, parts)
     if chips == 2:
         sums = [gain_sum] + [branch_send(gain_sum, chips, s, e) for s, e in offsets[1:]]
-        grad_gain = total_of_four(sums, tokens[-1])
+        grad_gain = total_of_four(sums, grad_input)
     else:
         grad_gain = lax.psum(gain_sum, "branch").reshape(column_width)
     return (grad_input, *weights, grad_gain)

time: 85.9 us -> 81.9 us (0.953)
  Pallas kernels: 47.7 us -> 44.7 us
  starting transfers between devices: 22.2 us -> 20.1 us
  waiting for transfers between devices: 14.9 us -> 16.1 us
    ppermute x1, waiting for transfers between devices: 6.05 us -> 9.15 us  [scatter_begin(): from_ends = lax.ppermute(parts[2], 'tensor', [(0, 2), (3, 1)])]
    pallas_call x2 -> x1, Pallas kernels: 12.9 us -> 9.85 us  [weight_gradients(): pl.pallas_call(functools.partial(weight_kernel, outs, sources), out_shape...]
    ppermute x12 -> x9, waiting for transfers between devices: 4.72 us -> 3.03 us  [branch_send(): return lax.ppermute(array, 'branch', pairs)]
    ppermute x1, waiting for transfers between devices: 4.16 us -> 2.56 us  [scatter_end(): lax.ppermute(joined, 'tensor', [(1, 3), (2, 0), (0, 1), (3, 2)])]
    ppermute x1, waiting for transfers between devices: 0.01 us -> 1.39 us  [scatter_begin(): lax.ppermute(parts[0], 'tensor', [(0, 1), (1, 0), (2, 3), (3, 2)])]
    ppermute x12 -> x9, starting transfers between devices: 7.94 us -> 6.87 us  [branch_send(): return lax.ppermute(array, 'branch', pairs)]
  transfers between devices with their start and end apart: 16 -> 13, of which waited for: 4 -> 5; matrix products, arithmetic and copies ran while one was open for 0% -> 0% of each run, Pallas kernels for 50% -> 45%
where the time goes in v12:
time: 81.9 us; the launch traced here: 81.6 us
  Pallas kernels  44.7 us (55%)
  starting transfers between devices  20.1 us (25%)
  waiting for transfers between devices  16.1 us (20%)
    pallas_call x1, Pallas kernels, attention_backward(): pl.pallas_call(functools.partial(attention_kernel, slots, group, kv_local...  18.6 us
    pallas_call x1, Pallas kernels, weight_gradients(): pl.pallas_call(functools.partial(weight_kernel, outs, sources), out_shape...  9.85 us
    ppermute x1, waiting for transfers between devices, scatter_begin(): from_ends = lax.ppermute(parts[2], 'tensor', [(0, 2), (3, 1)])  9.15 us
    ppermute x9, starting transfers between devices, branch_send(): return lax.ppermute(array, 'branch', pairs)  6.87 us
    ppermute x1, starting transfers between devices, scatter_begin(): from_ends = lax.ppermute(parts[2], 'tensor', [(0, 2), (3, 1)])  5.27 us
    ppermute x1, starting transfers between devices, scatter_end(): lax.ppermute(joined, 'tensor', [(1, 3), (2, 0), (0, 1), (3, 2)])  4.99 us
    pallas_call x1, Pallas kernels, back_project(): pl.pallas_call(back_kernel, out_shape=(jax.ShapeDtypeStruct((depth + CENT...  3.94 us
    pallas_call x1, Pallas kernels, normalize(): pl.pallas_call(functools.partial(norm_kernel, targets), out_shape=(jax.Sh...  3.44 us
  transfers between devices with their start and end apart: 13, of which 5 were waited for; matrix products, arithmetic and copies ran while one was open for 0% of the time, Pallas kernels for 45%

profile of v12, /device:TPU:0, one launch (start us, length us, event | category | flops | bytes accessed | tf_op | source)
XLA Modules:
  0.0 81.6 jit_solution(10227771855622835912)
XLA Ops:
  0.6 3.4 %norm.1 = (f32[256,1]{1,0:T(8,128)}, bf16[896,256]{1,0:T(8,128)(2,1)}, bf16[896,256]{1,0:T(8,128)(2,1)}, bf16[896,256]{1,0:T(8,128)(2,1)}, bf16[896,256]{1,0:T(8,128)(2,1)}) custom-call(bf16[256,3584]{1,0:T(8,128)(2,1)} %input_hbm.1, f32[3584]{0:T(1024)} %gain_ref.3), custom_call_target="tpu_custom_call" | custom-call | flops 1000000 | bytes 100000 | tf_op jit(solution)/shard_map/norm/pallas_call | solution.py:59
  4.1 2.9 %collective-permute-start.4 = (bf16[896,256]{1,0:T(8,128)(2,1)}, bf16[896,256]{1,0:T(8,128)(2,1)}, u32[]{:S(2)}, u32[]{:S(2)}) collective-permute-start(bf16[896,256]{1,0:T(8,128)(2,1)} %get-tuple-element.40), channel_id=1, source_target_pairs={{0,8},{4,12},{8,0},{12,4},{1,9},{5,13},{9,1},{13,5},{2,10},{6,14},... | collective-permute-start | bytes 1376264 | tf_op jit(solution)/shard_map/ppermute | solution.py:666
  7.0 0.0 collective-permute-start.5
  7.0 0.2 collective-permute-start.6
  7.2 18.6 %attention.1 = (bf16[2048,256]{1,0:T(8,128)(2,1)}, bf16[912,256]{1,0:T(8,128)(2,1)}, bf16[912,256]{1,0:T(8,128)(2,1)}, bf16[912,256]{1,0:T(8,128)(2,1)}, bf16[10...) custom-call(s32[8]{0:T(128)} %count_ref.1, ...), custom_call_target="tpu_custom_call" | custom-call | flops 1000000 | bytes 100000 | tf_op jit(solution)/shard_map/attention/pallas_call | solution.py:319
  25.8 0.0 collective-permute-done.4.refs_2_.refs_1_
  25.8 0.0 collective-permute-done.5.refs_1_.refs_2_
  25.8 1.2 %collective-permute-done.6.refs_3_ = bf16[896,256]{1,0:T(8,128)(2,1)} collective-permute-done((bf16[896,256]{1,0:T(8,128)(2,1)}, bf16[896,256]{1,0:T(8,128)(2,1)}, u32[]{:S(2)}, u32[]{:S(2)}) %collective-permute-start.6) | collective-permute-done | bytes 458784 | tf_op jit(solution)/shard_map/ppermute | solution.py:666
  26.9 1.3 %collective-permute-start.7 = (bf16[2048,256]{1,0:T(8,128)(2,1)}, bf16[2048,256]{1,0:T(8,128)(2,1)}, u32[]{:S(2)}, u32[]{:S(2)}) collective-permute-start(bf16[2048,256]{1,0:T(8,128)(2,1)} %gate.2.refs_0_), channel_id=1, source_target_pairs={{0,8},{4,12},{8,0},{12,4},{1,9},{5,13},{9,1},{13,5},{2,10},{6,14},... | collective-permute-start | bytes 3145736 | tf_op jit(solution)/shard_map/ppermute | solution.py:666
  28.3 1.6 %collective-permute-start = (bf16[912,256]{1,0:T(8,128)(2,1)}, bf16[912,256]{1,0:T(8,128)(2,1)}, u32[]{:S(2)}, u32[]{:S(2)}) collective-permute-start(bf16[912,256]{1,0:T(8,128)(2,1)} %get-tuple-element.31), channel_id=1, source_target_pairs={{0,1},{1,0},{2,3},{3,2},{4,5},{5,4},{6,7},{7,6},{8,9},{9,8},{10,11... | collective-permute-start | bytes 1400840 | tf_op jit(solution)/shard_map/ppermute | solution.py:691
  29.8 5.3 %collective-permute-start.2 = (bf16[912,256]{1,0:T(8,128)(2,1)}, bf16[912,256]{1,0:T(8,128)(2,1)}, u32[]{:S(2)}, u32[]{:S(2)}) collective-permute-start(bf16[912,256]{1,0:T(8,128)(2,1)} %get-tuple-element.37.inner_ref), channel_id=1, source_target_pairs={{0,2},{3,1},{4,6},{7,5},{8,10},{11,9},{12,14},{15,13},{16,18},{19,... | collective-permute-start | bytes 1400840 | tf_op jit(solution)/shard_map/ppermute | solution.py:693
  35.1 1.4 %collective-permute-start.1 = (bf16[912,256]{1,0:T(8,128)(2,1)}, bf16[912,256]{1,0:T(8,128)(2,1)}, u32[]{:S(2)}, u32[]{:S(2)}) collective-permute-start(bf16[912,256]{1,0:T(8,128)(2,1)} %get-tuple-element.32.refs_1_), channel_id=1, source_target_pairs={{1,2},{2,1},{5,6},{6,5},{9,10},{10,9},{13,14},{14,13},{17,18},{18,... | collective-permute-start | bytes 1400840 | tf_op jit(solution)/shard_map/ppermute | solution.py:692
  36.6 3.9 %back.1.end_ref.refs_2_ = bf16[912,256]{1,0:T(8,128)(2,1)} custom-call(bf16[16,256]{1,0:T(8,128)(2,1)} %get-tuple-element.33.centre_ref, bf16[1024,256]{1,0:T(8,128)(2,1)} %get-tuple-element.34.refs_0_, bf16[512,256]{1,0:T(8,128)(2,1)} %get-tuple-element.35.refs_1_, bf16[512,256]{1,0:T(8,128)(2,1)} %get-tuple-element.36.refs_2_, bf16[3584,1024]{1,0:T(8,128)(2,1)} %refs_3_.1, ...), custom_call_target="tpu_custom_call" | custom-call | flops 1000000 | bytes 100000 | tf_op jit(solution)/shard_map/back/pallas_call | solution.py:398
  40.5 1.4 %collective-permute-done.other_ref.refs_3_.refs_0_ = bf16[912,256]{1,0:T(8,128)(2,1)} collective-permute-done((bf16[912,256]{1,0:T(8,128)(2,1)}, bf16[912,256]{1,0:T(8,128)(2,1)}, u32[]{:S(2)}, u32[]{:S(2)}) %collective-permute-start) | collective-permute-done | bytes 466976 | tf_op jit(solution)/shard_map/ppermute | solution.py:691
  41.9 9.1 %collective-permute-done.2.rest_1_.refs_5_.refs_4_ = bf16[912,256]{1,0:T(8,128)(2,1)} collective-permute-done((bf16[912,256]{1,0:T(8,128)(2,1)}, bf16[912,256]{1,0:T(8,128)(2,1)}, u32[]{:S(2)}, u32[]{:S(2)}) %collective-permute-start.2) | collective-permute-done | bytes 466976 | tf_op jit(solution)/shard_map/ppermute | solution.py:693
  51.0 0.0 collective-permute-done.1.rest_0_.refs_4_.refs_3_
  51.0 1.9 %collective-permute-done.7.refs_1_ = bf16[2048,256]{1,0:T(8,128)(2,1)} collective-permute-done((bf16[2048,256]{1,0:T(8,128)(2,1)}, bf16[2048,256]{1,0:T(8,128)(2,1)}, u32[]{:S(2)}, u32[]{:S(2)}) %collective-permute-start.7) | collective-permute-done | bytes 1048608 | tf_op jit(solution)/shard_map/ppermute | solution.py:666
  52.9 0.0 collective-permute-start.8
  52.9 0.5 collective-permute-start.9
  53.4 2.1 %join.1 = (bf16[912,256]{1,0:T(8,128)(2,1)}, f32[8,128]{1,0:T(8,128)}) custom-call(bf16[912,256]{1,0:T(8,128)(2,1)} %get-tuple-element.37.inner_ref, bf16[912,256]{1,0:T(8,128)(2,1)} %collective-permute-done.other_ref.refs_3_.refs_0_, bf16[912,256]{1,0:T(8,128)(2,1)} %back.1.end_ref.refs_2_, bf16[912,256]{1,0:T(8,128)(2,1)} %collective-permute-done.1.rest_0_.refs_4_.refs_3_, ...), custom_call_target="tpu_custom_call" | custom-call | flops 1000000 | bytes 100000 | tf_op jit(solution)/shard_map/join/pallas_call | solution.py:543
  55.5 5.0 %collective-permute-start.3 = (bf16[912,256]{1,0:T(8,128)(2,1)}, bf16[912,256]{1,0:T(8,128)(2,1)}, u32[]{:S(2)}, u32[]{:S(2)}) collective-permute-start(bf16[912,256]{1,0:T(8,128)(2,1)} %get-tuple-element.38), channel_id=1, source_target_pairs={{1,3},{2,0},{0,1},{3,2},{5,7},{6,4},{4,5},{7,6},{9,11},{10,8},{8,9... | collective-permute-start | bytes 1400840 | tf_op jit(solution)/shard_map/ppermute | solution.py:702
  60.5 0.0 collective-permute-done.8.refs_6_
  60.5 0.0 collective-permute-done.9.refs_7_
  60.5 9.8 %weights.1 = (f32[896,1024]{1,0:T(8,128)}, f32[896,512]{1,0:T(8,128)}, f32[896,512]{1,0:T(8,128)}, f32[8,128]{1,0:T(8,128)}) custom-call(bf16[896,256]{1,0:T(8,128)(2,1)} %get-tuple-element.39.refs_0_, bf16[896,256]{1,0:T(8,128)(2,1)} %collective-permute-done.4.refs_2_.refs_1_, bf16[896,256]{1,0:T(8,128)(2,1)} %collective-permute-done.5.refs_1_.refs_2_, ...), custom_call_target="tpu_custom_call" | custom-call | flops 1000000 | bytes 100000 | tf_op jit(solution)/shard_map/weights/pallas_call | solution.py:481
  70.3 2.6 %collective-permute-done.3.refs_5_ = bf16[912,256]{1,0:T(8,128)(2,1)} collective-permute-done((bf16[912,256]{1,0:T(8,128)(2,1)}, bf16[912,256]{1,0:T(8,128)(2,1)}, u32[]{:S(2)}, u32[]{:S(2)}) %collective-permute-start.3) | collective-permute-done | bytes 466976 | tf_op jit(solution)/shard_map/ppermute | solution.py:702
  72.9 3.1 %gains.1 = (f32[1,896]{1,0:T(1,128)}, f32[256,896]{1,0:T(8,128)}) custom-call(bf16[256,896]{1,0:T(8,128)(2,1)} %get-tuple-element.30.input_ref, f32[256,1]{1,0:T(8,128)} %get-tuple-element.29.inverse_ref, bf16[912,256]{1,0:T(8,128)(2,1)} %collective-permute-done.other_ref.refs_3_.refs_0_, bf16[912,256]{1,0:T(8,128)(2,1)} %get-tuple-element.32.refs_1_, ...), custom_call_target="tpu_custom_call" | custom-call | flops 1000000 | bytes 100000 | tf_op jit(solution)/shard_map/gains/pallas_call | solution.py:587
  76.0 0.1 collective-permute-start.12
  76.0 1.2 %collective-permute-start.11 = (f32[1,896]{1,0:T(1,128)}, f32[1,896]{1,0:T(1,128)}, u32[]{:S(2)}, u32[]{:S(2)}) collective-permute-start(f32[1,896]{1,0:T(1,128)} %get-tuple-element.52.refs_0_), channel_id=1, source_target_pairs={{0,8},{4,12},{8,0},{12,4},{1,9},{5,13},{9,1},{13,5},{2,10},{6,14},... | collective-permute-start | bytes 10760 | tf_op jit(solution)/shard_map/ppermute | solution.py:666
  77.2 0.7 collective-permute-start.10
  77.9 2.4 %finish.1.refs_4_ = bf16[256,896]{1,0:T(8,128)(2,1)} custom-call(f32[256,896]{1,0:T(8,128)} %get-tuple-element.47.total_ref, bf16[256,896]{1,0:T(8,128)(2,1)} %get-tuple-element.30.input_ref, f32[1,896]{1,0:T(1,128)} %get-tuple-element.48.gain_ref, f32[256,1]{1,0:T(8,128)} %get-tuple-element.29.inverse_ref, ...), custom_call_target="tpu_custom_call" | custom-call | flops 1000000 | bytes 100000 | tf_op jit(solution)/shard_map/finish/pallas_call | solution.py:624
  80.3 0.0 collective-permute-done.12.refs_3_
  80.3 0.0 collective-permute-done.11.refs_2_
  80.3 0.0 collective-permute-done.10.refs_1_
  80.3 1.3 %total.1 = f32[896]{0:T(1024)} custom-call(f32[1,896]{1,0:T(1,128)} %get-tuple-element.52.refs_0_, f32[1,896]{1,0:T(1,128)} %collective-permute-done.10.refs_1_, f32[1,896]{1,0:T(1,128)} %collective-permute-done.11.refs_2_, f32[1,896]{1,0:T(1,128)} %collective-permute-done.12.refs_3_, bf16[256,896]{1,0:T(8,128)(2,1)} %finish.1.refs_4_), custom_call_target="tpu_custom_call" | custom-call | flops 1000000 | bytes 100000 | tf_op jit(solution)/shard_map/total/pallas_call | solution.py:650
  (2 shorter events, 0.0 us)
Async XLA Ops:
  4.1 21.7 %collective-permute-start.4 = (bf16[896,256]{1,0:T(8,128)(2,1)}, bf16[896,256]{1,0:T(8,128)(2,1)}, u32[]{:S(2)}, u32[]{:S(2)}) collective-permute-start(bf16[896,256]{1,0:T(8,128)(2,1)} %get-tuple-element.40), channel_id=1, source_target_pairs={{0,8},{4,12},{8,0},{12,4},{1,9},{5,13},{9,1},{13,5},{2,10},{6,14},... | collective-permute-start | bytes 1376264 | tf_op jit(solution)/shard_map/ppermute | solution.py:666
  7.0 18.8 %collective-permute-start.5 = (bf16[896,256]{1,0:T(8,128)(2,1)}, bf16[896,256]{1,0:T(8,128)(2,1)}, u32[]{:S(2)}, u32[]{:S(2)}) collective-permute-start(bf16[896,256]{1,0:T(8,128)(2,1)} %get-tuple-element.41), channel_id=1, source_target_pairs={{0,4},{4,0},{8,12},{12,8},{1,5},{5,1},{9,13},{13,9},{2,6},{6,2},{1... | collective-permute-start | bytes 1376264 | tf_op jit(solution)/shard_map/ppermute | solution.py:666
  7.0 19.9 %collective-permute-start.6 = (bf16[896,256]{1,0:T(8,128)(2,1)}, bf16[896,256]{1,0:T(8,128)(2,1)}, u32[]{:S(2)}, u32[]{:S(2)}) collective-permute-start(bf16[896,256]{1,0:T(8,128)(2,1)} %get-tuple-element.42), channel_id=1, source_target_pairs={{0,12},{4,8},{8,4},{12,0},{1,13},{5,9},{9,5},{13,1},{2,14},{6,10},... | collective-permute-start | bytes 1376264 | tf_op jit(solution)/shard_map/ppermute | solution.py:666
  26.9 25.9 %collective-permute-start.7 = (bf16[2048,256]{1,0:T(8,128)(2,1)}, bf16[2048,256]{1,0:T(8,128)(2,1)}, u32[]{:S(2)}, u32[]{:S(2)}) collective-permute-start(bf16[2048,256]{1,0:T(8,128)(2,1)} %gate.2.refs_0_), channel_id=1, source_target_pairs={{0,8},{4,12},{8,0},{12,4},{1,9},{5,13},{9,1},{13,5},{2,10},{6,14},... | collective-permute-start | bytes 3145736 | tf_op jit(solution)/shard_map/ppermute | solution.py:666
  28.3 13.6 %collective-permute-start = (bf16[912,256]{1,0:T(8,128)(2,1)}, bf16[912,256]{1,0:T(8,128)(2,1)}, u32[]{:S(2)}, u32[]{:S(2)}) collective-permute-start(bf16[912,256]{1,0:T(8,128)(2,1)} %get-tuple-element.31), channel_id=1, source_target_pairs={{0,1},{1,0},{2,3},{3,2},{4,5},{5,4},{6,7},{7,6},{8,9},{9,8},{10,11... | collective-permute-start | bytes 1400840 | tf_op jit(solution)/shard_map/ppermute | solution.py:691
  29.8 21.2 %collective-permute-start.2 = (bf16[912,256]{1,0:T(8,128)(2,1)}, bf16[912,256]{1,0:T(8,128)(2,1)}, u32[]{:S(2)}, u32[]{:S(2)}) collective-permute-start(bf16[912,256]{1,0:T(8,128)(2,1)} %get-tuple-element.37.inner_ref), channel_id=1, source_target_pairs={{0,2},{3,1},{4,6},{7,5},{8,10},{11,9},{12,14},{15,13},{16,18},{19,... | collective-permute-start | bytes 1400840 | tf_op jit(solution)/shard_map/ppermute | solution.py:693
  35.1 15.9 %collective-permute-start.1 = (bf16[912,256]{1,0:T(8,128)(2,1)}, bf16[912,256]{1,0:T(8,128)(2,1)}, u32[]{:S(2)}, u32[]{:S(2)}) collective-permute-start(bf16[912,256]{1,0:T(8,128)(2,1)} %get-tuple-element.32.refs_1_), channel_id=1, source_target_pairs={{1,2},{2,1},{5,6},{6,5},{9,10},{10,9},{13,14},{14,13},{17,18},{18,... | collective-permute-start | bytes 1400840 | tf_op jit(solution)/shard_map/ppermute | solution.py:692
  52.9 7.6 %collective-permute-start.8 = (bf16[2048,256]{1,0:T(8,128)(2,1)}, bf16[2048,256]{1,0:T(8,128)(2,1)}, u32[]{:S(2)}, u32[]{:S(2)}) collective-permute-start(bf16[2048,256]{1,0:T(8,128)(2,1)} %get-tuple-element.44.refs_4_), channel_id=1, source_target_pairs={{0,4},{4,0},{8,12},{12,8},{1,5},{5,1},{9,13},{13,9},{2,6},{6,2},{1... | collective-permute-start | bytes 3145736 | tf_op jit(solution)/shard_map/ppermute | solution.py:666
  52.9 7.6 %collective-permute-start.9 = (bf16[2048,256]{1,0:T(8,128)(2,1)}, bf16[2048,256]{1,0:T(8,128)(2,1)}, u32[]{:S(2)}, u32[]{:S(2)}) collective-permute-start(bf16[2048,256]{1,0:T(8,128)(2,1)} %get-tuple-element.45.refs_5_), channel_id=1, source_target_pairs={{0,4},{4,0},{8,12},{12,8},{1,5},{5,1},{9,13},{13,9},{2,6},{6,2},{1... | collective-permute-start | bytes 3145736 | tf_op jit(solution)/shard_map/ppermute | solution.py:666
  55.5 17.4 %collective-permute-start.3 = (bf16[912,256]{1,0:T(8,128)(2,1)}, bf16[912,256]{1,0:T(8,128)(2,1)}, u32[]{:S(2)}, u32[]{:S(2)}) collective-permute-start(bf16[912,256]{1,0:T(8,128)(2,1)} %get-tuple-element.38), channel_id=1, source_target_pairs={{1,3},{2,0},{0,1},{3,2},{5,7},{6,4},{4,5},{7,6},{9,11},{10,8},{8,9... | collective-permute-start | bytes 1400840 | tf_op jit(solution)/shard_map/ppermute | solution.py:702
  76.0 4.3 %collective-permute-start.12 = (f32[1,896]{1,0:T(1,128)}, f32[1,896]{1,0:T(1,128)}, u32[]{:S(2)}, u32[]{:S(2)}) collective-permute-start(f32[1,896]{1,0:T(1,128)} %get-tuple-element.52.refs_0_), channel_id=1, source_target_pairs={{0,12},{4,8},{8,4},{12,0},{1,13},{5,9},{9,5},{13,1},{2,14},{6,10},... | collective-permute-start | bytes 10760 | tf_op jit(solution)/shard_map/ppermute | solution.py:666
  76.0 4.3 %collective-permute-start.11 = (f32[1,896]{1,0:T(1,128)}, f32[1,896]{1,0:T(1,128)}, u32[]{:S(2)}, u32[]{:S(2)}) collective-permute-start(f32[1,896]{1,0:T(1,128)} %get-tuple-element.52.refs_0_), channel_id=1, source_target_pairs={{0,8},{4,12},{8,0},{12,4},{1,9},{5,13},{9,1},{13,5},{2,10},{6,14},... | collective-permute-start | bytes 10760 | tf_op jit(solution)/shard_map/ppermute | solution.py:666
  77.2 3.1 %collective-permute-start.10 = (f32[1,896]{1,0:T(1,128)}, f32[1,896]{1,0:T(1,128)}, u32[]{:S(2)}, u32[]{:S(2)}) collective-permute-start(f32[1,896]{1,0:T(1,128)} %get-tuple-element.52.refs_0_), channel_id=1, source_target_pairs={{0,4},{4,0},{8,12},{12,8},{1,5},{5,1},{9,13},{13,9},{2,6},{6,2},{1... | collective-permute-start | bytes 10760 | tf_op jit(solution)/shard_map/ppermute | solution.py:666

commit v13 on v12

--- a/solution.py
+++ b/solution.py
@@ -135,12 +135,13 @@
     block = rows // slots
     mid = group * head_dim
     steps = weight_sem.shape[0]
-    chunk = width // steps
+    chunk = width // 7 if steps > 1 else width
+    edges = [0] + [width - (steps - 1 - step) * 2 * chunk for step in range(steps)]
     weights = ((query_hbm, query_ref, mid, 0), (key_hbm, key_ref, head_dim, mid))
     weights += ((value_hbm, value_ref, head_dim, mid + head_dim),)
 
     def fetch(step, which):
-        lines = pl.ds(step * chunk, chunk)
+        lines = pl.ds(edges[step], edges[step + 1] - edges[step])
         source, kept_ref = weights[which][:2]
         return pltpu.make_async_copy(
             source.at[lines, :], kept_ref.at[lines, :], weight_sem.at[step, which]
@@ -175,7 +176,7 @@
         column_gain_ref[...] = jnp.zeros_like(column_gain_ref)
 
     for step in range(steps):
-        lines = slice(step * chunk, (step + 1) * chunk)
+        lines = slice(edges[step], edges[step + 1])
         gain = 1.0 + gain_row[:, lines]
         normed = (input_ref[:, lines].astype(jnp.float32) * inverse * gain).astype(jnp.bfloat16)
         for which, (_, kept_ref, wide, place) in enumerate(weights):
@@ -190,13 +191,13 @@
     scale = head_dim ** (-0.5)
     centre_ref[...] = jnp.zeros_like(centre_ref)
 
-    def attend(h, carry):
+    def attend(h):
         for slot in range(slots):
             lines = slice(slot * block, (slot + 1) * block)
             live = (
                 lax.broadcasted_iota(jnp.int32, (block, mid), 0) < count_ref[first_count + slot]
             )
-            columns = pl.ds(pl.multiple_of(h * mid, mid), mid)
+            columns = slice(h * mid, (h + 1) * mid)
             grad_rows = jnp.where(live, grad_ref[lines, columns].astype(jnp.float32), 0.0)
             pair = [slice(g * head_dim, (g + 1) * head_dim) for g in range(group)]
             grads = jnp.concatenate([grad_rows[:, p] for p in pair], axis=0).astype(jnp.bfloat16)
@@ -227,16 +228,16 @@
                 half = part.astype(jnp.bfloat16)
                 line = which * rows + slot * block
                 delta_ref[h, line : line + block, :] = half
-                spot = pl.ds(pl.multiple_of(start, head_dim), head_dim)
+                spot = slice(start, start + head_dim)
                 turned_ref[spot, lines] = half.T
                 term = half.astype(jnp.float32) * sum_ref[
                     h, lines, which * head_dim : (which + 1) * head_dim
                 ]
                 product = term if product is None else product + term
             centre_ref[lines, :] += jnp.sum(product, axis=-1, keepdims=True)
-        return carry
-
-    lax.fori_loop(0, kv_local, attend, 0)
+
+    for h in range(kv_local):
+        attend(h)
     lasts = []
     for share, out in zip(shares, delta_hbm):
         for place, block_index in enumerate(share):
@@ -311,7 +312,7 @@
     column_width = width // blocks
     cut = column_width % 128 == 0
     wide = column_width if cut else 128
-    steps = 2 if width % 512 == 0 else 1
+    steps = 4 if width % (7 * 256) == 0 else 1
     part_shape = (column_width + CENTRE_ROWS, rows)
     hbm = pl.BlockSpec(memory_space=pl.ANY)
     vmem = pl.BlockSpec(memory_space=pltpu.VMEM)
@@ -539,15 +540,18 @@
 
 
 def join(inner_part, other, end_part, tokens):
-    vmem = pl.BlockSpec(memory_space=pltpu.VMEM)
+    lines, rows = end_part.shape
+    cuts = 3 if lines % 48 == 0 else 1
+    some = pl.BlockSpec((lines // cuts, rows), lambda i: (i, 0))
     return pl.pallas_call(
         join_kernel,
         out_shape=(
             jax.ShapeDtypeStruct(end_part.shape, end_part.dtype),
             jax.ShapeDtypeStruct((8, 128), jnp.float32),
         ),
-        in_specs=[vmem] * 3 + [pl.BlockSpec(memory_space=pl.ANY)] * len(tokens),
-        out_specs=(vmem, vmem),
+        grid=(cuts,),
+        in_specs=[some] * 3 + [pl.BlockSpec(memory_space=pl.ANY)] * len(tokens),
+        out_specs=(some, pl.BlockSpec((8, 128), lambda i: (0, 0))),
         compiler_params=pltpu.CompilerParams(vmem_limit_bytes=VMEM_LIMIT),
         cost_estimate=small_cost(),
         name="join",

time: 81.9 us -> 82.7 us (level)
  Pallas kernels: 44.7 us -> 46 us
    pallas_call x1, Pallas kernels: 2.1 us -> 2.94 us  [join(): pl.pallas_call(join_kernel, out_shape=(jax.ShapeDtypeStruct(end_part.shap...]
  transfers between devices with their start and end apart: 13 -> 13, of which waited for: 5 -> 5; matrix products, arithmetic and copies ran while one was open for 0% -> 0% of each run, Pallas kernels for 45% -> 46%
where the time goes in v13:
time: 82.7 us; the launch traced here: 82.4 us
  Pallas kernels  46 us (56%)
  starting transfers between devices  20.2 us (24%)
  waiting for transfers between devices  15.5 us (19%)
    pallas_call x1, Pallas kernels, attention_backward(): pl.pallas_call(functools.partial(attention_kernel, slots, group, kv_local...  19.1 us
    pallas_call x1, Pallas kernels, weight_gradients(): pl.pallas_call(functools.partial(weight_kernel, outs, sources), out_shape...  9.85 us
    ppermute x1, waiting for transfers between devices, scatter_begin(): from_ends = lax.ppermute(parts[2], 'tensor', [(0, 2), (3, 1)])  9.15 us
    ppermute x9, starting transfers between devices, branch_send(): return lax.ppermute(array, 'branch', pairs)  6.95 us
    ppermute x1, starting transfers between devices, scatter_begin(): from_ends = lax.ppermute(parts[2], 'tensor', [(0, 2), (3, 1)])  5.27 us
    ppermute x1, starting transfers between devices, scatter_end(): lax.ppermute(joined, 'tensor', [(1, 3), (2, 0), (0, 1), (3, 2)])  4.96 us
    pallas_call x1, Pallas kernels, back_project(): pl.pallas_call(back_kernel, out_shape=(jax.ShapeDtypeStruct((depth + CENT...  3.93 us
    pallas_call x1, Pallas kernels, normalize(): pl.pallas_call(functools.partial(norm_kernel, targets), out_shape=(jax.Sh...  3.44 us
  transfers between devices with their start and end apart: 13, of which 5 were waited for; matrix products, arithmetic and copies ran while one was open for 0% of the time, Pallas kernels for 46%

profile of v13, /device:TPU:0, one launch (start us, length us, event | category | flops | bytes accessed | tf_op | source)
XLA Modules:
  0.0 82.4 jit_solution(7724570889417530222)
XLA Ops:
  0.6 3.4 %norm.1 = (f32[256,1]{1,0:T(8,128)}, bf16[896,256]{1,0:T(8,128)(2,1)}, bf16[896,256]{1,0:T(8,128)(2,1)}, bf16[896,256]{1,0:T(8,128)(2,1)}, bf16[896,256]{1,0:T(8,128)(2,1)}) custom-call(bf16[256,3584]{1,0:T(8,128)(2,1)} %input_hbm.1, f32[3584]{0:T(1024)} %gain_ref.3), custom_call_target="tpu_custom_call" | custom-call | flops 1000000 | bytes 100000 | tf_op jit(solution)/shard_map/norm/pallas_call | solution.py:59
  4.1 2.9 %collective-permute-start.4 = (bf16[896,256]{1,0:T(8,128)(2,1)}, bf16[896,256]{1,0:T(8,128)(2,1)}, u32[]{:S(2)}, u32[]{:S(2)}) collective-permute-start(bf16[896,256]{1,0:T(8,128)(2,1)} %get-tuple-element.40), channel_id=1, source_target_pairs={{0,8},{4,12},{8,0},{12,4},{1,9},{5,13},{9,1},{13,5},{2,10},{6,14},... | collective-permute-start | bytes 1376264 | tf_op jit(solution)/shard_map/ppermute | solution.py:670
  7.0 0.0 collective-permute-start.5
  7.0 0.2 collective-permute-start.6
  7.2 19.1 %attention.1 = (bf16[2048,256]{1,0:T(8,128)(2,1)}, bf16[912,256]{1,0:T(8,128)(2,1)}, bf16[912,256]{1,0:T(8,128)(2,1)}, bf16[912,256]{1,0:T(8,128)(2,1)}, bf16[10...) custom-call(s32[8]{0:T(128)} %count_ref.1, ...), custom_call_target="tpu_custom_call" | custom-call | flops 1000000 | bytes 100000 | tf_op jit(solution)/shard_map/attention/pallas_call | solution.py:320
  26.3 0.0 collective-permute-done.4.refs_2_.refs_1_
  26.3 0.0 collective-permute-done.5.refs_1_.refs_2_
  26.3 0.6 collective-permute-done.6.refs_3_
  26.9 1.4 %collective-permute-start.7 = (bf16[2048,256]{1,0:T(8,128)(2,1)}, bf16[2048,256]{1,0:T(8,128)(2,1)}, u32[]{:S(2)}, u32[]{:S(2)}) collective-permute-start(bf16[2048,256]{1,0:T(8,128)(2,1)} %gate.2.refs_0_), channel_id=1, source_target_pairs={{0,8},{4,12},{8,0},{12,4},{1,9},{5,13},{9,1},{13,5},{2,10},{6,14},... | collective-permute-start | bytes 3145736 | tf_op jit(solution)/shard_map/ppermute | solution.py:670
  28.3 1.6 %collective-permute-start = (bf16[912,256]{1,0:T(8,128)(2,1)}, bf16[912,256]{1,0:T(8,128)(2,1)}, u32[]{:S(2)}, u32[]{:S(2)}) collective-permute-start(bf16[912,256]{1,0:T(8,128)(2,1)} %get-tuple-element.31), channel_id=1, source_target_pairs={{0,1},{1,0},{2,3},{3,2},{4,5},{5,4},{6,7},{7,6},{8,9},{9,8},{10,11... | collective-permute-start | bytes 1400840 | tf_op jit(solution)/shard_map/ppermute | solution.py:695
  29.9 5.3 %collective-permute-start.2 = (bf16[912,256]{1,0:T(8,128)(2,1)}, bf16[912,256]{1,0:T(8,128)(2,1)}, u32[]{:S(2)}, u32[]{:S(2)}) collective-permute-start(bf16[912,256]{1,0:T(8,128)(2,1)} %get-tuple-element.37.inner_ref), channel_id=1, source_target_pairs={{0,2},{3,1},{4,6},{7,5},{8,10},{11,9},{12,14},{15,13},{16,18},{19,... | collective-permute-start | bytes 1400840 | tf_op jit(solution)/shard_map/ppermute | solution.py:697
  35.2 1.4 %collective-permute-start.1 = (bf16[912,256]{1,0:T(8,128)(2,1)}, bf16[912,256]{1,0:T(8,128)(2,1)}, u32[]{:S(2)}, u32[]{:S(2)}) collective-permute-start(bf16[912,256]{1,0:T(8,128)(2,1)} %get-tuple-element.32.refs_1_), channel_id=1, source_target_pairs={{1,2},{2,1},{5,6},{6,5},{9,10},{10,9},{13,14},{14,13},{17,18},{18,... | collective-permute-start | bytes 1400840 | tf_op jit(solution)/shard_map/ppermute | solution.py:696
  36.6 3.9 %back.1.end_ref.refs_2_ = bf16[912,256]{1,0:T(8,128)(2,1)} custom-call(bf16[16,256]{1,0:T(8,128)(2,1)} %get-tuple-element.33.centre_ref, bf16[1024,256]{1,0:T(8,128)(2,1)} %get-tuple-element.34.refs_0_, bf16[512,256]{1,0:T(8,128)(2,1)} %get-tuple-element.35.refs_1_, bf16[512,256]{1,0:T(8,128)(2,1)} %get-tuple-element.36.refs_2_, bf16[3584,1024]{1,0:T(8,128)(2,1)} %refs_3_.1, ...), custom_call_target="tpu_custom_call" | custom-call | flops 1000000 | bytes 100000 | tf_op jit(solution)/shard_map/back/pallas_call | solution.py:399
  40.6 1.3 %collective-permute-done.other_ref.refs_3_.refs_0_ = bf16[912,256]{1,0:T(8,128)(2,1)} collective-permute-done((bf16[912,256]{1,0:T(8,128)(2,1)}, bf16[912,256]{1,0:T(8,128)(2,1)}, u32[]{:S(2)}, u32[]{:S(2)}) %collective-permute-start) | collective-permute-done | bytes 466976 | tf_op jit(solution)/shard_map/ppermute | solution.py:695
  41.9 9.1 %collective-permute-done.2.rest_1_.refs_5_.refs_4_ = bf16[912,256]{1,0:T(8,128)(2,1)} collective-permute-done((bf16[912,256]{1,0:T(8,128)(2,1)}, bf16[912,256]{1,0:T(8,128)(2,1)}, u32[]{:S(2)}, u32[]{:S(2)}) %collective-permute-start.2) | collective-permute-done | bytes 466976 | tf_op jit(solution)/shard_map/ppermute | solution.py:697
  51.0 0.0 collective-permute-done.1.rest_0_.refs_4_.refs_3_
  51.0 1.9 %collective-permute-done.7.refs_1_ = bf16[2048,256]{1,0:T(8,128)(2,1)} collective-permute-done((bf16[2048,256]{1,0:T(8,128)(2,1)}, bf16[2048,256]{1,0:T(8,128)(2,1)}, u32[]{:S(2)}, u32[]{:S(2)}) %collective-permute-start.7) | collective-permute-done | bytes 1048608 | tf_op jit(solution)/shard_map/ppermute | solution.py:670
  52.9 0.0 collective-permute-start.8
  52.9 0.5 collective-permute-start.9
  53.4 2.9 %join.1 = (bf16[912,256]{1,0:T(8,128)(2,1)}, f32[8,128]{1,0:T(8,128)}) custom-call(bf16[912,256]{1,0:T(8,128)(2,1)} %get-tuple-element.37.inner_ref, bf16[912,256]{1,0:T(8,128)(2,1)} %collective-permute-done.other_ref.refs_3_.refs_0_, bf16[912,256]{1,0:T(8,128)(2,1)} %back.1.end_ref.refs_2_, bf16[912,256]{1,0:T(8,128)(2,1)} %collective-permute-done.1.rest_0_.refs_4_.refs_3_, ...), custom_call_target="tpu_custom_call" | custom-call | flops 1000000 | bytes 100000 | tf_op jit(solution)/shard_map/join/pallas_call | solution.py:546
  56.3 5.0 %collective-permute-start.3 = (bf16[912,256]{1,0:T(8,128)(2,1)}, bf16[912,256]{1,0:T(8,128)(2,1)}, u32[]{:S(2)}, u32[]{:S(2)}) collective-permute-start(bf16[912,256]{1,0:T(8,128)(2,1)} %get-tuple-element.38), channel_id=1, source_target_pairs={{1,3},{2,0},{0,1},{3,2},{5,7},{6,4},{4,5},{7,6},{9,11},{10,8},{8,9... | collective-permute-start | bytes 1400840 | tf_op jit(solution)/shard_map/ppermute | solution.py:706
  61.3 0.0 collective-permute-done.8.refs_6_
  61.3 0.0 collective-permute-done.9.refs_7_
  61.3 9.8 %weights.1 = (f32[896,1024]{1,0:T(8,128)}, f32[896,512]{1,0:T(8,128)}, f32[896,512]{1,0:T(8,128)}, f32[8,128]{1,0:T(8,128)}) custom-call(bf16[896,256]{1,0:T(8,128)(2,1)} %get-tuple-element.39.refs_0_, bf16[896,256]{1,0:T(8,128)(2,1)} %collective-permute-done.4.refs_2_.refs_1_, bf16[896,256]{1,0:T(8,128)(2,1)} %collective-permute-done.5.refs_1_.refs_2_, ...), custom_call_target="tpu_custom_call" | custom-call | flops 1000000 | bytes 100000 | tf_op jit(solution)/shard_map/weights/pallas_call | solution.py:482
  71.1 2.5 %collective-permute-done.3.refs_5_ = bf16[912,256]{1,0:T(8,128)(2,1)} collective-permute-done((bf16[912,256]{1,0:T(8,128)(2,1)}, bf16[912,256]{1,0:T(8,128)(2,1)}, u32[]{:S(2)}, u32[]{:S(2)}) %collective-permute-start.3) | collective-permute-done | bytes 466976 | tf_op jit(solution)/shard_map/ppermute | solution.py:706
  73.7 3.1 %gains.1 = (f32[1,896]{1,0:T(1,128)}, f32[256,896]{1,0:T(8,128)}) custom-call(bf16[256,896]{1,0:T(8,128)(2,1)} %get-tuple-element.30.input_ref, f32[256,1]{1,0:T(8,128)} %get-tuple-element.29.inverse_ref, bf16[912,256]{1,0:T(8,128)(2,1)} %collective-permute-done.other_ref.refs_3_.refs_0_, bf16[912,256]{1,0:T(8,128)(2,1)} %get-tuple-element.32.refs_1_, ...), custom_call_target="tpu_custom_call" | custom-call | flops 1000000 | bytes 100000 | tf_op jit(solution)/shard_map/gains/pallas_call | solution.py:591
  76.8 0.1 collective-permute-start.12
  76.8 1.2 %collective-permute-start.11 = (f32[1,896]{1,0:T(1,128)}, f32[1,896]{1,0:T(1,128)}, u32[]{:S(2)}, u32[]{:S(2)}) collective-permute-start(f32[1,896]{1,0:T(1,128)} %get-tuple-element.52.refs_0_), channel_id=1, source_target_pairs={{0,8},{4,12},{8,0},{12,4},{1,9},{5,13},{9,1},{13,5},{2,10},{6,14},... | collective-permute-start | bytes 10760 | tf_op jit(solution)/shard_map/ppermute | solution.py:670
  78.0 0.7 collective-permute-start.10
  78.7 2.4 %finish.1.refs_4_ = bf16[256,896]{1,0:T(8,128)(2,1)} custom-call(f32[256,896]{1,0:T(8,128)} %get-tuple-element.47.total_ref, bf16[256,896]{1,0:T(8,128)(2,1)} %get-tuple-element.30.input_ref, f32[1,896]{1,0:T(1,128)} %get-tuple-element.48.gain_ref, f32[256,1]{1,0:T(8,128)} %get-tuple-element.29.inverse_ref, ...), custom_call_target="tpu_custom_call" | custom-call | flops 1000000 | bytes 100000 | tf_op jit(solution)/shard_map/finish/pallas_call | solution.py:628
  81.1 0.0 collective-permute-done.12.refs_3_
  81.1 0.0 collective-permute-done.11.refs_2_
  81.1 0.0 collective-permute-done.10.refs_1_
  81.1 1.3 %total.1 = f32[896]{0:T(1024)} custom-call(f32[1,896]{1,0:T(1,128)} %get-tuple-element.52.refs_0_, f32[1,896]{1,0:T(1,128)} %collective-permute-done.10.refs_1_, f32[1,896]{1,0:T(1,128)} %collective-permute-done.11.refs_2_, f32[1,896]{1,0:T(1,128)} %collective-permute-done.12.refs_3_, bf16[256,896]{1,0:T(8,128)(2,1)} %finish.1.refs_4_), custom_call_target="tpu_custom_call" | custom-call | flops 1000000 | bytes 100000 | tf_op jit(solution)/shard_map/total/pallas_call | solution.py:654
  (2 shorter events, 0.0 us)
Async XLA Ops:
  4.1 22.2 %collective-permute-start.4 = (bf16[896,256]{1,0:T(8,128)(2,1)}, bf16[896,256]{1,0:T(8,128)(2,1)}, u32[]{:S(2)}, u32[]{:S(2)}) collective-permute-start(bf16[896,256]{1,0:T(8,128)(2,1)} %get-tuple-element.40), channel_id=1, source_target_pairs={{0,8},{4,12},{8,0},{12,4},{1,9},{5,13},{9,1},{13,5},{2,10},{6,14},... | collective-permute-start | bytes 1376264 | tf_op jit(solution)/shard_map/ppermute | solution.py:670
  7.0 19.3 %collective-permute-start.5 = (bf16[896,256]{1,0:T(8,128)(2,1)}, bf16[896,256]{1,0:T(8,128)(2,1)}, u32[]{:S(2)}, u32[]{:S(2)}) collective-permute-start(bf16[896,256]{1,0:T(8,128)(2,1)} %get-tuple-element.41), channel_id=1, source_target_pairs={{0,4},{4,0},{8,12},{12,8},{1,5},{5,1},{9,13},{13,9},{2,6},{6,2},{1... | collective-permute-start | bytes 1376264 | tf_op jit(solution)/shard_map/ppermute | solution.py:670
  7.0 19.9 %collective-permute-start.6 = (bf16[896,256]{1,0:T(8,128)(2,1)}, bf16[896,256]{1,0:T(8,128)(2,1)}, u32[]{:S(2)}, u32[]{:S(2)}) collective-permute-start(bf16[896,256]{1,0:T(8,128)(2,1)} %get-tuple-element.42), channel_id=1, source_target_pairs={{0,12},{4,8},{8,4},{12,0},{1,13},{5,9},{9,5},{13,1},{2,14},{6,10},... | collective-permute-start | bytes 1376264 | tf_op jit(solution)/shard_map/ppermute | solution.py:670
  26.9 25.9 %collective-permute-start.7 = (bf16[2048,256]{1,0:T(8,128)(2,1)}, bf16[2048,256]{1,0:T(8,128)(2,1)}, u32[]{:S(2)}, u32[]{:S(2)}) collective-permute-start(bf16[2048,256]{1,0:T(8,128)(2,1)} %gate.2.refs_0_), channel_id=1, source_target_pairs={{0,8},{4,12},{8,0},{12,4},{1,9},{5,13},{9,1},{13,5},{2,10},{6,14},... | collective-permute-start | bytes 3145736 | tf_op jit(solution)/shard_map/ppermute | solution.py:670
  28.3 13.5 %collective-permute-start = (bf16[912,256]{1,0:T(8,128)(2,1)}, bf16[912,256]{1,0:T(8,128)(2,1)}, u32[]{:S(2)}, u32[]{:S(2)}) collective-permute-start(bf16[912,256]{1,0:T(8,128)(2,1)} %get-tuple-element.31), channel_id=1, source_target_pairs={{0,1},{1,0},{2,3},{3,2},{4,5},{5,4},{6,7},{7,6},{8,9},{9,8},{10,11... | collective-permute-start | bytes 1400840 | tf_op jit(solution)/shard_map/ppermute | solution.py:695
  29.9 21.1 %collective-permute-start.2 = (bf16[912,256]{1,0:T(8,128)(2,1)}, bf16[912,256]{1,0:T(8,128)(2,1)}, u32[]{:S(2)}, u32[]{:S(2)}) collective-permute-start(bf16[912,256]{1,0:T(8,128)(2,1)} %get-tuple-element.37.inner_ref), channel_id=1, source_target_pairs={{0,2},{3,1},{4,6},{7,5},{8,10},{11,9},{12,14},{15,13},{16,18},{19,... | collective-permute-start | bytes 1400840 | tf_op jit(solution)/shard_map/ppermute | solution.py:697
  35.2 15.8 %collective-permute-start.1 = (bf16[912,256]{1,0:T(8,128)(2,1)}, bf16[912,256]{1,0:T(8,128)(2,1)}, u32[]{:S(2)}, u32[]{:S(2)}) collective-permute-start(bf16[912,256]{1,0:T(8,128)(2,1)} %get-tuple-element.32.refs_1_), channel_id=1, source_target_pairs={{1,2},{2,1},{5,6},{6,5},{9,10},{10,9},{13,14},{14,13},{17,18},{18,... | collective-permute-start | bytes 1400840 | tf_op jit(solution)/shard_map/ppermute | solution.py:696
  52.9 8.4 %collective-permute-start.8 = (bf16[2048,256]{1,0:T(8,128)(2,1)}, bf16[2048,256]{1,0:T(8,128)(2,1)}, u32[]{:S(2)}, u32[]{:S(2)}) collective-permute-start(bf16[2048,256]{1,0:T(8,128)(2,1)} %get-tuple-element.44.refs_4_), channel_id=1, source_target_pairs={{0,4},{4,0},{8,12},{12,8},{1,5},{5,1},{9,13},{13,9},{2,6},{6,2},{1... | collective-permute-start | bytes 3145736 | tf_op jit(solution)/shard_map/ppermute | solution.py:670
  52.9 8.4 %collective-permute-start.9 = (bf16[2048,256]{1,0:T(8,128)(2,1)}, bf16[2048,256]{1,0:T(8,128)(2,1)}, u32[]{:S(2)}, u32[]{:S(2)}) collective-permute-start(bf16[2048,256]{1,0:T(8,128)(2,1)} %get-tuple-element.45.refs_5_), channel_id=1, source_target_pairs={{0,4},{4,0},{8,12},{12,8},{1,5},{5,1},{9,13},{13,9},{2,6},{6,2},{1... | collective-permute-start | bytes 3145736 | tf_op jit(solution)/shard_map/ppermute | solution.py:670
  56.3 17.4 %collective-permute-start.3 = (bf16[912,256]{1,0:T(8,128)(2,1)}, bf16[912,256]{1,0:T(8,128)(2,1)}, u32[]{:S(2)}, u32[]{:S(2)}) collective-permute-start(bf16[912,256]{1,0:T(8,128)(2,1)} %get-tuple-element.38), channel_id=1, source_target_pairs={{1,3},{2,0},{0,1},{3,2},{5,7},{6,4},{4,5},{7,6},{9,11},{10,8},{8,9... | collective-permute-start | bytes 1400840 | tf_op jit(solution)/shard_map/ppermute | solution.py:706
  76.8 4.3 %collective-permute-start.12 = (f32[1,896]{1,0:T(1,128)}, f32[1,896]{1,0:T(1,128)}, u32[]{:S(2)}, u32[]{:S(2)}) collective-permute-start(f32[1,896]{1,0:T(1,128)} %get-tuple-element.52.refs_0_), channel_id=1, source_target_pairs={{0,12},{4,8},{8,4},{12,0},{1,13},{5,9},{9,5},{13,1},{2,14},{6,10},... | collective-permute-start | bytes 10760 | tf_op jit(solution)/shard_map/ppermute | solution.py:670
  76.8 4.3 %collective-permute-start.11 = (f32[1,896]{1,0:T(1,128)}, f32[1,896]{1,0:T(1,128)}, u32[]{:S(2)}, u32[]{:S(2)}) collective-permute-start(f32[1,896]{1,0:T(1,128)} %get-tuple-element.52.refs_0_), channel_id=1, source_target_pairs={{0,8},{4,12},{8,0},{12,4},{1,9},{5,13},{9,1},{13,5},{2,10},{6,14},... | collective-permute-start | bytes 10760 | tf_op jit(solution)/shard_map/ppermute | solution.py:670
  78.0 3.1 %collective-permute-start.10 = (f32[1,896]{1,0:T(1,128)}, f32[1,896]{1,0:T(1,128)}, u32[]{:S(2)}, u32[]{:S(2)}) collective-permute-start(f32[1,896]{1,0:T(1,128)} %get-tuple-element.52.refs_0_), channel_id=1, source_target_pairs={{0,4},{4,0},{8,12},{12,8},{1,5},{5,1},{9,13},{13,9},{2,6},{6,2},{1... | collective-permute-start | bytes 10760 | tf_op jit(solution)/shard_map/ppermute | solution.py:670
